TPU v7x, 32 devices: a whole 2x2x4 slice. The times are simulated.
32 devices in a mesh: replica: 4 (over z), shard: 4 (over y, x), half: 2 (over core).
Axes of the slice: x: 2, y: 2, z: 4, core: 2. Of those that a mesh axis runs over, the one named last changes fastest.
Arguments:
- images: bfloat16 [64, 24, 24, 768], P(('replica', 'shard'), 'half'), may hold values from -6 to 6
- cotangent: bfloat16 [64, 24, 24, 768], P(('replica', 'shard'), 'half'), may hold values from -6 to 6
- present: int32 [64], P(('replica', 'shard')), may hold values 0 or 1
- threshold: float32 [24], replicated, may hold values from 3 to 12
- inner_weight: bfloat16 [768, 2304], P('shard'), may hold values from -0.3125 to 0.3125
- inner_bias: bfloat16 [1536], P('shard'), may hold values from -3 to 3
- outer_weight: bfloat16 [768, 768], P('shard'), may hold values from -0.625 to 0.625
- outer_bias: bfloat16 [768], P('shard'), may hold values from -2 to 2
- expand_weight: bfloat16 [768, 3072], P('shard'), may hold values from -0.21875 to 0.21875
- expand_bias: bfloat16 [3072], P('shard'), may hold values from -2 to 2
- reduce_weight: bfloat16 [3072, 768], P('shard'), may hold values from -0.15625 to 0.15625
- reduce_bias: bfloat16 [768], P('shard'), may hold values from -2 to 2
- first_gain: bfloat16 [768], P('shard'), may hold values from 0.5 to 1.5
- first_shift: bfloat16 [768], P('shard'), may hold values from -2 to 2
- second_gain: bfloat16 [768], P('shard'), may hold values from 0.5 to 1.5
- second_shift: bfloat16 [768], P('shard'), may hold values from -2 to 2
- bias_table: bfloat16 [529, 24], replicated, may hold values from -4 to 4
Outputs:
- block_out: bfloat16 [64, 24, 24, 768], P(('replica', 'shard'), 'half')
- grad_images: bfloat16 [64, 24, 24, 768], P(('replica', 'shard'), 'half')
- grad_inner_weight: float32 [768, 2304], P('shard')
- grad_inner_bias: float32 [1536], P('shard')
- grad_outer_weight: float32 [768, 768], P('shard')
- grad_outer_bias: float32 [768], P('shard')
- grad_expand_weight: float32 [768, 3072], P('shard')
- grad_expand_bias: float32 [3072], P('shard')
- grad_reduce_weight: float32 [3072, 768], P('shard')
- grad_reduce_bias: float32 [768], P('shard')
- grad_first_gain: float32 [768], P('shard')
- grad_first_shift: float32 [768], P('shard')
- grad_second_gain: float32 [768], P('shard')
- grad_second_shift: float32 [768], P('shard')
- grad_bias_table: float32 [529, 24], replicated
- clipped_inner: bfloat16 [768, 2304], P('shard')
- factors: float32 [24], replicated
- maxima: float32 [24], replicated
All inputs are finite; a program needn't handle non-finite values. No bound on the sum of `present` on one device may be relied on, other than what follows from the above.
Results may differ from a plain program's by a relative error of at most 0.019.
Values may be sent and summed in bfloat16 or wider, within the bound.
No kernel may reach another device: no remote copies, remote signals or barrier semaphores. Data moves between devices by JAX's collectives and lax.ppermute only.
A program may use at most 320 MiB of HBM per device.

v0:
```python
import math

import jax
import jax.numpy as jnp
from jax import lax
from jax.sharding import PartitionSpec as P

D = 768
HEADS = 24
HEAD_DIM = 32
WIN = 12
GRID = 24
SHIFT = 6


EPSILON = 1e-05
MASKED = -100.0
NEGATIVE = -1e30
PRECISE = lax.Precision.HIGHEST


def partner(block, axis, distance):
    count = lax.axis_size(axis)
    route = []
    for low in range(count):
        high = low | 1 << distance
        if high != low and high < count:
            route += [(low, high), (high, low)]
    return lax.ppermute(block, axis, route)


def normalize(rows_in, gain_row, shifts):
    centre = rows_in - jnp.mean(rows_in, axis=-1, keepdims=True)
    inverse = lax.rsqrt(jnp.mean(centre * centre, axis=-1, keepdims=True) + EPSILON)
    scaled = centre * inverse
    return (scaled * gain_row + shifts, scaled, inverse)


def normalize_back(grad_out, gain_row, scaled, inverse):
    grad_scaled = grad_out * gain_row
    plain_mean = jnp.mean(grad_scaled, axis=-1, keepdims=True)
    cross_mean = jnp.mean(grad_scaled * scaled, axis=-1, keepdims=True)
    grad_rows = inverse * (grad_scaled - plain_mean - scaled * cross_mean)
    return (grad_rows, jnp.sum(grad_out * scaled, axis=0), jnp.sum(grad_out, axis=0))


def to_windows(field_in):
    amount = field_in.shape[0]
    across = GRID // WIN
    rolled = jnp.roll(field_in, -SHIFT, axis=2)
    return (
        rolled.reshape(amount, WIN, across, WIN, D)
        .transpose(0, 2, 1, 3, 4)
        .reshape(amount * across * WIN * WIN, D)
    )


def from_windows(flat_rows, amount):
    across = GRID // WIN
    field_out = (
        flat_rows.reshape(amount, across, WIN, WIN, D)
        .transpose(0, 2, 1, 3, 4)
        .reshape(amount, WIN, GRID, D)
    )
    return jnp.roll(field_out, SHIFT, axis=2)


def offset_picker():
    cells = jnp.arange(WIN, dtype=jnp.int32)
    spans_all = jnp.arange(2 * WIN - 1, dtype=jnp.int32)
    return (
        spans_all[None, None, :] == cells[:, None, None] - cells[None, :, None] + WIN - 1
    ).astype(jnp.float32)


def bias_from_table(table_rows, picker):
    grid_table = table_rows.reshape(2 * WIN - 1, 2 * WIN - 1, HEADS)
    partial_rows = jnp.einsum("acu,uvh->acvh", picker, grid_table, precision=PRECISE)
    full_bias = jnp.einsum("acvh,bdv->habcd", partial_rows, picker, precision=PRECISE)
    return full_bias.reshape(HEADS, WIN * WIN, WIN * WIN)


def table_from_bias(grad_heads, picker):
    grid_grad = grad_heads.reshape(HEADS, WIN, WIN, WIN, WIN)
    partial_rows = jnp.einsum("habcd,bdv->hacv", grid_grad, picker, precision=PRECISE)
    grad_grid = jnp.einsum("hacv,acu->uvh", partial_rows, picker, precision=PRECISE)
    return grad_grid.reshape((2 * WIN - 1) * (2 * WIN - 1), HEADS)


def window_masks(half_index):
    across = GRID // WIN
    line_index = jnp.arange(WIN, dtype=jnp.int32) + half_index * WIN
    row_region = (line_index >= GRID - WIN).astype(jnp.int32) + (line_index >= GRID - SHIFT).astype(
        jnp.int32
    )
    col_index = jnp.arange(GRID, dtype=jnp.int32)
    col_region = (col_index >= GRID - WIN).astype(jnp.int32) + (col_index >= GRID - SHIFT).astype(
        jnp.int32
    )
    labels = 3 * row_region[:, None] + col_region[None, :]
    labels = labels.reshape(WIN, across, WIN).transpose(1, 0, 2).reshape(across, WIN * WIN)
    return jnp.where(labels[:, :, None] != labels[:, None, :], MASKED, 0.0).astype(jnp.float32)


def shards(
    images,
    cotangent,
    present,
    threshold,
    inner_weight,
    inner_bias,
    outer_weight,
    outer_bias,
    expand_weight,
    expand_bias,
    reduce_weight,
    reduce_bias,
    first_gain,
    first_shift,
    second_gain,
    second_shift,
    bias_table,
):
    amount = images.shape[0]
    across = GRID // WIN
    scaling = HEAD_DIM ** (-0.5)
    half_index = lax.axis_index("half")
    upper_images, upper_grad = partner((images[:, :SHIFT], cotangent[:, :SHIFT]), "half", 0)
    local_images = jnp.concatenate([images[:, SHIFT:], upper_images], axis=1)
    local_grad = jnp.concatenate([cotangent[:, SHIFT:], upper_grad], axis=1)
    tokens = to_windows(local_images).astype(jnp.float32)
    token_weight = jnp.repeat(present.astype(jnp.float32), WIN * GRID)[:, None]
    grad_rows = to_windows(local_grad).astype(jnp.float32) * token_weight
    gathered = (
        lax.all_gather(inner_weight, "shard", axis=0, tiled=True),
        lax.all_gather(inner_bias, "shard", axis=0, tiled=True),
        lax.all_gather(outer_weight, "shard", axis=0, tiled=True),
        lax.all_gather(outer_bias, "shard", axis=0, tiled=True),
        lax.all_gather(expand_weight, "shard", axis=0, tiled=True),
        lax.all_gather(expand_bias, "shard", axis=0, tiled=True),
        lax.all_gather(reduce_weight, "shard", axis=0, tiled=True),
        lax.all_gather(reduce_bias, "shard", axis=0, tiled=True),
        lax.all_gather(first_gain, "shard", axis=0, tiled=True),
        lax.all_gather(first_shift, "shard", axis=0, tiled=True),
        lax.all_gather(second_gain, "shard", axis=0, tiled=True),
        lax.all_gather(second_shift, "shard", axis=0, tiled=True),
    )
    (
        inner_full,
        inbias_full,
        outer_full,
        outbias_full,
        expand_full,
        upbias_full,
        reduce_full,
        downbias_full,
        gain_first,
        shift_first,
        gain_second,
        shift_second,
    ) = gathered
    picker = offset_picker()
    bias_heads = bias_from_table(bias_table.astype(jnp.float32), picker)
    per_block = 2
    blocks = amount // per_block
    region_masks = jnp.tile(window_masks(half_index), (per_block, 1, 1))
    alive_windows = jnp.repeat(present > 0, across).reshape(blocks, per_block * across)
    normed, scaled_one, inverse_one = normalize(
        tokens, gain_first.astype(jnp.float32), shift_first.astype(jnp.float32)
    )
    first_low = normed.astype(jnp.bfloat16)
    bias_in = jnp.concatenate(
        [inbias_full[:D], jnp.zeros((D,), jnp.bfloat16), inbias_full[D:]]
    ).astype(jnp.float32)
    projected = (
        jnp.dot(first_low, inner_full, preferred_element_type=jnp.float32) + bias_in
    ).astype(jnp.bfloat16)
    heads_view = projected.reshape(blocks, per_block * across, WIN * WIN, 3, HEADS, HEAD_DIM)

    def attend(pieces):
        packed, alive_now = pieces
        queries = packed[:, :, 0]
        key_rows = packed[:, :, 1]
        values = packed[:, :, 2]
        logits = (
            jnp.einsum("wqhd,wkhd->whqk", queries, key_rows, preferred_element_type=jnp.float32)
            * scaling
        )
        peak_now = jnp.max(
            jnp.where(alive_now[:, None, None, None], logits, NEGATIVE), axis=(0, 2, 3)
        )
        scores = logits + bias_heads[None] + region_masks[:, None]
        highest = jnp.max(scores, axis=-1, keepdims=True)
        log_total = jnp.log(jnp.sum(jnp.exp(scores - highest), axis=-1, keepdims=True)) + highest
        weights = jnp.exp(scores - log_total).astype(jnp.bfloat16)
        mixed_out = jnp.einsum(
            "whqk,wkhd->wqhd", weights, values, preferred_element_type=jnp.float32
        )
        return (mixed_out.astype(jnp.bfloat16), log_total[..., 0], peak_now)

    mixed_all, log_totals, peaks = lax.map(attend, (heads_view, alive_windows))
    maxima = lax.pmax(jnp.max(peaks, axis=0), ("replica", "shard", "half"))
    attended = mixed_all.reshape(-1, D)
    middle = (
        tokens
        + jnp.dot(attended, outer_full, preferred_element_type=jnp.float32)
        + outbias_full.astype(jnp.float32)
    )
    normed_two, scaled_two, inverse_two = normalize(
        middle, gain_second.astype(jnp.float32), shift_second.astype(jnp.float32)
    )
    second_low = normed_two.astype(jnp.bfloat16)
    hidden = jnp.dot(
        second_low, expand_full, preferred_element_type=jnp.float32
    ) + upbias_full.astype(jnp.float32)
    active = jax.nn.gelu(hidden, approximate=False).astype(jnp.bfloat16)
    result = (
        middle
        + jnp.dot(active, reduce_full, preferred_element_type=jnp.float32)
        + downbias_full.astype(jnp.float32)
    )
    again = (
        lax.all_gather(inner_weight, "shard", axis=0, tiled=True),
        lax.all_gather(inner_bias, "shard", axis=0, tiled=True),
        lax.all_gather(outer_weight, "shard", axis=0, tiled=True),
        lax.all_gather(outer_bias, "shard", axis=0, tiled=True),
        lax.all_gather(expand_weight, "shard", axis=0, tiled=True),
        lax.all_gather(expand_bias, "shard", axis=0, tiled=True),
        lax.all_gather(reduce_weight, "shard", axis=0, tiled=True),
        lax.all_gather(reduce_bias, "shard", axis=0, tiled=True),
        lax.all_gather(first_gain, "shard", axis=0, tiled=True),
        lax.all_gather(first_shift, "shard", axis=0, tiled=True),
        lax.all_gather(second_gain, "shard", axis=0, tiled=True),
        lax.all_gather(second_shift, "shard", axis=0, tiled=True),
    )
    inner_back = again[0]
    outer_back = again[2]
    expand_back = again[4]
    reduce_back = again[6]
    gain_first_back = again[8].astype(jnp.float32)
    gain_second_back = again[10].astype(jnp.float32)
    gout_low = grad_rows.astype(jnp.bfloat16)
    grad_reduce = jnp.einsum("nf,nd->fd", active, gout_low, preferred_element_type=jnp.float32)
    grad_downbias = jnp.sum(gout_low.astype(jnp.float32), axis=0)
    grad_active = jnp.einsum("nd,fd->nf", gout_low, reduce_back, preferred_element_type=jnp.float32)
    cumulative = 0.5 * (1.0 + lax.erf(hidden * 0.5**0.5))
    density = jnp.exp(-0.5 * hidden * hidden) * (2.0 * math.pi) ** (-0.5)
    grad_hidden = (grad_active * (cumulative + hidden * density)).astype(jnp.bfloat16)
    grad_expand = jnp.einsum(
        "nd,nf->df", second_low, grad_hidden, preferred_element_type=jnp.float32
    )
    grad_upbias = jnp.sum(grad_hidden.astype(jnp.float32), axis=0)
    grad_second = jnp.einsum(
        "nf,df->nd", grad_hidden, expand_back, preferred_element_type=jnp.float32
    )
    grad_norm_two, grad_gain_two, grad_shift_two = normalize_back(
        grad_second, gain_second_back, scaled_two, inverse_two
    )
    grad_middle = grad_rows + grad_norm_two
    grad_branch = grad_middle.astype(jnp.bfloat16)
    grad_outer = jnp.einsum("nd,ne->de", attended, grad_branch, preferred_element_type=jnp.float32)
    grad_outbias = jnp.sum(grad_branch.astype(jnp.float32), axis=0)
    grad_attended = jnp.einsum(
        "ne,de->nd", grad_branch, outer_back, preferred_element_type=jnp.float32
    ).astype(jnp.bfloat16)
    grad_mixed_view = grad_attended.reshape(blocks, per_block * across, WIN * WIN, HEADS, HEAD_DIM)

    def attend_back(pieces):
        packed, grad_mixed, total_now = pieces
        queries = packed[:, :, 0]
        key_rows = packed[:, :, 1]
        values = packed[:, :, 2]
        logits = (
            jnp.einsum("wqhd,wkhd->whqk", queries, key_rows, preferred_element_type=jnp.float32)
            * scaling
        )
        scores = logits + bias_heads[None] + region_masks[:, None]
        weights = jnp.exp(scores - total_now[..., None])
        grad_values = jnp.einsum(
            "whqk,wqhd->wkhd",
            weights.astype(jnp.bfloat16),
            grad_mixed,
            preferred_element_type=jnp.float32,
        )
        grad_weights = jnp.einsum(
            "wqhd,wkhd->whqk", grad_mixed, values, preferred_element_type=jnp.float32
        )
        grad_scores = (
            weights * (grad_weights - jnp.sum(weights * grad_weights, axis=-1, keepdims=True))
        ).astype(jnp.bfloat16)
        grad_queries = (
            jnp.einsum("whqk,wkhd->wqhd", grad_scores, key_rows, preferred_element_type=jnp.float32)
            * scaling
        )
        grad_keys = (
            jnp.einsum("whqk,wqhd->wkhd", grad_scores, queries, preferred_element_type=jnp.float32)
            * scaling
        )
        stacked = jnp.stack([grad_queries, grad_keys, grad_values], axis=2).astype(jnp.bfloat16)
        return (stacked, jnp.sum(grad_scores.astype(jnp.float32), axis=0))

    grad_packed, grad_biases = lax.map(attend_back, (heads_view, grad_mixed_view, log_totals))
    grad_table = table_from_bias(jnp.sum(grad_biases, axis=0), picker)
    grad_projected = grad_packed.reshape(-1, 3 * D)
    grad_inner = jnp.einsum(
        "nd,ne->de", first_low, grad_projected, preferred_element_type=jnp.float32
    )
    column_sums = jnp.sum(grad_projected.astype(jnp.float32), axis=0)
    grad_inbias = jnp.concatenate([column_sums[:D], column_sums[2 * D :]])
    grad_first = jnp.einsum(
        "ne,de->nd", grad_projected, inner_back, preferred_element_type=jnp.float32
    )
    grad_norm_one, grad_gain_one, grad_shift_one = normalize_back(
        grad_first, gain_first_back, scaled_one, inverse_one
    )
    grad_tokens = grad_middle + grad_norm_one
    owned = (
        lax.psum_scatter(
            grad_inner.astype(jnp.bfloat16), "shard", scatter_dimension=0, tiled=True
        ).astype(jnp.float32),
        lax.psum_scatter(
            grad_inbias.astype(jnp.bfloat16), "shard", scatter_dimension=0, tiled=True
        ).astype(jnp.float32),
        lax.psum_scatter(
            grad_outer.astype(jnp.bfloat16), "shard", scatter_dimension=0, tiled=True
        ).astype(jnp.float32),
        lax.psum_scatter(
            grad_outbias.astype(jnp.bfloat16), "shard", scatter_dimension=0, tiled=True
        ).astype(jnp.float32),
        lax.psum_scatter(
            grad_expand.astype(jnp.bfloat16), "shard", scatter_dimension=0, tiled=True
        ).astype(jnp.float32),
        lax.psum_scatter(
            grad_upbias.astype(jnp.bfloat16), "shard", scatter_dimension=0, tiled=True
        ).astype(jnp.float32),
        lax.psum_scatter(
            grad_reduce.astype(jnp.bfloat16), "shard", scatter_dimension=0, tiled=True
        ).astype(jnp.float32),
        lax.psum_scatter(
            grad_downbias.astype(jnp.bfloat16), "shard", scatter_dimension=0, tiled=True
        ).astype(jnp.float32),
        lax.psum_scatter(
            grad_gain_one.astype(jnp.bfloat16), "shard", scatter_dimension=0, tiled=True
        ).astype(jnp.float32),
        lax.psum_scatter(
            grad_shift_one.astype(jnp.bfloat16), "shard", scatter_dimension=0, tiled=True
        ).astype(jnp.float32),
        lax.psum_scatter(
            grad_gain_two.astype(jnp.bfloat16), "shard", scatter_dimension=0, tiled=True
        ).astype(jnp.float32),
        lax.psum_scatter(
            grad_shift_two.astype(jnp.bfloat16), "shard", scatter_dimension=0, tiled=True
        ).astype(jnp.float32),
    )
    finished = (
        lax.psum(owned[0].astype(jnp.bfloat16), ("replica", "half")).astype(jnp.float32),
        lax.psum(owned[1].astype(jnp.bfloat16), ("replica", "half")).astype(jnp.float32),
        lax.psum(owned[2].astype(jnp.bfloat16), ("replica", "half")).astype(jnp.float32),
        lax.psum(owned[3].astype(jnp.bfloat16), ("replica", "half")).astype(jnp.float32),
        lax.psum(owned[4].astype(jnp.bfloat16), ("replica", "half")).astype(jnp.float32),
        lax.psum(owned[5].astype(jnp.bfloat16), ("replica", "half")).astype(jnp.float32),
        lax.psum(owned[6].astype(jnp.bfloat16), ("replica", "half")).astype(jnp.float32),
        lax.psum(owned[7].astype(jnp.bfloat16), ("replica", "half")).astype(jnp.float32),
        lax.psum(owned[8].astype(jnp.bfloat16), ("replica", "half")).astype(jnp.float32),
        lax.psum(owned[9].astype(jnp.bfloat16), ("replica", "half")).astype(jnp.float32),
        lax.psum(owned[10].astype(jnp.bfloat16), ("replica", "half")).astype(jnp.float32),
        lax.psum(owned[11].astype(jnp.bfloat16), ("replica", "half")).astype(jnp.float32),
    )
    table_total = lax.psum(grad_table, ("replica", "shard", "half"))
    factors = threshold / jnp.maximum(maxima, threshold)
    root_factor = jnp.sqrt(factors)
    column_scale = jnp.concatenate(
        [
            jnp.repeat(root_factor, HEAD_DIM),
            jnp.repeat(root_factor, HEAD_DIM),
            jnp.ones((D,), jnp.float32),
        ]
    )
    clipped_inner = (inner_weight.astype(jnp.float32) * column_scale[None, :]).astype(jnp.bfloat16)
    out_local = from_windows(result.astype(jnp.bfloat16), amount)
    grad_local = from_windows(grad_tokens.astype(jnp.bfloat16), amount)
    lower_out, lower_grad = partner((out_local[:, SHIFT:], grad_local[:, SHIFT:]), "half", 0)
    block_out = jnp.concatenate([lower_out, out_local[:, :SHIFT]], axis=1)
    grad_images = jnp.concatenate([lower_grad, grad_local[:, :SHIFT]], axis=1)
    return (
        block_out,
        grad_images,
        finished[0],
        finished[1],
        finished[2],
        finished[3],
        finished[4],
        finished[5],
        finished[6],
        finished[7],
        finished[8],
        finished[9],
        finished[10],
        finished[11],
        table_total,
        clipped_inner,
        factors,
        maxima,
    )


def solution(mesh):
    return jax.shard_map(
        shards,
        mesh=mesh,
        in_specs=(
            P(("replica", "shard"), "half", None, None),
            P(("replica", "shard"), "half", None, None),
            P(("replica", "shard")),
            P(),
            P("shard", None),
            P("shard"),
            P("shard", None),
            P("shard"),
            P("shard", None),
            P("shard"),
            P("shard", None),
            P("shard"),
            P("shard"),
            P("shard"),
            P("shard"),
            P("shard"),
            P(),
        ),
        out_specs=(
            P(("replica", "shard"), "half", None, None),
            P(("replica", "shard"), "half", None, None),
            P("shard", None),
            P("shard"),
            P("shard", None),
            P("shard"),
            P("shard", None),
            P("shard"),
            P("shard", None),
            P("shard"),
            P("shard"),
            P("shard"),
            P("shard"),
            P("shard"),
            P(),
            P("shard", None),
            P(),
            P(),
        ),
        check_vma=False,
    )
```

profile of v0, /device:TPU:0, one launch (start us, length us, event | category | flops | bytes accessed | tf_op | source)
XLA Modules:
  0.0 925.9 jit_solution(4757141041265330461)
XLA Ops:
  23.5 12.1 %copy.89 = f32[24,12,12,12,12]{0,4,3,2,1:T(8,128)} copy(f32[24,12,12,12,12]{0,4,3,1,2:T(8,128)} %convolution_bitcast_fusion) | data formatting | bytes 3981312
  35.6 12.4 %add.457 = f32[24,144,144]{0,2,1:T(8,128)} reshape(f32[24,12,12,12,12]{0,4,3,2,1:T(8,128)} %copy.89) | data formatting | bytes 3981312 | tf_op jit(solution)/shard_map/while/body/eval_jaxpr/add | solution.py:277
  48.0 13.1 %add.446 = f32[24,144,144]{0,2,1:T(8,128)} reshape(f32[24,12,12,12,12]{0,4,3,2,1:T(8,128)} %copy.89) | data formatting | bytes 3981312 | tf_op jit(solution)/shard_map/while/body/eval_jaxpr/add | solution.py:192
  64.3 17.8 %all-reduce.17 = (bf16[768]{0:T(1024)(128)(2,1)S(1)}, bf16[768]{0:T(1024)(128)(2,1)S(1)}, bf16[768]{0:T(1024)(128)(2,1)S(1)}, bf16[768]{0:T(1024)(128)(2,1)S(1)}, bf16[768]{0:T(1024)(128)(2,1)S(1)}) all-reduce(bf16[768]{0:T(1024)(128)(2,1)S(1)} %dynamic-update-slice.1, ...), channel_id=1, replica_groups=mesh['replica'=4,'shard'=4,'half'=2] {'shard'}, use_global_device_ids=true, to_apply=%add.1 | all-reduce | flops 3840 | bytes 15360
  162.3 29.9 %reshape.349 = bf16[2,4,144,3,24,32]{2,1,0,5,4,3:T(4,128)(2,1)} reshape(bf16[1152,2304]{0,1:T(8,128)(2,1)} %copy.85) | data formatting | bytes 10616832 | tf_op jit(solution)/shard_map/reshape | solution.py:178
  201.8 95.1 %while.30 = (s32[]{:T(128)}, bf16[2,4,144,24,32]{2,1,0,4,3:T(4,128)(2,1)}, f32[2,4,24,144]{3,2,1,0:T(8,128)}, f32[2,24]{1,0:T(2,128)}, bf16[2,4,144,3,24,32]{2,5...) while((s32[]{:T(128)}, ...), condition=%wide.wide.region_6.7_spmd.clone, body=%wide.wide.region_2.6_spmd.clone.sunk | while | flops 287082976 | bytes 114807360 | solution.py:201
  203.8 12.0 %copy.172 = f32[24,144,144]{1,2,0:T(8,128)S(1)} copy(f32[24,144,144]{0,2,1:T(8,128)} %get-tuple-element.566) | data formatting | bytes 3981312 | tf_op jit(solution)/shard_map/while/body/eval_jaxpr/add | solution.py:192
  223.9 9.7 %select_reduce_fusion.3 = (f32[24]{0:T(128)S(1)}, f32[4,24,144]{2,1,0:T(8,128)}) fusion(f32[4,24,144,144]{2,3,1,0:T(8,128)S(1)} %get-tuple-element.517, pred[4]{0:T(512)(128)(4,1)S(1)} %dynamic-slice_bitcast_fusion.13, f32[4,24,144]{2,1,0:T(8,128)S(1)} %get-tuple-element.518, f32[4,144,144]{1,2,0:T(8,128)} %bitcast.222, ...), kind=kLoop, calls=%fused_computation.2.clone.clone.1 | loop fusion | flops 13920744 | bytes 10395748 | tf_op jit(solution)/shard_map/while/body/eval_jaxpr/reduce_max | solution.py:189
  251.1 12.0 %copy.172 = f32[24,144,144]{1,2,0:T(8,128)S(1)} copy(f32[24,144,144]{0,2,1:T(8,128)} %get-tuple-element.566) | data formatting | bytes 3981312 | tf_op jit(solution)/shard_map/while/body/eval_jaxpr/add | solution.py:192
  271.2 9.7 %select_reduce_fusion.3 = (f32[24]{0:T(128)S(1)}, f32[4,24,144]{2,1,0:T(8,128)}) fusion(f32[4,24,144,144]{2,3,1,0:T(8,128)S(1)} %get-tuple-element.517, pred[4]{0:T(512)(128)(4,1)S(1)} %dynamic-slice_bitcast_fusion.13, f32[4,24,144]{2,1,0:T(8,128)S(1)} %get-tuple-element.518, f32[4,144,144]{1,2,0:T(8,128)} %bitcast.222, ...), kind=kLoop, calls=%fused_computation.2.clone.clone.1 | loop fusion | flops 13920744 | bytes 10395748 | tf_op jit(solution)/shard_map/while/body/eval_jaxpr/reduce_max | solution.py:189
  310.7 41.6 %fusion.25 = (bf16[1152,3072]{1,0:T(8,128)(2,1)}, f32[1152,3072]{1,0:T(8,128)}) fusion(f32[3072]{0:T(1024)} %bitcast.238, bf16[768,3072]{1,0:T(8,128)(2,1)} %all-gather.11.cloned.1.call-done, f32[1152,768]{1,0:T(8,128)} %copy-done.13, f32[768]{0:T(1024)} %convert_element_type.281, f32[768]{0:T(1024)} %convert_element_type.280, f32[1152]{0:T(1024)} %add_rsqrt_fusion.1, ...), kind=kOutput, calls=%fused_computation.49 | convolution fusion | flops 5673811968 | bytes 29518848 | tf_op jit(solution)/shard_map/dot_general | solution.py:213
  352.3 15.6 %fusion.90 = (bf16[3072]{0:T(1024)(128)(2,1)}, bf16[1152,3072]{1,0:T(8,128)(2,1)}) fusion(f32[1152,3072]{1,0:T(8,128)} %get-tuple-element.325, bf16[3072,768]{1,0:T(8,128)(2,1)} %all-gather.13.cloned.1.call-done, f32[1152,768]{1,0:T(8,128)S(1)} %copy-done.19, f32[1152]{0:T(1024)S(1)} %copy-done.44), kind=kOutput, calls=%fused_computation.176 | convolution fusion | flops 5476512768 | bytes 29501952 | tf_op jit(solution)/shard_map/nd,fd->nf/dot_general | solution.py:245
  394.5 153.2 %while.31 = (s32[]{:T(128)}, bf16[2,4,144,3,24,32]{2,5,4,1,3,0:T(8,128)(2,1)}, f32[2,24,144,144]{3,2,1,0:T(8,128)}, bf16[2,4,144,3,24,32]{2,5,4,1,3,0:T(8,128)(2...) while((s32[]{:T(128)}, ...), condition=%wide.wide.region_14.15_spmd.clone, body=%wide.wide.region_11.14_spmd.clone.sunk | while | flops 670560768 | bytes 193837376 | solution.py:302
  397.6 12.6 %copy.175 = f32[24,144,144]{1,2,0:T(8,128)} copy(f32[24,144,144]{0,2,1:T(8,128)} %get-tuple-element.597) | data formatting | bytes 3981312 | tf_op jit(solution)/shard_map/while/body/eval_jaxpr/add | solution.py:277
  420.3 11.0 %multiply_reduce_fusion.11 = (f32[4,24,144]{2,1,0:T(8,128)S(1)}, f32[4,24,144,144]{2,3,1,0:T(8,128)}) fusion(f32[4,24,144,144]{2,3,1,0:T(8,128)} %fusion.133, f32[4,24,144]{2,1,0:T(8,128)S(1)} %dynamic-slice_bitcast_fusion.15, f32[4,144,144]{1,2,0:T(8,128)S(1)} %bitcast.228, f32[24,144,144]{1,2,0:T(8,128)S(1)} %copy-done.4, ...), kind=kOutput, calls=%fused_computation.22.clone.clone.1 | convolution fusion | flops 139332096 | bytes 23353344 | tf_op jit(solution)/shard_map/while/body/eval_jaxpr/wqhd,wkhd->whqk/dot_general | solution.py:274
  431.3 15.6 %convert_reduce_fusion.4 = (f32[24,144,144]{1,2,0:T(8,128)}, bf16[4,24,144,144]{2,3,1,0:T(8,128)(2,1)}) fusion(f32[4,24,144,144]{2,3,1,0:T(8,128)} %get-tuple-element.532, f32[4,24,144,144]{2,3,1,0:T(8,128)} %fusion.133, f32[4,24,144]{2,1,0:T(8,128)S(1)} %get-tuple-element.533), kind=kLoop, calls=%fused_computation.20.clone.clone.1 | loop fusion | flops 9455616 | bytes 21952512 | tf_op jit(solution)/shard_map/while/body/eval_jaxpr/reduce_sum | solution.py:300
  474.1 12.5 %copy.175 = f32[24,144,144]{1,2,0:T(8,128)} copy(f32[24,144,144]{0,2,1:T(8,128)} %get-tuple-element.597) | data formatting | bytes 3981312 | tf_op jit(solution)/shard_map/while/body/eval_jaxpr/add | solution.py:277
  496.7 11.0 %multiply_reduce_fusion.11 = (f32[4,24,144]{2,1,0:T(8,128)S(1)}, f32[4,24,144,144]{2,3,1,0:T(8,128)}) fusion(f32[4,24,144,144]{2,3,1,0:T(8,128)} %fusion.133, f32[4,24,144]{2,1,0:T(8,128)S(1)} %dynamic-slice_bitcast_fusion.15, f32[4,144,144]{1,2,0:T(8,128)S(1)} %bitcast.228, f32[24,144,144]{1,2,0:T(8,128)S(1)} %copy-done.4, ...), kind=kOutput, calls=%fused_computation.22.clone.clone.1 | convolution fusion | flops 139332096 | bytes 23353344 | tf_op jit(solution)/shard_map/while/body/eval_jaxpr/wqhd,wkhd->whqk/dot_general | solution.py:274
  507.7 15.6 %convert_reduce_fusion.4 = (f32[24,144,144]{1,2,0:T(8,128)}, bf16[4,24,144,144]{2,3,1,0:T(8,128)(2,1)}) fusion(f32[4,24,144,144]{2,3,1,0:T(8,128)} %get-tuple-element.532, f32[4,24,144,144]{2,3,1,0:T(8,128)} %fusion.133, f32[4,24,144]{2,1,0:T(8,128)S(1)} %get-tuple-element.533), kind=kLoop, calls=%fused_computation.20.clone.clone.1 | loop fusion | flops 9455616 | bytes 21952512 | tf_op jit(solution)/shard_map/while/body/eval_jaxpr/reduce_sum | solution.py:300
  547.8 12.3 %copy.98 = bf16[2,4,144,3,24,32]{2,1,0,5,4,3:T(4,128)(2,1)} copy(bf16[2,4,144,3,24,32]{2,5,4,1,3,0:T(8,128)(2,1)} %get-tuple-element.107) | data formatting | bytes 10616832 | tf_op jit(solution)/shard_map/while | solution.py:302
  560.1 17.8 %reshape.355 = bf16[1152,2304]{0,1:T(8,128)(2,1)} reshape(bf16[2,4,144,3,24,32]{2,1,0,5,4,3:T(4,128)(2,1)} %copy.98) | data formatting | bytes 10616832 | tf_op jit(solution)/shard_map/reshape | solution.py:304
  588.8 11.4 %convolution_convert_fusion.1 = bf16[768,3072]{1,0:T(8,128)(2,1)} fusion(bf16[1152,3072]{1,0:T(8,128)(2,1)} %get-tuple-element.328, f32[1152,768]{1,0:T(8,128)S(1)} %copy-done.15, f32[768]{0:T(1024)} %convert_element_type.281, f32[768]{0:T(1024)} %convert_element_type.280, f32[1152]{0:T(1024)S(1)} %copy-done.47, f32[1152]{0:T(1024)S(1)} %copy-done.41), kind=kOutput, calls=%fused_computation.75 | convolution fusion | flops 5442600960 | bytes 15350784 | tf_op jit(solution)/shard_map/nd,nf->df/dot_general | solution.py:249
  602.3 12.1 %convolution_convert_fusion = bf16[3072,768]{1,0:T(8,128)(2,1)} fusion(bf16[1152,3072]{1,0:T(8,128)(2,1)} %get-tuple-element.324, f32[1152,768]{1,0:T(8,128)S(1)} %copy-done.21, f32[1152]{0:T(1024)S(1)} %copy-done.45), kind=kOutput, calls=%fused_computation.74 | convolution fusion | flops 5439946752 | bytes 15340032 | tf_op jit(solution)/shard_map/nf,nd->fd/dot_general | solution.py:243
  621.0 40.3 %pmax.7 = f32[24]{0:T(128)S(1)} all-reduce(f32[24]{0:T(128)} %reduce_max.27), channel_id=1, replica_groups=mesh['replica'=4,'shard'=4,'half'=2] {'replica','shard','half'}, use_global_device_ids=true, to_apply=%region_52.53 | all-reduce | flops 24 | bytes 192 | tf_op jit(solution)/shard_map/pmax | solution.py:202
  664.9 11.2 %multiply_reduce_fusion.2 = (bf16[768]{0:T(1024)(128)(2,1)}, f32[1152]{0:T(1024)S(1)}, f32[1152]{0:T(1024)S(1)}, bf16[768]{0:T(1024)(128)(2,1)}, f32[1152,768]{1,0:T(8,128)S(1)}) fusion(f32[1152,768]{1,0:T(8,128)} %copy-done.10, f32[1152]{0:T(1024)} %rsqrt.21, f32[1152]{0:T(1024)S(1)} %copy-done.49, f32[768]{0:T(1024)S(1)} %copy-done.43, ...), kind=kOutput, calls=%fused_computation.82 | convolution fusion | flops 4084822272 | bytes 15949824 | tf_op jit(solution)/shard_map/ne,de->nd/dot_general | solution.py:310
  693.1 17.8 %all-reduce.16 = (bf16[768]{0:T(1024)(128)(2,1)S(1)}, bf16[1536]{0:T(1024)(128)(2,1)S(1)}, bf16[768]{0:T(1024)(128)(2,1)}, bf16[3072]{0:T(1024)(128)(2,1)}, bf16...) all-reduce(bf16[768]{0:T(1024)(128)(2,1)} %copy-done.52, ...), channel_id=1, replica_groups=mesh['replica'=4,'shard'=4,'half'=2] {'shard'}, use_global_device_ids=true, to_apply=%add.5 | all-reduce | flops 9984 | bytes 39936
  710.9 10.5 %fusion.41 = bf16[1152,768]{1,0:T(8,128)(2,1)} fusion(f32[1152,768]{1,0:T(8,128)S(1)} %copy-done.16, bf16[1152,3072]{1,0:T(8,128)(2,1)} %get-tuple-element.324, bf16[3072,768]{1,0:T(8,128)(2,1)} %all-gather.13.cloned.1.call-done, f32[768]{0:T(1024)S(1)} %convert_element_type.285), kind=kOutput, calls=%fused_computation.94 | convolution fusion | flops 5438472192 | bytes 17107968 | tf_op jit(solution)/shard_map/dot_general | solution.py:219
  721.4 34.4 %reduce-scatter.11.cloned.1.call-done = bf16[768,768]{1,0:T(8,128)(2,1)} async-done(((bf16[3072,768]{1,0:T(8,128)(2,1)}), bf16[768,768]{1,0:T(8,128)(2,1)}) %reduce-scatter.11.cloned.1.call-update) | async-done | bytes 1179664 | tf_op jit(solution)/shard_map/reduce_scatter | solution.py:336
  770.9 16.0 %reshape.410 = f32[24,12,12,12,12]{4,3,2,1,0:T(8,128)} reshape(f32[24,144,144]{2,1,0:T(8,128)S(1)} %reduce_sum.205) | data formatting | bytes 3981312 | tf_op jit(solution)/shard_map/reshape | solution.py:84
  786.9 39.6 %fusion.57 = f32[24,12,12,23]{0,3,2,1:T(8,128)S(1)} fusion(f32[24,12,12,12,12]{4,3,2,1,0:T(8,128)} %reshape.410, s32[12,12]{1,0:T(8,128)S(1)} %copy-done.39), kind=kOutput, calls=%fused_computation.126 | convolution fusion | flops 137358576 | bytes 2309184 | tf_op jit(solution)/shard_map/habcd,bdv->hacv/dot_general | solution.py:85
  834.4 18.0 %all-reduce.14 = (bf16[384]{0:T(512)(128)(2,1)}, bf16[192]{0:T(256)(128)(2,1)}, bf16[768]{0:T(1024)(128)(2,1)}, bf16[192]{0:T(256)(128)(2,1)}, bf16[192]{0:T(256...) all-reduce(bf16[384]{0:T(512)(128)(2,1)S(1)} %dynamic-slice.7, ...), channel_id=1, replica_groups=mesh['replica'=4,'shard'=4,'half'=2] {'replica','half'}, use_global_device_ids=true, to_apply=%region_21.22 | all-reduce | flops 2304 | bytes 9216 | tf_op jit(solution)/shard_map/psum | solution.py:357
  865.3 38.3 %psum.103 = f32[529,24]{0,1:T(8,128)} all-reduce(f32[529,24]{0,1:T(8,128)S(1)} %reshape.359), channel_id=1, replica_groups=mesh['replica'=4,'shard'=4,'half'=2] {'replica','shard','half'}, use_global_device_ids=true, to_apply=%region_50.51 | all-reduce | flops 12696 | bytes 101568 | tf_op jit(solution)/shard_map/psum | solution.py:369
  (383 shorter events, 362.5 us)
Async XLA Ops:
  7.2 137.8 %all-gather.7.cloned.1.call-start = ((), (), s32[]{:S(2)}) async-start(), calls=%async_computation.4 | async-start | bytes 4423680 | tf_op jit(solution)/shard_map/all_gather | solution.py:135
  7.9 296.1 %all-gather.9.cloned.1.call-start = ((), (), s32[]{:S(2)}) async-start(), calls=%async_computation.5 | async-start | bytes 1474560 | tf_op jit(solution)/shard_map/all_gather | solution.py:137
  8.7 302.0 %all-gather.11.cloned.1.call-start = ((), (), s32[]{:S(2)}) async-start(), calls=%async_computation.6 | async-start | bytes 5898240 | tf_op jit(solution)/shard_map/all_gather | solution.py:139
  9.4 342.8 %all-gather.13.cloned.1.call-start = ((), (), s32[]{:S(2)}) async-start(), calls=%async_computation.7 | async-start | bytes 5898240 | tf_op jit(solution)/shard_map/all_gather | solution.py:141
  9.6 92.9 %collective-permute-start = (bf16[4,6,24,768]{3,2,1,0:T(8,128)(2,1)S(1)}, bf16[4,6,24,768]{3,2,1,0:T(8,128)(2,1)S(1)}, u32[]{:S(2)}, u32[]{:S(2)}) collective-permute-start(bf16[4,6,24,768]{3,2,1,0:T(8,128)(2,1)S(1)} %get-tuple-element.317), channel_id=1, source_target_pairs={{0,1},{1,0},{2,3},{3,2},{4,5},{5,4},{6,7},{7,6},{8,9},{9,8},{10,11... | collective-permute-start | bytes 2654216 | tf_op jit(solution)/shard_map/ppermute | solution.py:29
  12.3 116.4 %collective-permute-start.2 = (bf16[4,6,24,768]{3,2,1,0:T(8,128)(2,1)}, bf16[4,6,24,768]{3,2,1,0:T(8,128)(2,1)}, u32[]{:S(2)}, u32[]{:S(2)}) collective-permute-start(bf16[4,6,24,768]{3,2,1,0:T(8,128)(2,1)} %get-tuple-element.315), channel_id=1, source_target_pairs={{0,1},{1,0},{2,3},{3,2},{4,5},{5,4},{6,7},{7,6},{8,9},{9,8},{10,11... | collective-permute-start | bytes 2654216 | tf_op jit(solution)/shard_map/ppermute | solution.py:29
  12.8 708.6 %reduce-scatter.7.cloned.1.call-start = ((), (), s32[]{:S(2)}) async-start(), calls=%async_computation.9 | async-start | bytes 1474560 | tf_op jit(solution)/shard_map/reduce_scatter | solution.py:324
  12.8 78.3 %copy-start.54 = (f32[4]{0:T(128)}, f32[4]{0:T(128)S(1)}, u32[]{:S(2)}) copy-start(f32[4]{0:T(128)S(1)} %convert_element_type.291) | copy-start | bytes 52
  48.0 34.1 %copy-start.56 = (bf16[768]{0:T(1024)(128)(2,1)S(1)}, bf16[768]{0:T(1024)(128)(2,1)}, u32[]{:S(2)}) copy-start(bf16[768]{0:T(1024)(128)(2,1)} %param.30) | copy-start | bytes 4612
  82.2 62.8 %copy-start.42 = (f32[768]{0:T(1024)}, f32[768]{0:T(1024)S(1)}, u32[]{:S(2)}) copy-start(f32[768]{0:T(1024)S(1)} %convert_element_type.270) | copy-start | bytes 9220
  114.2 30.8 %copy-start.48 = (f32[1152]{0:T(1024)}, f32[1152]{0:T(1024)S(1)}, u32[]{:S(2)}) copy-start(f32[1152]{0:T(1024)S(1)} %div.30) | copy-start | bytes 13828
  307.7 69.9 %copy-start.40 = (f32[1152]{0:T(1024)}, f32[1152]{0:T(1024)S(1)}, u32[]{:S(2)}) copy-start(f32[1152]{0:T(1024)S(1)} %broadcast_multiply_fusion.5) | copy-start | bytes 13828
  310.6 41.6 %copy-start.19 = (f32[1152,768]{1,0:T(8,128)S(1)}, f32[1152,768]{1,0:T(8,128)}, u32[]{:S(2)}) copy-start(f32[1152,768]{1,0:T(8,128)} %reshape.362) | copy-start | bytes 10616836
  310.6 41.6 %copy-start.44 = (f32[1152]{0:T(1024)S(1)}, f32[1152]{0:T(1024)}, u32[]{:S(2)}) copy-start(f32[1152]{0:T(1024)} %mul.211) | copy-start | bytes 13828
  382.7 338.7 %reduce-scatter.5.cloned.1.call-start = ((), (), s32[]{:S(2)}) async-start(), calls=%async_computation.8 | async-start | bytes 4423680 | tf_op jit(solution)/shard_map/reduce_scatter | solution.py:318
  431.3 17.1 %copy-start = (f32[4,24,144,144]{2,3,1,0:T(8,128)S(1)}, f32[4,24,144,144]{2,3,1,0:T(8,128)}, u32[]{:S(2)}) copy-start(f32[4,24,144,144]{2,3,1,0:T(8,128)} %get-tuple-element.532) | copy-start | bytes 23887876 | tf_op jit(solution)/shard_map/while
  507.7 17.1 %copy-start = (f32[4,24,144,144]{2,3,1,0:T(8,128)S(1)}, f32[4,24,144,144]{2,3,1,0:T(8,128)}, u32[]{:S(2)}) copy-start(f32[4,24,144,144]{2,3,1,0:T(8,128)} %get-tuple-element.532) | copy-start | bytes 23887876 | tf_op jit(solution)/shard_map/while
  560.1 17.9 %copy-start.34 = (bf16[1152,768]{1,0:T(8,128)(2,1)S(1)}, bf16[1152,768]{1,0:T(8,128)(2,1)}, u32[]{:S(2)}) copy-start(bf16[1152,768]{1,0:T(8,128)(2,1)} %convert_element_type.298) | copy-start | bytes 5308420
  586.8 134.6 %reduce-scatter.9.cloned.1.call-start = ((), (), s32[]{:S(2)}) async-start(), calls=%async_computation.10 | async-start | bytes 5898240 | tf_op jit(solution)/shard_map/reduce_scatter | solution.py:330
  600.3 155.5 %reduce-scatter.11.cloned.1.call-start = ((), (), s32[]{:S(2)}) async-start(), calls=%async_computation.11 | async-start | bytes 5898240 | tf_op jit(solution)/shard_map/reduce_scatter | solution.py:336
  614.4 50.4 %copy-start.43 = (f32[768]{0:T(1024)S(1)}, f32[768]{0:T(1024)}, u32[]{:S(2)}) copy-start(f32[768]{0:T(1024)} %copy-done.42) | copy-start | bytes 9220
  614.4 50.4 %copy-start.49 = (f32[1152]{0:T(1024)S(1)}, f32[1152]{0:T(1024)}, u32[]{:S(2)}) copy-start(f32[1152]{0:T(1024)} %copy-done.48) | copy-start | bytes 13828
  614.4 296.8 %all-reduce.20.cloned.1.call-start = ((), (), s32[]{:S(2)}) async-start(), calls=%async_computation.12 | async-start | bytes 7077888 | tf_op jit(solution)/shard_map/psum | solution.py:356
  617.7 58.4 %copy-start.52 = (bf16[768]{0:T(1024)(128)(2,1)}, bf16[768]{0:T(1024)(128)(2,1)S(1)}, u32[]{:S(2)}) copy-start(bf16[768]{0:T(1024)(128)(2,1)S(1)} %dynamic-update-slice.5) | copy-start | bytes 4612
  684.8 26.1 %copy-start.16 = (f32[1152,768]{1,0:T(8,128)S(1)}, f32[1152,768]{1,0:T(8,128)}, u32[]{:S(2)}) copy-start(f32[1152,768]{1,0:T(8,128)} %copy-done.13) | copy-start | bytes 10616836
  721.3 34.5 %copy-start.22 = (bf16[4,12,18,768]{3,0,2,1:T(4,128)(2,1)S(1)}, bf16[4,12,18,768]{3,0,2,1:T(4,128)(2,1)}, u32[]{:S(2)}) copy-start(bf16[4,12,18,768]{3,0,2,1:T(4,128)(2,1)} %slice.137) | copy-start | bytes 3981316
  721.3 34.5 %copy-start.26 = (bf16[4,12,6,768]{3,0,2,1:T(4,128)(2,1)S(1)}, bf16[4,12,6,768]{3,0,2,1:T(4,128)(2,1)}, u32[]{:S(2)}) copy-start(bf16[4,12,6,768]{3,0,2,1:T(4,128)(2,1)} %slice.136) | copy-start | bytes 1327108
  767.6 136.0 %collective-permute-start.3 = (bf16[4,6,24,768]{3,0,2,1:T(4,128)(2,1)}, bf16[4,6,24,768]{3,0,2,1:T(4,128)(2,1)}, u32[]{:S(2)}, u32[]{:S(2)}) collective-permute-start(bf16[4,6,24,768]{3,0,2,1:T(4,128)(2,1)} %fusion.63), channel_id=1, source_target_pairs={{0,1},{1,0},{2,3},{3,2},{4,5},{5,4},{6,7},{7,6},{8,9},{9,8},{10,11... | collective-permute-start | bytes 2654216 | tf_op jit(solution)/shard_map/ppermute | solution.py:29
  770.4 16.4 %copy-start.39 = (s32[12,12]{1,0:T(8,128)S(1)}, s32[12,12]{1,0:T(8,128)}, u32[]{:S(2)}) copy-start(s32[12,12]{1,0:T(8,128)} %copy-done.38) | copy-start | bytes 1732
  770.4 137.1 %collective-permute-start.1 = (bf16[4,6,24,768]{3,0,2,1:T(4,128)(2,1)}, bf16[4,6,24,768]{3,0,2,1:T(4,128)(2,1)}, u32[]{:S(2)}, u32[]{:S(2)}) collective-permute-start(bf16[4,6,24,768]{3,0,2,1:T(4,128)(2,1)} %fusion.64), channel_id=1, source_target_pairs={{0,1},{1,0},{2,3},{3,2},{4,5},{5,4},{6,7},{7,6},{8,9},{9,8},{10,11... | collective-permute-start | bytes 2654216 | tf_op jit(solution)/shard_map/ppermute | solution.py:29
  826.5 77.1 %copy-start.23 = (bf16[4,12,18,768]{3,0,2,1:T(4,128)(2,1)S(1)}, bf16[4,12,18,768]{3,0,2,1:T(4,128)(2,1)}, u32[]{:S(2)}) copy-start(bf16[4,12,18,768]{3,0,2,1:T(4,128)(2,1)} %slice.137) | copy-start | bytes 3981316
  826.5 77.1 %copy-start.27 = (bf16[4,12,6,768]{3,0,2,1:T(4,128)(2,1)S(1)}, bf16[4,12,6,768]{3,0,2,1:T(4,128)(2,1)}, u32[]{:S(2)}) copy-start(bf16[4,12,6,768]{3,0,2,1:T(4,128)(2,1)} %slice.136) | copy-start | bytes 1327108
  (62 other events, 479.5 us)
Sparse Core Ops, SparseCore 0:
  9.9 49.9 all-gather.6
  61.7 27.8 all-gather.8
  91.4 57.0 all-gather.10
  150.2 57.0 all-gather.12
  382.8 28.6 reduce-scatter.6
  587.0 47.8 reduce-scatter.4
  637.8 57.7 reduce-scatter.8
  698.6 57.1 reduce-scatter.10
  758.5 85.5 all-reduce.19
where the time goes:
time: 936 us; the launch traced here: 926 us
  local copies, waits for them, and re-layouts  314 us (34%)
  matrix products  280 us (30%)
  blocking collectives  148 us (16%)
  other arithmetic  127 us (14%)
  waiting for transfers between devices  36.6 us (4%)
  between operations  18.2 us (2%)
    unnamed x142, local copies, waits for them, and re-layouts  43.5 us
    dot_general x1, matrix products, shards(): jnp.dot(second_low, expand_full, preferred_element_type=jnp.float32)  41.6 us
    pmax x1, blocking collectives, shards(): maxima = lax.pmax(jnp.max(peaks, axis=0), ('replica', 'shard', 'half'))  40.3 us
    dot_general x1, matrix products, table_from_bias(): jnp.einsum('habcd,bdv->hacv', grid_grad, picker, precision=PRECISE)  39.6 us
    psum x1, blocking collectives, shards(): table_total = lax.psum(grad_table, ('replica', 'shard', 'half'))  38.3 us
    add x3, local copies, waits for them, and re-layouts, attend_back(): scores = logits + bias_heads[None] + region_masks[:, None]  37.5 us
    add x3, local copies, waits for them, and re-layouts, attend(): scores = logits + bias_heads[None] + region_masks[:, None]  37.1 us
    unnamed x2, blocking collectives  35.6 us
  transfers between devices with their start and end apart: 13, of which 1 were waited for; matrix products, arithmetic and copies ran while one was open for 72% of the time, Pallas kernels for 0%

commit v1 on v0

v1 whole, which is shorter than its diff:
```python
import functools
import math

import numpy as np
import jax
import jax.numpy as jnp
from jax import lax
from jax.experimental import pallas as pl
from jax.experimental.pallas import tpu as pltpu
from jax.sharding import PartitionSpec as P

D = 768
HEADS = 24
HD = 32
WIN = 12
GRID = 24
SHIFT = 6
FF = 3072
TOK = WIN * WIN
ROWS = WIN * GRID
SPAN = 2 * WIN - 1
EPS = 1e-5
MASKED = -100.0
NEGATIVE = -1e30
LOG2E = math.log2(math.e)
BF = jnp.bfloat16
F32 = jnp.float32
MB = 1 << 20
OWN = 192
CH = 384
WIDE = 640
NARROW = 384
TALL = WIN * 16
HB = 4
LB = HB * HD
NB = 384
ONE = dict(pipeline_mode=pl.Buffered(1))
SD = jax.ShapeDtypeStruct


def nn(a, b):
    return lax.dot_general(a, b, (((1,), (0,)), ((), ())), preferred_element_type=F32)


def nt(a, b):
    return lax.dot_general(a, b, (((1,), (1,)), ((), ())), preferred_element_type=F32)


def tn(a, b):
    return lax.dot_general(a, b, (((0,), (0,)), ((), ())), preferred_element_type=F32)


def full(shape, **kw):
    return pl.BlockSpec(shape, lambda *_: (0,) * len(shape), **kw)


def any_space():
    return pl.BlockSpec(memory_space=pl.ANY)


def smem():
    return pl.BlockSpec(memory_space=pltpu.SMEM)


def params(limit=60):
    return pltpu.CompilerParams(vmem_limit_bytes=limit * MB)


def cost(flops, moved, exps=0):
    return pl.CostEstimate(flops=int(flops), bytes_accessed=int(moved), transcendentals=int(exps))


def colsum(v):
    return jnp.sum(v, axis=0, keepdims=True)


def norm_parts(x):
    c = x - jnp.mean(x, axis=-1, keepdims=True)
    r = lax.rsqrt(jnp.mean(c * c, axis=-1, keepdims=True) + EPS)
    return c * r, r


def row_order():
    cells = np.arange(ROWS)
    win, rest = cells // TOK, cells % TOK
    a, b = rest // WIN, rest % WIN
    m = np.zeros((ROWS, ROWS), np.float32)
    m[cells, a * GRID + (win * WIN + b + SHIFT) % GRID] = 1
    return m


def spread_q(reverse):
    q = np.arange(TOK)
    s = SPAN * (q // WIN) + q % WIN
    if reverse:
        s = SPAN * (WIN - 1) + WIN - 1 - s
    m = np.zeros((TOK, NARROW), np.float32)
    m[q, s] = 1
    return m


def spread_k():
    k = np.arange(TOK)
    m = np.zeros((TALL, TOK), np.float32)
    m[16 * (k // WIN) + k % WIN, k] = 1
    return m


def start_pieces(refs, at, target, sems):
    for i, ref in enumerate(refs):
        rows = pl.ds(pl.multiple_of(at[i], 16), ref.shape[0])
        pltpu.make_async_copy(ref, target.at[rows, :], sems.at[i]).start()


def wait_pieces(refs, at, target, sems):
    for i, ref in enumerate(refs):
        rows = pl.ds(pl.multiple_of(at[i], 16), ref.shape[0])
        pltpu.make_async_copy(ref, target.at[rows, :], sems.at[i]).wait()


def bias_kernel(table_ref, mask_ref, sq_ref, sk_ref, out_ref, tall):
    for h in range(HEADS):
        row = pltpu.roll(jnp.broadcast_to(table_ref[h : h + 1, :], (16, WIDE)), 0, 1, stride=1, stride_axis=0)
        for a in range(WIN):
            off = (SPAN * a - SPAN * (WIN - 1) - (WIN - 1)) % WIDE
            tall[16 * a : 16 * a + 16, :] = pltpu.roll(row, off, 1)[:, :NARROW].astype(BF)
        wide = nn(tall[...], sq_ref[...]).astype(BF)
        bias = nn(sk_ref[...], wide)
        for w in range(2):
            out_ref[w, h] = (bias + mask_ref[w]) * LOG2E


def bias_call(table, half):
    t = jnp.pad(table.astype(F32).T, ((0, 0), (0, WIDE - table.shape[0])))
    line = jnp.arange(WIN, dtype=jnp.int32) + half * WIN
    row = (line >= GRID - WIN).astype(jnp.int32) + (line >= GRID - SHIFT).astype(jnp.int32)
    col = np.arange(GRID)
    col = (col >= GRID - WIN).astype(np.int32) + (col >= GRID - SHIFT).astype(np.int32)
    lab = 3 * row[:, None] + jnp.asarray(col)[None, :]
    lab = lab.reshape(WIN, 2, WIN).transpose(1, 0, 2).reshape(2, TOK)
    mask = jnp.where(lab[:, :, None] != lab[:, None, :], MASKED, 0.0).astype(F32)
    return pl.pallas_call(
        bias_kernel,
        out_shape=SD((2, HEADS, TOK, TOK), F32),
        scratch_shapes=[pltpu.VMEM((TALL, NARROW), BF)],
        compiler_params=params(40),
        cost_estimate=cost(4e9, 8 * MB),
        name="bias",
    )(t, mask, jnp.asarray(spread_q(False).T, BF), jnp.asarray(spread_k().T, BF))


def table_kernel(db_ref, sq_ref, sk_ref, out_ref):
    def split(v):
        hi = v.astype(BF)
        return hi, (v - hi.astype(F32)).astype(BF)

    for h in range(HEADS):
        hi, lo = split(db_ref[h])
        tall = nn(sk_ref[...], hi) + nn(sk_ref[...], lo)
        hi, lo = split(tall)
        wide = nn(hi, sq_ref[...]) + nn(lo, sq_ref[...])
        wide = jnp.concatenate([wide, jnp.zeros((TALL, WIDE - NARROW), F32)], axis=1)
        tot = jnp.zeros((16, WIDE), F32)
        for a in range(WIN):
            tot = tot + pltpu.roll(wide[16 * a : 16 * a + 16, :], SPAN * a, 1)
        tot = pltpu.roll(tot, 0, 1, stride=1, stride_axis=0)
        out_ref[h : h + 1, :] = colsum(tot)


def table_call(db):
    return pl.pallas_call(
        table_kernel,
        out_shape=SD((HEADS, WIDE), F32),
        compiler_params=params(40),
        cost_estimate=cost(4e9, 4 * MB),
        name="table",
    )(db, jnp.asarray(spread_q(True), BF), jnp.asarray(spread_k(), BF))


def lane_head(shape):
    return lax.broadcasted_iota(jnp.int32, shape, len(shape) - 1) // HD


def attend_kernel(np_, own_ref, recv_ref, pm_ref, gain_ref, shift_ref, b_ref, bm_ref, at_ref, *rest):
    pieces = rest[:np_]
    tok_ref, n1_ref, proj_ref, pt_ref, att_ref, peak_ref, w_ref, sems = rest[np_:]

    @pl.when(pl.program_id(0) == 0)
    def _():
        start_pieces(pieces, at_ref, w_ref, sems)

    x = jnp.concatenate([own_ref[0, TOK:, :], recv_ref[0]], axis=0)
    tok = nn(pm_ref[...], x)
    tok_ref[0] = tok.astype(BF)
    xh, _ = norm_parts(tok)
    n1_ref[0] = (xh * gain_ref[...] + shift_ref[...]).astype(BF)

    @pl.when(pl.program_id(0) == 0)
    def _():
        wait_pieces(pieces, at_ref, w_ref, sems)

    n1 = n1_ref[0]
    for c in range(0, 3 * D, D):
        proj_ref[0, :, c : c + D] = (nn(n1, w_ref[:, c : c + D]) + b_ref[:, c : c + D]).astype(BF)
    hid = lane_head((TOK, LB))
    scale = HD**-0.5
    for w in range(2):
        r = slice(w * TOK, (w + 1) * TOK)
        for blk in range(D // LB):
            l = blk * LB
            q = proj_ref[0, r, l : l + LB]
            k = proj_ref[0, r, D + l : D + l + LB]
            v = proj_ref[0, r, 2 * D + l : 2 * D + l + LB]
            vt = v.T
            outs = []
            for h in range(HB):
                hh = blk * HB + h
                km = jnp.where(hid == h, k, jnp.zeros_like(k))
                st = nt(km, q)
                peak_ref[0, w, hh : hh + 1, :] = jnp.max(st, axis=0, keepdims=True) * scale
                t = st * (scale * LOG2E) + bm_ref[w, hh]
                e = jnp.exp2(t - jnp.max(t, axis=0, keepdims=True))
                p = (e * (1.0 / colsum(e))).astype(BF)
                pt_ref[0, w, hh] = p
                outs.append(nn(vt[HD * h : HD * h + HD, :], p))
            att_ref[0, r, l : l + LB] = jnp.concatenate(outs, axis=0).astype(BF).T


def attend_call(own, recv, pm, gain, shift, b, bm, at, pieces):
    n = own.shape[0]

    def blk(*s):
        return pl.BlockSpec((1,) + s, lambda i: (i,) + (0,) * len(s))

    return pl.pallas_call(
        functools.partial(attend_kernel, len(pieces)),
        grid=(n,),
        in_specs=[blk(ROWS, D), blk(TOK, D), full((ROWS, ROWS)), full((1, D)), full((1, D)), full((1, 3 * D)),
                  full((2, HEADS, TOK, TOK), **ONE), smem()] + [any_space()] * len(pieces),
        out_specs=[blk(ROWS, D), blk(ROWS, D), blk(ROWS, 3 * D), blk(2, HEADS, TOK, TOK), blk(ROWS, D), blk(2, HEADS, TOK)],
        out_shape=[SD((n, ROWS, D), BF), SD((n, ROWS, D), BF), SD((n, ROWS, 3 * D), BF),
                   SD((n, 2, HEADS, TOK, TOK), BF), SD((n, ROWS, D), BF), SD((n, 2, HEADS, TOK), F32)],
        scratch_shapes=[pltpu.VMEM((D, 3 * D), BF), pltpu.SemaphoreType.DMA((len(pieces),))],
        compiler_params=params(),
        cost_estimate=cost(4e10, 30 * MB, 4e6),
        name="attend",
    )(own, recv, pm, gain, shift, b, bm, at, *pieces)


def gelu_parts(h):
    d = 1.0 + (0.3275911 * 0.5**0.5) * jnp.abs(h)
    t = pl.reciprocal(d, approx=True)
    t = t * (2.0 - d * t)
    e = jnp.exp2(h * h * (-0.5 * LOG2E))
    p = (((0.5 * 1.061405429) * t - 0.5 * 1.453152027) * t + 0.5 * 1.421413741) * t - 0.5 * 0.284496736
    p = (p * t + 0.5 * 0.254829592) * t * e
    cdf = jnp.where(h >= 0, 1.0 - p, p)
    return cdf, cdf + h * (e * ((2 * math.pi) ** -0.5))


def middle_kernel(na, nb_, spot_ref, tok_ref, att_ref, gown_ref, grecv_ref, alive_ref, pm_ref, pmt_ref, ob_ref, gain_ref,
                  shift_ref, rb_ref, eb_ref, ata_ref, atb_ref, *rest):
    pa, pb = rest[:na], rest[na : na + nb_]
    (stay_ref, send_ref, gmid_ref, datt_ref, os_ref, ok_ref, es_ref, ek_ref, rs_ref, rk_ref, geb_ref, small_ref,
     wa, wb, mid, n2, g, n2t, acc, e2, act, gh, sema, semb) = rest[na + nb_ :]
    j = pl.program_id(0)
    n = tok_ref.shape[0]
    N = n * ROWS
    me = spot_ref[0]
    core = spot_ref[1]

    @pl.when(j == 0)
    def _():
        start_pieces(pa, ata_ref, wa, sema)
        start_pieces(pb, atb_ref, wb, semb)
        tot = jnp.zeros((1, D), F32)
        for i in range(n):
            s = slice(i * ROWS, (i + 1) * ROWS)
            x = jnp.concatenate([gown_ref[i, TOK:, :], grecv_ref[i]], axis=0)
            gi = nn(pm_ref[...], x) * alive_ref[0:1, i : i + 1]
            tot = tot + colsum(gi)
            g[s, :] = gi.astype(BF)
        small_ref[0:1, :] = tot
        wait_pieces(pa, ata_ref, wa, sema)
        for i in range(n):
            s = slice(i * ROWS, (i + 1) * ROWS)
            m = tok_ref[i].astype(F32) + nn(att_ref[i], wa[:, :D]) + ob_ref[...]
            mid[s, :] = m
            xh, _ = norm_parts(m)
            x2 = (xh * gain_ref[...] + shift_ref[...]).astype(BF)
            n2[s, :] = x2
            n2t[:, s] = x2.T
            acc[s, :] = m + rb_ref[...]
            e2[s, :] = jnp.zeros((ROWS, D), F32)
        wait_pieces(pb, atb_ref, wb, semb)

    sh = jnp.bitwise_xor(me, j % 4)
    at = (2 * sh + jnp.bitwise_xor(core, 1 - j // 4)) * CH
    ecol = pl.ds(pl.multiple_of(D + at, 128), CH)
    rrow = pl.ds(pl.multiple_of(at, CH), CH)
    tot = jnp.zeros((1, CH), F32)
    for s0 in range(0, N, NB):
        s = slice(s0, s0 + NB)
        h = nn(n2[s, :], wa[:, ecol]) + eb_ref[0]
        cdf, dg = gelu_parts(h)
        act[s, :] = (h * cdf).astype(BF)
        x = (nt(g[s, :], wb[rrow, :]) * dg).astype(BF)
        gh[s, :] = x
        tot = tot + colsum(x.astype(F32))
    geb_ref[0] = tot
    ge = nn(n2t[...], gh[...]).astype(BF)
    gr = tn(act[...], g[...]).astype(BF)

    def put(e_ref, r_ref):
        for b in range(4):
            e_ref[jnp.bitwise_xor(me, b), 0] = ge[b * OWN : (b + 1) * OWN, :]
            r_ref[0, b] = gr[(b // 2) * OWN : (b // 2 + 1) * OWN, (b % 2) * CH : (b % 2 + 1) * CH]

    @pl.when(j < 4)
    def _():
        put(es_ref, rs_ref)

    @pl.when(j >= 4)
    def _():
        put(ek_ref, rk_ref)

    for s0 in range(0, N, NB):
        s = slice(s0, s0 + NB)
        acc[s, :] += nn(act[s, :], wb[rrow, :])
        e2[s, :] += nt(gh[s, :], wa[:, ecol])

    @pl.when(j == 7)
    def _():
        gn = jnp.zeros((1, D), F32)
        shf = gn
        ob = gn
        for i in range(n):
            s = slice(i * ROWS, (i + 1) * ROWS)
            o = nn(pmt_ref[...], acc[s, :].astype(BF)).astype(BF)
            stay_ref[i] = o[:TOK]
            send_ref[i] = o[TOK:]
            xh, r = norm_parts(mid[s, :])
            d = e2[s, :]
            gn = gn + colsum(d * xh)
            shf = shf + colsum(d)
            d = d * gain_ref[...]
            gm = g[s, :].astype(F32) + r * (
                d - jnp.mean(d, axis=-1, keepdims=True) - xh * jnp.mean(d * xh, axis=-1, keepdims=True)
            )
            gmid_ref[i] = gm
            gb = gm.astype(BF)
            ob = ob + colsum(gb.astype(F32))
            g[s, :] = gb
            datt_ref[i] = nt(gb, wa[:, :D]).astype(BF)
            n2[s, :] = att_ref[i]
        for c, ref in ((1 - core, os_ref), (core, ok_ref)):
            go = tn(n2[...], g[:, pl.ds(pl.multiple_of(c * CH, 128), CH)]).astype(BF)
            for b in range(4):
                ref[jnp.bitwise_xor(me, b), 0] = go[b * OWN : (b + 1) * OWN, :]
        small_ref[1:2, :] = gn
        small_ref[2:3, :] = shf
        small_ref[3:4, :] = ob
        small_ref[4:8, :] = jnp.zeros((4, D), F32)


def middle_call(spot, tok, att, gown, grecv, alive, pm, pmt, ob, gain, shift, rb, eb, ata, pa, atb, pb):
    n = tok.shape[0]
    N = n * ROWS
    blocks = SD((4, 4, OWN, CH), BF)

    def chunk(j, spot):
        return 2 * jnp.bitwise_xor(spot[0], j % 4) + jnp.bitwise_xor(spot[1], 1 - j // 4)

    def early(j, spot):
        return jnp.bitwise_xor(spot[0], jnp.minimum(j, 3))

    def late(j, spot):
        return jnp.bitwise_xor(spot[0], jnp.maximum(j, 4) - 4)

    grid_spec = pltpu.PrefetchScalarGridSpec(
        num_scalar_prefetch=1,
        grid=(8,),
        in_specs=[full((n, ROWS, D), **ONE), full((n, ROWS, D), **ONE), full((n, ROWS, D), **ONE), full((n, TOK, D), **ONE),
                  full((1, n)), full((ROWS, ROWS)), full((ROWS, ROWS)), full((1, D)), full((1, D)), full((1, D)), full((1, D)),
                  pl.BlockSpec((1, 1, CH), lambda j, spot: (chunk(j, spot), 0, 0)), smem(), smem()]
        + [any_space()] * (len(pa) + len(pb)),
        out_specs=[full((n, TOK, D), **ONE), full((n, TOK, D), **ONE), full((n, ROWS, D), **ONE), full((n, ROWS, D), **ONE),
                   full((4, 1, OWN, CH), **ONE), full((4, 1, OWN, CH), **ONE),
                   pl.BlockSpec((4, 1, OWN, CH), lambda j, spot: (0, early(j, spot), 0, 0)),
                   pl.BlockSpec((4, 1, OWN, CH), lambda j, spot: (0, late(j, spot), 0, 0)),
                   pl.BlockSpec((1, 4, OWN, CH), lambda j, spot: (jnp.minimum(j, 3), 0, 0, 0)),
                   pl.BlockSpec((1, 4, OWN, CH), lambda j, spot: (jnp.maximum(j, 4) - 4, 0, 0, 0)),
                   pl.BlockSpec((1, 1, CH), lambda j, spot: (chunk(j, spot), 0, 0)), full((8, D))],
        scratch_shapes=[pltpu.VMEM((D, D + FF), BF), pltpu.VMEM((FF, D), BF),
                        pltpu.VMEM((N, D), F32), pltpu.VMEM((N, D), BF), pltpu.VMEM((N, D), BF), pltpu.VMEM((D, N), BF),
                        pltpu.VMEM((N, D), F32), pltpu.VMEM((N, D), F32), pltpu.VMEM((N, CH), BF), pltpu.VMEM((N, CH), BF),
                        pltpu.SemaphoreType.DMA((len(pa),)), pltpu.SemaphoreType.DMA((len(pb),))],
    )
    return pl.pallas_call(
        functools.partial(middle_kernel, len(pa), len(pb)),
        grid_spec=grid_spec,
        out_shape=[SD((n, TOK, D), BF), SD((n, TOK, D), BF), SD((n, ROWS, D), F32), SD((n, ROWS, D), BF),
                   SD((4, 1, OWN, CH), BF), SD((4, 1, OWN, CH), BF), blocks, blocks, blocks, blocks,
                   SD((8, 1, CH), F32), SD((8, D), F32)],
        compiler_params=params(62),
        cost_estimate=cost(6e10, 40 * MB, 7e6),
        name="middle",
    )(spot, tok, att, gown, grecv, alive, pm, pmt, ob, gain, shift, rb, eb, ata, atb, *pa, *pb)


def back_kernel(proj_ref, pt_ref, da_ref, gp_ref, db_ref):
    @pl.when(pl.program_id(0) == 0)
    def _():
        db_ref[...] = jnp.zeros_like(db_ref)

    hid = lane_head((TOK, LB))
    scale = HD**-0.5
    for w in range(2):
        r = slice(w * TOK, (w + 1) * TOK)
        for blk in range(D // LB):
            l = blk * LB
            q = proj_ref[0, r, l : l + LB]
            k = proj_ref[0, r, D + l : D + l + LB]
            v = proj_ref[0, r, 2 * D + l : 2 * D + l + LB]
            do = da_ref[0, r, l : l + LB]
            qt, kt, dt = q.T, k.T, do.T
            dq, dk, dv = [], [], []
            for h in range(HB):
                hh = blk * HB + h
                s = slice(HD * h, HD * h + HD)
                dp = nt(jnp.where(hid == h, v, jnp.zeros_like(v)), do)
                pb = pt_ref[0, w, hh]
                p = pb.astype(F32)
                pd = p * dp
                ds = pd - p * colsum(pd)
                db_ref[hh] += ds
                dsb = ds.astype(BF)
                dq.append(nn(kt[s, :], dsb))
                dk.append(nt(qt[s, :], dsb))
                dv.append(nt(dt[s, :], pb))
            gp_ref[0, r, l : l + LB] = (jnp.concatenate(dq, axis=0) * scale).astype(BF).T
            gp_ref[0, r, D + l : D + l + LB] = (jnp.concatenate(dk, axis=0) * scale).astype(BF).T
            gp_ref[0, r, 2 * D + l : 2 * D + l + LB] = jnp.concatenate(dv, axis=0).astype(BF).T


def back_call(proj, pt, da):
    n = proj.shape[0]

    def blk(*s):
        return pl.BlockSpec((1,) + s, lambda i: (i,) + (0,) * len(s))

    return pl.pallas_call(
        back_kernel,
        grid=(n,),
        in_specs=[blk(ROWS, 3 * D), blk(2, HEADS, TOK, TOK), blk(ROWS, D)],
        out_specs=[blk(ROWS, 3 * D), full((HEADS, TOK, TOK))],
        out_shape=[SD((n, ROWS, 3 * D), BF), SD((HEADS, TOK, TOK), F32)],
        compiler_params=params(),
        cost_estimate=cost(5e10, 30 * MB),
        name="attend_back",
    )(proj, pt, da)


def inner_kernel(spot_ref, n1_ref, gp_ref, is_ref, ik_ref, gb_ref):
    me = spot_ref[0]
    core = spot_ref[1]
    n = n1_ref.shape[0]
    gp = gp_ref[...].reshape(n * ROWS, D)
    gb_ref[0] = colsum(gp.astype(F32))
    gi = tn(n1_ref[...].reshape(n * ROWS, D), gp).astype(BF)

    for c in range(2):
        @pl.when(core == c)
        def _():
            for b in range(4):
                r = slice(b * OWN, (b + 1) * OWN)
                ik_ref[jnp.bitwise_xor(me, b), 0] = gi[r, c * CH : (c + 1) * CH]
                is_ref[jnp.bitwise_xor(me, b), 0] = gi[r, (1 - c) * CH : (2 - c) * CH]


def inner_call(spot, n1, gp):
    n = n1.shape[0]
    out = pl.BlockSpec((4, 1, OWN, CH), lambda j: (0, j, 0, 0))
    return pl.pallas_call(
        inner_kernel,
        grid=(3,),
        in_specs=[smem(), full((n, ROWS, D), **ONE), pl.BlockSpec((n, ROWS, D), lambda j: (0, 0, j))],
        out_specs=[out, out, pl.BlockSpec((1, 1, D), lambda j: (j, 0, 0))],
        out_shape=[SD((4, 3, OWN, CH), BF), SD((4, 3, OWN, CH), BF), SD((3, 1, D), F32)],
        compiler_params=params(),
        cost_estimate=cost(8e9, 15 * MB),
        name="inner_grad",
    )(spot, n1, gp)


def last_kernel(np_, tok_ref, gp_ref, gmid_ref, gain_ref, pmt_ref, at_ref, *rest):
    pieces = rest[:np_]
    small_ref, stay_ref, send_ref, w_ref, sems = rest[np_:]
    i = pl.program_id(0)

    @pl.when(i == 0)
    def _():
        start_pieces(pieces, at_ref, w_ref, sems)
        wait_pieces(pieces, at_ref, w_ref, sems)
        small_ref[...] = jnp.zeros_like(small_ref)

    d = nt(gp_ref[0], w_ref[...])
    xh, r = norm_parts(tok_ref[0].astype(F32))
    small_ref[0:1, :] += colsum(d * xh)
    small_ref[1:2, :] += colsum(d)
    d = d * gain_ref[...]
    gm = gmid_ref[0] + r * (d - jnp.mean(d, axis=-1, keepdims=True) - xh * jnp.mean(d * xh, axis=-1, keepdims=True))
    o = nn(pmt_ref[...], gm.astype(BF)).astype(BF)
    stay_ref[0] = o[:TOK]
    send_ref[0] = o[TOK:]


def last_call(tok, gp, gmid, gain, pmt, at, pieces):
    n = tok.shape[0]

    def blk(*s):
        return pl.BlockSpec((1,) + s, lambda i: (i,) + (0,) * len(s))

    return pl.pallas_call(
        functools.partial(last_kernel, len(pieces)),
        grid=(n,),
        in_specs=[blk(ROWS, D), blk(ROWS, 3 * D), blk(ROWS, D), full((1, D)), full((ROWS, ROWS)), smem()]
        + [any_space()] * len(pieces),
        out_specs=[full((8, D)), blk(TOK, D), blk(TOK, D)],
        out_shape=[SD((8, D), F32), SD((n, TOK, D), BF), SD((n, TOK, D), BF)],
        scratch_shapes=[pltpu.VMEM((D, 3 * D), BF), pltpu.SemaphoreType.DMA((len(pieces),))],
        compiler_params=params(),
        cost_estimate=cost(1e10, 20 * MB),
        name="last",
    )(tok, gp, gmid, gain, pmt, at, *pieces)


def swap(block, axis, bit):
    count = lax.axis_size(axis)
    return lax.ppermute(block, axis, [(i, i ^ bit) for i in range(count) if i ^ bit < count])


def everywhere(value, op):
    for axis in ("half", "shard", "replica"):
        bit = 1
        while bit < lax.axis_size(axis):
            value = op(value, swap(value, axis, bit))
            bit *= 2
    return value


def gather_rows(own, me, core):
    rows = own.shape[0]
    mine = lax.dynamic_slice_in_dim(own, core * (rows // 2), rows // 2, 0)
    by_x = swap(mine, "shard", 1)
    by_y = swap(mine, "shard", 2)
    far_a = swap(by_x[: rows // 4], "shard", 2)
    far_b = swap(by_y[rows // 4 :], "shard", 1)
    got = [by_x, by_y, far_a, far_b]
    other = [swap(v, "half", 1) for v in got]
    at = [me * rows]
    for c in (core, 1 - core):
        base = c * (rows // 2)
        at += [(me ^ 1) * rows + base, (me ^ 2) * rows + base, (me ^ 3) * rows + base, (me ^ 3) * rows + base + rows // 4]
    return [own] + got + other, jnp.stack(at).astype(jnp.int32)


def add(a, b):
    return (a.astype(F32) + b.astype(F32)).astype(BF)


def reduce_blocks(send, keep, replica):
    hlf = OWN // 2
    t = add(keep, swap(send, "half", 1))
    tx = jnp.stack([t[1, :, :hlf], t[3, :, :hlf]])
    ty = jnp.stack([t[2, :, hlf:], t[3, :, hlf:]])
    a = add(jnp.stack([t[0, :, :hlf], t[2, :, :hlf]]), swap(tx, "shard", 1))
    b = add(jnp.stack([t[0, :, hlf:], t[1, :, hlf:]]), swap(ty, "shard", 2))
    z0 = add(a[0], swap(a[1], "shard", 2))
    z1 = add(b[0], swap(b[1], "shard", 1))
    low = (replica & 1) == 0
    u = add(jnp.where(low, z0, z1), swap(jnp.where(low, z1, z0), "replica", 1))
    q = hlf // 2
    low2 = (replica & 2) == 0
    v = add(jnp.where(low2, u[:, :q], u[:, q:]), swap(jnp.where(low2, u[:, q:], u[:, :q]), "replica", 2))
    w = swap(v, "replica", 2)
    u = jnp.concatenate([jnp.where(low2, v, w), jnp.where(low2, w, v)], axis=1)
    w = swap(u, "replica", 1)
    z = jnp.concatenate([jnp.where(low, u, w), jnp.where(low, w, u)], axis=1)
    return z, swap(z, "half", 1)


def shards(images, cotangent, present, threshold, inner_weight, inner_bias, outer_weight, outer_bias, expand_weight,
           expand_bias, reduce_weight, reduce_bias, first_gain, first_shift, second_gain, second_shift, bias_table):
    n = images.shape[0]
    core = lax.axis_index("half")
    shard = lax.axis_index("shard")
    replica = lax.axis_index("replica")
    shard_count = lax.axis_size("shard")
    quick = shard_count == 4 and lax.axis_size("replica") == 4
    own_images = images.reshape(n, ROWS, D)
    own_grad = cotangent.reshape(n, ROWS, D)
    upper_images = swap(own_images[:, :TOK], "half", 1)
    vectors = (inner_bias, outer_bias, expand_bias, reduce_bias, first_gain, first_shift, second_gain, second_shift)
    outer_expand = jnp.concatenate([outer_weight, expand_weight], axis=1)
    if quick:
        me = shard
        packed = jnp.concatenate(vectors).reshape(1, -1)
        near = [packed] + [swap(packed, "shard", bit) for bit in (1, 2, 3)]
        packed = jnp.concatenate([lax.dynamic_index_in_dim(jnp.stack(near), me ^ s, 0, False) for s in range(4)], axis=0)
        inner_pieces, inner_at = gather_rows(inner_weight, me, core)
        outer_pieces, outer_at = gather_rows(outer_expand, me, core)
        reduce_pieces, reduce_at = gather_rows(reduce_weight, me, core)
    else:
        me = jnp.int32(0)
        packed = lax.all_gather(jnp.concatenate(vectors), "shard", axis=0)
        zero = jnp.zeros((1,), jnp.int32)
        inner_pieces, inner_at = [lax.all_gather(inner_weight, "shard", axis=0, tiled=True)], zero
        outer_pieces, outer_at = [lax.all_gather(outer_expand, "shard", axis=0, tiled=True)], zero
        reduce_pieces, reduce_at = [lax.all_gather(reduce_weight, "shard", axis=0, tiled=True)], zero
    wide, start = [], 0
    for v in vectors:
        wide.append(packed[:, start : start + v.shape[0]].reshape(1, -1))
        start += v.shape[0]
    in_bias, out_bias, up_bias, down_bias, gain_1, shift_1, gain_2, shift_2 = (v.astype(F32) for v in wide)
    upper_grad = swap(own_grad[:, :TOK], "half", 1)
    spot = jnp.stack([me, core]).astype(jnp.int32)
    order = jnp.asarray(row_order(), BF)
    back_order = jnp.asarray(row_order().T, BF)
    bias_all = jnp.concatenate([in_bias[:, :D], jnp.zeros((1, D), F32), in_bias[:, D:]], axis=1)

    bias_masks = bias_call(bias_table, core)
    tok, n1, proj, pt, att, peak = attend_call(
        own_images, upper_images, order, gain_1, shift_1, bias_all, bias_masks, inner_at, inner_pieces
    )
    alive = present.astype(F32).reshape(1, n)
    (stay, send, gmid, datt, out_send, out_keep, e_send, e_keep, r_send, r_keep, grad_up, small) = middle_call(
        spot, tok, att, own_grad, upper_grad, alive, order, back_order, out_bias, gain_2, shift_2, down_bias,
        up_bias.reshape(8, 1, CH), outer_at, outer_pieces, reduce_at, reduce_pieces
    )
    lower_out = swap(send, "half", 1)
    gp, db = back_call(proj, pt, datt)
    table = table_call(db)
    i_send, i_keep, in_sums = inner_call(spot, n1, gp)
    small_one, gstay, gsend = last_call(tok, gp, gmid, gain_1, back_order, inner_at, inner_pieces)
    lower_grad = swap(gsend, "half", 1)

    peaks = jnp.max(jnp.where((present > 0)[:, None, None, None], peak, NEGATIVE), axis=(0, 1, 3))
    maxima = everywhere(peaks, jnp.maximum)
    sums = jnp.concatenate(
        [grad_up.reshape(-1), small[:4].reshape(-1), in_sums.reshape(-1), table.reshape(-1)]
    ).reshape(1, -1)
    sums = everywhere(sums, jnp.add).reshape(-1)
    sums_one = everywhere(small_one, jnp.add)

    def part(vec):
        size = vec.shape[0] // shard_count
        return lax.dynamic_slice_in_dim(vec, shard * size, size, 0)

    grad_up = sums[:FF]
    small = sums[FF : FF + 4 * D].reshape(4, D)
    at = FF + 4 * D
    grad_inbias = jnp.concatenate([sums[at : at + D], sums[at + 2 * D : at + 3 * D]])
    at += 3 * D
    grad_table = sums[at : at + HEADS * WIDE].reshape(HEADS, WIDE)[:, : SPAN * SPAN][:, ::-1].T

    def halves(mine, other, axis):
        lo = jnp.where(core == 0, mine, other)
        hi = jnp.where(core == 0, other, mine)
        return jnp.concatenate([lo, hi], axis=axis).astype(F32)

    if quick:
        er = reduce_blocks(jnp.concatenate([r_send, e_send, out_send], axis=1), jnp.concatenate([r_keep, e_keep, out_keep], axis=1), replica)
        ii = reduce_blocks(i_send, i_keep, replica)
        grad_reduce = halves(*(v[:4].reshape(2, 2, OWN, CH).transpose(0, 2, 1, 3).reshape(CH, D) for v in er), 0)
        grad_expand = halves(*(v[4:8].transpose(1, 0, 2)[:, :, None] for v in er), 2).reshape(OWN, FF)
        grad_outer = halves(*(v[8] for v in er), 1)
        grad_inner = halves(*(v.transpose(1, 0, 2)[:, :, None] for v in ii), 2).reshape(OWN, 3 * D)
    else:
        def whole(other, mine):
            both = halves(mine[:, :, :, None], other[:, :, :, None], 3)
            return both.transpose(0, 2, 1, 3, 4).reshape(D, -1)

        def settle(v):
            v = lax.psum_scatter(v.astype(BF), "shard", scatter_dimension=0, tiled=True)
            return lax.psum(v, ("replica", "half")).astype(F32)

        def rows_of(v):
            return v.reshape(4, 1, 2, 2, OWN, CH).transpose(0, 1, 2, 4, 3, 5).reshape(4, 1, CH, D)

        grad_reduce = settle(halves(rows_of(r_keep), rows_of(r_send), 1).reshape(FF, D))
        grad_expand = settle(whole(e_send, e_keep))
        grad_outer = settle(whole(out_send, out_keep))
        grad_inner = settle(whole(i_send, i_keep))

    factors = threshold / jnp.maximum(maxima, threshold)
    root = jnp.repeat(jnp.sqrt(factors), HD)
    column_scale = jnp.concatenate([root, root, jnp.ones((D,), F32)])
    clipped = (inner_weight.astype(F32) * column_scale[None, :]).astype(BF)
    block_out = jnp.concatenate([lower_out, stay], axis=1).reshape(images.shape)
    grad_images = jnp.concatenate([lower_grad, gstay], axis=1).reshape(images.shape)
    return (
        block_out,
        grad_images,
        grad_inner,
        part(grad_inbias),
        grad_outer,
        part(small[3]),
        grad_expand,
        part(grad_up),
        grad_reduce,
        part(small[0]),
        part(sums_one[0]),
        part(sums_one[1]),
        part(small[1]),
        part(small[2]),
        grad_table,
        clipped,
        factors,
        maxima,
    )


def solution(mesh):
    rows = P(("replica", "shard"), "half", None, None)
    cut = P("shard", None)
    line = P("shard")
    return jax.shard_map(
        shards,
        mesh=mesh,
        in_specs=(rows, rows, P(("replica", "shard")), P(), cut, line, cut, line, cut, line, cut, line, line, line, line,
                  line, P()),
        out_specs=(rows, rows, cut, line, cut, line, cut, line, cut, line, line, line, line, line, P(), cut, P(), P()),
        check_vma=False,
    )
```

time: 936 us -> 496 us (0.53)
  matrix products: 280 us -> 0 us
  local copies, waits for them, and re-layouts: 314 us -> 58.8 us
  Pallas kernels: 0 us -> 221 us
  blocking collectives: 148 us -> 0 us
  other arithmetic: 127 us -> 35.4 us
  waiting for transfers between devices: 36.6 us -> 111 us
  starting transfers between devices: 1.88 us -> 61.3 us
  between operations: 18.2 us -> 2.24 us
    dot_general x30 -> x0, matrix products: 280 us -> none  [the longest x1 41.6 us: shards(): jnp.dot(second_low, expand_full, preferred_element_type=jnp.float32)]
    pallas_call x0 -> x7, Pallas kernels: none -> 221 us  [the longest x1 83.8 us: middle_call(): pl.pallas_call(functools.partial(middle_kernel, len(pa), len(pb)), grid_s...]
    ppermute x4 -> x66, waiting for transfers between devices: 0.01 us -> 111 us  [swap(): lax.ppermute(block, axis, [(i, i ^ bit) for i in range(count) if i ^ bit...]
    reshape x11 -> x7, local copies, waits for them, and re-layouts: 82.2 us -> 2.25 us  [the longest x1 1.47 us: shards(): sums[at:at + HEADS * WIDE].reshape(HEADS, WIDE)[:, :SPAN * SPAN][:, ::-1]]
    add x10 -> x4, local copies, waits for them, and re-layouts: 74.8 us -> 0.92 us  [bias_call(): lab = 3 * row[:, None] + jnp.asarray(col)[None, :]]
    ppermute x4 -> x66, starting transfers between devices: 1.52 us -> 61.3 us  [swap(): lax.ppermute(block, axis, [(i, i ^ bit) for i in range(count) if i ^ bit...]
    psum x2 -> x0, blocking collectives: 56.3 us -> none  [the longest x1 38.3 us: shards(): table_total = lax.psum(grad_table, ('replica', 'shard', 'half'))]
    reduce_sum x9 -> x0, other arithmetic: 49.6 us -> none  [the longest x2 31.2 us: attend_back(): return (stacked, jnp.sum(grad_scores.astype(jnp.float32), axis=0))]
  transfers between devices with their start and end apart: 13 -> 66, of which waited for: 1 -> 21; matrix products, arithmetic and copies ran while one was open for 72% -> 13% of each run, Pallas kernels for 0% -> 12%
where the time goes in v1:
time: 496 us; the launch traced here: 490 us
  Pallas kernels  221 us (45%)
  waiting for transfers between devices  111 us (22%)
  starting transfers between devices  61.3 us (12%)
  local copies, waits for them, and re-layouts  58.8 us (12%)
  other arithmetic  35.4 us (7%)
    ppermute x66, waiting for transfers between devices, swap(): lax.ppermute(block, axis, [(i, i ^ bit) for i in range(count) if i ^ bit...  111 us
    pallas_call x1, Pallas kernels, middle_call(): pl.pallas_call(functools.partial(middle_kernel, len(pa), len(pb)), grid_s...  83.8 us
    ppermute x66, starting transfers between devices, swap(): lax.ppermute(block, axis, [(i, i ^ bit) for i in range(count) if i ^ bit...  61.3 us
    pallas_call x1, Pallas kernels, back_call(): pl.pallas_call(back_kernel, grid=(n,), in_specs=[blk(ROWS, 3 * D), blk(2,...  56 us
    pallas_call x1, Pallas kernels, attend_call(): pl.pallas_call(functools.partial(attend_kernel, len(pieces)), grid=(n,),...  46.8 us
    pallas_call x1, Pallas kernels, last_call(): pl.pallas_call(functools.partial(last_kernel, len(pieces)), grid=(n,), in...  14.4 us
    unnamed x91, local copies, waits for them, and re-layouts  13.3 us
    convert_element_type x4, local copies, waits for them, and re-layouts, halves(): return jnp.concatenate([lo, hi], axis=axis).astype(F32)  11.3 us
  transfers between devices with their start and end apart: 66, of which 21 were waited for; matrix products, arithmetic and copies ran while one was open for 13% of the time, Pallas kernels for 12%

profile of v1, /device:TPU:0, one launch (start us, length us, event | category | flops | bytes accessed | tf_op | source)
XLA Modules:
  0.0 489.7 jit_solution(14942229115861226189)
XLA Ops:
  0.7 5.6 %concatenate.57 = bf16[2304]{0:T(1024)(128)(2,1)S(1)} concatenate(bf16[384]{0:T(512)(128)(2,1)} %param.29, bf16[192]{0:T(256)(128)(2,1)} %param.31, bf16[768]{0:T(1024)(128)(2,1)} %param.33, bf16[192]{0:T(256)(128)(2,1)} %param.35, bf16[192]{0:T(256)(128)(2,1)} %param.36, bf16[192]{0:T(256)(128)(2,1)} %param.37, bf16[192]{0:T(256)(128)(2,1)} %param.38, bf16[192]{0:T(256)(128)(2,1)} %param.39), dimensions={0} | concatenate | bytes 9216 | tf_op jit(solution)/shard_map/concatenate | solution.py:608
  6.8 3.9 collective-permute-start.3
  20.1 6.3 %bias.1.bm_ref = f32[2,24,144,144]{3,2,1,0:T(8,128)S(1)} custom-call(f32[24,640]{1,0:T(8,128)S(1)} %pad_convert_fusion.table_ref, f32[2,144,144]{2,1,0:T(8,128)S(1)} %compare_select_fusion.mask_ref, bf16[384,144]{1,0:T(8,128)(2,1)S(1)} %copy-done, bf16[144,192]{1,0:T(8,128)(2,1)S(1)} %copy-done.3), custom_call_target="tpu_custom_call" | custom-call | flops 4000000000 | bytes 8388608 | tf_op jit(solution)/shard_map/bias/pallas_call | solution.py:142
  26.4 2.9 copy-done.4
  39.3 10.0 %collective-permute-done.21.rest_10_ = bf16[384,768]{1,0:T(8,128)(2,1)} collective-permute-done((bf16[384,768]{1,0:T(8,128)(2,1)S(1)}, bf16[384,768]{1,0:T(8,128)(2,1)}, u32[]{:S(2)}, u32[]{:S(2)}) %collective-permute-start.21) | collective-permute-done | bytes 589856 | tf_op jit(solution)/shard_map/ppermute | solution.py:540
  59.3 46.8 %attend.1 = (bf16[4,288,768]{2,1,0:T(8,128)(2,1)}, bf16[4,288,768]{2,1,0:T(8,128)(2,1)}, bf16[4,288,2304]{2,1,0:T(8,128)(2,1)}, bf16[4,2,24,144,144]{4,3,2,1,0:T...) custom-call(bf16[4,288,768]{2,1,0:T(8,128)(2,1)} %bitcast.138, ...), custom_call_target="tpu_custom_call" | custom-call | flops 40000000000 | bytes 31457280 | tf_op jit(solution)/shard_map/attend/pallas_call | solution.py:235
  116.6 2.7 collective-permute-done.63
  124.4 2.6 collective-permute-start.65
  137.6 83.8 %middle.1 = (bf16[4,144,768]{2,1,0:T(8,128)(2,1)}, bf16[4,144,768]{2,1,0:T(8,128)(2,1)}, f32[4,288,768]{2,1,0:T(8,128)}, bf16[4,288,768]{2,1,0:T(8,128)(2,1)}, b...) custom-call(s32[2]{0:T(128)} %pad_add_fusion.spot_ref, ...), custom_call_target="tpu_custom_call" | custom-call | flops 60000002048 | bytes 41943040 | tf_op jit(solution)/shard_map/middle/pallas_call | solution.py:399
  221.4 56.0 %attend_back.1 = (bf16[4,288,2304]{2,1,0:T(8,128)(2,1)}, f32[24,144,144]{2,1,0:T(8,128)}) custom-call(bf16[4,288,2304]{2,1,0:T(8,128)(2,1)} %get-tuple-element.48.proj_ref, bf16[4,2,24,144,144]{4,3,2,1,0:T(8,128)(2,1)} %get-tuple-element.49.pt_ref, bf16[4,288,768]{2,1,0:T(8,128)(2,1)} %get-tuple-element.50.da_ref), custom_call_target="tpu_custom_call" | custom-call | flops 49999998976 | bytes 31457280 | tf_op jit(solution)/shard_map/attend_back/pallas_call | solution.py:452
  277.4 8.7 %inner_grad.1 = (bf16[4,3,192,384]{3,2,1,0:T(8,128)(2,1)}, bf16[4,3,192,384]{3,2,1,0:T(8,128)(2,1)}, f32[3,1,768]{2,1,0:T(1,128)}) custom-call(s32[2]{0:T(128)} %pad_add_fusion.spot_ref, bf16[4,288,768]{2,1,0:T(8,128)(2,1)} %get-tuple-element.55.n1_ref, bf16[4,288,2304]{2,1,0:T(8,128)(2,1)} %get-tuple-element.51.gp_ref), custom_call_target="tpu_custom_call" | custom-call | flops 8000000000 | bytes 15728640 | tf_op jit(solution)/shard_map/inner_grad/pallas_call | solution.py:484
  286.2 14.4 %last.1 = (f32[8,768]{1,0:T(8,128)}, bf16[4,144,768]{2,1,0:T(8,128)(2,1)}, bf16[4,144,768]{2,1,0:T(8,128)(2,1)}) custom-call(bf16[4,288,768]{2,1,0:T(8,128)(2,1)} %get-tuple-element.44.tok_ref, bf16[4,288,2304]{2,1,0:T(8,128)(2,1)} %get-tuple-element.51.gp_ref, f32[4,288,768]{2,1,0:T(8,128)} %get-tuple-element.52.gmid_ref, f32[1,768]{1,0:T(1,128)} %reshape.299.gain_ref, ...), custom_call_target="tpu_custom_call" | custom-call | flops 10000000000 | bytes 20971520 | tf_op jit(solution)/shard_map/last/pallas_call | solution.py:524
  303.0 5.0 %table.1 = f32[24,640]{1,0:T(8,128)S(1)} custom-call(f32[24,144,144]{2,1,0:T(8,128)S(1)} %copy-done.5, bf16[144,384]{1,0:T(8,128)(2,1)S(1)} %copy-done.1, bf16[192,144]{1,0:T(8,128)(2,1)S(1)} %copy-done.2), custom_call_target="tpu_custom_call" | custom-call | flops 4000000000 | bytes 4194304 | tf_op jit(solution)/shard_map/table/pallas_call | solution.py:171
  309.5 2.6 collective-permute-done.57
  313.6 3.7 pad_maximum_fusion
  321.3 2.6 collective-permute-start.60
  336.5 24.3 %collective-permute-done.47 = bf16[2,9,96,384]{3,2,1,0:T(8,128)(2,1)S(1)} collective-permute-done((bf16[2,9,96,384]{3,2,1,0:T(8,128)(2,1)S(1)}, bf16[2,9,96,384]{3,2,1,0:T(8,128)(2,1)S(1)}, u32[]{:S(2)}, u32[]{:S(2)}) %collective-permute-start.47) | collective-permute-done | bytes 1327136 | tf_op jit(solution)/shard_map/ppermute | solution.py:540
  365.2 2.7 collective-permute-start.45
  373.8 3.2 reverse
  380.4 3.4 collective-permute-done.50
  387.5 3.5 collective-permute-done.34
  393.2 8.2 %collective-permute-done.51 = bf16[9,96,384]{2,1,0:T(8,128)(2,1)S(1)} collective-permute-done((bf16[9,96,384]{2,1,0:T(8,128)(2,1)S(1)}, bf16[9,96,384]{2,1,0:T(8,128)(2,1)S(1)}, u32[]{:S(2)}, u32[]{:S(2)}) %collective-permute-start.51) | collective-permute-done | bytes 663584 | tf_op jit(solution)/shard_map/ppermute | solution.py:540
  402.9 2.7 collective-permute-start.52
  408.1 11.0 %collective-permute-done.52 = bf16[9,48,384]{2,1,0:T(8,128)(2,1)S(1)} collective-permute-done((bf16[9,48,384]{2,1,0:T(8,128)(2,1)S(1)}, bf16[9,48,384]{2,1,0:T(8,128)(2,1)S(1)}, u32[]{:S(2)}, u32[]{:S(2)}) %collective-permute-start.52) | collective-permute-done | bytes 331808 | tf_op jit(solution)/shard_map/ppermute | solution.py:540
  419.5 3.0 collective-permute-start.37
  422.4 17.1 %collective-permute-done.53 = bf16[9,48,384]{2,1,0:T(8,128)(2,1)S(1)} collective-permute-done((bf16[9,48,384]{2,1,0:T(8,128)(2,1)S(1)}, bf16[9,48,384]{2,1,0:T(8,128)(2,1)S(1)}, u32[]{:S(2)}, u32[]{:S(2)}) %collective-permute-start.53) | collective-permute-done | bytes 331808 | tf_op jit(solution)/shard_map/ppermute | solution.py:540
  440.9 12.7 %collective-permute-done.38 = bf16[3,48,384]{2,1,0:T(8,128)(2,1)S(1)} collective-permute-done((bf16[3,48,384]{2,1,0:T(8,128)(2,1)S(1)}, bf16[3,48,384]{2,1,0:T(8,128)(2,1)S(1)}, u32[]{:S(2)}, u32[]{:S(2)}) %collective-permute-start.38) | collective-permute-done | bytes 110624 | tf_op jit(solution)/shard_map/ppermute | solution.py:540
  453.7 5.2 %collective-permute-start.39 = (bf16[3,96,384]{2,1,0:T(8,128)(2,1)S(1)}, bf16[3,96,384]{2,1,0:T(8,128)(2,1)S(1)}, u32[]{:S(2)}, u32[]{:S(2)}) collective-permute-start(bf16[3,96,384]{2,1,0:T(8,128)(2,1)S(1)} %pad_maximum_fusion.8), channel_id=1, source_target_pairs={{0,8},{8,0},{16,24},{24,16},{1,9},{9,1},{17,25},{25,17},{2,10},{10... | collective-permute-start | bytes 663560 | tf_op jit(solution)/shard_map/ppermute | solution.py:540
  464.9 2.6 pad_maximum_fusion.2
  471.7 2.6 reshape.309
  476.1 3.2 copy.45
  479.4 4.1 reshape.312
  (333 shorter events, 120.5 us)
Async XLA Ops:
  6.8 26.2 %collective-permute-start.3 = (bf16[1,2304]{1,0:T(2,128)(2,1)}, bf16[1,2304]{1,0:T(2,128)(2,1)}, u32[]{:S(2)}, u32[]{:S(2)}) collective-permute-start(bf16[1,2304]{1,0:T(2,128)(2,1)} %reshape.287), channel_id=1, source_target_pairs={{0,6},{2,4},{4,2},{6,0},{1,7},{3,5},{5,3},{7,1},{8,14},{10,12},{12... | collective-permute-start | bytes 13832 | tf_op jit(solution)/shard_map/ppermute | solution.py:540
  10.7 22.3 %collective-permute-start.2 = (bf16[1,2304]{1,0:T(2,128)(2,1)}, bf16[1,2304]{1,0:T(2,128)(2,1)}, u32[]{:S(2)}, u32[]{:S(2)}) collective-permute-start(bf16[1,2304]{1,0:T(2,128)(2,1)} %reshape.287), channel_id=1, source_target_pairs={{0,4},{2,6},{4,0},{6,2},{1,5},{3,7},{5,1},{7,3},{8,12},{10,14},{12... | collective-permute-start | bytes 13832 | tf_op jit(solution)/shard_map/ppermute | solution.py:540
  11.2 22.4 %collective-permute-start.1 = (bf16[1,2304]{1,0:T(2,128)(2,1)}, bf16[1,2304]{1,0:T(2,128)(2,1)}, u32[]{:S(2)}, u32[]{:S(2)}) collective-permute-start(bf16[1,2304]{1,0:T(2,128)(2,1)} %reshape.287), channel_id=1, source_target_pairs={{0,2},{2,0},{4,6},{6,4},{1,3},{3,1},{5,7},{7,5},{8,10},{10,8},{12,... | collective-permute-start | bytes 13832 | tf_op jit(solution)/shard_map/ppermute | solution.py:540
  12.3 22.3 %collective-permute-start.4 = (bf16[96,2304]{1,0:T(8,128)(2,1)S(1)}, bf16[96,2304]{1,0:T(8,128)(2,1)}, u32[]{:S(2)}, u32[]{:S(2)}) collective-permute-start(bf16[96,2304]{1,0:T(8,128)(2,1)S(1)} %constant_dynamic-slice_fusion.9), channel_id=1, source_target_pairs={{0,2},{2,0},{4,6},{6,4},{1,3},{3,1},{5,7},{7,5},{8,10},{10,8},{12,... | collective-permute-start | bytes 1327112 | tf_op jit(solution)/shard_map/ppermute | solution.py:540
  14.4 22.0 %collective-permute-start.5 = (bf16[96,2304]{1,0:T(8,128)(2,1)S(1)}, bf16[96,2304]{1,0:T(8,128)(2,1)}, u32[]{:S(2)}, u32[]{:S(2)}) collective-permute-start(bf16[96,2304]{1,0:T(8,128)(2,1)S(1)} %constant_dynamic-slice_fusion.9), channel_id=1, source_target_pairs={{0,4},{2,6},{4,0},{6,2},{1,5},{3,7},{5,1},{7,3},{8,12},{10,14},{12... | collective-permute-start | bytes 1327112 | tf_op jit(solution)/shard_map/ppermute | solution.py:540
  33.1 22.9 %collective-permute-start = (bf16[4,144,768]{2,1,0:T(8,128)(2,1)S(1)}, bf16[4,144,768]{2,1,0:T(8,128)(2,1)}, u32[]{:S(2)}, u32[]{:S(2)}) collective-permute-start(bf16[4,144,768]{2,1,0:T(8,128)(2,1)S(1)} %slice.260), channel_id=1, source_target_pairs={{0,1},{1,0},{2,3},{3,2},{4,5},{5,4},{6,7},{7,6},{8,9},{9,8},{10,11... | collective-permute-start | bytes 2654216 | tf_op jit(solution)/shard_map/ppermute | solution.py:540
  33.1 16.3 %collective-permute-start.21 = (bf16[384,768]{1,0:T(8,128)(2,1)S(1)}, bf16[384,768]{1,0:T(8,128)(2,1)}, u32[]{:S(2)}, u32[]{:S(2)}) collective-permute-start(bf16[384,768]{1,0:T(8,128)(2,1)S(1)} %constant_dynamic-slice_fusion.7), channel_id=1, source_target_pairs={{0,2},{2,0},{4,6},{6,4},{1,3},{3,1},{5,7},{7,5},{8,10},{10,8},{12,... | collective-permute-start | bytes 1769480 | tf_op jit(solution)/shard_map/ppermute | solution.py:540
  36.3 14.5 %collective-permute-start.6 = (bf16[48,2304]{1,0:T(8,128)(2,1)}, bf16[48,2304]{1,0:T(8,128)(2,1)}, u32[]{:S(2)}, u32[]{:S(2)}) collective-permute-start(bf16[48,2304]{1,0:T(8,128)(2,1)} %slice.264), channel_id=1, source_target_pairs={{0,4},{2,6},{4,0},{6,2},{1,5},{3,7},{5,1},{7,3},{8,12},{10,14},{12... | collective-permute-start | bytes 663560 | tf_op jit(solution)/shard_map/ppermute | solution.py:540
  37.3 16.3 %collective-permute-start.7 = (bf16[48,2304]{1,0:T(8,128)(2,1)S(1)}, bf16[48,2304]{1,0:T(8,128)(2,1)}, u32[]{:S(2)}, u32[]{:S(2)}) collective-permute-start(bf16[48,2304]{1,0:T(8,128)(2,1)S(1)} %slice.265), channel_id=1, source_target_pairs={{0,2},{2,0},{4,6},{6,4},{1,3},{3,1},{5,7},{7,5},{8,10},{10,8},{12,... | collective-permute-start | bytes 663560 | tf_op jit(solution)/shard_map/ppermute | solution.py:540
  39.3 17.2 %collective-permute-start.8 = (bf16[96,2304]{1,0:T(8,128)(2,1)}, bf16[96,2304]{1,0:T(8,128)(2,1)}, u32[]{:S(2)}, u32[]{:S(2)}) collective-permute-start(bf16[96,2304]{1,0:T(8,128)(2,1)} %collective-permute-done.4.rest_1_), channel_id=1, source_target_pairs={{0,1},{1,0},{2,3},{3,2},{4,5},{5,4},{6,7},{7,6},{8,9},{9,8},{10,11... | collective-permute-start | bytes 1327112 | tf_op jit(solution)/shard_map/ppermute | solution.py:540
  56.0 51.3 %collective-permute-start.13 = (bf16[96,3840]{1,0:T(8,128)(2,1)S(1)}, bf16[96,3840]{1,0:T(8,128)(2,1)S(1)}, u32[]{:S(2)}, u32[]{:S(2)}) collective-permute-start(bf16[96,3840]{1,0:T(8,128)(2,1)S(1)} %constant_dynamic-slice_fusion.8), channel_id=1, source_target_pairs={{0,2},{2,0},{4,6},{6,4},{1,3},{3,1},{5,7},{7,5},{8,10},{10,8},{12,... | collective-permute-start | bytes 2211848 | tf_op jit(solution)/shard_map/ppermute | solution.py:540
  56.6 58.4 %collective-permute-start.14 = (bf16[96,3840]{1,0:T(8,128)(2,1)S(1)}, bf16[96,3840]{1,0:T(8,128)(2,1)}, u32[]{:S(2)}, u32[]{:S(2)}) collective-permute-start(bf16[96,3840]{1,0:T(8,128)(2,1)S(1)} %constant_dynamic-slice_fusion.8), channel_id=1, source_target_pairs={{0,4},{2,6},{4,0},{6,2},{1,5},{3,7},{5,1},{7,3},{8,12},{10,14},{12... | collective-permute-start | bytes 2211848 | tf_op jit(solution)/shard_map/ppermute | solution.py:540
  56.8 53.1 %collective-permute-start.22 = (bf16[384,768]{1,0:T(8,128)(2,1)S(1)}, bf16[384,768]{1,0:T(8,128)(2,1)}, u32[]{:S(2)}, u32[]{:S(2)}) collective-permute-start(bf16[384,768]{1,0:T(8,128)(2,1)S(1)} %constant_dynamic-slice_fusion.7), channel_id=1, source_target_pairs={{0,4},{2,6},{4,0},{6,2},{1,5},{3,7},{5,1},{7,3},{8,12},{10,14},{12... | collective-permute-start | bytes 1769480 | tf_op jit(solution)/shard_map/ppermute | solution.py:540
  58.6 62.2 %collective-permute-start.12 = (bf16[4,144,768]{2,1,0:T(8,128)(2,1)S(1)}, bf16[4,144,768]{2,1,0:T(8,128)(2,1)}, u32[]{:S(2)}, u32[]{:S(2)}) collective-permute-start(bf16[4,144,768]{2,1,0:T(8,128)(2,1)S(1)} %slice.266), channel_id=1, source_target_pairs={{0,1},{1,0},{2,3},{3,2},{4,5},{5,4},{6,7},{7,6},{8,9},{9,8},{10,11... | collective-permute-start | bytes 2654216 | tf_op jit(solution)/shard_map/ppermute | solution.py:540
  58.6 63.7 %collective-permute-start.23 = (bf16[192,768]{1,0:T(8,128)(2,1)S(1)}, bf16[192,768]{1,0:T(8,128)(2,1)}, u32[]{:S(2)}, u32[]{:S(2)}) collective-permute-start(bf16[192,768]{1,0:T(8,128)(2,1)S(1)} %slice.269), channel_id=1, source_target_pairs={{0,4},{2,6},{4,0},{6,2},{1,5},{3,7},{5,1},{7,3},{8,12},{10,14},{12... | collective-permute-start | bytes 884744 | tf_op jit(solution)/shard_map/ppermute | solution.py:540
  108.5 20.4 %collective-permute-start.15 = (bf16[48,3840]{1,0:T(8,128)(2,1)S(1)}, bf16[48,3840]{1,0:T(8,128)(2,1)}, u32[]{:S(2)}, u32[]{:S(2)}) collective-permute-start(bf16[48,3840]{1,0:T(8,128)(2,1)S(1)} %slice.267), channel_id=1, source_target_pairs={{0,4},{2,6},{4,0},{6,2},{1,5},{3,7},{5,1},{7,3},{8,12},{10,14},{12... | collective-permute-start | bytes 1105928 | tf_op jit(solution)/shard_map/ppermute | solution.py:540
  328.8 32.0 %collective-permute-start.47 = (bf16[2,9,96,384]{3,2,1,0:T(8,128)(2,1)S(1)}, bf16[2,9,96,384]{3,2,1,0:T(8,128)(2,1)S(1)}, u32[]{:S(2)}, u32[]{:S(2)}) collective-permute-start(bf16[2,9,96,384]{3,2,1,0:T(8,128)(2,1)S(1)} %pad_maximum_fusion.4), channel_id=1, source_target_pairs={{0,2},{2,0},{4,6},{6,4},{1,3},{3,1},{5,7},{7,5},{8,10},{10,8},{12,... | collective-permute-start | bytes 3981320 | tf_op jit(solution)/shard_map/ppermute | solution.py:540
  329.6 33.1 %collective-permute-start.49 = (bf16[2,9,96,384]{3,2,1,0:T(8,128)(2,1)S(1)}, bf16[2,9,96,384]{3,2,1,0:T(8,128)(2,1)S(1)}, u32[]{:S(2)}, u32[]{:S(2)}) collective-permute-start(bf16[2,9,96,384]{3,2,1,0:T(8,128)(2,1)S(1)} %stack.165), channel_id=1, source_target_pairs={{0,4},{2,6},{4,0},{6,2},{1,5},{3,7},{5,1},{7,3},{8,12},{10,14},{12... | collective-permute-start | bytes 3981320 | tf_op jit(solution)/shard_map/ppermute | solution.py:540
  331.6 133.3 %collective-permute-start.29 = (bf16[4,144,768]{2,1,0:T(8,128)(2,1)}, bf16[4,144,768]{2,1,0:T(8,128)(2,1)}, u32[]{:S(2)}, u32[]{:S(2)}) collective-permute-start(bf16[4,144,768]{2,1,0:T(8,128)(2,1)} %get-tuple-element.46), channel_id=1, source_target_pairs={{0,1},{1,0},{2,3},{3,2},{4,5},{5,4},{6,7},{7,6},{8,9},{9,8},{10,11... | collective-permute-start | bytes 2654216 | tf_op jit(solution)/shard_map/ppermute | solution.py:540
  331.7 33.4 %collective-permute-start.44 = (f32[1,23808]{1,0:T(1,128)S(1)}, f32[1,23808]{1,0:T(1,128)S(1)}, u32[]{:S(2)}, u32[]{:S(2)}) collective-permute-start(f32[1,23808]{1,0:T(1,128)S(1)} %add.252), channel_id=1, source_target_pairs={{0,8},{8,0},{16,24},{24,16},{1,9},{9,1},{17,25},{25,17},{2,10},{10... | collective-permute-start | bytes 285704 | tf_op jit(solution)/shard_map/ppermute | solution.py:540
  335.6 42.4 %collective-permute-start.32 = (bf16[2,3,96,384]{3,2,1,0:T(8,128)(2,1)}, bf16[2,3,96,384]{3,2,1,0:T(8,128)(2,1)}, u32[]{:S(2)}, u32[]{:S(2)}) collective-permute-start(bf16[2,3,96,384]{3,2,1,0:T(8,128)(2,1)} %pad_maximum_fusion.6), channel_id=1, source_target_pairs={{0,2},{2,0},{4,6},{6,4},{1,3},{3,1},{5,7},{7,5},{8,10},{10,8},{12,... | collective-permute-start | bytes 1327112 | tf_op jit(solution)/shard_map/ppermute | solution.py:540
  362.1 18.3 %collective-permute-start.48 = (bf16[9,96,384]{2,1,0:T(8,128)(2,1)}, bf16[9,96,384]{2,1,0:T(8,128)(2,1)S(1)}, u32[]{:S(2)}, u32[]{:S(2)}) collective-permute-start(bf16[9,96,384]{2,1,0:T(8,128)(2,1)} %slice_bitcast_fusion.2), channel_id=1, source_target_pairs={{0,4},{2,6},{4,0},{6,2},{1,5},{3,7},{5,1},{7,3},{8,12},{10,14},{12... | collective-permute-start | bytes 1990664 | tf_op jit(solution)/shard_map/ppermute | solution.py:540
  364.0 19.8 %collective-permute-start.50 = (bf16[9,96,384]{2,1,0:T(8,128)(2,1)}, bf16[9,96,384]{2,1,0:T(8,128)(2,1)}, u32[]{:S(2)}, u32[]{:S(2)}) collective-permute-start(bf16[9,96,384]{2,1,0:T(8,128)(2,1)} %slice_bitcast_fusion), channel_id=1, source_target_pairs={{0,2},{2,0},{4,6},{6,4},{1,3},{3,1},{5,7},{7,5},{8,10},{10,8},{12,... | collective-permute-start | bytes 1990664 | tf_op jit(solution)/shard_map/ppermute | solution.py:540
  370.8 96.7 %collective-permute-start.30 = (bf16[4,144,768]{2,1,0:T(8,128)(2,1)}, bf16[4,144,768]{2,1,0:T(8,128)(2,1)}, u32[]{:S(2)}, u32[]{:S(2)}) collective-permute-start(bf16[4,144,768]{2,1,0:T(8,128)(2,1)} %get-tuple-element.53), channel_id=1, source_target_pairs={{0,1},{1,0},{2,3},{3,2},{4,5},{5,4},{6,7},{7,6},{8,9},{9,8},{10,11... | collective-permute-start | bytes 2654216 | tf_op jit(solution)/shard_map/ppermute | solution.py:540
  385.2 16.2 %collective-permute-start.51 = (bf16[9,96,384]{2,1,0:T(8,128)(2,1)S(1)}, bf16[9,96,384]{2,1,0:T(8,128)(2,1)S(1)}, u32[]{:S(2)}, u32[]{:S(2)}) collective-permute-start(bf16[9,96,384]{2,1,0:T(8,128)(2,1)S(1)} %broadcast_select_fusion.2), channel_id=1, source_target_pairs={{0,8},{8,0},{16,24},{24,16},{1,9},{9,1},{17,25},{25,17},{2,10},{10... | collective-permute-start | bytes 1990664 | tf_op jit(solution)/shard_map/ppermute | solution.py:540
  386.9 19.4 %collective-permute-start.33 = (bf16[3,96,384]{2,1,0:T(8,128)(2,1)S(1)}, bf16[3,96,384]{2,1,0:T(8,128)(2,1)S(1)}, u32[]{:S(2)}, u32[]{:S(2)}) collective-permute-start(bf16[3,96,384]{2,1,0:T(8,128)(2,1)S(1)} %slice_bitcast_fusion.6), channel_id=1, source_target_pairs={{0,4},{2,6},{4,0},{6,2},{1,5},{3,7},{5,1},{7,3},{8,12},{10,14},{12... | collective-permute-start | bytes 663560 | tf_op jit(solution)/shard_map/ppermute | solution.py:540
  392.2 14.1 %collective-permute-start.35 = (bf16[3,96,384]{2,1,0:T(8,128)(2,1)S(1)}, bf16[3,96,384]{2,1,0:T(8,128)(2,1)S(1)}, u32[]{:S(2)}, u32[]{:S(2)}) collective-permute-start(bf16[3,96,384]{2,1,0:T(8,128)(2,1)S(1)} %slice_bitcast_fusion.4), channel_id=1, source_target_pairs={{0,2},{2,0},{4,6},{6,4},{1,3},{3,1},{5,7},{7,5},{8,10},{10,8},{12,... | collective-permute-start | bytes 663560 | tf_op jit(solution)/shard_map/ppermute | solution.py:540
  402.9 16.1 %collective-permute-start.52 = (bf16[9,48,384]{2,1,0:T(8,128)(2,1)S(1)}, bf16[9,48,384]{2,1,0:T(8,128)(2,1)S(1)}, u32[]{:S(2)}, u32[]{:S(2)}) collective-permute-start(bf16[9,48,384]{2,1,0:T(8,128)(2,1)S(1)} %broadcast_select_fusion.7), channel_id=1, source_target_pairs={{0,16},{8,24},{16,0},{24,8},{1,17},{9,25},{17,1},{25,9},{2,18},{10... | collective-permute-start | bytes 995336 | tf_op jit(solution)/shard_map/ppermute | solution.py:540
  419.2 20.3 %collective-permute-start.53 = (bf16[9,48,384]{2,1,0:T(8,128)(2,1)S(1)}, bf16[9,48,384]{2,1,0:T(8,128)(2,1)S(1)}, u32[]{:S(2)}, u32[]{:S(2)}) collective-permute-start(bf16[9,48,384]{2,1,0:T(8,128)(2,1)S(1)} %add_convert_fusion.7), channel_id=1, source_target_pairs={{0,16},{8,24},{16,0},{24,8},{1,17},{9,25},{17,1},{25,9},{2,18},{10... | collective-permute-start | bytes 995336 | tf_op jit(solution)/shard_map/ppermute | solution.py:540
  419.5 21.3 %collective-permute-start.37 = (bf16[3,48,384]{2,1,0:T(8,128)(2,1)S(1)}, bf16[3,48,384]{2,1,0:T(8,128)(2,1)S(1)}, u32[]{:S(2)}, u32[]{:S(2)}) collective-permute-start(bf16[3,48,384]{2,1,0:T(8,128)(2,1)S(1)} %broadcast_select_fusion.13), channel_id=1, source_target_pairs={{0,16},{8,24},{16,0},{24,8},{1,17},{9,25},{17,1},{25,9},{2,18},{10... | collective-permute-start | bytes 331784 | tf_op jit(solution)/shard_map/ppermute | solution.py:540
  439.7 19.2 %collective-permute-start.54 = (bf16[9,96,384]{2,1,0:T(8,128)(2,1)S(1)}, bf16[9,96,384]{2,1,0:T(8,128)(2,1)S(1)}, u32[]{:S(2)}, u32[]{:S(2)}) collective-permute-start(bf16[9,96,384]{2,1,0:T(8,128)(2,1)S(1)} %pad_maximum_fusion.5), channel_id=1, source_target_pairs={{0,8},{8,0},{16,24},{24,16},{1,9},{9,1},{17,25},{25,17},{2,10},{10... | collective-permute-start | bytes 1990664 | tf_op jit(solution)/shard_map/ppermute | solution.py:540
  460.4 13.9 %collective-permute-start.55 = (bf16[9,192,384]{2,1,0:T(8,128)(2,1)}, bf16[9,192,384]{2,1,0:T(8,128)(2,1)}, u32[]{:S(2)}, u32[]{:S(2)}) collective-permute-start(bf16[9,192,384]{2,1,0:T(8,128)(2,1)} %pad_maximum_fusion.1), channel_id=1, source_target_pairs={{0,1},{1,0},{2,3},{3,2},{4,5},{5,4},{6,7},{7,6},{8,9},{9,8},{10,11... | collective-permute-start | bytes 3981320 | tf_op jit(solution)/shard_map/ppermute | solution.py:540
  (78 other events, 689.5 us)

commit v2 on v1

v2 whole, which is shorter than its diff:
```python
import functools
import math

import numpy as np
import jax
import jax.numpy as jnp
from jax import lax
from jax.experimental import pallas as pl
from jax.experimental.pallas import tpu as pltpu
from jax.sharding import PartitionSpec as P

D = 768
HEADS = 24
HD = 32
WIN = 12
GRID = 24
SHIFT = 6
FF = 3072
TOK = WIN * WIN
ROWS = WIN * GRID
SPAN = 2 * WIN - 1
EPS = 1e-5
MASKED = -100.0
NEGATIVE = -1e30
LOG2E = math.log2(math.e)
BF = jnp.bfloat16
F32 = jnp.float32
MB = 1 << 20
OWN = 192
CH = 384
WIDE = 640
NARROW = 384
TALL = WIN * 16
HB = 4
LB = HB * HD
HP = 8
LP = HP * HD
NB = 384
SCALE = 1e-3
ONE = dict(pipeline_mode=pl.Buffered(1))
SD = jax.ShapeDtypeStruct


def nn(a, b):
    return lax.dot_general(a, b, (((1,), (0,)), ((), ())), preferred_element_type=F32)


def nt(a, b):
    return lax.dot_general(a, b, (((1,), (1,)), ((), ())), preferred_element_type=F32)


def tn(a, b):
    return lax.dot_general(a, b, (((0,), (0,)), ((), ())), preferred_element_type=F32)


def full(shape, **kw):
    return pl.BlockSpec(shape, lambda *_: (0,) * len(shape), **kw)


def any_space():
    return pl.BlockSpec(memory_space=pl.ANY)


def smem():
    return pl.BlockSpec(memory_space=pltpu.SMEM)


def run(kernel, count, args, after, in_specs, **kw):
    def body(*refs):
        kernel(*refs[:count], *refs[count + len(after) :])

    return pl.pallas_call(body, in_specs=list(in_specs) + [any_space()] * len(after), **kw)(*args, *after)


def params(limit=60):
    return pltpu.CompilerParams(vmem_limit_bytes=limit * MB)


def cost(flops, moved, exps=0):
    return pl.CostEstimate(flops=int(flops * SCALE), bytes_accessed=int(moved * SCALE), transcendentals=0)


def whole(array):
    return full(array.shape, **ONE)


def single(kernel, args, out_shape, after=(), scratch=(), **kw):
    specs = [smem() if v.dtype == jnp.int32 else whole(v) for v in args]
    shapes = out_shape if isinstance(out_shape, (list, tuple)) else [out_shape]
    out = run(
        kernel, len(args), args, after, grid=(1,), in_specs=specs, out_specs=[whole(v) for v in shapes], out_shape=list(shapes),
        scratch_shapes=list(scratch), compiler_params=params(), **kw
    )
    return out if isinstance(out_shape, (list, tuple)) else out[0]


def colsum(v):
    return jnp.sum(v, axis=0, keepdims=True)


def norm_parts(x):
    c = x - jnp.mean(x, axis=-1, keepdims=True)
    r = lax.rsqrt(jnp.mean(c * c, axis=-1, keepdims=True) + EPS)
    return c * r, r


def row_order():
    cells = np.arange(ROWS)
    win, rest = cells // TOK, cells % TOK
    a, b = rest // WIN, rest % WIN
    m = np.zeros((ROWS, ROWS), np.float32)
    m[cells, a * GRID + (win * WIN + b + SHIFT) % GRID] = 1
    return m


def spread_q():
    q = np.arange(TOK)
    m = np.zeros((TOK, NARROW), np.float32)
    m[q, SPAN * (q // WIN) + q % WIN] = 1
    return m


def spread_k(reverse):
    k = np.arange(TOK)
    b = k % WIN
    m = np.zeros((TALL, TOK), np.float32)
    m[16 * (k // WIN) + (WIN - 1 - b if reverse else b), k] = 1
    return m


def copies(plan, refs, at, targets, sems):
    for i, (src, row, rows, col, cols, dst, put) in enumerate(plan):
        place = pl.ds(pl.multiple_of(at[i], 16), rows)
        yield pltpu.make_async_copy(
            refs[src].at[pl.ds(row, rows), pl.ds(col, cols)], targets[dst].at[place, pl.ds(put, cols)], sems.at[i]
        )


def region_masks():
    line = np.arange(GRID)
    region = (line >= GRID - WIN).astype(np.int32) + (line >= GRID - SHIFT).astype(np.int32)
    lab = 3 * region[:, None] + region[None, :]
    lab = lab.reshape(2, WIN, 2, WIN).transpose(0, 2, 1, 3).reshape(2, 2, TOK)
    return np.where(lab[:, :, :, None] != lab[:, :, None, :], MASKED, 0.0).astype(np.float32)


def bias_kernel(spot_ref, table_ref, mask_ref, sq_ref, sk_ref, out_ref, tall):
    masks = [mask_ref[spot_ref[1], w].astype(F32) for w in range(2)]
    for h in range(HP):
        row = pltpu.roll(jnp.broadcast_to(table_ref[h : h + 1, :], (16, WIDE)), 0, 1, stride=1, stride_axis=0)
        for a in range(WIN):
            off = (SPAN * a - SPAN * (WIN - 1) - (WIN - 1)) % WIDE
            tall[16 * a : 16 * a + 16, :] = pltpu.roll(row, off, 1)[:, :NARROW].astype(BF)
        wide = nn(tall[...], sq_ref[...]).astype(BF)
        bias = nn(sk_ref[...], wide)
        for w in range(2):
            out_ref[w, h] = (bias + masks[w]) * LOG2E


def bias_call(group, spot, table):
    args = (spot, table, jnp.asarray(region_masks(), BF), jnp.asarray(spread_q().T, BF), jnp.asarray(spread_k(False).T, BF))
    out = SD((2, HP, TOK, TOK), F32)
    return pl.pallas_call(
        bias_kernel,
        grid=(1,),
        in_specs=[smem(), pl.BlockSpec((HP, WIDE), lambda i: (group, 0))] + [whole(v) for v in args[2:]],
        out_specs=whole(out),
        out_shape=out,
        scratch_shapes=[pltpu.VMEM((TALL, NARROW), BF)],
        compiler_params=params(),
        cost_estimate=cost(2e9, 3 * MB),
        name="bias",
    )(*args)


V_UP, V_SMALL, V_IN, V_ONE, V_PEAK, V_TABLE, V_ROWS = 0, 4, 8, 11, 13, 16, 40


def table_kernel(db0_ref, db1_ref, db2_ref, up_ref, down_ref, small_ref, in01_ref, in2_ref, one_ref, peak_ref, sq_ref, sk_ref, out_ref):
    def split(v):
        hi = v.astype(BF)
        return hi, (v - hi.astype(F32)).astype(BF)

    out_ref[...] = jnp.zeros_like(out_ref)
    for j in range(8):
        out_ref[V_UP + j // 2 : V_UP + j // 2 + 1, (j % 2) * CH : (j % 2 + 1) * CH] = up_ref[j]
    out_ref[V_SMALL : V_SMALL + 1, :] = down_ref[...]
    out_ref[V_SMALL + 1 : V_SMALL + 4, :] = small_ref[1:4, :]
    for p in range(3):
        row = in01_ref[p] if p < 2 else in2_ref[0]
        for k in range(3):
            out_ref[V_IN + k : V_IN + k + 1, p * LP : (p + 1) * LP] = row[:, k * LP : (k + 1) * LP]
    out_ref[V_ONE : V_ONE + 2, :] = one_ref[0:2, :]
    out_ref[V_PEAK : V_PEAK + 1, :HEADS] = peak_ref[...]
    for h in range(HEADS):
        hi, lo = split((db0_ref, db1_ref, db2_ref)[h // HP][h % HP])
        tall = nn(sk_ref[...], hi) + nn(sk_ref[...], lo)
        hi, lo = split(tall)
        wide = nn(hi, sq_ref[...]) + nn(lo, sq_ref[...])
        wide = jnp.concatenate([wide, jnp.zeros((TALL, WIDE - NARROW), F32)], axis=1)
        tot = jnp.zeros((16, WIDE), F32)
        for a in range(WIN):
            tot = tot + pltpu.roll(wide[16 * a : 16 * a + 16, :], SPAN * (WIN - 1 - a), 1)
        tot = pltpu.roll(tot, 0, 1, stride=1, stride_axis=0)
        out_ref[V_TABLE + h : V_TABLE + h + 1, :WIDE] = colsum(tot)


def table_call(dbs, up, down, small, in01, in2, one, peaks, after):
    args = (*dbs, up, down, small, in01, in2, one, peaks, jnp.asarray(spread_q(), BF), jnp.asarray(spread_k(True), BF))
    return single(table_kernel, args, SD((V_ROWS, D), F32), after, cost_estimate=cost(6e9, 4 * MB), name="table")


def lane_head(shape):
    return lax.broadcasted_iota(jnp.int32, shape, len(shape) - 1) // HD


VECTORS = (2 * D, D, FF, D, D, D, D, D)


def first_kernel(spot_ref, *refs):
    vecs, inner_ref, first_ref, others_ref, half_ref = refs[:8], refs[8], refs[9], refs[10], refs[11]
    mine = pl.ds(pl.multiple_of(spot_ref[1] * (OWN // 2), 16), OWN // 2)
    for k in range(3):
        first_ref[:OWN, k * LP : (k + 1) * LP] = inner_ref[:, k * D : k * D + LP]
        for p in (1, 2):
            src = slice(k * D + p * LP, k * D + (p + 1) * LP)
            dst = slice(((p - 1) * 3 + k) * LP, ((p - 1) * 3 + k + 1) * LP)
            others_ref[:, dst] = inner_ref[:, src]
            half_ref[:, dst] = inner_ref[mine, src]
    rows = [jnp.zeros((8, D), F32)]
    for v in vecs:
        row = v[...].astype(F32).reshape(1, v.shape[0])
        if v.shape[0] < D:
            row = jnp.concatenate([row, jnp.zeros((1, D - v.shape[0]), F32)], axis=1)
        rows.insert(-1, row)
    first_ref[OWN:, :] = jnp.concatenate(rows, axis=0).astype(BF)


def first_call(spot, vectors, inner):
    return single(
        first_kernel, (spot, *vectors, inner), [SD((OWN + 16, D), BF), SD((OWN, 6 * LP), BF), SD((OWN // 2, 6 * LP), BF)],
        cost_estimate=cost(1e6, 3 * MB), name="first",
    )


BIG = 4 * (OWN // 2) + OWN // 2 + 2 * OWN


def cut_kernel(spot_ref, outer_ref, expand_ref, reduce_ref, own_ref, gown_ref, big_ref, up_ref):
    core = spot_ref[1]
    hlf = OWN // 2
    n = own_ref.shape[0]
    mine = pl.ds(pl.multiple_of(core * hlf, 16), hlf)
    for k in range(4):
        big_ref[k * hlf : (k + 1) * hlf, :] = expand_ref[mine, k * D : (k + 1) * D]
    big_ref[4 * hlf : 5 * hlf, :] = outer_ref[mine, :]
    big_ref[5 * hlf :, :] = reduce_ref[pl.ds(pl.multiple_of(core * 2 * OWN, 16), 2 * OWN), :]
    up_ref[:n] = own_ref[...]
    up_ref[n:] = gown_ref[...]


def cut_call(spot, outer, expand, reduce, own, gown):
    n = own.shape[0]
    top = full((n, TOK, D))
    shapes = [SD((BIG, D), BF), SD((2 * n, TOK, D), BF)]
    return pl.pallas_call(
        cut_kernel,
        grid=(1,),
        in_specs=[smem(), whole(outer), whole(expand), whole(reduce), top, top],
        out_specs=[whole(v) for v in shapes],
        out_shape=shapes,
        compiler_params=params(),
        cost_estimate=cost(1e6, 8 * MB),
        name="cut",
    )(spot, outer, expand, reduce, own, gown)


def prep_kernel(own_ref, gown_ref, recv_ref, alive_ref, pm_ref, tok_ref, g_ref, sum_ref):
    n = own_ref.shape[0]
    tot = jnp.zeros((1, D), F32)
    for i in range(n):
        tok_ref[i] = nn(pm_ref[...], jnp.concatenate([own_ref[i, TOK:, :], recv_ref[i]], axis=0)).astype(BF)
        g = nn(pm_ref[...], jnp.concatenate([gown_ref[i, TOK:, :], recv_ref[n + i]], axis=0)) * alive_ref[0:1, i : i + 1]
        g_ref[i] = g.astype(BF)
        tot = tot + colsum(g)
    sum_ref[...] = tot


def prep_call(own, gown, recv, alive, pm):
    rows = SD(own.shape, BF)
    return single(
        prep_kernel, (own, gown, recv, alive, pm), [rows, rows, SD((1, D), F32)], cost_estimate=cost(3e9, 16 * MB), name="prep"
    )


def vector_kernel(spot_ref, pa_ref, pb_ref, pc_ref, pd_ref, tok_ref, inb_ref, up_ref, vec_ref, n1_ref, n1t_ref, parts):
    n = tok_ref.shape[0]
    for r, ref in enumerate((pa_ref, pb_ref, pc_ref, pd_ref)):
        parts[jnp.bitwise_xor(spot_ref[0], r)] = ref[:8, :].astype(F32)

    def vector(i):
        size = VECTORS[i] // 4
        return jnp.concatenate([parts[s][i : i + 1, :size] for s in range(4)], axis=1)

    vin = vector(0)
    for p in range(3):
        inb_ref[p] = jnp.concatenate(
            [vin[:, p * LP : (p + 1) * LP], jnp.zeros((1, LP), F32), vin[:, D + p * LP : D + (p + 1) * LP]], axis=1
        )
    vup = vector(2)
    for j in range(8):
        up_ref[j] = vup[:, j * CH : (j + 1) * CH]
    gain, shift = vector(4), vector(5)
    vec_ref[...] = jnp.zeros_like(vec_ref)
    for r, v in enumerate((vector(1), vector(3), gain, vector(6), vector(7))):
        vec_ref[r : r + 1, :] = v
    for i in range(n):
        xh, _ = norm_parts(tok_ref[i].astype(F32))
        n1 = (xh * gain + shift).astype(BF)
        n1_ref[i] = n1
        n1t_ref[:, i * ROWS : (i + 1) * ROWS] = n1.T


def vector_call(spot, parts, tok):
    n = tok.shape[0]
    last = parts[0].shape[0] // 16 - 1
    shapes = [SD((3, 1, 3 * LP), F32), SD((8, 1, CH), F32), SD((8, D), F32), SD(tok.shape, BF), SD((D, n * ROWS), BF)]
    return pl.pallas_call(
        vector_kernel,
        grid=(1,),
        in_specs=[smem()] + [pl.BlockSpec((16, D), lambda i: (last, 0))] * 4 + [whole(tok)],
        out_specs=[whole(v) for v in shapes],
        out_shape=shapes,
        scratch_shapes=[pltpu.VMEM((4, 8, D), F32)],
        compiler_params=params(),
        cost_estimate=cost(5e9, 8 * MB),
        name="vectors",
    )(spot, *parts, tok)


def attend_kernel(plan, count, n1_ref, b_ref, bm_ref, at_ref, *rest):
    pieces = rest[:count]
    proj_ref, pt_ref, att_ref, peak_ref, w_ref, sems = rest[count:]

    @pl.when(pl.program_id(0) == 0)
    def _():
        for c in copies(plan, pieces, at_ref, (w_ref,), sems):
            c.start()
        for c in copies(plan, pieces, at_ref, (w_ref,), sems):
            c.wait()

    proj_ref[0] = (nn(n1_ref[0], w_ref[...]) + b_ref[0]).astype(BF)
    hid = lane_head((TOK, LB))
    scale = HD**-0.5
    for w in range(2):
        r = slice(w * TOK, (w + 1) * TOK)
        for blk in range(LP // LB):
            l = blk * LB
            q = proj_ref[0, r, l : l + LB]
            k = proj_ref[0, r, LP + l : LP + l + LB]
            v = proj_ref[0, r, 2 * LP + l : 2 * LP + l + LB]
            vt = v.T
            outs = []
            for h in range(HB):
                hh = blk * HB + h
                km = jnp.where(hid == h, k, jnp.zeros_like(k))
                st = nt(km, q)
                peak_ref[0, w, hh : hh + 1, :] = jnp.max(st, axis=0, keepdims=True) * scale
                t = st * (scale * LOG2E) + bm_ref[w, hh]
                e = jnp.exp2(t - jnp.max(t, axis=0, keepdims=True))
                p = (e * (1.0 / colsum(e))).astype(BF)
                pt_ref[0, w, hh] = p
                outs.append(nn(vt[HD * h : HD * h + HD, :], p))
            att_ref[0, r, l : l + LB] = jnp.concatenate(outs, axis=0).astype(BF).T


def attend_call(group, n1, b, bm, at, plan, pieces, after):
    n = n1.shape[0]

    def blk(*s):
        return pl.BlockSpec((1,) + s, lambda i: (i,) + (0,) * len(s))

    return run(
        functools.partial(attend_kernel, plan, len(pieces)), 4 + len(pieces), (n1, b, bm, at, *pieces), after,
        grid=(n,),
        in_specs=[blk(ROWS, D), pl.BlockSpec((1, 1, 3 * LP), lambda i: (group, 0, 0)), full((2, HP, TOK, TOK), **ONE), smem()]
        + [any_space()] * len(pieces),
        out_specs=[blk(ROWS, 3 * LP), blk(2, HP, TOK, TOK), blk(ROWS, LP), blk(2, HP, TOK), full((D, 3 * LP), **ONE)],
        out_shape=[SD((n, ROWS, 3 * LP), BF), SD((n, 2, HP, TOK, TOK), BF), SD((n, ROWS, LP), BF), SD((n, 2, HP, TOK), F32),
                   SD((D, 3 * LP), BF)],
        scratch_shapes=[pltpu.SemaphoreType.DMA((len(plan),))],
        compiler_params=params(),
        cost_estimate=cost(1.3e10, 12 * MB, 1.4e6),
        name="attend",
    )


def gelu_parts(h):
    d = 1.0 + (0.3275911 * 0.5**0.5) * jnp.abs(h)
    t = pl.reciprocal(d, approx=True)
    t = t * (2.0 - d * t)
    e = jnp.exp2(h * h * (-0.5 * LOG2E))
    p = (((0.5 * 1.061405429) * t - 0.5 * 1.453152027) * t + 0.5 * 1.421413741) * t - 0.5 * 0.284496736
    p = (p * t + 0.5 * 0.254829592) * t * e
    cdf = jnp.where(h >= 0, 1.0 - p, p)
    return cdf, cdf + h * (e * ((2 * math.pi) ** -0.5))


def middle_kernel(plan, count, spot_ref, tok_ref, att0_ref, att1_ref, att2_ref, gin_ref, pmt_ref, vec_ref, eb_ref,
                  at_ref, *rest):
    pieces = rest[:count]
    (stay_ref, send_ref, gmid_ref, datt_ref, os_ref, ok_ref, es_ref, ek_ref, rs_ref, rk_ref, geb_ref, small_ref,
     wo, we, wr, mid, n2, g, n2t, acc, e2, act, gh, sems) = rest[count:]
    j = pl.program_id(0)
    n = tok_ref.shape[0]
    N = n * ROWS
    me = spot_ref[0]
    core = spot_ref[1]
    early = [k for k, entry in enumerate(plan) if entry[5] == 0]
    out_b, red_b, gain, shift = vec_ref[0:1, :], vec_ref[1:2, :], vec_ref[3:4, :], vec_ref[4:5, :]

    def attended(i):
        return jnp.concatenate([att0_ref[i], att1_ref[i], att2_ref[i]], axis=-1)

    @pl.when(j == 0)
    def _():
        moves = list(copies(plan, pieces, at_ref, (wo, we, wr), sems))
        for c in moves:
            c.start()
        for k in early:
            moves[k].wait()
        for i in range(n):
            s = slice(i * ROWS, (i + 1) * ROWS)
            g[s, :] = gin_ref[i]
            m = tok_ref[i].astype(F32) + nn(attended(i), wo[...]) + out_b
            mid[s, :] = m
            xh, _ = norm_parts(m)
            x2 = (xh * gain + shift).astype(BF)
            n2[s, :] = x2
            n2t[:, s] = x2.T
            acc[s, :] = m + red_b
            e2[s, :] = jnp.zeros((ROWS, D), F32)
        for k, c in enumerate(moves):
            if k not in early:
                c.wait()

    sh = jnp.bitwise_xor(me, j % 4)
    at = (2 * sh + jnp.bitwise_xor(core, 1 - j // 4)) * CH
    ecol = pl.ds(pl.multiple_of(at, CH), CH)
    tot = jnp.zeros((1, CH), F32)
    for s0 in range(0, N, NB):
        s = slice(s0, s0 + NB)
        h = nn(n2[s, :], we[:, ecol]) + eb_ref[0]
        cdf, dg = gelu_parts(h)
        act[s, :] = (h * cdf).astype(BF)
        x = (nt(g[s, :], wr[ecol, :]) * dg).astype(BF)
        gh[s, :] = x
        tot = tot + colsum(x.astype(F32))
    geb_ref[0] = tot
    ge = nn(n2t[...], gh[...]).astype(BF)
    gr = tn(act[...], g[...]).astype(BF)

    def put(e_ref, r_ref):
        for b in range(4):
            e_ref[jnp.bitwise_xor(me, b), 0] = ge[b * OWN : (b + 1) * OWN, :]
            r_ref[0, b] = gr[(b // 2) * OWN : (b // 2 + 1) * OWN, (b % 2) * CH : (b % 2 + 1) * CH]

    @pl.when(j < 4)
    def _():
        put(es_ref, rs_ref)

    @pl.when(j >= 4)
    def _():
        put(ek_ref, rk_ref)

    for s0 in range(0, N, NB):
        s = slice(s0, s0 + NB)
        acc[s, :] += nn(act[s, :], wr[ecol, :])
        e2[s, :] += nt(gh[s, :], we[:, ecol])

    @pl.when(j == 7)
    def _():
        gn = jnp.zeros((1, D), F32)
        shf = gn
        ob = gn
        for i in range(n):
            s = slice(i * ROWS, (i + 1) * ROWS)
            o = nn(pmt_ref[...], acc[s, :].astype(BF)).astype(BF)
            stay_ref[i] = o[:TOK]
            send_ref[i] = o[TOK:]
            xh, r = norm_parts(mid[s, :])
            d = e2[s, :]
            gn = gn + colsum(d * xh)
            shf = shf + colsum(d)
            d = d * gain
            gm = g[s, :].astype(F32) + r * (
                d - jnp.mean(d, axis=-1, keepdims=True) - xh * jnp.mean(d * xh, axis=-1, keepdims=True)
            )
            gmid_ref[i] = gm
            gb = gm.astype(BF)
            ob = ob + colsum(gb.astype(F32))
            g[s, :] = gb
            datt_ref[i] = nt(gb, wo[...]).astype(BF)
            n2[s, :] = attended(i)
        for c, ref in ((1 - core, os_ref), (core, ok_ref)):
            go = tn(n2[...], g[:, pl.ds(pl.multiple_of(c * CH, 128), CH)]).astype(BF)
            for b in range(4):
                ref[jnp.bitwise_xor(me, b), 0] = go[b * OWN : (b + 1) * OWN, :]
        small_ref[1:2, :] = gn
        small_ref[2:3, :] = shf
        small_ref[3:4, :] = ob


def crossed(r):
    return 2 * (r % 2) + r // 2


def middle_call(spot, tok, atts, g, pmt, vecs, eb, at, plan, pieces, after):
    n = tok.shape[0]
    N = n * ROWS
    blocks = SD((4, 4, OWN, CH), BF)

    def chunk(j, spot):
        return 2 * jnp.bitwise_xor(spot[0], j % 4) + jnp.bitwise_xor(spot[1], 1 - j // 4)

    def early(j, spot):
        return jnp.bitwise_xor(spot[0], jnp.minimum(j, 3))

    def late(j, spot):
        return jnp.bitwise_xor(spot[0], jnp.maximum(j, 4) - 4)

    rows = full((n, ROWS, D), **ONE)
    third = full((n, ROWS, LP), **ONE)
    cut = full((n, TOK, D), **ONE)
    outer = full((4, 1, OWN, CH), **ONE)
    args = (spot, tok, *atts, g, pmt, vecs, eb, at, *pieces)

    def body(*refs):
        middle_kernel(plan, len(pieces), *refs[: len(args)], *refs[len(args) + len(after) :])

    grid_spec = pltpu.PrefetchScalarGridSpec(
        num_scalar_prefetch=1,
        grid=(8,),
        in_specs=[rows, third, third, third, rows, full((ROWS, ROWS)), full((8, D)),
                  pl.BlockSpec((1, 1, CH), lambda j, spot: (chunk(j, spot), 0, 0)), smem()]
        + [any_space()] * (len(pieces) + len(after)),
        out_specs=[cut, cut, rows, rows, outer, outer,
                   pl.BlockSpec((4, 1, OWN, CH), lambda j, spot: (0, early(j, spot), 0, 0)),
                   pl.BlockSpec((4, 1, OWN, CH), lambda j, spot: (0, late(j, spot), 0, 0)),
                   pl.BlockSpec((1, 4, OWN, CH), lambda j, spot: (crossed(jnp.minimum(j, 3)), 0, 0, 0)),
                   pl.BlockSpec((1, 4, OWN, CH), lambda j, spot: (crossed(jnp.maximum(j, 4) - 4), 0, 0, 0)),
                   pl.BlockSpec((1, 1, CH), lambda j, spot: (chunk(j, spot), 0, 0)), full((8, D))],
        scratch_shapes=[pltpu.VMEM((D, D), BF), pltpu.VMEM((D, FF), BF), pltpu.VMEM((FF, D), BF),
                        pltpu.VMEM((N, D), F32), pltpu.VMEM((N, D), BF), pltpu.VMEM((N, D), BF), pltpu.VMEM((D, N), BF),
                        pltpu.VMEM((N, D), F32), pltpu.VMEM((N, D), F32), pltpu.VMEM((N, CH), BF), pltpu.VMEM((N, CH), BF),
                        pltpu.SemaphoreType.DMA((len(plan),))],
    )
    return pl.pallas_call(
        body,
        grid_spec=grid_spec,
        out_shape=[SD((n, TOK, D), BF), SD((n, TOK, D), BF), SD((n, ROWS, D), F32), SD((n, ROWS, D), BF),
                   SD((4, 1, OWN, CH), BF), SD((4, 1, OWN, CH), BF), blocks, blocks, blocks, blocks,
                   SD((8, 1, CH), F32), SD((8, D), F32)],
        compiler_params=params(62),
        cost_estimate=cost(6e10, 40 * MB, 7e6),
        name="middle",
    )(*args, *after)


def back_kernel(proj_ref, pt_ref, da_ref, gp_ref, db_ref):
    @pl.when(pl.program_id(0) == 0)
    def _():
        db_ref[...] = jnp.zeros_like(db_ref)

    hid = lane_head((TOK, LB))
    scale = HD**-0.5
    for w in range(2):
        r = slice(w * TOK, (w + 1) * TOK)
        for blk in range(LP // LB):
            l = blk * LB
            q = proj_ref[0, r, l : l + LB]
            k = proj_ref[0, r, LP + l : LP + l + LB]
            v = proj_ref[0, r, 2 * LP + l : 2 * LP + l + LB]
            do = da_ref[0, r, l : l + LB]
            qt, kt, dt = q.T, k.T, do.T
            dq, dk, dv = [], [], []
            for h in range(HB):
                hh = blk * HB + h
                s = slice(HD * h, HD * h + HD)
                dp = nt(jnp.where(hid == h, v, jnp.zeros_like(v)), do)
                pb = pt_ref[0, w, hh]
                p = pb.astype(F32)
                pd = p * dp
                ds = pd - p * colsum(pd)
                db_ref[hh] += ds
                dsb = ds.astype(BF)
                dq.append(nn(kt[s, :], dsb))
                dk.append(nt(qt[s, :], dsb))
                dv.append(nt(dt[s, :], pb))
            gp_ref[0, r, l : l + LB] = (jnp.concatenate(dq, axis=0) * scale).astype(BF).T
            gp_ref[0, r, LP + l : LP + l + LB] = (jnp.concatenate(dk, axis=0) * scale).astype(BF).T
            gp_ref[0, r, 2 * LP + l : 2 * LP + l + LB] = jnp.concatenate(dv, axis=0).astype(BF).T


def back_call(group, proj, pt, da, after):
    n = proj.shape[0]

    def blk(*s):
        return pl.BlockSpec((1,) + s, lambda i: (i,) + (0,) * len(s))

    return run(
        back_kernel, 3, (proj, pt, da), after,
        grid=(n,),
        in_specs=[blk(ROWS, 3 * LP), blk(2, HP, TOK, TOK), pl.BlockSpec((1, ROWS, LP), lambda i: (i, 0, group))],
        out_specs=[blk(ROWS, 3 * LP), full((HP, TOK, TOK))],
        out_shape=[SD((n, ROWS, 3 * LP), BF), SD((HP, TOK, TOK), F32)],
        compiler_params=params(),
        cost_estimate=cost(1.8e10, 10 * MB),
        name="attend_back",
    )


def inner_kernel(spot_ref, n1t_ref, *rest):
    me = spot_ref[0]
    core = spot_ref[1]
    gp_refs, outs, sum_ref = rest[: len(rest) // 3], rest[len(rest) // 3 : -1], rest[-1]
    for k, gp_ref in enumerate(gp_refs):
        n = gp_ref.shape[0]
        gp = gp_ref[...].reshape(n * ROWS, 3 * LP)
        sum_ref[k] = colsum(gp.astype(F32))
        gi = nn(n1t_ref[...], gp).astype(BF)
        send, keep = outs[2 * k], outs[2 * k + 1]

        for c in range(2):
            @pl.when(core == c)
            def _():
                for b in range(4):
                    r = slice(b * OWN, (b + 1) * OWN)
                    rel = jnp.bitwise_xor(me, b)
                    rel = crossed(rel) if k == 0 else rel
                    keep[rel, 0] = gi[r, c * CH : (c + 1) * CH]
                    send[rel, 0] = gi[r, (1 - c) * CH : (2 - c) * CH]


def inner_call(spot, n1t, gps, after):
    block = SD((4, 1, OWN, CH), BF)
    return single(
        inner_kernel, (spot, n1t, *gps), [block] * (2 * len(gps)) + [SD((len(gps), 1, 3 * LP), F32)], after,
        cost_estimate=cost(4e9 * len(gps), 6 * MB), name="inner_grad",
    )


def last_kernel(tok_ref, gmid_ref, vec_ref, pmt_ref, gp0_ref, gp1_ref, gp2_ref, w0_ref, w1_ref, w2_ref,
                small_ref, stay_ref, send_ref):
    @pl.when(pl.program_id(0) == 0)
    def _():
        small_ref[...] = jnp.zeros_like(small_ref)

    d = nt(gp0_ref[0], w0_ref[...]) + nt(gp1_ref[0], w1_ref[...]) + nt(gp2_ref[0], w2_ref[...])
    xh, r = norm_parts(tok_ref[0].astype(F32))
    small_ref[0:1, :] += colsum(d * xh)
    small_ref[1:2, :] += colsum(d)
    d = d * vec_ref[2:3, :]
    gm = gmid_ref[0] + r * (d - jnp.mean(d, axis=-1, keepdims=True) - xh * jnp.mean(d * xh, axis=-1, keepdims=True))
    o = nn(pmt_ref[...], gm.astype(BF)).astype(BF)
    stay_ref[0] = o[:TOK]
    send_ref[0] = o[TOK:]


def last_call(tok, gmid, gain, pmt, gps, ws, after):
    n = tok.shape[0]

    def blk(*s):
        return pl.BlockSpec((1,) + s, lambda i: (i,) + (0,) * len(s))

    return run(
        last_kernel, 10, (tok, gmid, gain, pmt, *gps, *ws), after,
        grid=(n,),
        in_specs=[blk(ROWS, D), blk(ROWS, D), full((8, D)), full((ROWS, ROWS))] + [blk(ROWS, 3 * LP)] * 3
        + [full((D, 3 * LP), **ONE)] * 3,
        out_specs=[full((8, D)), blk(TOK, D), blk(TOK, D)],
        out_shape=[SD((8, D), F32), SD((n, TOK, D), BF), SD((n, TOK, D), BF)],
        compiler_params=params(),
        cost_estimate=cost(2e10, 20 * MB),
        name="last",
    )


def vector_finish_kernel(count, spot_ref, sums_ref, thr_ref, inner_ref, inb_ref, outb_ref, upb_ref, downb_ref, g1_ref, s1_ref,
                         g2_ref, s2_ref, table_ref, clip_ref, factor_ref, max_ref):
    shard = spot_ref[2]

    def part(ref, rows, step=1):
        size = ref.shape[0]
        start = shard * size
        row = sums_ref[pl.ds(rows + step * (start // D), 1), :]
        row = jnp.broadcast_to(row, (8, D))
        ref[...] = pltpu.roll(row, D - start % D, 1)[0:1, :size].reshape(size)

    part(inb_ref, V_IN, 2)
    part(upb_ref, V_UP)
    for i, ref in enumerate((downb_ref, g2_ref, s2_ref, outb_ref)):
        part(ref, V_SMALL + i)
    part(g1_ref, V_ONE)
    part(s1_ref, V_ONE + 1)
    table_ref[...] = sums_ref[V_TABLE : V_TABLE + HEADS, :WIDE].T[: SPAN * SPAN, :]
    top = sums_ref[V_PEAK : V_PEAK + 1, :HEADS]
    factor = thr_ref[...].reshape(1, HEADS)
    factor = factor / jnp.maximum(top, factor)
    max_ref[...] = top.reshape(HEADS)
    factor_ref[...] = factor.reshape(HEADS)
    root = jnp.broadcast_to(jnp.sqrt(factor), (8, HEADS))
    head = lax.broadcasted_iota(jnp.int32, (HEADS, D), 0)
    col = lax.broadcasted_iota(jnp.int32, (HEADS, D), 1) // HD
    scale = lax.dot_general(root, (head == col).astype(F32), (((1,), (0,)), ((), ())), preferred_element_type=F32,
                            precision=lax.Precision.HIGHEST)[0:1, :]
    for k in range(2):
        clip_ref[:, k * D : (k + 1) * D] = (inner_ref[:, k * D : (k + 1) * D].astype(F32) * scale).astype(BF)
    clip_ref[:, 2 * D :] = inner_ref[:, 2 * D :]


def vector_finish(place, sums, threshold, inner, count):
    line = SD((D // count,), F32)
    return single(
        functools.partial(vector_finish_kernel, count), (place, sums, threshold, inner),
        [SD((2 * D // count,), F32), line, SD((FF // count,), F32), line, line, line, line, line,
         SD((SPAN * SPAN, HEADS), F32), SD(inner.shape, BF), SD((HEADS,), F32), SD((HEADS,), F32)],
        cost_estimate=cost(1e7, 3 * MB), name="vector_finish",
    )


def feed_finish_kernel(spot_ref, em_ref, eo_ref, rm_ref, ro_ref, ge_ref, gr_ref):
    for core in range(2):
        @pl.when(spot_ref[1] == core)
        def _():
            for c, e_ref, r_ref in ((core, em_ref, rm_ref), (1 - core, eo_ref, ro_ref)):
                for b in range(4):
                    ge_ref[:, (2 * b + c) * CH : (2 * b + c + 1) * CH] = e_ref[b].astype(F32)
                    r = c * CH + (b // 2) * OWN
                    gr_ref[r : r + OWN, (b % 2) * CH : (b % 2 + 1) * CH] = r_ref[b].astype(F32)


def feed_finish(spot, em, eo, rm, ro):
    return single(
        feed_finish_kernel, (spot, em, eo, rm, ro), [SD((OWN, FF), F32), SD((2 * CH, D), F32)],
        cost_estimate=cost(1e7, 8 * MB), name="feed_finish",
    )


def inner_columns(p, c):
    if c == 0:
        return [(0, LP, p * LP), (LP, LP // 2, D + p * LP)]
    return [(0, LP // 2, D + p * LP + LP // 2), (LP // 2, LP, 2 * D + p * LP)]


def inner_finish_kernel(spot_ref, *refs):
    mine, other, (gi_ref, go_ref) = refs[:4], refs[4:8], refs[8:]
    for core in range(2):
        @pl.when(spot_ref[1] == core)
        def _():
            for c, blocks in ((core, mine), (1 - core, other)):
                for p in range(3):
                    for at, size, put in inner_columns(p, c):
                        gi_ref[:, put : put + size] = blocks[p][0, :, at : at + size].astype(F32)
                go_ref[:, c * CH : (c + 1) * CH] = blocks[3][0].astype(F32)


def inner_finish(spot, mine, other):
    return single(
        inner_finish_kernel, (spot, *mine, *other), [SD((OWN, 3 * D), F32), SD((OWN, D), F32)],
        cost_estimate=cost(1e7, 4 * MB), name="inner_finish",
    )


def swap(block, axis, bit):
    count = lax.axis_size(axis)
    return lax.ppermute(block, axis, [(i, i ^ bit) for i in range(count) if i ^ bit < count])


def everywhere_hops():
    for axis in ("half", "shard", "replica"):
        bit = 1
        while bit < lax.axis_size(axis):
            yield axis, bit
            bit *= 2


def join_vectors(a, b):
    row = lax.broadcasted_iota(jnp.int32, a.shape, 0)
    return jnp.where(row == V_PEAK, jnp.maximum(a, b), a + b)


class Everywhere:
    def __init__(self, value):
        self.value = value
        self.hops = list(everywhere_hops())
        self.flying = None
        self.step()

    def step(self):
        if self.flying is not None:
            self.value = join_vectors(self.value, self.flying)
            self.flying = None
        if self.hops:
            self.flying = swap(self.value, *self.hops.pop(0))
        return [self.value]

    @property
    def done(self):
        return self.flying is None


def near(block):
    return [swap(block, "shard", 1), swap(block, "shard", 2)]


def fence(*values):
    return lax.optimization_barrier(values)


def add(a, b):
    return (a.astype(F32) + b.astype(F32)).astype(BF)


class Reduction:
    def __init__(self, sends, keeps, replica, short):
        self.short = short
        self.low = (replica & 1) == 0
        self.low2 = (replica & 2) == 0
        self.keep = keeps
        self.sent = sends
        self.stage = 0
        self.flying = [swap(v, "half", 1) for v in sends]

    def step(self):
        hlf = OWN // 2
        got, low, low2 = self.flying, self.low, self.low2
        if self.stage == 0:
            self.sent = [add(k[2:], g[2:]) for k, g in zip(self.keep, got)]
            self.keep = [add(k[:2], g[:2]) for k, g in zip(self.keep, got)]
            self.flying = [swap(self.sent[0], "shard", 1), swap(self.sent[1], "shard", 2)]
        elif self.stage == 1:
            self.sent = [add(k[1], g[1]) for k, g in zip(self.keep, got)]
            self.keep = [add(k[0], g[0]) for k, g in zip(self.keep, got)]
            self.flying = [swap(self.sent[0], "shard", 2), swap(self.sent[1], "shard", 1)]
        elif self.stage == 2:
            a, b = (add(k, g) for k, g in zip(self.keep, got))
            self.keep = jnp.where(low, a, b)
            self.sent = [jnp.where(low, b, a)]
            self.flying = swap(self.sent[0], "replica", 1)
        elif self.stage == 3 and self.short:
            self.keep = add(self.keep, got)
            self.sent = [self.keep]
            self.flying = swap(self.keep, "replica", 2)
            self.stage = 4
        elif self.stage == 3:
            u = add(self.keep, got)
            self.keep = jnp.where(low2, u[:, :hlf], u[:, hlf:])
            self.sent = [jnp.where(low2, u[:, hlf:], u[:, :hlf])]
            self.flying = swap(self.sent[0], "replica", 2)
        elif self.stage == 4:
            self.keep = add(self.keep, got)
            self.sent = [self.keep]
            self.flying = swap(self.keep, "replica", 2)
        elif self.stage == 5:
            v = self.keep
            if self.short:
                self.keep = add(v, got)
            else:
                self.keep = jnp.concatenate([jnp.where(low2, v, got), jnp.where(low2, got, v)], axis=1)
            self.sent = [self.keep]
            self.flying = swap(self.keep, "replica", 1)
        elif self.stage == 6:
            v = self.keep
            self.keep = [jnp.where(low, v, got), jnp.where(low, got, v)]
            self.sent = self.keep
            self.flying = [swap(v, "half", 1) for v in self.keep]
        self.stage += 1
        return list(self.sent)

    @property
    def done(self):
        return self.stage == 7


def together(chains, *others):
    left = [c for c in chains if not c.done]
    flying, others = fence([c.flying for c in left], others)
    for c, v in zip(left, flying):
        c.flying = v
        c.step()
    return others


def shards(images, cotangent, present, threshold, inner_weight, inner_bias, outer_weight, outer_bias, expand_weight,
           expand_bias, reduce_weight, reduce_bias, first_gain, first_shift, second_gain, second_shift, bias_table):
    n = images.shape[0]
    core = lax.axis_index("half")
    shard = lax.axis_index("shard")
    replica = lax.axis_index("replica")
    shard_count = lax.axis_size("shard")
    quick = shard_count == 4 and lax.axis_size("replica") == 4
    me = shard if quick else jnp.int32(0)
    spot = jnp.stack([me, core]).astype(jnp.int32)
    own_images = images.reshape(n, ROWS, D)
    own_grad = cotangent.reshape(n, ROWS, D)
    vectors = (inner_bias, outer_bias, expand_bias, reduce_bias, first_gain, first_shift, second_gain, second_shift)
    order = jnp.asarray(row_order(), BF)
    back_order = jnp.asarray(row_order().T, BF)
    alive = present.astype(F32).reshape(1, n)
    table_rows = jnp.pad(bias_table.astype(F32).T, ((0, 0), (0, WIDE - bias_table.shape[0])))
    if quick:
        first, others, others_half = first_call(spot, vectors, inner_weight)
        get_first, get_others = near(first), near(others_half)
        expand_weight, first = fence(expand_weight, first)
        big, up = cut_call(spot, outer_weight, expand_weight, reduce_weight, own_images, own_grad)
        spot, up, big = fence(spot, up, big)
        upper = swap(up, "half", 1)
        masks_0 = bias_call(0, spot, table_rows)
        get_first, upper, masks_0 = fence(get_first, upper, masks_0)
        get_first.append(swap(get_first[0], "shard", 2))
        tok, g, grad_down = prep_call(own_images, own_grad, upper, alive, order)
        get_first, get_others, tok = fence(get_first, get_others, tok)
        first_pieces = [first] + get_first
        get_others.append(swap(get_others[1], "shard", 1))
        others_back = [swap(v, "half", 1) for v in get_others[:2]]
        in_bias, up_bias, vecs, n1, n1t = vector_call(spot, first_pieces, tok)
        n1, big = fence(n1, big)
        get_big = near(big)
    else:
        masks_0 = bias_call(0, spot, table_rows)
        upper = jnp.concatenate([swap(own_images[:, :TOK], "half", 1), swap(own_grad[:, :TOK], "half", 1)])
        whole_vectors = [lax.all_gather(v, "shard", axis=0, tiled=True).reshape(4, -1) for v in vectors]
        parts = jnp.stack([jnp.pad(v, ((0, 0), (0, D - v.shape[1]))) for v in whole_vectors], axis=1)
        parts = [jnp.pad(parts[r], ((0, 8), (0, 0))) for r in range(4)]
        thirds = inner_weight.reshape(-1, 3, 3, LP).transpose(0, 2, 1, 3).reshape(-1, 3, 3 * LP)
        first = thirds[:, 0]
        others = thirds[:, 1:].reshape(-1, 6 * LP)

        tok, g, grad_down = prep_call(own_images, own_grad, upper, alive, order)
        in_bias, up_bias, vecs, n1, n1t = vector_call(spot, parts, tok)

    if quick:
        def places(rows):
            at = [me * rows]
            for c in (core, 1 - core):
                at += [(me ^ 1) * rows + c * (rows // 2), (me ^ 2) * rows + c * (rows // 2), (me ^ 3) * rows + c * (rows // 2)]
            return at

        first_at = jnp.stack([(me ^ r) * OWN for r in range(4)]).astype(jnp.int32)
        in_at = jnp.stack(places(OWN)).astype(jnp.int32)

        def in_plan(columns):
            return [(k, 0, OWN if k == 0 else OWN // 2, columns, 3 * LP, 0, 0) for k in range(7)]

        in_plans = [[(k, 0, OWN, 0, 3 * LP, 0, 0) for k in range(4)], in_plan(0), in_plan(3 * LP)]
    else:
        first_at = in_at = jnp.zeros((1,), jnp.int32)
        first_pieces = [lax.all_gather(first, "shard", axis=0, tiled=True)]
        others_pieces = [lax.all_gather(others, "shard", axis=0, tiled=True)]
        in_plans = [[(0, 0, D, k, 3 * LP, 0, 0)] for k in (0, 0, 3 * LP)]

    results = [attend_call(0, n1, in_bias, masks_0, first_at, in_plans[0], first_pieces, [])]
    if quick:
        get_others, others_back, results, spot = fence(get_others, others_back, results, spot)
        others_back.append(swap(get_others[2], "half", 1))
    masks_1 = bias_call(1, spot, table_rows)
    masks_2 = bias_call(2, spot, table_rows)
    if quick:
        others_back, masks_1, masks_2 = fence(others_back, masks_1, masks_2)
        others_pieces = [others] + get_others + others_back
    results.append(attend_call(1, n1, in_bias, masks_1, in_at, in_plans[1], others_pieces, [masks_2]))
    if quick:
        get_big, results, masks_2 = fence(get_big, results, masks_2)
        far = [swap(get_big[0][: BIG // 2], "shard", 2), swap(get_big[1][BIG // 2 :], "shard", 1)]
        big_back = [swap(v, "half", 1) for v in get_big]
    results.append(attend_call(2, n1, in_bias, masks_2, in_at, in_plans[2], others_pieces, []))
    if quick:
        far, big_back, results = fence(far, big_back, results)
        far_back = [swap(v, "half", 1) for v in far]
        far_back, results = fence(far_back, results)
        pieces = [outer_weight, expand_weight, reduce_weight] + get_big + far + big_back + far_back
        hlf = OWN // 2
        plan = [(0, 0, OWN, 0, D, 0, 0), (1, 0, OWN, 0, FF, 1, 0), (2, 0, 4 * OWN, 0, D, 2, 0)]
        short, long = places(OWN), places(4 * OWN)
        at = [short[0], short[0], long[0]]
        parts = [(b * hlf, hlf, 1, b * D) for b in range(4)] + [(4 * hlf, hlf, 0, 0), (5 * hlf, 4 * hlf, 2, 0)]

        def add_piece(source, lo, hi, place):
            for row, rows, target, column in parts:
                a, b = max(row, lo), min(row + rows, hi)
                if a < b:
                    plan.append((source, a - lo, b - a, 0, D, target, column))
                    at.append((long if target == 2 else short)[place] + (a - row))

        for side in range(2):
            for k in range(2):
                add_piece(3 + 4 * side + k, 0, BIG, 1 + 3 * side + k)
            add_piece(5 + 4 * side, 0, BIG // 2, 3 + 3 * side)
            add_piece(6 + 4 * side, BIG // 2, BIG, 3 + 3 * side)
        at = jnp.stack(at).astype(jnp.int32)
    else:
        pieces = [lax.all_gather(v, "shard", axis=0, tiled=True) for v in (outer_weight, expand_weight, reduce_weight)]
        plan = [(0, 0, D, 0, D, 0, 0), (1, 0, D, 0, FF, 1, 0), (2, 0, FF, 0, D, 2, 0)]
        at = jnp.zeros((3,), jnp.int32)
    projs, pts, atts, peak, ws = zip(*results)
    (stay, send, gmid, datt, out_send, out_keep, e_send, e_keep, r_send, r_keep, grad_up, small) = middle_call(
        spot, tok, atts, g, back_order, vecs, up_bias, at, plan, pieces, []
    )
    if quick:
        feed = Reduction([r_send, e_send], [r_keep, e_keep], replica, False)
    lower_out = swap(send, "half", 1)
    gp0, db0 = back_call(0, projs[0], pts[0], datt, [])
    if quick:
        (gp0, lower_out, projs) = together([feed], gp0, lower_out, projs)
    gp1, db1 = back_call(1, projs[1], pts[1], datt, feed.sent if quick else [])
    i0_send, i0_keep, i1_send, i1_keep, in01 = inner_call(spot, n1t, (gp0, gp1), [])
    chains = []
    if quick:
        i0_send, i1_send, projs = together([feed], i0_send, i1_send, projs)
        ahead = Reduction([i0_send, i1_send], [i0_keep, i1_keep], replica, True)
        chains = [feed, ahead]
    gp2, db2 = back_call(2, projs[2], pts[2], datt, feed.sent if quick else [])
    if quick:
        gp2, db2 = together(chains, gp2, db2)
    i2_send, i2_keep, in2 = inner_call(spot, n1t, (gp2,), feed.sent + ahead.sent if quick else [])
    if quick:
        rest = Reduction([i2_send, out_send], [i2_keep, out_keep], replica, True)
        chains = [feed, ahead, rest]
    one, gstay, gsend = last_call(tok, gmid, vecs, back_order, (gp0, gp1, gp2), ws, [i2_send])
    after = []
    if quick:
        gsend, one = together(chains, gsend, one)
        after = feed.sent + ahead.sent + rest.sent
    lower_grad = swap(gsend, "half", 1)
    peak = jnp.concatenate(peak, axis=2)
    peaks = jnp.max(jnp.where((present > 0)[:, None, None, None], peak, NEGATIVE), axis=(0, 1, 3)).reshape(1, HEADS)
    sums = table_call((db0, db1, db2), grad_up, grad_down, small, in01, in2, one, peaks, after)
    if quick:
        sums, lower_grad = together(chains, sums, lower_grad)
    every = Everywhere(sums)
    chains.append(every)
    while not all(c.done for c in chains):
        together(chains)
    sums = every.value

    place = jnp.stack([me, core, shard]).astype(jnp.int32)
    (grad_inbias, grad_outbias, grad_upbias, grad_downbias, grad_gain_1, grad_shift_1, grad_gain_2, grad_shift_2, grad_table,
     clipped, factors, maxima) = vector_finish(place, sums, threshold, inner_weight, shard_count)

    if quick:
        (rm, em), (ro, eo) = feed.keep, feed.flying
        grad_expand, grad_reduce = feed_finish(spot, em, eo, rm, ro)
        grad_inner, grad_outer = inner_finish(spot, ahead.keep + rest.keep, ahead.flying + rest.flying)
    else:
        def halves(keep, send, axis):
            lo = jnp.where(core == 0, keep, send)
            hi = jnp.where(core == 0, send, keep)
            return jnp.concatenate([lo, hi], axis=axis)

        def whole(keep, send):
            both = halves(keep[:, :, :, None], send[:, :, :, None], 3)
            return both.transpose(0, 2, 1, 3, 4).reshape(D, -1)

        def settle(v):
            v = lax.psum_scatter(v.astype(BF), "shard", scatter_dimension=0, tiled=True)
            return lax.psum(v, ("replica", "half")).astype(F32)

        def rows_of(v):
            return straight(v).reshape(4, 1, 2, 2, OWN, CH).transpose(0, 1, 2, 4, 3, 5).reshape(4, 1, CH, D)

        def straight(v):
            return jnp.stack([v[0], v[2], v[1], v[3]])

        grad_reduce = settle(halves(rows_of(r_keep), rows_of(r_send), 1).reshape(FF, D))
        grad_expand = settle(whole(e_keep, e_send))
        grad_outer = settle(whole(out_keep, out_send))
        by_third = [
            whole(straight(i0_keep), straight(i0_send)), whole(i1_keep, i1_send), whole(straight(i2_keep), straight(i2_send))
        ]
        by_third = jnp.stack(by_third, axis=1).reshape(D, 3, 3, LP).transpose(0, 2, 1, 3).reshape(D, 3 * D)
        grad_inner = settle(by_third)

    block_out = jnp.concatenate([lower_out, stay], axis=1).reshape(images.shape)
    grad_images = jnp.concatenate([lower_grad, gstay], axis=1).reshape(images.shape)
    return (
        block_out,
        grad_images,
        grad_inner,
        grad_inbias,
        grad_outer,
        grad_outbias,
        grad_expand,
        grad_upbias,
        grad_reduce,
        grad_downbias,
        grad_gain_1,
        grad_shift_1,
        grad_gain_2,
        grad_shift_2,
        grad_table,
        clipped,
        factors,
        maxima,
    )


def solution(mesh):
    rows = P(("replica", "shard"), "half", None, None)
    cut = P("shard", None)
    line = P("shard")
    return jax.shard_map(
        shards,
        mesh=mesh,
        in_specs=(rows, rows, P(("replica", "shard")), P(), cut, line, cut, line, cut, line, cut, line, line, line, line,
                  line, P()),
        out_specs=(rows, rows, cut, line, cut, line, cut, line, cut, line, line, line, line, line, P(), cut, P(), P()),
        check_vma=False,
    )
```

time: 496 us -> 449 us (0.905)
  Pallas kernels: 221 us -> 275 us
  local copies, waits for them, and re-layouts: 58.8 us -> 11.9 us
  waiting for transfers between devices: 111 us -> 65.3 us
  starting transfers between devices: 61.3 us -> 49.6 us
    pallas_call x7 -> x21, Pallas kernels: 221 us -> 275 us  [the longest x15 167 us: run(): pl.pallas_call(body, in_specs=list(in_specs) + [any_space()] * len(after)...]
    ppermute x66 -> x59, waiting for transfers between devices: 111 us -> 65.3 us  [swap(): lax.ppermute(block, axis, [(i, i ^ bit) for i in range(count) if i ^ bit...]
    convert_element_type x10 -> x18, other arithmetic: 7.43 us -> 26 us  [add(): return (a.astype(F32) + b.astype(F32)).astype(BF)]
    convert_element_type x11 -> x0, local copies, waits for them, and re-layouts: 16 us -> none  [the longest x4 11.3 us: halves(): return jnp.concatenate([lo, hi], axis=axis).astype(F32)]
    ppermute x66 -> x59, starting transfers between devices: 61.3 us -> 49.6 us  [swap(): lax.ppermute(block, axis, [(i, i ^ bit) for i in range(count) if i ^ bit...]
    slice x17 -> x2, local copies, waits for them, and re-layouts: 10 us -> 1.94 us  [the longest x1 1.06 us: shards(): get_big[0][:BIG // 2]]
    concatenate x10 -> x1, other arithmetic: 7.13 us -> 0.06 us  [step(): jnp.concatenate([jnp.where(low2, v, got), jnp.where(low2, got, v)], axis=1)]
    concatenate x3 -> x0, local copies, waits for them, and re-layouts: 6.24 us -> none  [the longest x1 5.56 us: shards(): packed = jnp.concatenate(vectors).reshape(1, -1)]
  transfers between devices with their start and end apart: 66 -> 59, of which waited for: 21 -> 15; matrix products, arithmetic and copies ran while one was open for 13% -> 8% of each run, Pallas kernels for 12% -> 39%
where the time goes in v2:
time: 449 us; the launch traced here: 443 us
  Pallas kernels  275 us (61%)
  waiting for transfers between devices  65.3 us (15%)
  starting transfers between devices  49.6 us (11%)
  other arithmetic  39.7 us (9%)
  local copies, waits for them, and re-layouts  11.9 us (3%)
    pallas_call x15, Pallas kernels, run(): pl.pallas_call(body, in_specs=list(in_specs) + [any_space()] * len(after)...  167 us
    pallas_call x1, Pallas kernels, middle_call(): pl.pallas_call(body, grid_spec=grid_spec, out_shape=[SD((n, TOK, D), BF),...  84.3 us
    ppermute x59, waiting for transfers between devices, swap(): lax.ppermute(block, axis, [(i, i ^ bit) for i in range(count) if i ^ bit...  65.3 us
    ppermute x59, starting transfers between devices, swap(): lax.ppermute(block, axis, [(i, i ^ bit) for i in range(count) if i ^ bit...  49.6 us
    convert_element_type x18, other arithmetic, add(): return (a.astype(F32) + b.astype(F32)).astype(BF)  26 us
    pallas_call x3, Pallas kernels, bias_call(): pl.pallas_call(bias_kernel, grid=(1,), in_specs=[smem(), pl.BlockSpec((HP...  14.1 us
  transfers between devices with their start and end apart: 59, of which 15 were waited for; matrix products, arithmetic and copies ran while one was open for 8% of the time, Pallas kernels for 39%

profile of v2, /device:TPU:0, one launch (start us, length us, event | category | flops | bytes accessed | tf_op | source)
XLA Modules:
  0.0 443.4 jit_solution(11625420927153522167)
XLA Ops:
  3.6 4.0 cut.1
  12.8 4.7 %bias.3.refs_2_ = f32[2,8,144,144]{3,2,1,0:T(8,128)} custom-call(s32[2]{0:T(128)} %pad_add_fusion.refs_0_.spot_ref, f32[24,640]{1,0:T(8,128)} %pad_convert_fusion.table_ref, bf16[2,2,144,144]{3,2,1,0:T(8,128)(2,1)} %constant.55.clone.mask_ref, bf16[384,144]{1,0:T(8,128)(2,1)} %constant.56.clone.sq_ref, bf16[144,192]{1,0:T(8,128)(2,1)} %constant.57.clone.sk_ref), custom_call_target="tpu_custom_call" | custom-call | flops 2000000 | bytes 3145 | tf_op jit(solution)/shard_map/bias/pallas_call | solution.py:163
  23.2 6.2 %prep.1 = (bf16[4,288,768]{2,1,0:T(8,128)(2,1)}, bf16[4,288,768]{2,1,0:T(8,128)(2,1)}, f32[1,768]{1,0:T(1,128)}) custom-call(bf16[4,288,768]{2,1,0:T(8,128)(2,1)} %bitcast.96, bf16[4,288,768]{2,1,0:T(8,128)(2,1)} %bitcast.98, bf16[8,144,768]{2,1,0:T(8,128)(2,1)} %copy-done.16, f32[1,4]{1,0:T(1,128)} %convert_bitcast_fusion.refs_3_, ...), custom_call_target="tpu_custom_call" | custom-call | flops 3000000 | bytes 16777 | tf_op jit(solution)/shard_map/prep/pallas_call | solution.py:72
  29.8 5.6 %collective-permute-done.5.refs_6_ = bf16[96,1536]{1,0:T(8,128)(2,1)S(1)} collective-permute-done((bf16[96,1536]{1,0:T(8,128)(2,1)S(1)}, bf16[96,1536]{1,0:T(8,128)(2,1)S(1)}, u32[]{:S(2)}, u32[]{:S(2)}) %collective-permute-start.5) | collective-permute-done | bytes 294944 | tf_op jit(solution)/shard_map/ppermute | solution.py:777
  36.2 5.4 %vectors.1 = (f32[3,1,768]{2,1,0:T(1,128)}, f32[8,1,384]{2,1,0:T(1,128)}, f32[8,768]{1,0:T(8,128)}, bf16[4,288,768]{2,1,0:T(8,128)(2,1)}, bf16[768,1152]{1,0:T(8,128)(2,1)}) custom-call(s32[2]{0:T(128)} %pad_add_fusion.refs_0_.spot_ref, bf16[208,768]{1,0:T(8,128)(2,1)} %get-tuple-element.231.pa_ref.refs_4_, bf16[208,768]{1,0:T(8,128)(2,1)} %copy-done.18, ...), custom_call_target="tpu_custom_call" | custom-call | flops 5000000 | bytes 8388 | tf_op jit(solution)/shard_map/vectors/pallas_call | solution.py:328
  46.2 18.2 %attend.3 = (bf16[4,288,768]{2,1,0:T(8,128)(2,1)}, bf16[4,2,8,144,144]{4,3,2,1,0:T(8,128)(2,1)}, bf16[4,288,256]{2,1,0:T(8,128)(2,1)}, f32[4,2,8,144]{3,2,1,0:T(8,128)}, bf16[768,768]{1,0:T(8,128)(2,1)}) custom-call(bf16[4,288,768]{2,1,0:T(8,128)(2,1)} %get-tuple-element.238.refs_0_, f32[3,1,768]{2,1,0:T(1,128)} %get-tuple-element.239.refs_1_, ...), custom_call_target="tpu_custom_call" | custom-call | flops 13000000 | bytes 12582 | tf_op jit(solution)/shard_map/attend/pallas_call | solution.py:72
  64.4 14.3 %collective-permute-done.6.refs_7_ = bf16[96,1536]{1,0:T(8,128)(2,1)S(1)} collective-permute-done((bf16[96,1536]{1,0:T(8,128)(2,1)S(1)}, bf16[96,1536]{1,0:T(8,128)(2,1)S(1)}, u32[]{:S(2)}, u32[]{:S(2)}) %collective-permute-start.6) | collective-permute-done | bytes 294944 | tf_op jit(solution)/shard_map/ppermute | solution.py:777
  79.6 4.7 %bias.4.refs_2_ = f32[2,8,144,144]{3,2,1,0:T(8,128)} custom-call(s32[2]{0:T(128)} %pad_add_fusion.refs_0_.spot_ref, f32[24,640]{1,0:T(8,128)} %pad_convert_fusion.table_ref, bf16[2,2,144,144]{3,2,1,0:T(8,128)(2,1)} %constant.55.clone.mask_ref, bf16[384,144]{1,0:T(8,128)(2,1)} %constant.56.clone.sq_ref, bf16[144,192]{1,0:T(8,128)(2,1)} %constant.57.clone.sk_ref), custom_call_target="tpu_custom_call" | custom-call | flops 2000000 | bytes 3145 | tf_op jit(solution)/shard_map/bias/pallas_call | solution.py:163
  84.2 4.7 %bias.5.refs_11_.refs_2_ = f32[2,8,144,144]{3,2,1,0:T(8,128)} custom-call(s32[2]{0:T(128)} %pad_add_fusion.refs_0_.spot_ref, f32[24,640]{1,0:T(8,128)} %pad_convert_fusion.table_ref, bf16[2,2,144,144]{3,2,1,0:T(8,128)(2,1)} %constant.55.clone.mask_ref, bf16[384,144]{1,0:T(8,128)(2,1)} %constant.56.clone.sq_ref, bf16[144,192]{1,0:T(8,128)(2,1)} %constant.57.clone.sk_ref), custom_call_target="tpu_custom_call" | custom-call | flops 2000000 | bytes 3145 | tf_op jit(solution)/shard_map/bias/pallas_call | solution.py:163
  89.6 17.9 %attend.4 = (bf16[4,288,768]{2,1,0:T(8,128)(2,1)}, bf16[4,2,8,144,144]{4,3,2,1,0:T(8,128)(2,1)}, bf16[4,288,256]{2,1,0:T(8,128)(2,1)}, f32[4,2,8,144]{3,2,1,0:T(8,128)}, bf16[768,768]{1,0:T(8,128)(2,1)}) custom-call(bf16[4,288,768]{2,1,0:T(8,128)(2,1)} %get-tuple-element.238.refs_0_, f32[3,1,768]{2,1,0:T(1,128)} %get-tuple-element.239.refs_1_, ...), custom_call_target="tpu_custom_call" | custom-call | flops 13000000 | bytes 12582 | tf_op jit(solution)/shard_map/attend/pallas_call | solution.py:72
  111.6 18.1 %attend.5 = (bf16[4,288,768]{2,1,0:T(8,128)(2,1)}, bf16[4,2,8,144,144]{4,3,2,1,0:T(8,128)(2,1)}, bf16[4,288,256]{2,1,0:T(8,128)(2,1)}, f32[4,2,8,144]{3,2,1,0:T(8,128)}, bf16[768,768]{1,0:T(8,128)(2,1)}) custom-call(bf16[4,288,768]{2,1,0:T(8,128)(2,1)} %get-tuple-element.238.refs_0_, f32[3,1,768]{2,1,0:T(1,128)} %get-tuple-element.239.refs_1_, ...), custom_call_target="tpu_custom_call" | custom-call | flops 13000000 | bytes 12582 | tf_op jit(solution)/shard_map/attend/pallas_call | solution.py:72
  133.2 84.3 %middle.1 = (bf16[4,144,768]{2,1,0:T(8,128)(2,1)}, bf16[4,144,768]{2,1,0:T(8,128)(2,1)}, f32[4,288,768]{2,1,0:T(8,128)}, bf16[4,288,768]{2,1,0:T(8,128)(2,1)}, b...) custom-call(s32[2]{0:T(128)} %pad_add_fusion.refs_0_.spot_ref, ...), custom_call_target="tpu_custom_call" | custom-call | flops 60000000 | bytes 41943 | tf_op jit(solution)/shard_map/middle/pallas_call | solution.py:558
  218.2 20.1 %attend_back.3 = (bf16[4,288,768]{2,1,0:T(8,128)(2,1)}, f32[8,144,144]{2,1,0:T(8,128)}) custom-call(bf16[4,288,768]{2,1,0:T(8,128)(2,1)} %get-tuple-element.316.refs_0_, bf16[4,2,8,144,144]{4,3,2,1,0:T(8,128)(2,1)} %get-tuple-element.317.refs_1_, bf16[4,288,768]{2,1,0:T(8,128)(2,1)} %get-tuple-element.318.refs_2_), custom_call_target="tpu_custom_call" | custom-call | flops 18000000 | bytes 10485 | tf_op jit(solution)/shard_map/attend_back/pallas_call | solution.py:72
  239.9 3.2 add_convert_fusion
  247.5 20.1 %attend_back.4 = (bf16[4,288,768]{2,1,0:T(8,128)(2,1)}, f32[8,144,144]{2,1,0:T(8,128)}) custom-call(bf16[4,288,768]{2,1,0:T(8,128)(2,1)} %get-tuple-element.331.refs_0_, bf16[4,2,8,144,144]{4,3,2,1,0:T(8,128)(2,1)} %get-tuple-element.332.refs_1_, bf16[4,288,768]{2,1,0:T(8,128)(2,1)} %get-tuple-element.318.refs_2_, ...), custom_call_target="tpu_custom_call" | custom-call | flops 18000000 | bytes 10485 | tf_op jit(solution)/shard_map/attend_back/pallas_call | solution.py:72
  267.5 8.6 %inner_grad.2 = (bf16[4,1,192,384]{3,2,1,0:T(8,128)(2,1)}, bf16[4,1,192,384]{3,2,1,0:T(8,128)(2,1)}, bf16[4,1,192,384]{3,2,1,0:T(8,128)(2,1)}, bf16[4,1,192,384]{3,2,1,0:T(8,128)(2,1)}, f32[2,1,768]{2,1,0:T(1,128)}) custom-call(s32[2]{0:T(128)} %pad_add_fusion.refs_0_.spot_ref, bf16[768,1152]{1,0:T(8,128)(2,1)} %get-tuple-element.329.refs_1_, ...), custom_call_target="tpu_custom_call" | custom-call | flops 8000000 | bytes 6291 | tf_op jit(solution)/shard_map/inner_grad/pallas_call | solution.py:72
  282.2 20.1 %attend_back.5 = (bf16[4,288,768]{2,1,0:T(8,128)(2,1)}, f32[8,144,144]{2,1,0:T(8,128)}) custom-call(bf16[4,288,768]{2,1,0:T(8,128)(2,1)} %get-tuple-element.341.refs_0_, bf16[4,2,8,144,144]{4,3,2,1,0:T(8,128)(2,1)} %get-tuple-element.342.refs_1_, bf16[4,288,768]{2,1,0:T(8,128)(2,1)} %get-tuple-element.318.refs_2_, bf16[4,192,384]{2,1,0:T(8,128)(2,1)} %fusion.3.refs_3_, ...), custom_call_target="tpu_custom_call" | custom-call | flops 18000000 | bytes 10485 | tf_op jit(solution)/shard_map/attend_back/pallas_call | solution.py:72
  309.3 5.0 %inner_grad.3 = (bf16[4,1,192,384]{3,2,1,0:T(8,128)(2,1)}, bf16[4,1,192,384]{3,2,1,0:T(8,128)(2,1)}, f32[1,1,768]{2,1,0:T(1,128)}) custom-call(s32[2]{0:T(128)} %pad_add_fusion.refs_0_.spot_ref, bf16[768,1152]{1,0:T(8,128)(2,1)} %get-tuple-element.329.refs_1_, bf16[4,288,768]{2,1,0:T(8,128)(2,1)} %get-tuple-element.351.refs_2_.refs_6_, ...), custom_call_target="tpu_custom_call" | custom-call | flops 4000000 | bytes 6291 | tf_op jit(solution)/shard_map/inner_grad/pallas_call | solution.py:72
  319.0 13.3 %last.1 = (f32[8,768]{1,0:T(8,128)}, bf16[4,144,768]{2,1,0:T(8,128)(2,1)}, bf16[4,144,768]{2,1,0:T(8,128)(2,1)}) custom-call(bf16[4,288,768]{2,1,0:T(8,128)(2,1)} %get-tuple-element.235.tok_ref.refs_1_.refs_0_, f32[4,288,768]{2,1,0:T(8,128)} %get-tuple-element.354.refs_1_, f32[8,768]{1,0:T(8,128)} %get-tuple-element.308.refs_7_.refs_2_, ...), custom_call_target="tpu_custom_call" | custom-call | flops 20000000 | bytes 20971 | tf_op jit(solution)/shard_map/last/pallas_call | solution.py:72
  342.1 2.7 collective-permute-start.32
  345.7 3.4 collective-permute-done.34
  351.9 7.8 %table.1 = f32[40,768]{1,0:T(8,128)} custom-call(f32[8,144,144]{2,1,0:T(8,128)} %get-tuple-element.367.refs_0_, f32[8,144,144]{2,1,0:T(8,128)} %get-tuple-element.368.refs_1_, f32[8,144,144]{2,1,0:T(8,128)} %get-tuple-element.369.refs_2_, f32[8,1,384]{2,1,0:T(1,128)} %get-tuple-element.370.refs_3_, f32[1,768]{1,0:T(1,128)} %get-tuple-element.371.refs_4_, ...), custom_call_target="tpu_custom_call" | custom-call | flops 6000000 | bytes 4194 | tf_op jit(solution)/shard_map/table/pallas_call | solution.py:72
  364.5 2.7 collective-permute-start.38
  370.1 4.4 collective-permute-done.39
  374.5 4.9 %collective-permute-done.38 = bf16[4,96,384]{2,1,0:T(8,128)(2,1)S(1)} collective-permute-done((bf16[4,96,384]{2,1,0:T(8,128)(2,1)S(1)}, bf16[4,96,384]{2,1,0:T(8,128)(2,1)S(1)}, u32[]{:S(2)}, u32[]{:S(2)}) %collective-permute-start.38) | collective-permute-done | bytes 294944 | tf_op jit(solution)/shard_map/ppermute | solution.py:777
  388.8 13.7 %collective-permute-done.45 = bf16[1,192,384]{2,1,0:T(8,128)(2,1)S(1)} collective-permute-done((bf16[1,192,384]{2,1,0:T(8,128)(2,1)S(1)}, bf16[1,192,384]{2,1,0:T(8,128)(2,1)S(1)}, u32[]{:S(2)}, u32[]{:S(2)}) %collective-permute-start.45) | collective-permute-done | bytes 147488 | tf_op jit(solution)/shard_map/ppermute | solution.py:777
  408.6 4.3 collective-permute-done.48
  415.3 2.6 collective-permute-done.51
  419.6 2.7 collective-permute-start.56
  422.4 5.0 %collective-permute-done.56 = f32[40,768]{1,0:T(8,128)S(1)} collective-permute-done((f32[40,768]{1,0:T(8,128)S(1)}, f32[40,768]{1,0:T(8,128)S(1)}, u32[]{:S(2)}, u32[]{:S(2)}) %collective-permute-start.56) | collective-permute-done | bytes 122912 | tf_op jit(solution)/shard_map/ppermute | solution.py:777
  434.3 2.9 inner_finish.1
  438.9 4.1 feed_finish.1
  (276 shorter events, 102.0 us)
Async XLA Ops:
  20.3 15.2 %collective-permute-start.3 = (bf16[208,768]{1,0:T(8,128)(2,1)S(1)}, bf16[208,768]{1,0:T(8,128)(2,1)S(1)}, u32[]{:S(2)}, u32[]{:S(2)}) collective-permute-start(bf16[208,768]{1,0:T(8,128)(2,1)S(1)} %collective-permute-done.pb_ref.refs_5_), channel_id=1, source_target_pairs={{0,4},{2,6},{4,0},{6,2},{1,5},{3,7},{5,1},{7,3},{8,12},{10,14},{12... | collective-permute-start | bytes 958472 | tf_op jit(solution)/shard_map/ppermute | solution.py:777
  41.6 65.9 %collective-permute-start.10 = (bf16[864,768]{1,0:T(8,128)(2,1)}, bf16[864,768]{1,0:T(8,128)(2,1)S(1)}, u32[]{:S(2)}, u32[]{:S(2)}) collective-permute-start(bf16[864,768]{1,0:T(8,128)(2,1)} %get-tuple-element.247), channel_id=1, source_target_pairs={{0,4},{2,6},{4,0},{6,2},{1,5},{3,7},{5,1},{7,3},{8,12},{10,14},{12... | collective-permute-start | bytes 3981320 | tf_op jit(solution)/shard_map/ppermute | solution.py:777
  43.1 64.4 %collective-permute-start.9 = (bf16[864,768]{1,0:T(8,128)(2,1)}, bf16[864,768]{1,0:T(8,128)(2,1)S(1)}, u32[]{:S(2)}, u32[]{:S(2)}) collective-permute-start(bf16[864,768]{1,0:T(8,128)(2,1)} %get-tuple-element.247), channel_id=1, source_target_pairs={{0,2},{2,0},{4,6},{6,4},{1,3},{3,1},{5,7},{7,5},{8,10},{10,8},{12,... | collective-permute-start | bytes 3981320 | tf_op jit(solution)/shard_map/ppermute | solution.py:777
  43.7 35.1 %collective-permute-start.6 = (bf16[96,1536]{1,0:T(8,128)(2,1)S(1)}, bf16[96,1536]{1,0:T(8,128)(2,1)S(1)}, u32[]{:S(2)}, u32[]{:S(2)}) collective-permute-start(bf16[96,1536]{1,0:T(8,128)(2,1)S(1)} %collective-permute-done.5.refs_6_), channel_id=1, source_target_pairs={{0,2},{2,0},{4,6},{6,4},{1,3},{3,1},{5,7},{7,5},{8,10},{10,8},{12,... | collective-permute-start | bytes 884744 | tf_op jit(solution)/shard_map/ppermute | solution.py:777
  45.1 33.7 %collective-permute-start.7 = (bf16[96,1536]{1,0:T(8,128)(2,1)S(1)}, bf16[96,1536]{1,0:T(8,128)(2,1)}, u32[]{:S(2)}, u32[]{:S(2)}) collective-permute-start(bf16[96,1536]{1,0:T(8,128)(2,1)S(1)} %collective-permute-done.4.refs_5_), channel_id=1, source_target_pairs={{0,1},{1,0},{2,3},{3,2},{4,5},{5,4},{6,7},{7,6},{8,9},{9,8},{10,11... | collective-permute-start | bytes 884744 | tf_op jit(solution)/shard_map/ppermute | solution.py:777
  45.1 33.7 %collective-permute-start.8 = (bf16[96,1536]{1,0:T(8,128)(2,1)S(1)}, bf16[96,1536]{1,0:T(8,128)(2,1)}, u32[]{:S(2)}, u32[]{:S(2)}) collective-permute-start(bf16[96,1536]{1,0:T(8,128)(2,1)S(1)} %collective-permute-done.5.refs_6_), channel_id=1, source_target_pairs={{0,1},{1,0},{2,3},{3,2},{4,5},{5,4},{6,7},{7,6},{8,9},{9,8},{10,11... | collective-permute-start | bytes 884744 | tf_op jit(solution)/shard_map/ppermute | solution.py:777
  107.5 22.2 %collective-permute-start.14 = (bf16[864,768]{1,0:T(8,128)(2,1)S(1)}, bf16[864,768]{1,0:T(8,128)(2,1)}, u32[]{:S(2)}, u32[]{:S(2)}) collective-permute-start(bf16[864,768]{1,0:T(8,128)(2,1)S(1)} %collective-permute-done.9.refs_13_), channel_id=1, source_target_pairs={{0,1},{1,0},{2,3},{3,2},{4,5},{5,4},{6,7},{7,6},{8,9},{9,8},{10,11... | collective-permute-start | bytes 3981320 | tf_op jit(solution)/shard_map/ppermute | solution.py:777
  108.1 21.6 %collective-permute-start.15 = (bf16[864,768]{1,0:T(8,128)(2,1)S(1)}, bf16[864,768]{1,0:T(8,128)(2,1)}, u32[]{:S(2)}, u32[]{:S(2)}) collective-permute-start(bf16[864,768]{1,0:T(8,128)(2,1)S(1)} %collective-permute-done.10.refs_14_), channel_id=1, source_target_pairs={{0,1},{1,0},{2,3},{3,2},{4,5},{5,4},{6,7},{7,6},{8,9},{9,8},{10,11... | collective-permute-start | bytes 3981320 | tf_op jit(solution)/shard_map/ppermute | solution.py:777
  110.1 19.6 %collective-permute-start.12 = (bf16[432,768]{1,0:T(8,128)(2,1)}, bf16[432,768]{1,0:T(8,128)(2,1)S(1)}, u32[]{:S(2)}, u32[]{:S(2)}) collective-permute-start(bf16[432,768]{1,0:T(8,128)(2,1)} %slice.158), channel_id=1, source_target_pairs={{0,4},{2,6},{4,0},{6,2},{1,5},{3,7},{5,1},{7,3},{8,12},{10,14},{12... | collective-permute-start | bytes 1990664 | tf_op jit(solution)/shard_map/ppermute | solution.py:777
  110.6 19.1 %collective-permute-start.13 = (bf16[432,768]{1,0:T(8,128)(2,1)}, bf16[432,768]{1,0:T(8,128)(2,1)}, u32[]{:S(2)}, u32[]{:S(2)}) collective-permute-start(bf16[432,768]{1,0:T(8,128)(2,1)} %slice.159), channel_id=1, source_target_pairs={{0,2},{2,0},{4,6},{6,4},{1,3},{3,1},{5,7},{7,5},{8,10},{10,8},{12,... | collective-permute-start | bytes 1990664 | tf_op jit(solution)/shard_map/ppermute | solution.py:777
  217.5 20.8 %collective-permute-start.18 = (bf16[4,4,192,384]{3,2,1,0:T(8,128)(2,1)}, bf16[4,4,192,384]{3,2,1,0:T(8,128)(2,1)S(1)}, u32[]{:S(2)}, u32[]{:S(2)}) collective-permute-start(bf16[4,4,192,384]{3,2,1,0:T(8,128)(2,1)} %get-tuple-element.314), channel_id=1, source_target_pairs={{0,1},{1,0},{2,3},{3,2},{4,5},{5,4},{6,7},{7,6},{8,9},{9,8},{10,11... | collective-permute-start | bytes 7077896 | tf_op jit(solution)/shard_map/ppermute | solution.py:777
  217.7 20.6 %collective-permute-start.19 = (bf16[4,4,192,384]{3,2,1,0:T(8,128)(2,1)}, bf16[4,4,192,384]{3,2,1,0:T(8,128)(2,1)}, u32[]{:S(2)}, u32[]{:S(2)}) collective-permute-start(bf16[4,4,192,384]{3,2,1,0:T(8,128)(2,1)} %get-tuple-element.315), channel_id=1, source_target_pairs={{0,1},{1,0},{2,3},{3,2},{4,5},{5,4},{6,7},{7,6},{8,9},{9,8},{10,11... | collective-permute-start | bytes 7077896 | tf_op jit(solution)/shard_map/ppermute | solution.py:777
  218.0 20.2 %collective-permute-start.20 = (bf16[4,144,768]{2,1,0:T(8,128)(2,1)}, bf16[4,144,768]{2,1,0:T(8,128)(2,1)S(1)}, u32[]{:S(2)}, u32[]{:S(2)}) collective-permute-start(bf16[4,144,768]{2,1,0:T(8,128)(2,1)} %get-tuple-element.320), channel_id=1, source_target_pairs={{0,1},{1,0},{2,3},{3,2},{4,5},{5,4},{6,7},{7,6},{8,9},{9,8},{10,11... | collective-permute-start | bytes 2654216 | tf_op jit(solution)/shard_map/ppermute | solution.py:777
  243.1 33.0 %collective-permute-start.22 = (bf16[2,4,192,384]{3,2,1,0:T(8,128)(2,1)S(1)}, bf16[2,4,192,384]{3,2,1,0:T(8,128)(2,1)}, u32[]{:S(2)}, u32[]{:S(2)}) collective-permute-start(bf16[2,4,192,384]{3,2,1,0:T(8,128)(2,1)S(1)} %get-tuple-element.437.refs_4_), channel_id=1, source_target_pairs={{0,4},{2,6},{4,0},{6,2},{1,5},{3,7},{5,1},{7,3},{8,12},{10,14},{12... | collective-permute-start | bytes 3538952 | tf_op jit(solution)/shard_map/ppermute | solution.py:777
  246.1 30.0 %collective-permute-start.21 = (bf16[2,4,192,384]{3,2,1,0:T(8,128)(2,1)}, bf16[2,4,192,384]{3,2,1,0:T(8,128)(2,1)}, u32[]{:S(2)}, u32[]{:S(2)}) collective-permute-start(bf16[2,4,192,384]{3,2,1,0:T(8,128)(2,1)} %get-tuple-element.439.refs_3_), channel_id=1, source_target_pairs={{0,2},{2,0},{4,6},{6,4},{1,3},{3,1},{5,7},{7,5},{8,10},{10,8},{12,... | collective-permute-start | bytes 3538952 | tf_op jit(solution)/shard_map/ppermute | solution.py:777
  278.2 24.1 %collective-permute-start.24 = (bf16[4,192,384]{2,1,0:T(8,128)(2,1)}, bf16[4,192,384]{2,1,0:T(8,128)(2,1)S(1)}, u32[]{:S(2)}, u32[]{:S(2)}) collective-permute-start(bf16[4,192,384]{2,1,0:T(8,128)(2,1)} %fusion.4.refs_4_), channel_id=1, source_target_pairs={{0,2},{2,0},{4,6},{6,4},{1,3},{3,1},{5,7},{7,5},{8,10},{10,8},{12,... | collective-permute-start | bytes 1769480 | tf_op jit(solution)/shard_map/ppermute | solution.py:777
  280.9 21.4 %collective-permute-start.23 = (bf16[4,192,384]{2,1,0:T(8,128)(2,1)}, bf16[4,192,384]{2,1,0:T(8,128)(2,1)S(1)}, u32[]{:S(2)}, u32[]{:S(2)}) collective-permute-start(bf16[4,192,384]{2,1,0:T(8,128)(2,1)} %fusion.3.refs_3_), channel_id=1, source_target_pairs={{0,4},{2,6},{4,0},{6,2},{1,5},{3,7},{5,1},{7,3},{8,12},{10,14},{12... | collective-permute-start | bytes 1769480 | tf_op jit(solution)/shard_map/ppermute | solution.py:777
  281.7 20.6 %collective-permute-start.25 = (bf16[4,1,192,384]{3,2,1,0:T(8,128)(2,1)}, bf16[4,1,192,384]{3,2,1,0:T(8,128)(2,1)}, u32[]{:S(2)}, u32[]{:S(2)}) collective-permute-start(bf16[4,1,192,384]{3,2,1,0:T(8,128)(2,1)} %get-tuple-element.339), channel_id=1, source_target_pairs={{0,1},{1,0},{2,3},{3,2},{4,5},{5,4},{6,7},{7,6},{8,9},{9,8},{10,11... | collective-permute-start | bytes 1769480 | tf_op jit(solution)/shard_map/ppermute | solution.py:777
  281.7 20.6 %collective-permute-start.26 = (bf16[4,1,192,384]{3,2,1,0:T(8,128)(2,1)}, bf16[4,1,192,384]{3,2,1,0:T(8,128)(2,1)}, u32[]{:S(2)}, u32[]{:S(2)}) collective-permute-start(bf16[4,1,192,384]{3,2,1,0:T(8,128)(2,1)} %get-tuple-element.340), channel_id=1, source_target_pairs={{0,1},{1,0},{2,3},{3,2},{4,5},{5,4},{6,7},{7,6},{8,9},{9,8},{10,11... | collective-permute-start | bytes 1769480 | tf_op jit(solution)/shard_map/ppermute | solution.py:777
  282.2 50.1 %collective-permute-start.31 = (bf16[4,1,192,384]{3,2,1,0:T(8,128)(2,1)}, bf16[4,1,192,384]{3,2,1,0:T(8,128)(2,1)}, u32[]{:S(2)}, u32[]{:S(2)}) collective-permute-start(bf16[4,1,192,384]{3,2,1,0:T(8,128)(2,1)} %get-tuple-element.353), channel_id=1, source_target_pairs={{0,1},{1,0},{2,3},{3,2},{4,5},{5,4},{6,7},{7,6},{8,9},{9,8},{10,11... | collective-permute-start | bytes 1769480 | tf_op jit(solution)/shard_map/ppermute | solution.py:777
  314.3 18.1 %collective-permute-start.30 = (bf16[4,1,192,384]{3,2,1,0:T(8,128)(2,1)}, bf16[4,1,192,384]{3,2,1,0:T(8,128)(2,1)}, u32[]{:S(2)}, u32[]{:S(2)}) collective-permute-start(bf16[4,1,192,384]{3,2,1,0:T(8,128)(2,1)} %get-tuple-element.352.refs_10_), channel_id=1, source_target_pairs={{0,1},{1,0},{2,3},{3,2},{4,5},{5,4},{6,7},{7,6},{8,9},{9,8},{10,11... | collective-permute-start | bytes 1769480 | tf_op jit(solution)/shard_map/ppermute | solution.py:777
  314.8 17.6 %collective-permute-start.27 = (bf16[4,192,384]{2,1,0:T(8,128)(2,1)S(1)}, bf16[4,192,384]{2,1,0:T(8,128)(2,1)}, u32[]{:S(2)}, u32[]{:S(2)}) collective-permute-start(bf16[4,192,384]{2,1,0:T(8,128)(2,1)S(1)} %copy-done.5), channel_id=1, source_target_pairs={{0,8},{8,0},{16,24},{24,16},{1,9},{9,1},{17,25},{25,17},{2,10},{10... | collective-permute-start | bytes 1769480 | tf_op jit(solution)/shard_map/ppermute | solution.py:777
  316.1 16.2 %collective-permute-start.29 = (bf16[2,1,192,384]{3,2,1,0:T(8,128)(2,1)}, bf16[2,1,192,384]{3,2,1,0:T(8,128)(2,1)S(1)}, u32[]{:S(2)}, u32[]{:S(2)}) collective-permute-start(bf16[2,1,192,384]{3,2,1,0:T(8,128)(2,1)} %get-tuple-element.447.refs_5_), channel_id=1, source_target_pairs={{0,4},{2,6},{4,0},{6,2},{1,5},{3,7},{5,1},{7,3},{8,12},{10,14},{12... | collective-permute-start | bytes 884744 | tf_op jit(solution)/shard_map/ppermute | solution.py:777
  335.2 24.5 %collective-permute-start.36 = (bf16[2,1,192,384]{3,2,1,0:T(8,128)(2,1)}, bf16[2,1,192,384]{3,2,1,0:T(8,128)(2,1)}, u32[]{:S(2)}, u32[]{:S(2)}) collective-permute-start(bf16[2,1,192,384]{3,2,1,0:T(8,128)(2,1)} %get-tuple-element.443.refs_16_), channel_id=1, source_target_pairs={{0,4},{2,6},{4,0},{6,2},{1,5},{3,7},{5,1},{7,3},{8,12},{10,14},{12... | collective-permute-start | bytes 884744 | tf_op jit(solution)/shard_map/ppermute | solution.py:777
  337.9 21.9 %collective-permute-start.35 = (bf16[2,1,192,384]{3,2,1,0:T(8,128)(2,1)}, bf16[2,1,192,384]{3,2,1,0:T(8,128)(2,1)}, u32[]{:S(2)}, u32[]{:S(2)}) collective-permute-start(bf16[2,1,192,384]{3,2,1,0:T(8,128)(2,1)} %get-tuple-element.445.refs_15_), channel_id=1, source_target_pairs={{0,2},{2,0},{4,6},{6,4},{1,3},{3,1},{5,7},{7,5},{8,10},{10,8},{12,... | collective-permute-start | bytes 884744 | tf_op jit(solution)/shard_map/ppermute | solution.py:777
  340.0 19.8 %collective-permute-start.37 = (bf16[4,144,768]{2,1,0:T(8,128)(2,1)}, bf16[4,144,768]{2,1,0:T(8,128)(2,1)}, u32[]{:S(2)}, u32[]{:S(2)}) collective-permute-start(bf16[4,144,768]{2,1,0:T(8,128)(2,1)} %get-tuple-element.379), channel_id=1, source_target_pairs={{0,1},{1,0},{2,3},{3,2},{4,5},{5,4},{6,7},{7,6},{8,9},{9,8},{10,11... | collective-permute-start | bytes 2654216 | tf_op jit(solution)/shard_map/ppermute | solution.py:777
  342.1 17.7 %collective-permute-start.32 = (bf16[4,96,384]{2,1,0:T(8,128)(2,1)S(1)}, bf16[4,96,384]{2,1,0:T(8,128)(2,1)S(1)}, u32[]{:S(2)}, u32[]{:S(2)}) collective-permute-start(bf16[4,96,384]{2,1,0:T(8,128)(2,1)S(1)} %broadcast_select_fusion.5.refs_12_), channel_id=1, source_target_pairs={{0,16},{8,24},{16,0},{24,8},{1,17},{9,25},{17,1},{25,9},{2,18},{10... | collective-permute-start | bytes 884744 | tf_op jit(solution)/shard_map/ppermute | solution.py:777
  381.1 21.4 %collective-permute-start.43 = (bf16[4,192,384]{2,1,0:T(8,128)(2,1)S(1)}, bf16[4,192,384]{2,1,0:T(8,128)(2,1)S(1)}, u32[]{:S(2)}, u32[]{:S(2)}) collective-permute-start(bf16[4,192,384]{2,1,0:T(8,128)(2,1)S(1)} %pad_maximum_fusion.2), channel_id=1, source_target_pairs={{0,8},{8,0},{16,24},{24,16},{1,9},{9,1},{17,25},{25,17},{2,10},{10... | collective-permute-start | bytes 1769480 | tf_op jit(solution)/shard_map/ppermute | solution.py:777
  382.3 20.1 %collective-permute-start.45 = (bf16[1,192,384]{2,1,0:T(8,128)(2,1)S(1)}, bf16[1,192,384]{2,1,0:T(8,128)(2,1)S(1)}, u32[]{:S(2)}, u32[]{:S(2)}) collective-permute-start(bf16[1,192,384]{2,1,0:T(8,128)(2,1)S(1)} %broadcast_select_fusion.10), channel_id=1, source_target_pairs={{0,8},{8,0},{16,24},{24,16},{1,9},{9,1},{17,25},{25,17},{2,10},{10... | collective-permute-start | bytes 442376 | tf_op jit(solution)/shard_map/ppermute | solution.py:777
  385.4 17.0 %collective-permute-start.44 = (bf16[1,192,384]{2,1,0:T(8,128)(2,1)S(1)}, bf16[1,192,384]{2,1,0:T(8,128)(2,1)S(1)}, u32[]{:S(2)}, u32[]{:S(2)}) collective-permute-start(bf16[1,192,384]{2,1,0:T(8,128)(2,1)S(1)} %add_convert_fusion.23), channel_id=1, source_target_pairs={{0,16},{8,24},{16,0},{24,8},{1,17},{9,25},{17,1},{25,9},{2,18},{10... | collective-permute-start | bytes 442376 | tf_op jit(solution)/shard_map/ppermute | solution.py:777
  408.0 29.2 %collective-permute-start.57 = (bf16[4,192,384]{2,1,0:T(8,128)(2,1)S(1)}, bf16[4,192,384]{2,1,0:T(8,128)(2,1)S(1)}, u32[]{:S(2)}, u32[]{:S(2)}) collective-permute-start(bf16[4,192,384]{2,1,0:T(8,128)(2,1)S(1)} %get-tuple-element.441.refs_1_), channel_id=1, source_target_pairs={{0,1},{1,0},{2,3},{3,2},{4,5},{5,4},{6,7},{7,6},{8,9},{9,8},{10,11... | collective-permute-start | bytes 1769480 | tf_op jit(solution)/shard_map/ppermute | solution.py:777
  408.1 29.2 %collective-permute-start.58 = (bf16[4,192,384]{2,1,0:T(8,128)(2,1)S(1)}, bf16[4,192,384]{2,1,0:T(8,128)(2,1)S(1)}, u32[]{:S(2)}, u32[]{:S(2)}) collective-permute-start(bf16[4,192,384]{2,1,0:T(8,128)(2,1)S(1)} %get-tuple-element.440.refs_3_), channel_id=1, source_target_pairs={{0,1},{1,0},{2,3},{3,2},{4,5},{5,4},{6,7},{7,6},{8,9},{9,8},{10,11... | collective-permute-start | bytes 1769480 | tf_op jit(solution)/shard_map/ppermute | solution.py:777
  (88 other events, 643.5 us)

commit v3 on v2

--- a/solution.py
+++ b/solution.py
@@ -31,11 +31,11 @@
 WIDE = 640
 NARROW = 384
 TALL = WIN * 16
-HB = 4
+HB = 8
 LB = HB * HD
 HP = 8
 LP = HP * HD
-NB = 384
+NB = 576
 SCALE = 1e-3
 ONE = dict(pipeline_mode=pl.Buffered(1))
 SD = jax.ShapeDtypeStruct
@@ -134,6 +134,10 @@
         yield pltpu.make_async_copy(
             refs[src].at[pl.ds(row, rows), pl.ds(col, cols)], targets[dst].at[place, pl.ds(put, cols)], sems.at[i]
         )
+
+
+def hidden_block(k):
+    return 2 * (k % 4) + k // 4
 
 
 def region_masks():
@@ -182,8 +186,11 @@
         return hi, (v - hi.astype(F32)).astype(BF)
 
     out_ref[...] = jnp.zeros_like(out_ref)
-    for j in range(8):
-        out_ref[V_UP + j // 2 : V_UP + j // 2 + 1, (j % 2) * CH : (j % 2 + 1) * CH] = up_ref[j]
+    for k in range(8):
+        b = hidden_block(k)
+        out_ref[V_UP + b // 2 : V_UP + b // 2 + 1, (b % 2) * CH : (b % 2 + 1) * CH] = up_ref[
+            k // 2, :, (k % 2) * CH : (k % 2 + 1) * CH
+        ]
     out_ref[V_SMALL : V_SMALL + 1, :] = down_ref[...]
     out_ref[V_SMALL + 1 : V_SMALL + 4, :] = small_ref[1:4, :]
     for p in range(3):
@@ -218,7 +225,10 @@
 
 
 def first_kernel(spot_ref, *refs):
-    vecs, inner_ref, first_ref, others_ref, half_ref = refs[:8], refs[8], refs[9], refs[10], refs[11]
+    vecs, (inner_ref, own_ref, gown_ref, first_ref, others_ref, half_ref, up_ref) = refs[:8], refs[8:]
+    n = own_ref.shape[0]
+    up_ref[:n] = own_ref[...]
+    up_ref[n:] = gown_ref[...]
     mine = pl.ds(pl.multiple_of(spot_ref[1] * (OWN // 2), 16), OWN // 2)
     for k in range(3):
         first_ref[:OWN, k * LP : (k + 1) * LP] = inner_ref[:, k * D : k * D + LP]
@@ -236,43 +246,39 @@
     first_ref[OWN:, :] = jnp.concatenate(rows, axis=0).astype(BF)
 
 
-def first_call(spot, vectors, inner):
-    return single(
-        first_kernel, (spot, *vectors, inner), [SD((OWN + 16, D), BF), SD((OWN, 6 * LP), BF), SD((OWN // 2, 6 * LP), BF)],
-        cost_estimate=cost(1e6, 3 * MB), name="first",
-    )
+def first_call(spot, vectors, inner, own, gown):
+    n = own.shape[0]
+    top = full((n, TOK, D))
+    shapes = [SD((OWN + 16, D), BF), SD((OWN, 6 * LP), BF), SD((OWN // 2, 6 * LP), BF), SD((2 * n, TOK, D), BF)]
+    return pl.pallas_call(
+        first_kernel,
+        grid=(1,),
+        in_specs=[smem()] + [whole(v) for v in vectors] + [whole(inner), top, top],
+        out_specs=[whole(v) for v in shapes],
+        out_shape=shapes,
+        compiler_params=params(),
+        cost_estimate=cost(1e6, 6 * MB),
+        name="first",
+    )(spot, *vectors, inner, own, gown)
 
 
 BIG = 4 * (OWN // 2) + OWN // 2 + 2 * OWN
 
 
-def cut_kernel(spot_ref, outer_ref, expand_ref, reduce_ref, own_ref, gown_ref, big_ref, up_ref):
+def cut_kernel(spot_ref, outer_ref, expand_ref, reduce_ref, big_ref):
     core = spot_ref[1]
     hlf = OWN // 2
-    n = own_ref.shape[0]
     mine = pl.ds(pl.multiple_of(core * hlf, 16), hlf)
     for k in range(4):
         big_ref[k * hlf : (k + 1) * hlf, :] = expand_ref[mine, k * D : (k + 1) * D]
     big_ref[4 * hlf : 5 * hlf, :] = outer_ref[mine, :]
     big_ref[5 * hlf :, :] = reduce_ref[pl.ds(pl.multiple_of(core * 2 * OWN, 16), 2 * OWN), :]
-    up_ref[:n] = own_ref[...]
-    up_ref[n:] = gown_ref[...]
-
-
-def cut_call(spot, outer, expand, reduce, own, gown):
-    n = own.shape[0]
-    top = full((n, TOK, D))
-    shapes = [SD((BIG, D), BF), SD((2 * n, TOK, D), BF)]
-    return pl.pallas_call(
-        cut_kernel,
-        grid=(1,),
-        in_specs=[smem(), whole(outer), whole(expand), whole(reduce), top, top],
-        out_specs=[whole(v) for v in shapes],
-        out_shape=shapes,
-        compiler_params=params(),
-        cost_estimate=cost(1e6, 8 * MB),
-        name="cut",
-    )(spot, outer, expand, reduce, own, gown)
+
+
+def cut_call(spot, outer, expand, reduce):
+    return single(
+        cut_kernel, (spot, outer, expand, reduce), [SD((BIG, D), BF)], cost_estimate=cost(1e6, 3 * MB), name="cut"
+    )[0]
 
 
 def prep_kernel(own_ref, gown_ref, recv_ref, alive_ref, pm_ref, tok_ref, g_ref, sum_ref):
@@ -308,8 +314,8 @@
             [vin[:, p * LP : (p + 1) * LP], jnp.zeros((1, LP), F32), vin[:, D + p * LP : D + (p + 1) * LP]], axis=1
         )
     vup = vector(2)
-    for j in range(8):
-        up_ref[j] = vup[:, j * CH : (j + 1) * CH]
+    for k in range(8):
+        up_ref[k // 2, :, (k % 2) * CH : (k % 2 + 1) * CH] = vup[:, hidden_block(k) * CH : (hidden_block(k) + 1) * CH]
     gain, shift = vector(4), vector(5)
     vec_ref[...] = jnp.zeros_like(vec_ref)
     for r, v in enumerate((vector(1), vector(3), gain, vector(6), vector(7))):
@@ -324,7 +330,7 @@
 def vector_call(spot, parts, tok):
     n = tok.shape[0]
     last = parts[0].shape[0] // 16 - 1
-    shapes = [SD((3, 1, 3 * LP), F32), SD((8, 1, CH), F32), SD((8, D), F32), SD(tok.shape, BF), SD((D, n * ROWS), BF)]
+    shapes = [SD((3, 1, 3 * LP), F32), SD((4, 1, 2 * CH), F32), SD((8, D), F32), SD(tok.shape, BF), SD((D, n * ROWS), BF)]
     return pl.pallas_call(
         vector_kernel,
         grid=(1,),
@@ -360,11 +366,12 @@
             k = proj_ref[0, r, LP + l : LP + l + LB]
             v = proj_ref[0, r, 2 * LP + l : 2 * LP + l + LB]
             vt = v.T
+            apart = jnp.concatenate([jnp.where(hid == h, k, jnp.zeros_like(k)) for h in range(HB)], axis=0)
+            sts = nn(apart, q.T)
             outs = []
             for h in range(HB):
                 hh = blk * HB + h
-                km = jnp.where(hid == h, k, jnp.zeros_like(k))
-                st = nt(km, q)
+                st = sts[h * TOK : (h + 1) * TOK]
                 peak_ref[0, w, hh : hh + 1, :] = jnp.max(st, axis=0, keepdims=True) * scale
                 t = st * (scale * LOG2E) + bm_ref[w, hh]
                 e = jnp.exp2(t - jnp.max(t, axis=0, keepdims=True))
@@ -444,16 +451,15 @@
             if k not in early:
                 c.wait()
 
-    sh = jnp.bitwise_xor(me, j % 4)
-    at = (2 * sh + jnp.bitwise_xor(core, 1 - j // 4)) * CH
-    ecol = pl.ds(pl.multiple_of(at, CH), CH)
-    tot = jnp.zeros((1, CH), F32)
+    at = pl.multiple_of((2 * jnp.bitwise_xor(core, 1 - j // 2) + j % 2) * 2 * CH, 2 * CH)
+    cols = pl.ds(at, 2 * CH)
+    tot = jnp.zeros((1, 2 * CH), F32)
     for s0 in range(0, N, NB):
         s = slice(s0, s0 + NB)
-        h = nn(n2[s, :], we[:, ecol]) + eb_ref[0]
+        h = nn(n2[s, :], we[:, cols]) + eb_ref[0]
         cdf, dg = gelu_parts(h)
         act[s, :] = (h * cdf).astype(BF)
-        x = (nt(g[s, :], wr[ecol, :]) * dg).astype(BF)
+        x = (nt(g[s, :], wr[cols, :]) * dg).astype(BF)
         gh[s, :] = x
         tot = tot + colsum(x.astype(F32))
     geb_ref[0] = tot
@@ -461,24 +467,27 @@
     gr = tn(act[...], g[...]).astype(BF)
 
     def put(e_ref, r_ref):
-        for b in range(4):
-            e_ref[jnp.bitwise_xor(me, b), 0] = ge[b * OWN : (b + 1) * OWN, :]
-            r_ref[0, b] = gr[(b // 2) * OWN : (b // 2 + 1) * OWN, (b % 2) * CH : (b % 2 + 1) * CH]
-
-    @pl.when(j < 4)
+        for t in range(2):
+            for b in range(4):
+                e_ref[crossed(jnp.bitwise_xor(me, b)), t] = ge[b * OWN : (b + 1) * OWN, t * CH : (t + 1) * CH]
+                r_ref[jnp.bitwise_xor(me % 2, t), b] = gr[
+                    t * CH + (b // 2) * OWN : t * CH + (b // 2 + 1) * OWN, (b % 2) * CH : (b % 2 + 1) * CH
+                ]
+
+    @pl.when(j < 2)
     def _():
         put(es_ref, rs_ref)
 
-    @pl.when(j >= 4)
+    @pl.when(j >= 2)
     def _():
         put(ek_ref, rk_ref)
 
     for s0 in range(0, N, NB):
         s = slice(s0, s0 + NB)
-        acc[s, :] += nn(act[s, :], wr[ecol, :])
-        e2[s, :] += nt(gh[s, :], we[:, ecol])
-
-    @pl.when(j == 7)
+        acc[s, :] += nn(act[s, :], wr[cols, :])
+        e2[s, :] += nt(gh[s, :], we[:, cols])
+
+    @pl.when(j == 3)
     def _():
         gn = jnp.zeros((1, D), F32)
         shf = gn
@@ -521,13 +530,13 @@
     blocks = SD((4, 4, OWN, CH), BF)
 
     def chunk(j, spot):
-        return 2 * jnp.bitwise_xor(spot[0], j % 4) + jnp.bitwise_xor(spot[1], 1 - j // 4)
-
-    def early(j, spot):
-        return jnp.bitwise_xor(spot[0], jnp.minimum(j, 3))
-
-    def late(j, spot):
-        return jnp.bitwise_xor(spot[0], jnp.maximum(j, 4) - 4)
+        return 2 * jnp.bitwise_xor(spot[1], 1 - j // 2) + j % 2
+
+    def early(j):
+        return jnp.minimum(j, 1)
+
+    def late(j):
+        return jnp.maximum(j, 2) - 2
 
     rows = full((n, ROWS, D), **ONE)
     third = full((n, ROWS, LP), **ONE)
@@ -540,19 +549,19 @@
 
     grid_spec = pltpu.PrefetchScalarGridSpec(
         num_scalar_prefetch=1,
-        grid=(8,),
+        grid=(4,),
         in_specs=[rows, third, third, third, rows, full((ROWS, ROWS)), full((8, D)),
-                  pl.BlockSpec((1, 1, CH), lambda j, spot: (chunk(j, spot), 0, 0)), smem()]
+                  pl.BlockSpec((1, 1, 2 * CH), lambda j, spot: (chunk(j, spot), 0, 0)), smem()]
         + [any_space()] * (len(pieces) + len(after)),
         out_specs=[cut, cut, rows, rows, outer, outer,
-                   pl.BlockSpec((4, 1, OWN, CH), lambda j, spot: (0, early(j, spot), 0, 0)),
-                   pl.BlockSpec((4, 1, OWN, CH), lambda j, spot: (0, late(j, spot), 0, 0)),
-                   pl.BlockSpec((1, 4, OWN, CH), lambda j, spot: (crossed(jnp.minimum(j, 3)), 0, 0, 0)),
-                   pl.BlockSpec((1, 4, OWN, CH), lambda j, spot: (crossed(jnp.maximum(j, 4) - 4), 0, 0, 0)),
-                   pl.BlockSpec((1, 1, CH), lambda j, spot: (chunk(j, spot), 0, 0)), full((8, D))],
+                   pl.BlockSpec((4, 2, OWN, CH), lambda j, spot: (0, early(j), 0, 0)),
+                   pl.BlockSpec((4, 2, OWN, CH), lambda j, spot: (0, late(j), 0, 0)),
+                   pl.BlockSpec((2, 4, OWN, CH), lambda j, spot: (jnp.bitwise_xor(early(j), spot[0] // 2), 0, 0, 0)),
+                   pl.BlockSpec((2, 4, OWN, CH), lambda j, spot: (jnp.bitwise_xor(late(j), spot[0] // 2), 0, 0, 0)),
+                   pl.BlockSpec((1, 1, 2 * CH), lambda j, spot: (chunk(j, spot), 0, 0)), full((8, D))],
         scratch_shapes=[pltpu.VMEM((D, D), BF), pltpu.VMEM((D, FF), BF), pltpu.VMEM((FF, D), BF),
                         pltpu.VMEM((N, D), F32), pltpu.VMEM((N, D), BF), pltpu.VMEM((N, D), BF), pltpu.VMEM((D, N), BF),
-                        pltpu.VMEM((N, D), F32), pltpu.VMEM((N, D), F32), pltpu.VMEM((N, CH), BF), pltpu.VMEM((N, CH), BF),
+                        pltpu.VMEM((N, D), F32), pltpu.VMEM((N, D), F32), pltpu.VMEM((N, 2 * CH), BF), pltpu.VMEM((N, 2 * CH), BF),
                         pltpu.SemaphoreType.DMA((len(plan),))],
     )
     return pl.pallas_call(
@@ -560,7 +569,7 @@
         grid_spec=grid_spec,
         out_shape=[SD((n, TOK, D), BF), SD((n, TOK, D), BF), SD((n, ROWS, D), F32), SD((n, ROWS, D), BF),
                    SD((4, 1, OWN, CH), BF), SD((4, 1, OWN, CH), BF), blocks, blocks, blocks, blocks,
-                   SD((8, 1, CH), F32), SD((8, D), F32)],
+                   SD((4, 1, 2 * CH), F32), SD((8, D), F32)],
         compiler_params=params(62),
         cost_estimate=cost(6e10, 40 * MB, 7e6),
         name="middle",
@@ -584,10 +593,11 @@
             do = da_ref[0, r, l : l + LB]
             qt, kt, dt = q.T, k.T, do.T
             dq, dk, dv = [], [], []
+            dps = nn(jnp.concatenate([jnp.where(hid == h, v, jnp.zeros_like(v)) for h in range(HB)], axis=0), dt)
             for h in range(HB):
                 hh = blk * HB + h
                 s = slice(HD * h, HD * h + HD)
-                dp = nt(jnp.where(hid == h, v, jnp.zeros_like(v)), do)
+                dp = dps[h * TOK : (h + 1) * TOK]
                 pb = pt_ref[0, w, hh]
                 p = pb.astype(F32)
                 pd = p * dp
@@ -910,22 +920,22 @@
     alive = present.astype(F32).reshape(1, n)
     table_rows = jnp.pad(bias_table.astype(F32).T, ((0, 0), (0, WIDE - bias_table.shape[0])))
     if quick:
-        first, others, others_half = first_call(spot, vectors, inner_weight)
-        get_first, get_others = near(first), near(others_half)
-        expand_weight, first = fence(expand_weight, first)
-        big, up = cut_call(spot, outer_weight, expand_weight, reduce_weight, own_images, own_grad)
-        spot, up, big = fence(spot, up, big)
+        first, others, others_half, up = first_call(spot, vectors, inner_weight, own_images, own_grad)
+        first, up, spot, others_half = fence(first, up, spot, others_half)
+        get_first = near(first)
         upper = swap(up, "half", 1)
         masks_0 = bias_call(0, spot, table_rows)
-        get_first, upper, masks_0 = fence(get_first, upper, masks_0)
+        get_first, upper, masks_0, others_half = fence(get_first, upper, masks_0, others_half)
         get_first.append(swap(get_first[0], "shard", 2))
+        get_others = near(others_half)
         tok, g, grad_down = prep_call(own_images, own_grad, upper, alive, order)
-        get_first, get_others, tok = fence(get_first, get_others, tok)
+        big = cut_call(spot, outer_weight, expand_weight, reduce_weight)
+        get_first, get_others, tok, spot, big = fence(get_first, get_others, tok, spot, big)
         first_pieces = [first] + get_first
         get_others.append(swap(get_others[1], "shard", 1))
-        others_back = [swap(v, "half", 1) for v in get_others[:2]]
         in_bias, up_bias, vecs, n1, n1t = vector_call(spot, first_pieces, tok)
-        n1, big = fence(n1, big)
+        get_others, n1, big = fence(get_others, n1, big)
+        others_back = [swap(v, "half", 1) for v in get_others]
         get_big = near(big)
     else:
         masks_0 = bias_call(0, spot, table_rows)
@@ -962,12 +972,11 @@
 
     results = [attend_call(0, n1, in_bias, masks_0, first_at, in_plans[0], first_pieces, [])]
     if quick:
-        get_others, others_back, results, spot = fence(get_others, others_back, results, spot)
-        others_back.append(swap(get_others[2], "half", 1))
+        others_back, results, spot = fence(others_back, results, spot)
     masks_1 = bias_call(1, spot, table_rows)
     masks_2 = bias_call(2, spot, table_rows)
     if quick:
-        others_back, masks_1, masks_2 = fence(others_back, masks_1, masks_2)
+        masks_1, masks_2 = fence(masks_1, masks_2)
         others_pieces = [others] + get_others + others_back
     results.append(attend_call(1, n1, in_bias, masks_1, in_at, in_plans[1], others_pieces, [masks_2]))
     if quick:
@@ -981,15 +990,26 @@
         far_back, results = fence(far_back, results)
         pieces = [outer_weight, expand_weight, reduce_weight] + get_big + far + big_back + far_back
         hlf = OWN // 2
-        plan = [(0, 0, OWN, 0, D, 0, 0), (1, 0, OWN, 0, FF, 1, 0), (2, 0, 4 * OWN, 0, D, 2, 0)]
-        short, long = places(OWN), places(4 * OWN)
-        at = [short[0], short[0], long[0]]
+        plan = [(0, 0, OWN, 0, D, 0, 0)]
+        short = places(OWN)
+        long = [None] + [c * 4 * CH + (me ^ r) * CH for c in (core, 1 - core) for r in (1, 2, 3)]
+        at = [short[0]]
+        for k in range(8):
+            plan.append((1, 0, OWN, hidden_block(k) * CH, CH, 1, k * CH))
+            at.append(short[0])
+        for c in range(2):
+            plan.append((2, c * CH, CH, 0, D, 2, 0))
+            at.append(c * 4 * CH + me * CH)
         parts = [(b * hlf, hlf, 1, b * D) for b in range(4)] + [(4 * hlf, hlf, 0, 0), (5 * hlf, 4 * hlf, 2, 0)]
 
         def add_piece(source, lo, hi, place):
             for row, rows, target, column in parts:
                 a, b = max(row, lo), min(row + rows, hi)
-                if a < b:
+                if a < b and target == 1:
+                    for c in range(2):
+                        plan.append((source, a - lo, b - a, c * CH, CH, 1, c * 4 * CH + column // 2))
+                        at.append(short[place] + (a - row))
+                elif a < b:
                     plan.append((source, a - lo, b - a, 0, D, target, column))
                     at.append((long if target == 2 else short)[place] + (a - row))
 
@@ -1001,14 +1021,17 @@
         at = jnp.stack(at).astype(jnp.int32)
     else:
         pieces = [lax.all_gather(v, "shard", axis=0, tiled=True) for v in (outer_weight, expand_weight, reduce_weight)]
-        plan = [(0, 0, D, 0, D, 0, 0), (1, 0, D, 0, FF, 1, 0), (2, 0, FF, 0, D, 2, 0)]
-        at = jnp.zeros((3,), jnp.int32)
+        plan, at = [(0, 0, D, 0, D, 0, 0)], [0]
+        for k in range(8):
+            plan += [(1, 0, D, hidden_block(k) * CH, CH, 1, k * CH), (2, hidden_block(k) * CH, CH, 0, D, 2, 0)]
+            at += [0, k * CH]
+        at = jnp.asarray(at, jnp.int32)
     projs, pts, atts, peak, ws = zip(*results)
     (stay, send, gmid, datt, out_send, out_keep, e_send, e_keep, r_send, r_keep, grad_up, small) = middle_call(
         spot, tok, atts, g, back_order, vecs, up_bias, at, plan, pieces, []
     )
     if quick:
-        feed = Reduction([r_send, e_send], [r_keep, e_keep], replica, False)
+        feed = Reduction([e_send, r_send], [e_keep, r_keep], replica, False)
     lower_out = swap(send, "half", 1)
     gp0, db0 = back_call(0, projs[0], pts[0], datt, [])
     if quick:
@@ -1040,8 +1063,16 @@
         sums, lower_grad = together(chains, sums, lower_grad)
     every = Everywhere(sums)
     chains.append(every)
+    done = None
     while not all(c.done for c in chains):
-        together(chains)
+        if quick and done is None and feed.done:
+            swapped = fence(feed.flying)[0]
+            (em, rm), (eo, ro) = feed.keep, swapped
+            done = feed_finish(spot, em, eo, rm, ro)
+            chains = [c for c in chains if c is not feed]
+            done = together(chains, *done)
+        else:
+            together(chains)
     sums = every.value
 
     place = jnp.stack([me, core, shard]).astype(jnp.int32)
@@ -1049,8 +1080,7 @@
      clipped, factors, maxima) = vector_finish(place, sums, threshold, inner_weight, shard_count)
 
     if quick:
-        (rm, em), (ro, eo) = feed.keep, feed.flying
-        grad_expand, grad_reduce = feed_finish(spot, em, eo, rm, ro)
+        grad_expand, grad_reduce = done
         grad_inner, grad_outer = inner_finish(spot, ahead.keep + rest.keep, ahead.flying + rest.flying)
     else:
         def halves(keep, send, axis):
@@ -1067,13 +1097,13 @@
             return lax.psum(v, ("replica", "half")).astype(F32)
 
         def rows_of(v):
-            return straight(v).reshape(4, 1, 2, 2, OWN, CH).transpose(0, 1, 2, 4, 3, 5).reshape(4, 1, CH, D)
+            return v.reshape(4, 1, 2, 2, OWN, CH).transpose(0, 1, 2, 4, 3, 5).reshape(4, 1, CH, D)
 
         def straight(v):
             return jnp.stack([v[0], v[2], v[1], v[3]])
 
         grad_reduce = settle(halves(rows_of(r_keep), rows_of(r_send), 1).reshape(FF, D))
-        grad_expand = settle(whole(e_keep, e_send))
+        grad_expand = settle(whole(straight(e_keep), straight(e_send)))
         grad_outer = settle(whole(out_keep, out_send))
         by_third = [
             whole(straight(i0_keep), straight(i0_send)), whole(i1_keep, i1_send), whole(straight(i2_keep), straight(i2_send))

time: 449 us -> 384 us (0.86)
  Pallas kernels: 275 us -> 210 us
    pallas_call x15, Pallas kernels: 167 us -> 118 us  [run(): pl.pallas_call(body, in_specs=list(in_specs) + [any_space()] * len(after)...]
    pallas_call x1, Pallas kernels: 84.3 us -> 69.4 us  [middle_call(): pl.pallas_call(body, grid_spec=grid_spec, out_shape=[SD((n, TOK, D), BF),...]
  transfers between devices with their start and end apart: 59 -> 59, of which waited for: 15 -> 21; matrix products, arithmetic and copies ran while one was open for 8% -> 10% of each run, Pallas kernels for 39% -> 36%
where the time goes in v3:
time: 384 us; the launch traced here: 378 us
  Pallas kernels  210 us (55%)
  waiting for transfers between devices  67.2 us (18%)
  starting transfers between devices  48.4 us (13%)
  other arithmetic  40.4 us (11%)
  local copies, waits for them, and re-layouts  9.88 us (3%)
    pallas_call x15, Pallas kernels, run(): pl.pallas_call(body, in_specs=list(in_specs) + [any_space()] * len(after)...  118 us
    pallas_call x1, Pallas kernels, middle_call(): pl.pallas_call(body, grid_spec=grid_spec, out_shape=[SD((n, TOK, D), BF),...  69.4 us
    ppermute x59, waiting for transfers between devices, swap(): lax.ppermute(block, axis, [(i, i ^ bit) for i in range(count) if i ^ bit...  67.2 us
    ppermute x59, starting transfers between devices, swap(): lax.ppermute(block, axis, [(i, i ^ bit) for i in range(count) if i ^ bit...  48.4 us
    convert_element_type x18, other arithmetic, add(): return (a.astype(F32) + b.astype(F32)).astype(BF)  26.6 us
    pallas_call x3, Pallas kernels, bias_call(): pl.pallas_call(bias_kernel, grid=(1,), in_specs=[smem(), pl.BlockSpec((HP...  14.1 us
  transfers between devices with their start and end apart: 59, of which 21 were waited for; matrix products, arithmetic and copies ran while one was open for 10% of the time, Pallas kernels for 36%

profile of v3, /device:TPU:0, one launch (start us, length us, event | category | flops | bytes accessed | tf_op | source)
XLA Modules:
  0.0 377.9 jit_solution(14103986328581027605)
XLA Ops:
  1.3 3.5 first.1
  9.9 4.7 %bias.3.refs_2_ = f32[2,8,144,144]{3,2,1,0:T(8,128)} custom-call(s32[2]{0:T(128)} %pad_add_fusion.spot_ref.refs_0_, f32[24,640]{1,0:T(8,128)} %pad_convert_fusion.table_ref, bf16[2,2,144,144]{3,2,1,0:T(8,128)(2,1)} %constant.58.clone.mask_ref, bf16[384,144]{1,0:T(8,128)(2,1)} %constant.59.clone.sq_ref, bf16[144,192]{1,0:T(8,128)(2,1)} %constant.60.clone.sk_ref), custom_call_target="tpu_custom_call" | custom-call | flops 2000000 | bytes 3145 | tf_op jit(solution)/shard_map/bias/pallas_call | solution.py:167
  23.5 6.2 %prep.1 = (bf16[4,288,768]{2,1,0:T(8,128)(2,1)}, bf16[4,288,768]{2,1,0:T(8,128)(2,1)}, f32[1,768]{1,0:T(1,128)}) custom-call(bf16[4,288,768]{2,1,0:T(8,128)(2,1)} %bitcast.97, bf16[4,288,768]{2,1,0:T(8,128)(2,1)} %bitcast.99, bf16[8,144,768]{2,1,0:T(8,128)(2,1)} %copy-done.16, f32[1,4]{1,0:T(1,128)} %convert_bitcast_fusion.refs_3_, ...), custom_call_target="tpu_custom_call" | custom-call | flops 3000000 | bytes 16777 | tf_op jit(solution)/shard_map/prep/pallas_call | solution.py:72
  29.7 3.0 collective-permute-done.5.refs_6_
  33.5 5.4 %vectors.1 = (f32[3,1,768]{2,1,0:T(1,128)}, f32[4,1,768]{2,1,0:T(1,128)}, f32[8,768]{1,0:T(8,128)}, bf16[4,288,768]{2,1,0:T(8,128)(2,1)}, bf16[768,1152]{1,0:T(8,128)(2,1)}) custom-call(s32[2]{0:T(128)} %pad_add_fusion.spot_ref.refs_0_, bf16[208,768]{1,0:T(8,128)(2,1)} %get-tuple-element.224.pa_ref.refs_4_, bf16[208,768]{1,0:T(8,128)(2,1)} %copy-done.17, ...), custom_call_target="tpu_custom_call" | custom-call | flops 5000000 | bytes 8388 | tf_op jit(solution)/shard_map/vectors/pallas_call | solution.py:334
  44.0 12.3 %attend.3 = (bf16[4,288,768]{2,1,0:T(8,128)(2,1)}, bf16[4,2,8,144,144]{4,3,2,1,0:T(8,128)(2,1)}, bf16[4,288,256]{2,1,0:T(8,128)(2,1)}, f32[4,2,8,144]{3,2,1,0:T(8,128)}, bf16[768,768]{1,0:T(8,128)(2,1)}) custom-call(bf16[4,288,768]{2,1,0:T(8,128)(2,1)} %get-tuple-element.245.refs_0_, f32[3,1,768]{2,1,0:T(1,128)} %get-tuple-element.246.refs_1_, ...), custom_call_target="tpu_custom_call" | custom-call | flops 13000000 | bytes 12582 | tf_op jit(solution)/shard_map/attend/pallas_call | solution.py:72
  56.4 4.7 %bias.4.refs_2_ = f32[2,8,144,144]{3,2,1,0:T(8,128)} custom-call(s32[2]{0:T(128)} %pad_add_fusion.spot_ref.refs_0_, f32[24,640]{1,0:T(8,128)} %pad_convert_fusion.table_ref, bf16[2,2,144,144]{3,2,1,0:T(8,128)(2,1)} %constant.58.clone.mask_ref, bf16[384,144]{1,0:T(8,128)(2,1)} %constant.59.clone.sq_ref, bf16[144,192]{1,0:T(8,128)(2,1)} %constant.60.clone.sk_ref), custom_call_target="tpu_custom_call" | custom-call | flops 2000000 | bytes 3145 | tf_op jit(solution)/shard_map/bias/pallas_call | solution.py:167
  61.1 4.7 %bias.5.refs_11_.refs_2_ = f32[2,8,144,144]{3,2,1,0:T(8,128)} custom-call(s32[2]{0:T(128)} %pad_add_fusion.spot_ref.refs_0_, f32[24,640]{1,0:T(8,128)} %pad_convert_fusion.table_ref, bf16[2,2,144,144]{3,2,1,0:T(8,128)(2,1)} %constant.58.clone.mask_ref, bf16[384,144]{1,0:T(8,128)(2,1)} %constant.59.clone.sq_ref, bf16[144,192]{1,0:T(8,128)(2,1)} %constant.60.clone.sk_ref), custom_call_target="tpu_custom_call" | custom-call | flops 2000000 | bytes 3145 | tf_op jit(solution)/shard_map/bias/pallas_call | solution.py:167
  65.8 12.1 %attend.4 = (bf16[4,288,768]{2,1,0:T(8,128)(2,1)}, bf16[4,2,8,144,144]{4,3,2,1,0:T(8,128)(2,1)}, bf16[4,288,256]{2,1,0:T(8,128)(2,1)}, f32[4,2,8,144]{3,2,1,0:T(8,128)}, bf16[768,768]{1,0:T(8,128)(2,1)}) custom-call(bf16[4,288,768]{2,1,0:T(8,128)(2,1)} %get-tuple-element.245.refs_0_, f32[3,1,768]{2,1,0:T(1,128)} %get-tuple-element.246.refs_1_, ...), custom_call_target="tpu_custom_call" | custom-call | flops 13000000 | bytes 12582 | tf_op jit(solution)/shard_map/attend/pallas_call | solution.py:72
  82.3 12.2 %attend.5 = (bf16[4,288,768]{2,1,0:T(8,128)(2,1)}, bf16[4,2,8,144,144]{4,3,2,1,0:T(8,128)(2,1)}, bf16[4,288,256]{2,1,0:T(8,128)(2,1)}, f32[4,2,8,144]{3,2,1,0:T(8,128)}, bf16[768,768]{1,0:T(8,128)(2,1)}) custom-call(bf16[4,288,768]{2,1,0:T(8,128)(2,1)} %get-tuple-element.245.refs_0_, f32[3,1,768]{2,1,0:T(1,128)} %get-tuple-element.246.refs_1_, ...), custom_call_target="tpu_custom_call" | custom-call | flops 13000000 | bytes 12582 | tf_op jit(solution)/shard_map/attend/pallas_call | solution.py:72
  94.6 3.4 collective-permute-done.12.refs_15_
  102.0 69.4 %middle.1 = (bf16[4,144,768]{2,1,0:T(8,128)(2,1)}, bf16[4,144,768]{2,1,0:T(8,128)(2,1)}, f32[4,288,768]{2,1,0:T(8,128)}, bf16[4,288,768]{2,1,0:T(8,128)(2,1)}, b...) custom-call(s32[2]{0:T(128)} %pad_add_fusion.spot_ref.refs_0_, ...), custom_call_target="tpu_custom_call" | custom-call | flops 60000000 | bytes 41943 | tf_op jit(solution)/shard_map/middle/pallas_call | solution.py:567
  172.1 9.3 %attend_back.3 = (bf16[4,288,768]{2,1,0:T(8,128)(2,1)}, f32[8,144,144]{2,1,0:T(8,128)}) custom-call(bf16[4,288,768]{2,1,0:T(8,128)(2,1)} %get-tuple-element.318.refs_0_, bf16[4,2,8,144,144]{4,3,2,1,0:T(8,128)(2,1)} %get-tuple-element.319.refs_1_, bf16[4,288,768]{2,1,0:T(8,128)(2,1)} %get-tuple-element.320.refs_2_), custom_call_target="tpu_custom_call" | custom-call | flops 18000000 | bytes 10485 | tf_op jit(solution)/shard_map/attend_back/pallas_call | solution.py:72
  183.2 3.2 add_convert_fusion
  190.8 9.3 %attend_back.4 = (bf16[4,288,768]{2,1,0:T(8,128)(2,1)}, f32[8,144,144]{2,1,0:T(8,128)}) custom-call(bf16[4,288,768]{2,1,0:T(8,128)(2,1)} %get-tuple-element.333.refs_0_, bf16[4,2,8,144,144]{4,3,2,1,0:T(8,128)(2,1)} %get-tuple-element.334.refs_1_, bf16[4,288,768]{2,1,0:T(8,128)(2,1)} %get-tuple-element.320.refs_2_, ...), custom_call_target="tpu_custom_call" | custom-call | flops 18000000 | bytes 10485 | tf_op jit(solution)/shard_map/attend_back/pallas_call | solution.py:72
  200.1 8.6 %inner_grad.2 = (bf16[4,1,192,384]{3,2,1,0:T(8,128)(2,1)}, bf16[4,1,192,384]{3,2,1,0:T(8,128)(2,1)}, bf16[4,1,192,384]{3,2,1,0:T(8,128)(2,1)}, bf16[4,1,192,384]{3,2,1,0:T(8,128)(2,1)}, f32[2,1,768]{2,1,0:T(1,128)}) custom-call(s32[2]{0:T(128)} %pad_add_fusion.spot_ref.refs_0_, bf16[768,1152]{1,0:T(8,128)(2,1)} %get-tuple-element.331.refs_1_, ...), custom_call_target="tpu_custom_call" | custom-call | flops 8000000 | bytes 6291 | tf_op jit(solution)/shard_map/inner_grad/pallas_call | solution.py:72
  208.7 6.0 %collective-permute-done.22 = bf16[2,4,192,384]{3,2,1,0:T(8,128)(2,1)} collective-permute-done((bf16[2,4,192,384]{3,2,1,0:T(8,128)(2,1)S(1)}, bf16[2,4,192,384]{3,2,1,0:T(8,128)(2,1)}, u32[]{:S(2)}, u32[]{:S(2)}) %collective-permute-start.22) | collective-permute-done | bytes 1179680 | tf_op jit(solution)/shard_map/ppermute | solution.py:787
  214.8 3.0 collective-permute-done.21
  224.5 9.3 %attend_back.5 = (bf16[4,288,768]{2,1,0:T(8,128)(2,1)}, f32[8,144,144]{2,1,0:T(8,128)}) custom-call(bf16[4,288,768]{2,1,0:T(8,128)(2,1)} %get-tuple-element.343.refs_0_, bf16[4,2,8,144,144]{4,3,2,1,0:T(8,128)(2,1)} %get-tuple-element.344.refs_1_, bf16[4,288,768]{2,1,0:T(8,128)(2,1)} %get-tuple-element.320.refs_2_, bf16[4,192,384]{2,1,0:T(8,128)(2,1)} %fusion.3.refs_3_, ...), custom_call_target="tpu_custom_call" | custom-call | flops 18000000 | bytes 10485 | tf_op jit(solution)/shard_map/attend_back/pallas_call | solution.py:72
  234.5 3.1 collective-permute-done.23
  244.5 5.0 %inner_grad.3 = (bf16[4,1,192,384]{3,2,1,0:T(8,128)(2,1)}, bf16[4,1,192,384]{3,2,1,0:T(8,128)(2,1)}, f32[1,1,768]{2,1,0:T(1,128)}) custom-call(s32[2]{0:T(128)} %pad_add_fusion.spot_ref.refs_0_, bf16[768,1152]{1,0:T(8,128)(2,1)} %get-tuple-element.331.refs_1_, bf16[4,288,768]{2,1,0:T(8,128)(2,1)} %get-tuple-element.353.refs_2_.refs_6_, ...), custom_call_target="tpu_custom_call" | custom-call | flops 4000000 | bytes 6291 | tf_op jit(solution)/shard_map/inner_grad/pallas_call | solution.py:72
  253.0 13.3 %last.1 = (f32[8,768]{1,0:T(8,128)}, bf16[4,144,768]{2,1,0:T(8,128)(2,1)}, bf16[4,144,768]{2,1,0:T(8,128)(2,1)}) custom-call(bf16[4,288,768]{2,1,0:T(8,128)(2,1)} %get-tuple-element.239.tok_ref.refs_1_.refs_0_, f32[4,288,768]{2,1,0:T(8,128)} %get-tuple-element.356.refs_1_, f32[8,768]{1,0:T(8,128)} %get-tuple-element.310.refs_7_.refs_2_, ...), custom_call_target="tpu_custom_call" | custom-call | flops 20000000 | bytes 20971 | tf_op jit(solution)/shard_map/last/pallas_call | solution.py:72
  279.4 3.8 collective-permute-done.34
  286.5 7.8 %table.1 = f32[40,768]{1,0:T(8,128)} custom-call(f32[8,144,144]{2,1,0:T(8,128)} %get-tuple-element.369.refs_0_, f32[8,144,144]{2,1,0:T(8,128)} %get-tuple-element.370.refs_1_, f32[8,144,144]{2,1,0:T(8,128)} %get-tuple-element.371.refs_2_, f32[4,1,768]{2,1,0:T(1,128)} %get-tuple-element.372.refs_3_, f32[1,768]{1,0:T(1,128)} %get-tuple-element.373.refs_4_, ...), custom_call_target="tpu_custom_call" | custom-call | flops 6000000 | bytes 4194 | tf_op jit(solution)/shard_map/table/pallas_call | solution.py:72
  294.4 3.4 collective-permute-done.32
  303.6 3.2 collective-permute-start.39
  308.2 3.6 collective-permute-done.39
  311.8 5.1 %collective-permute-done.38 = bf16[4,96,384]{2,1,0:T(8,128)(2,1)S(1)} collective-permute-done((bf16[4,96,384]{2,1,0:T(8,128)(2,1)S(1)}, bf16[4,96,384]{2,1,0:T(8,128)(2,1)S(1)}, u32[]{:S(2)}, u32[]{:S(2)}) %collective-permute-start.38) | collective-permute-done | bytes 294944 | tf_op jit(solution)/shard_map/ppermute | solution.py:787
  324.8 14.7 %collective-permute-done.45 = bf16[1,192,384]{2,1,0:T(8,128)(2,1)S(1)} collective-permute-done((bf16[1,192,384]{2,1,0:T(8,128)(2,1)S(1)}, bf16[1,192,384]{2,1,0:T(8,128)(2,1)S(1)}, u32[]{:S(2)}, u32[]{:S(2)}) %collective-permute-start.45) | collective-permute-done | bytes 147488 | tf_op jit(solution)/shard_map/ppermute | solution.py:787
  349.2 4.1 %feed_finish.1 = (f32[192,3072]{1,0:T(8,128)}, f32[768,768]{1,0:T(8,128)}) custom-call(s32[2]{0:T(128)} %pad_add_fusion.spot_ref.refs_0_, bf16[4,192,384]{2,1,0:T(8,128)(2,1)} %copy-done.10, bf16[4,192,384]{2,1,0:T(8,128)(2,1)} %copy-done.33, bf16[4,192,384]{2,1,0:T(8,128)(2,1)} %copy-done.9, bf16[4,192,384]{2,1,0:T(8,128)(2,1)} %copy-done.34), custom_call_target="tpu_custom_call" | custom-call | flops 10000 | bytes 8388 | tf_op jit(solution)/shard_map/feed_finish/pallas_call | solution.py:72
  356.2 3.3 collective-permute-done.53
  363.5 4.9 %collective-permute-done.58 = f32[40,768]{1,0:T(8,128)S(1)} collective-permute-done((f32[40,768]{1,0:T(8,128)S(1)}, f32[40,768]{1,0:T(8,128)S(1)}, u32[]{:S(2)}, u32[]{:S(2)}) %collective-permute-start.58) | collective-permute-done | bytes 122912 | tf_op jit(solution)/shard_map/ppermute | solution.py:787
  (258 shorter events, 110.7 us)
Async XLA Ops:
  17.6 15.2 %collective-permute-start.3 = (bf16[208,768]{1,0:T(8,128)(2,1)S(1)}, bf16[208,768]{1,0:T(8,128)(2,1)S(1)}, u32[]{:S(2)}, u32[]{:S(2)}) collective-permute-start(bf16[208,768]{1,0:T(8,128)(2,1)S(1)} %collective-permute-done.pb_ref.refs_5_), channel_id=1, source_target_pairs={{0,4},{2,6},{4,0},{6,2},{1,5},{3,7},{5,1},{7,3},{8,12},{10,14},{12... | collective-permute-start | bytes 958472 | tf_op jit(solution)/shard_map/ppermute | solution.py:787
  40.1 37.8 %collective-permute-start.10 = (bf16[864,768]{1,0:T(8,128)(2,1)}, bf16[864,768]{1,0:T(8,128)(2,1)S(1)}, u32[]{:S(2)}, u32[]{:S(2)}) collective-permute-start(bf16[864,768]{1,0:T(8,128)(2,1)} %cut.1), channel_id=1, source_target_pairs={{0,2},{2,0},{4,6},{6,4},{1,3},{3,1},{5,7},{7,5},{8,10},{10,8},{12,... | collective-permute-start | bytes 3981320 | tf_op jit(solution)/shard_map/ppermute | solution.py:787
  41.0 36.9 %collective-permute-start.11 = (bf16[864,768]{1,0:T(8,128)(2,1)}, bf16[864,768]{1,0:T(8,128)(2,1)S(1)}, u32[]{:S(2)}, u32[]{:S(2)}) collective-permute-start(bf16[864,768]{1,0:T(8,128)(2,1)} %cut.1), channel_id=1, source_target_pairs={{0,4},{2,6},{4,0},{6,2},{1,5},{3,7},{5,1},{7,3},{8,12},{10,14},{12... | collective-permute-start | bytes 3981320 | tf_op jit(solution)/shard_map/ppermute | solution.py:787
  42.3 14.1 %collective-permute-start.7 = (bf16[96,1536]{1,0:T(8,128)(2,1)S(1)}, bf16[96,1536]{1,0:T(8,128)(2,1)}, u32[]{:S(2)}, u32[]{:S(2)}) collective-permute-start(bf16[96,1536]{1,0:T(8,128)(2,1)S(1)} %collective-permute-done.4.refs_5_), channel_id=1, source_target_pairs={{0,1},{1,0},{2,3},{3,2},{4,5},{5,4},{6,7},{7,6},{8,9},{9,8},{10,11... | collective-permute-start | bytes 884744 | tf_op jit(solution)/shard_map/ppermute | solution.py:787
  42.3 14.1 %collective-permute-start.8 = (bf16[96,1536]{1,0:T(8,128)(2,1)S(1)}, bf16[96,1536]{1,0:T(8,128)(2,1)}, u32[]{:S(2)}, u32[]{:S(2)}) collective-permute-start(bf16[96,1536]{1,0:T(8,128)(2,1)S(1)} %collective-permute-done.5.refs_6_), channel_id=1, source_target_pairs={{0,1},{1,0},{2,3},{3,2},{4,5},{5,4},{6,7},{7,6},{8,9},{9,8},{10,11... | collective-permute-start | bytes 884744 | tf_op jit(solution)/shard_map/ppermute | solution.py:787
  42.8 13.6 %collective-permute-start.9 = (bf16[96,1536]{1,0:T(8,128)(2,1)S(1)}, bf16[96,1536]{1,0:T(8,128)(2,1)}, u32[]{:S(2)}, u32[]{:S(2)}) collective-permute-start(bf16[96,1536]{1,0:T(8,128)(2,1)S(1)} %collective-permute-done.6.refs_7_), channel_id=1, source_target_pairs={{0,1},{1,0},{2,3},{3,2},{4,5},{5,4},{6,7},{7,6},{8,9},{9,8},{10,11... | collective-permute-start | bytes 884744 | tf_op jit(solution)/shard_map/ppermute | solution.py:787
  77.9 20.7 %collective-permute-start.14 = (bf16[864,768]{1,0:T(8,128)(2,1)S(1)}, bf16[864,768]{1,0:T(8,128)(2,1)}, u32[]{:S(2)}, u32[]{:S(2)}) collective-permute-start(bf16[864,768]{1,0:T(8,128)(2,1)S(1)} %collective-permute-done.10.refs_13_), channel_id=1, source_target_pairs={{0,1},{1,0},{2,3},{3,2},{4,5},{5,4},{6,7},{7,6},{8,9},{9,8},{10,11... | collective-permute-start | bytes 3981320 | tf_op jit(solution)/shard_map/ppermute | solution.py:787
  78.5 20.1 %collective-permute-start.15 = (bf16[864,768]{1,0:T(8,128)(2,1)S(1)}, bf16[864,768]{1,0:T(8,128)(2,1)}, u32[]{:S(2)}, u32[]{:S(2)}) collective-permute-start(bf16[864,768]{1,0:T(8,128)(2,1)S(1)} %collective-permute-done.11.refs_14_), channel_id=1, source_target_pairs={{0,1},{1,0},{2,3},{3,2},{4,5},{5,4},{6,7},{7,6},{8,9},{9,8},{10,11... | collective-permute-start | bytes 3981320 | tf_op jit(solution)/shard_map/ppermute | solution.py:787
  80.5 17.5 %collective-permute-start.12 = (bf16[432,768]{1,0:T(8,128)(2,1)}, bf16[432,768]{1,0:T(8,128)(2,1)S(1)}, u32[]{:S(2)}, u32[]{:S(2)}) collective-permute-start(bf16[432,768]{1,0:T(8,128)(2,1)} %slice.158), channel_id=1, source_target_pairs={{0,4},{2,6},{4,0},{6,2},{1,5},{3,7},{5,1},{7,3},{8,12},{10,14},{12... | collective-permute-start | bytes 1990664 | tf_op jit(solution)/shard_map/ppermute | solution.py:787
  81.2 17.4 %collective-permute-start.13 = (bf16[432,768]{1,0:T(8,128)(2,1)}, bf16[432,768]{1,0:T(8,128)(2,1)}, u32[]{:S(2)}, u32[]{:S(2)}) collective-permute-start(bf16[432,768]{1,0:T(8,128)(2,1)} %slice.159), channel_id=1, source_target_pairs={{0,2},{2,0},{4,6},{6,4},{1,3},{3,1},{5,7},{7,5},{8,10},{10,8},{12,... | collective-permute-start | bytes 1990664 | tf_op jit(solution)/shard_map/ppermute | solution.py:787
  186.3 28.4 %collective-permute-start.22 = (bf16[2,4,192,384]{3,2,1,0:T(8,128)(2,1)S(1)}, bf16[2,4,192,384]{3,2,1,0:T(8,128)(2,1)}, u32[]{:S(2)}, u32[]{:S(2)}) collective-permute-start(bf16[2,4,192,384]{3,2,1,0:T(8,128)(2,1)S(1)} %get-tuple-element.443.refs_4_), channel_id=1, source_target_pairs={{0,4},{2,6},{4,0},{6,2},{1,5},{3,7},{5,1},{7,3},{8,12},{10,14},{12... | collective-permute-start | bytes 3538952 | tf_op jit(solution)/shard_map/ppermute | solution.py:787
  189.5 28.3 %collective-permute-start.21 = (bf16[2,4,192,384]{3,2,1,0:T(8,128)(2,1)}, bf16[2,4,192,384]{3,2,1,0:T(8,128)(2,1)}, u32[]{:S(2)}, u32[]{:S(2)}) collective-permute-start(bf16[2,4,192,384]{3,2,1,0:T(8,128)(2,1)} %get-tuple-element.445.refs_3_), channel_id=1, source_target_pairs={{0,2},{2,0},{4,6},{6,4},{1,3},{3,1},{5,7},{7,5},{8,10},{10,8},{12,... | collective-permute-start | bytes 3538952 | tf_op jit(solution)/shard_map/ppermute | solution.py:787
  219.8 14.7 %collective-permute-start.24 = (bf16[4,192,384]{2,1,0:T(8,128)(2,1)}, bf16[4,192,384]{2,1,0:T(8,128)(2,1)S(1)}, u32[]{:S(2)}, u32[]{:S(2)}) collective-permute-start(bf16[4,192,384]{2,1,0:T(8,128)(2,1)} %fusion.4.refs_4_), channel_id=1, source_target_pairs={{0,2},{2,0},{4,6},{6,4},{1,3},{3,1},{5,7},{7,5},{8,10},{10,8},{12,... | collective-permute-start | bytes 1769480 | tf_op jit(solution)/shard_map/ppermute | solution.py:787
  223.1 14.4 %collective-permute-start.23 = (bf16[4,192,384]{2,1,0:T(8,128)(2,1)}, bf16[4,192,384]{2,1,0:T(8,128)(2,1)S(1)}, u32[]{:S(2)}, u32[]{:S(2)}) collective-permute-start(bf16[4,192,384]{2,1,0:T(8,128)(2,1)} %fusion.3.refs_3_), channel_id=1, source_target_pairs={{0,4},{2,6},{4,0},{6,2},{1,5},{3,7},{5,1},{7,3},{8,12},{10,14},{12... | collective-permute-start | bytes 1769480 | tf_op jit(solution)/shard_map/ppermute | solution.py:787
  224.0 13.6 %collective-permute-start.25 = (bf16[4,1,192,384]{3,2,1,0:T(8,128)(2,1)}, bf16[4,1,192,384]{3,2,1,0:T(8,128)(2,1)}, u32[]{:S(2)}, u32[]{:S(2)}) collective-permute-start(bf16[4,1,192,384]{3,2,1,0:T(8,128)(2,1)} %get-tuple-element.341), channel_id=1, source_target_pairs={{0,1},{1,0},{2,3},{3,2},{4,5},{5,4},{6,7},{7,6},{8,9},{9,8},{10,11... | collective-permute-start | bytes 1769480 | tf_op jit(solution)/shard_map/ppermute | solution.py:787
  224.0 13.6 %collective-permute-start.26 = (bf16[4,1,192,384]{3,2,1,0:T(8,128)(2,1)}, bf16[4,1,192,384]{3,2,1,0:T(8,128)(2,1)}, u32[]{:S(2)}, u32[]{:S(2)}) collective-permute-start(bf16[4,1,192,384]{3,2,1,0:T(8,128)(2,1)} %get-tuple-element.342), channel_id=1, source_target_pairs={{0,1},{1,0},{2,3},{3,2},{4,5},{5,4},{6,7},{7,6},{8,9},{9,8},{10,11... | collective-permute-start | bytes 1769480 | tf_op jit(solution)/shard_map/ppermute | solution.py:787
  224.5 41.9 %collective-permute-start.31 = (bf16[4,1,192,384]{3,2,1,0:T(8,128)(2,1)}, bf16[4,1,192,384]{3,2,1,0:T(8,128)(2,1)}, u32[]{:S(2)}, u32[]{:S(2)}) collective-permute-start(bf16[4,1,192,384]{3,2,1,0:T(8,128)(2,1)} %get-tuple-element.355), channel_id=1, source_target_pairs={{0,1},{1,0},{2,3},{3,2},{4,5},{5,4},{6,7},{7,6},{8,9},{9,8},{10,11... | collective-permute-start | bytes 1769480 | tf_op jit(solution)/shard_map/ppermute | solution.py:787
  249.5 16.9 %collective-permute-start.30 = (bf16[4,1,192,384]{3,2,1,0:T(8,128)(2,1)}, bf16[4,1,192,384]{3,2,1,0:T(8,128)(2,1)}, u32[]{:S(2)}, u32[]{:S(2)}) collective-permute-start(bf16[4,1,192,384]{3,2,1,0:T(8,128)(2,1)} %get-tuple-element.354.refs_10_), channel_id=1, source_target_pairs={{0,1},{1,0},{2,3},{3,2},{4,5},{5,4},{6,7},{7,6},{8,9},{9,8},{10,11... | collective-permute-start | bytes 1769480 | tf_op jit(solution)/shard_map/ppermute | solution.py:787
  249.5 16.9 %collective-permute-start.27 = (bf16[4,192,384]{2,1,0:T(8,128)(2,1)S(1)}, bf16[4,192,384]{2,1,0:T(8,128)(2,1)}, u32[]{:S(2)}, u32[]{:S(2)}) collective-permute-start(bf16[4,192,384]{2,1,0:T(8,128)(2,1)S(1)} %copy-done.5), channel_id=1, source_target_pairs={{0,8},{8,0},{16,24},{24,16},{1,9},{9,1},{17,25},{25,17},{2,10},{10... | collective-permute-start | bytes 1769480 | tf_op jit(solution)/shard_map/ppermute | solution.py:787
  251.2 15.2 %collective-permute-start.29 = (bf16[2,1,192,384]{3,2,1,0:T(8,128)(2,1)}, bf16[2,1,192,384]{3,2,1,0:T(8,128)(2,1)}, u32[]{:S(2)}, u32[]{:S(2)}) collective-permute-start(bf16[2,1,192,384]{3,2,1,0:T(8,128)(2,1)} %get-tuple-element.453.refs_5_), channel_id=1, source_target_pairs={{0,4},{2,6},{4,0},{6,2},{1,5},{3,7},{5,1},{7,3},{8,12},{10,14},{12... | collective-permute-start | bytes 884744 | tf_op jit(solution)/shard_map/ppermute | solution.py:787
  252.3 14.1 %collective-permute-start.28 = (bf16[2,1,192,384]{3,2,1,0:T(8,128)(2,1)}, bf16[2,1,192,384]{3,2,1,0:T(8,128)(2,1)}, u32[]{:S(2)}, u32[]{:S(2)}) collective-permute-start(bf16[2,1,192,384]{3,2,1,0:T(8,128)(2,1)} %get-tuple-element.455.refs_4_), channel_id=1, source_target_pairs={{0,2},{2,0},{4,6},{6,4},{1,3},{3,1},{5,7},{7,5},{8,10},{10,8},{12,... | collective-permute-start | bytes 884744 | tf_op jit(solution)/shard_map/ppermute | solution.py:787
  268.6 25.8 %collective-permute-start.36 = (bf16[2,1,192,384]{3,2,1,0:T(8,128)(2,1)}, bf16[2,1,192,384]{3,2,1,0:T(8,128)(2,1)}, u32[]{:S(2)}, u32[]{:S(2)}) collective-permute-start(bf16[2,1,192,384]{3,2,1,0:T(8,128)(2,1)} %get-tuple-element.449.refs_16_), channel_id=1, source_target_pairs={{0,4},{2,6},{4,0},{6,2},{1,5},{3,7},{5,1},{7,3},{8,12},{10,14},{12... | collective-permute-start | bytes 884744 | tf_op jit(solution)/shard_map/ppermute | solution.py:787
  271.6 22.8 %collective-permute-start.35 = (bf16[2,1,192,384]{3,2,1,0:T(8,128)(2,1)}, bf16[2,1,192,384]{3,2,1,0:T(8,128)(2,1)}, u32[]{:S(2)}, u32[]{:S(2)}) collective-permute-start(bf16[2,1,192,384]{3,2,1,0:T(8,128)(2,1)} %get-tuple-element.451.refs_15_), channel_id=1, source_target_pairs={{0,2},{2,0},{4,6},{6,4},{1,3},{3,1},{5,7},{7,5},{8,10},{10,8},{12,... | collective-permute-start | bytes 884744 | tf_op jit(solution)/shard_map/ppermute | solution.py:787
  276.3 18.1 %collective-permute-start.33 = (bf16[1,192,384]{2,1,0:T(8,128)(2,1)}, bf16[1,192,384]{2,1,0:T(8,128)(2,1)}, u32[]{:S(2)}, u32[]{:S(2)}) collective-permute-start(bf16[1,192,384]{2,1,0:T(8,128)(2,1)} %fusion.11.refs_13_), channel_id=1, source_target_pairs={{0,4},{2,6},{4,0},{6,2},{1,5},{3,7},{5,1},{7,3},{8,12},{10,14},{12... | collective-permute-start | bytes 442376 | tf_op jit(solution)/shard_map/ppermute | solution.py:787
  277.4 20.4 %collective-permute-start.37 = (bf16[4,144,768]{2,1,0:T(8,128)(2,1)}, bf16[4,144,768]{2,1,0:T(8,128)(2,1)}, u32[]{:S(2)}, u32[]{:S(2)}) collective-permute-start(bf16[4,144,768]{2,1,0:T(8,128)(2,1)} %get-tuple-element.381), channel_id=1, source_target_pairs={{0,1},{1,0},{2,3},{3,2},{4,5},{5,4},{6,7},{7,6},{8,9},{9,8},{10,11... | collective-permute-start | bytes 2654216 | tf_op jit(solution)/shard_map/ppermute | solution.py:787
  283.2 14.6 %collective-permute-start.32 = (bf16[4,96,384]{2,1,0:T(8,128)(2,1)S(1)}, bf16[4,96,384]{2,1,0:T(8,128)(2,1)S(1)}, u32[]{:S(2)}, u32[]{:S(2)}) collective-permute-start(bf16[4,96,384]{2,1,0:T(8,128)(2,1)S(1)} %broadcast_select_fusion.5.refs_12_), channel_id=1, source_target_pairs={{0,16},{8,24},{16,0},{24,8},{1,17},{9,25},{17,1},{25,9},{2,18},{10... | collective-permute-start | bytes 884744 | tf_op jit(solution)/shard_map/ppermute | solution.py:787
  302.3 14.5 %collective-permute-start.38 = (bf16[4,96,384]{2,1,0:T(8,128)(2,1)S(1)}, bf16[4,96,384]{2,1,0:T(8,128)(2,1)S(1)}, u32[]{:S(2)}, u32[]{:S(2)}) collective-permute-start(bf16[4,96,384]{2,1,0:T(8,128)(2,1)S(1)} %add_convert_fusion.11), channel_id=1, source_target_pairs={{0,16},{8,24},{16,0},{24,8},{1,17},{9,25},{17,1},{25,9},{2,18},{10... | collective-permute-start | bytes 884744 | tf_op jit(solution)/shard_map/ppermute | solution.py:787
  318.1 21.4 %collective-permute-start.43 = (bf16[4,192,384]{2,1,0:T(8,128)(2,1)S(1)}, bf16[4,192,384]{2,1,0:T(8,128)(2,1)S(1)}, u32[]{:S(2)}, u32[]{:S(2)}) collective-permute-start(bf16[4,192,384]{2,1,0:T(8,128)(2,1)S(1)} %pad_maximum_fusion.2), channel_id=1, source_target_pairs={{0,8},{8,0},{16,24},{24,16},{1,9},{9,1},{17,25},{25,17},{2,10},{10... | collective-permute-start | bytes 1769480 | tf_op jit(solution)/shard_map/ppermute | solution.py:787
  319.4 20.1 %collective-permute-start.45 = (bf16[1,192,384]{2,1,0:T(8,128)(2,1)S(1)}, bf16[1,192,384]{2,1,0:T(8,128)(2,1)S(1)}, u32[]{:S(2)}, u32[]{:S(2)}) collective-permute-start(bf16[1,192,384]{2,1,0:T(8,128)(2,1)S(1)} %broadcast_select_fusion.10), channel_id=1, source_target_pairs={{0,8},{8,0},{16,24},{24,16},{1,9},{9,1},{17,25},{25,17},{2,10},{10... | collective-permute-start | bytes 442376 | tf_op jit(solution)/shard_map/ppermute | solution.py:787
  322.5 16.9 %collective-permute-start.44 = (bf16[1,192,384]{2,1,0:T(8,128)(2,1)S(1)}, bf16[1,192,384]{2,1,0:T(8,128)(2,1)S(1)}, u32[]{:S(2)}, u32[]{:S(2)}) collective-permute-start(bf16[1,192,384]{2,1,0:T(8,128)(2,1)S(1)} %add_convert_fusion.23), channel_id=1, source_target_pairs={{0,16},{8,24},{16,0},{24,8},{1,17},{9,25},{17,1},{25,9},{2,18},{10... | collective-permute-start | bytes 442376 | tf_op jit(solution)/shard_map/ppermute | solution.py:787
  355.7 17.7 %collective-permute-start.54 = (bf16[1,192,384]{2,1,0:T(8,128)(2,1)S(1)}, bf16[1,192,384]{2,1,0:T(8,128)(2,1)S(1)}, u32[]{:S(2)}, u32[]{:S(2)}) collective-permute-start(bf16[1,192,384]{2,1,0:T(8,128)(2,1)S(1)} %get-tuple-element.461.refs_1_), channel_id=1, source_target_pairs={{0,1},{1,0},{2,3},{3,2},{4,5},{5,4},{6,7},{7,6},{8,9},{9,8},{10,11... | collective-permute-start | bytes 442376 | tf_op jit(solution)/shard_map/ppermute | solution.py:787
  355.7 17.7 %collective-permute-start.55 = (bf16[1,192,384]{2,1,0:T(8,128)(2,1)S(1)}, bf16[1,192,384]{2,1,0:T(8,128)(2,1)S(1)}, u32[]{:S(2)}, u32[]{:S(2)}) collective-permute-start(bf16[1,192,384]{2,1,0:T(8,128)(2,1)S(1)} %get-tuple-element.460.refs_2_), channel_id=1, source_target_pairs={{0,1},{1,0},{2,3},{3,2},{4,5},{5,4},{6,7},{7,6},{8,9},{9,8},{10,11... | collective-permute-start | bytes 442376 | tf_op jit(solution)/shard_map/ppermute | solution.py:787
  (79 other events, 588.2 us)

commit v4 on v3

--- a/solution.py
+++ b/solution.py
@@ -180,7 +180,7 @@
 V_UP, V_SMALL, V_IN, V_ONE, V_PEAK, V_TABLE, V_ROWS = 0, 4, 8, 11, 13, 16, 40
 
 
-def table_kernel(db0_ref, db1_ref, db2_ref, up_ref, down_ref, small_ref, in01_ref, in2_ref, one_ref, peak_ref, sq_ref, sk_ref, out_ref):
+def table_kernel(db0_ref, db1_ref, db2_ref, up_ref, down_ref, small_ref, in_ref, peak_ref, sq_ref, sk_ref, out_ref):
     def split(v):
         hi = v.astype(BF)
         return hi, (v - hi.astype(F32)).astype(BF)
@@ -194,10 +194,9 @@
     out_ref[V_SMALL : V_SMALL + 1, :] = down_ref[...]
     out_ref[V_SMALL + 1 : V_SMALL + 4, :] = small_ref[1:4, :]
     for p in range(3):
-        row = in01_ref[p] if p < 2 else in2_ref[0]
+        row = in_ref[p]
         for k in range(3):
             out_ref[V_IN + k : V_IN + k + 1, p * LP : (p + 1) * LP] = row[:, k * LP : (k + 1) * LP]
-    out_ref[V_ONE : V_ONE + 2, :] = one_ref[0:2, :]
     out_ref[V_PEAK : V_PEAK + 1, :HEADS] = peak_ref[...]
     for h in range(HEADS):
         hi, lo = split((db0_ref, db1_ref, db2_ref)[h // HP][h % HP])
@@ -212,8 +211,8 @@
         out_ref[V_TABLE + h : V_TABLE + h + 1, :WIDE] = colsum(tot)
 
 
-def table_call(dbs, up, down, small, in01, in2, one, peaks, after):
-    args = (*dbs, up, down, small, in01, in2, one, peaks, jnp.asarray(spread_q(), BF), jnp.asarray(spread_k(True), BF))
+def table_call(dbs, up, down, small, sums_in, peaks, after):
+    args = (*dbs, up, down, small, sums_in, peaks, jnp.asarray(spread_q(), BF), jnp.asarray(spread_k(True), BF))
     return single(table_kernel, args, SD((V_ROWS, D), F32), after, cost_estimate=cost(6e9, 4 * MB), name="table")
 
 
@@ -630,16 +629,16 @@
     )
 
 
-def inner_kernel(spot_ref, n1t_ref, *rest):
+def inner_kernel(spot_ref, n1t_ref, gp0_ref, gp1_ref, gp2_ref, os_ref, ok_ref, xs_ref, xk_ref, ys_ref, yk_ref, sum_ref):
     me = spot_ref[0]
     core = spot_ref[1]
-    gp_refs, outs, sum_ref = rest[: len(rest) // 3], rest[len(rest) // 3 : -1], rest[-1]
-    for k, gp_ref in enumerate(gp_refs):
-        n = gp_ref.shape[0]
+    n = gp0_ref.shape[0]
+    ys_ref[:, 1:2] = os_ref[...]
+    yk_ref[:, 1:2] = ok_ref[...]
+    for p, gp_ref, send, keep, m in ((0, gp0_ref, xs_ref, xk_ref, 0), (1, gp1_ref, ys_ref, yk_ref, 0), (2, gp2_ref, xs_ref, xk_ref, 1)):
         gp = gp_ref[...].reshape(n * ROWS, 3 * LP)
-        sum_ref[k] = colsum(gp.astype(F32))
+        sum_ref[p] = colsum(gp.astype(F32))
         gi = nn(n1t_ref[...], gp).astype(BF)
-        send, keep = outs[2 * k], outs[2 * k + 1]
 
         for c in range(2):
             @pl.when(core == c)
@@ -647,16 +646,16 @@
                 for b in range(4):
                     r = slice(b * OWN, (b + 1) * OWN)
                     rel = jnp.bitwise_xor(me, b)
-                    rel = crossed(rel) if k == 0 else rel
-                    keep[rel, 0] = gi[r, c * CH : (c + 1) * CH]
-                    send[rel, 0] = gi[r, (1 - c) * CH : (2 - c) * CH]
-
-
-def inner_call(spot, n1t, gps, after):
-    block = SD((4, 1, OWN, CH), BF)
+                    rel = rel if p == 1 else crossed(rel)
+                    keep[rel, m] = gi[r, c * CH : (c + 1) * CH]
+                    send[rel, m] = gi[r, (1 - c) * CH : (2 - c) * CH]
+
+
+def inner_call(spot, n1t, gps, outer, after):
+    block = SD((4, 2, OWN, CH), BF)
     return single(
-        inner_kernel, (spot, n1t, *gps), [block] * (2 * len(gps)) + [SD((len(gps), 1, 3 * LP), F32)], after,
-        cost_estimate=cost(4e9 * len(gps), 6 * MB), name="inner_grad",
+        inner_kernel, (spot, n1t, *gps, *outer), [block] * 4 + [SD((3, 1, 3 * LP), F32)], after,
+        cost_estimate=cost(1.2e10, 12 * MB), name="inner_grad",
     )
 
 
@@ -677,18 +676,18 @@
     send_ref[0] = o[TOK:]
 
 
-def last_call(tok, gmid, gain, pmt, gps, ws, after):
-    n = tok.shape[0]
-
+def last_call(first, n, tok, gmid, gain, pmt, gps, ws, after):
     def blk(*s):
-        return pl.BlockSpec((1,) + s, lambda i: (i,) + (0,) * len(s))
+        return pl.BlockSpec((1,) + s, lambda i: (first + i,) + (0,) * len(s))
+
+    cut = pl.BlockSpec((1, TOK, D), lambda i: (i, 0, 0))
 
     return run(
         last_kernel, 10, (tok, gmid, gain, pmt, *gps, *ws), after,
         grid=(n,),
         in_specs=[blk(ROWS, D), blk(ROWS, D), full((8, D)), full((ROWS, ROWS))] + [blk(ROWS, 3 * LP)] * 3
         + [full((D, 3 * LP), **ONE)] * 3,
-        out_specs=[full((8, D)), blk(TOK, D), blk(TOK, D)],
+        out_specs=[full((8, D)), cut, cut],
         out_shape=[SD((8, D), F32), SD((n, TOK, D), BF), SD((n, TOK, D), BF)],
         compiler_params=params(),
         cost_estimate=cost(2e10, 20 * MB),
@@ -739,20 +738,20 @@
     )
 
 
-def feed_finish_kernel(spot_ref, em_ref, eo_ref, rm_ref, ro_ref, ge_ref, gr_ref):
+def feed_finish_kernel(spot_ref, mine_ref, other_ref, ge_ref, gr_ref):
     for core in range(2):
         @pl.when(spot_ref[1] == core)
         def _():
-            for c, e_ref, r_ref in ((core, em_ref, rm_ref), (1 - core, eo_ref, ro_ref)):
+            for c, ref in ((core, mine_ref), (1 - core, other_ref)):
                 for b in range(4):
-                    ge_ref[:, (2 * b + c) * CH : (2 * b + c + 1) * CH] = e_ref[b].astype(F32)
+                    ge_ref[:, (2 * b + c) * CH : (2 * b + c + 1) * CH] = ref[b].astype(F32)
                     r = c * CH + (b // 2) * OWN
-                    gr_ref[r : r + OWN, (b % 2) * CH : (b % 2 + 1) * CH] = r_ref[b].astype(F32)
-
-
-def feed_finish(spot, em, eo, rm, ro):
+                    gr_ref[r : r + OWN, (b % 2) * CH : (b % 2 + 1) * CH] = ref[4 + b].astype(F32)
+
+
+def feed_finish(spot, mine, other):
     return single(
-        feed_finish_kernel, (spot, em, eo, rm, ro), [SD((OWN, FF), F32), SD((2 * CH, D), F32)],
+        feed_finish_kernel, (spot, mine, other), [SD((OWN, FF), F32), SD((2 * CH, D), F32)],
         cost_estimate=cost(1e7, 8 * MB), name="feed_finish",
     )
 
@@ -763,21 +762,20 @@
     return [(0, LP // 2, D + p * LP + LP // 2), (LP // 2, LP, 2 * D + p * LP)]
 
 
-def inner_finish_kernel(spot_ref, *refs):
-    mine, other, (gi_ref, go_ref) = refs[:4], refs[4:8], refs[8:]
+def inner_finish_kernel(spot_ref, mine_ref, other_ref, gi_ref, go_ref):
     for core in range(2):
         @pl.when(spot_ref[1] == core)
         def _():
-            for c, blocks in ((core, mine), (1 - core, other)):
-                for p in range(3):
+            for c, ref in ((core, mine_ref), (1 - core, other_ref)):
+                for k, p in enumerate((0, 2, 1)):
                     for at, size, put in inner_columns(p, c):
-                        gi_ref[:, put : put + size] = blocks[p][0, :, at : at + size].astype(F32)
-                go_ref[:, c * CH : (c + 1) * CH] = blocks[3][0].astype(F32)
+                        gi_ref[:, put : put + size] = ref[k, :, at : at + size].astype(F32)
+                go_ref[:, c * CH : (c + 1) * CH] = ref[3].astype(F32)
 
 
 def inner_finish(spot, mine, other):
     return single(
-        inner_finish_kernel, (spot, *mine, *other), [SD((OWN, 3 * D), F32), SD((OWN, D), F32)],
+        inner_finish_kernel, (spot, mine, other), [SD((OWN, 3 * D), F32), SD((OWN, D), F32)],
         cost_estimate=cost(1e7, 4 * MB), name="inner_finish",
     )
 
@@ -787,37 +785,41 @@
     return lax.ppermute(block, axis, [(i, i ^ bit) for i in range(count) if i ^ bit < count])
 
 
-def everywhere_hops():
-    for axis in ("half", "shard", "replica"):
-        bit = 1
-        while bit < lax.axis_size(axis):
-            yield axis, bit
-            bit *= 2
-
-
 def join_vectors(a, b):
     row = lax.broadcasted_iota(jnp.int32, a.shape, 0)
     return jnp.where(row == V_PEAK, jnp.maximum(a, b), a + b)
 
 
 class Everywhere:
-    def __init__(self, value):
-        self.value = value
-        self.hops = list(everywhere_hops())
-        self.flying = None
-        self.step()
-
-    def step(self):
-        if self.flying is not None:
-            self.value = join_vectors(self.value, self.flying)
-            self.flying = None
+    def __init__(self, sums, ones, direct):
+        self.value = [sums, *ones]
+        self.flying = []
+        self.hops = [("shard", (1, 2, 3)), ("replica", (1,)), ("replica", (2,)), ("half", (1,))]
+        if not direct:
+            self.hops = [
+                (axis, (1 << k,))
+                for axis in ("shard", "replica", "half") for k in range((lax.axis_size(axis) - 1).bit_length())
+            ]
+        self.done = False
+
+    def inputs(self):
+        return self.value + self.flying
+
+    def compute(self, values, low, low2):
+        v, *others = values
+        if not self.flying:
+            ones = others[0] + others[1]
+            return [jnp.concatenate([v[:V_ONE], ones[:2], v[V_ONE + 2 :]], axis=0)]
+        if len(others) == 3:
+            return [join_vectors(join_vectors(v, others[0]), join_vectors(others[1], others[2]))]
+        return [join_vectors(v, others[0])]
+
+    def launch(self, outs):
+        self.value = outs
+        self.done = not self.hops
         if self.hops:
-            self.flying = swap(self.value, *self.hops.pop(0))
-        return [self.value]
-
-    @property
-    def done(self):
-        return self.flying is None
+            axis, bits = self.hops.pop(0)
+            self.flying = [swap(outs[0], axis, bit) for bit in bits]
 
 
 def near(block):
@@ -833,72 +835,85 @@
 
 
 class Reduction:
-    def __init__(self, sends, keeps, replica, short):
-        self.short = short
-        self.low = (replica & 1) == 0
-        self.low2 = (replica & 2) == 0
+    def __init__(self, sends, keeps, quarters):
+        self.quarters = quarters
         self.keep = keeps
+        self.stage = 0
         self.sent = sends
-        self.stage = 0
         self.flying = [swap(v, "half", 1) for v in sends]
 
-    def step(self):
+    def inputs(self):
+        return list(self.keep) + list(self.flying)
+
+    def compute(self, values, low, low2):
         hlf = OWN // 2
-        got, low, low2 = self.flying, self.low, self.low2
+        kept, got = values[: len(self.keep)], values[len(self.keep) :]
         if self.stage == 0:
-            self.sent = [add(k[2:], g[2:]) for k, g in zip(self.keep, got)]
-            self.keep = [add(k[:2], g[:2]) for k, g in zip(self.keep, got)]
-            self.flying = [swap(self.sent[0], "shard", 1), swap(self.sent[1], "shard", 2)]
-        elif self.stage == 1:
-            self.sent = [add(k[1], g[1]) for k, g in zip(self.keep, got)]
-            self.keep = [add(k[0], g[0]) for k, g in zip(self.keep, got)]
-            self.flying = [swap(self.sent[0], "shard", 2), swap(self.sent[1], "shard", 1)]
-        elif self.stage == 2:
-            a, b = (add(k, g) for k, g in zip(self.keep, got))
-            self.keep = jnp.where(low, a, b)
-            self.sent = [jnp.where(low, b, a)]
-            self.flying = swap(self.sent[0], "replica", 1)
-        elif self.stage == 3 and self.short:
-            self.keep = add(self.keep, got)
-            self.sent = [self.keep]
-            self.flying = swap(self.keep, "replica", 2)
-            self.stage = 4
-        elif self.stage == 3:
-            u = add(self.keep, got)
-            self.keep = jnp.where(low2, u[:, :hlf], u[:, hlf:])
-            self.sent = [jnp.where(low2, u[:, hlf:], u[:, :hlf])]
-            self.flying = swap(self.sent[0], "replica", 2)
-        elif self.stage == 4:
-            self.keep = add(self.keep, got)
-            self.sent = [self.keep]
-            self.flying = swap(self.keep, "replica", 2)
-        elif self.stage == 5:
-            v = self.keep
-            if self.short:
-                self.keep = add(v, got)
+            return [add(k[:2], g[:2]) for k, g in zip(kept, got)] + [add(k[2:], g[2:]) for k, g in zip(kept, got)]
+        if self.stage == 1:
+            return [add(k[0], g[0]) for k, g in zip(kept, got)] + [add(k[1], g[1]) for k, g in zip(kept, got)]
+        if self.stage == 2:
+            if self.quarters:
+                u, v = (add(k, g) for k, g in zip(kept, got))
+                return [jnp.where(low, u, v), jnp.where(low, v, u)]
+            v = jnp.concatenate([add(k, g) for k, g in zip(kept, got)], axis=0)
+            return [jnp.where(low, v[:, :hlf], v[:, hlf:]), jnp.where(low, v[:, hlf:], v[:, :hlf])]
+        v = kept[0]
+        if self.quarters and self.stage == 3:
+            v = add(v, got[0])
+            return [jnp.where(low2, v[:, :hlf], v[:, hlf:]), jnp.where(low2, v[:, hlf:], v[:, :hlf])]
+        if self.quarters and self.stage == 5:
+            return [jnp.concatenate([jnp.where(low2, v, got[0]), jnp.where(low2, got[0], v)], axis=1)]
+        if self.quarters and self.stage == 6:
+            return [jnp.concatenate([jnp.where(low, v, got[0]), jnp.where(low, got[0], v)], axis=0)]
+        if self.stage in (3, 4):
+            return [add(v, got[0])]
+        return [jnp.concatenate([jnp.where(low, v, got[0]), jnp.where(low, got[0], v)], axis=1)]
+
+    def launch(self, outs):
+        if self.stage < 2:
+            half = len(outs) // 2
+            self.keep, self.sent = outs[:half], outs[half:]
+            bits = (1, 2) if self.stage == 0 else (2, 1)
+            self.flying = [swap(v, "shard", bit) for v, bit in zip(self.sent, bits)]
+        else:
+            self.keep, self.sent = outs[:1], outs[-1:]
+            if self.stage == (6 if self.quarters else 5):
+                self.flying = [swap(self.keep[0], "half", 1)]
             else:
-                self.keep = jnp.concatenate([jnp.where(low2, v, got), jnp.where(low2, got, v)], axis=1)
-            self.sent = [self.keep]
-            self.flying = swap(self.keep, "replica", 1)
-        elif self.stage == 6:
-            v = self.keep
-            self.keep = [jnp.where(low, v, got), jnp.where(low, got, v)]
-            self.sent = self.keep
-            self.flying = [swap(v, "half", 1) for v in self.keep]
+                far = (3, 4) if self.quarters else (3,)
+                self.flying = [swap(self.sent[0], "replica", 2 if self.stage in far else 1)]
         self.stage += 1
-        return list(self.sent)
-
-    @property
-    def done(self):
-        return self.stage == 7
-
-
-def together(chains, *others):
-    left = [c for c in chains if not c.done]
-    flying, others = fence([c.flying for c in left], others)
-    for c, v in zip(left, flying):
+
+
+def hop_kernel(chains, counts, place_ref, *refs):
+    replica = place_ref[3]
+    low, low2 = (replica & 1) == 0, (replica & 2) == 0
+    refs = list(refs)
+    inputs = [[refs.pop(0)[...] for _ in range(count)] for count in counts]
+    for chain, values in zip(chains, inputs):
+        for out in chain.compute(values, low, low2):
+            refs.pop(0)[...] = out
+
+
+def together(place, chains, *others, plain=False):
+    flying, others = fence([c.flying for c in chains], others)
+    for c, v in zip(chains, flying):
         c.flying = v
-        c.step()
+    inputs = [c.inputs() for c in chains]
+    low, low2 = (place[3] & 1) == 0, (place[3] & 2) == 0
+    shapes = [jax.eval_shape(c.compute, v, low, low2) for c, v in zip(chains, inputs)]
+    if plain:
+        outs = [c.compute(v, low, low2) for c, v in zip(chains, inputs)]
+    else:
+        flat = [x for v in inputs for x in v]
+        results = list(single(
+            functools.partial(hop_kernel, chains, [len(v) for v in inputs]), (place, *flat),
+            [SD(x.shape, x.dtype) for v in shapes for x in v], cost_estimate=cost(1e7, 4 * MB), name="hop",
+        ))
+        outs = [[results.pop(0) for _ in v] for v in shapes]
+    for c, v in zip(chains, outs):
+        c.launch(v)
     return others
 
 
@@ -912,6 +927,7 @@
     quick = shard_count == 4 and lax.axis_size("replica") == 4
     me = shard if quick else jnp.int32(0)
     spot = jnp.stack([me, core]).astype(jnp.int32)
+    place = jnp.stack([me, core, shard, replica]).astype(jnp.int32)
     own_images = images.reshape(n, ROWS, D)
     own_grad = cotangent.reshape(n, ROWS, D)
     vectors = (inner_bias, outer_bias, expand_bias, reduce_bias, first_gain, first_shift, second_gain, second_shift)
@@ -1030,58 +1046,62 @@
     (stay, send, gmid, datt, out_send, out_keep, e_send, e_keep, r_send, r_keep, grad_up, small) = middle_call(
         spot, tok, atts, g, back_order, vecs, up_bias, at, plan, pieces, []
     )
-    if quick:
-        feed = Reduction([e_send, r_send], [e_keep, r_keep], replica, False)
+    def wait_for(chains):
+        return [v for c in chains for v in c.sent]
+
+    after = []
+    if quick:
+        feed = Reduction([e_send, r_send], [e_keep, r_keep], True)
     lower_out = swap(send, "half", 1)
     gp0, db0 = back_call(0, projs[0], pts[0], datt, [])
     if quick:
-        (gp0, lower_out, projs) = together([feed], gp0, lower_out, projs)
-    gp1, db1 = back_call(1, projs[1], pts[1], datt, feed.sent if quick else [])
-    i0_send, i0_keep, i1_send, i1_keep, in01 = inner_call(spot, n1t, (gp0, gp1), [])
-    chains = []
-    if quick:
-        i0_send, i1_send, projs = together([feed], i0_send, i1_send, projs)
-        ahead = Reduction([i0_send, i1_send], [i0_keep, i1_keep], replica, True)
-        chains = [feed, ahead]
-    gp2, db2 = back_call(2, projs[2], pts[2], datt, feed.sent if quick else [])
-    if quick:
-        gp2, db2 = together(chains, gp2, db2)
-    i2_send, i2_keep, in2 = inner_call(spot, n1t, (gp2,), feed.sent + ahead.sent if quick else [])
-    if quick:
-        rest = Reduction([i2_send, out_send], [i2_keep, out_keep], replica, True)
-        chains = [feed, ahead, rest]
-    one, gstay, gsend = last_call(tok, gmid, vecs, back_order, (gp0, gp1, gp2), ws, [i2_send])
-    after = []
-    if quick:
-        gsend, one = together(chains, gsend, one)
-        after = feed.sent + ahead.sent + rest.sent
-    lower_grad = swap(gsend, "half", 1)
+        gp0, lower_out, projs = together(place, [feed], gp0, lower_out, projs, plain=True)
+        after = wait_for([feed])
+    gp1, db1 = back_call(1, projs[1], pts[1], datt, after)
+    gp2, db2 = back_call(2, projs[2], pts[2], datt, [gp1])
+    x_send, x_keep, y_send, y_keep, sums_in = inner_call(spot, n1t, (gp0, gp1, gp2), (out_send, out_keep), [])
     peak = jnp.concatenate(peak, axis=2)
     peaks = jnp.max(jnp.where((present > 0)[:, None, None, None], peak, NEGATIVE), axis=(0, 1, 3)).reshape(1, HEADS)
-    sums = table_call((db0, db1, db2), grad_up, grad_down, small, in01, in2, one, peaks, after)
-    if quick:
-        sums, lower_grad = together(chains, sums, lower_grad)
-    every = Everywhere(sums)
-    chains.append(every)
-    done = None
-    while not all(c.done for c in chains):
-        if quick and done is None and feed.done:
-            swapped = fence(feed.flying)[0]
-            (em, rm), (eo, ro) = feed.keep, swapped
-            done = feed_finish(spot, em, eo, rm, ro)
-            chains = [c for c in chains if c is not feed]
-            done = together(chains, *done)
-        else:
-            together(chains)
-    sums = every.value
-
-    place = jnp.stack([me, core, shard]).astype(jnp.int32)
+    after = [x_send]
+    if quick:
+        x_send, y_send, gp2 = together(place, [feed], x_send, y_send, gp2)
+        rest = Reduction([x_send, y_send], [x_keep, y_keep], False)
+        after = wait_for([feed])
+    half = n // 2
+    one_a, gstay_a, gsend_a = last_call(0, half, tok, gmid, vecs, back_order, (gp0, gp1, gp2), ws, after)
+    after = [gsend_a]
+    if quick:
+        gsend_a, one_a = together(place, [rest, feed], gsend_a, one_a)
+        after = wait_for([rest, feed])
+    lower_a = swap(gsend_a, "half", 1)
+    one_b, gstay_b, gsend_b = last_call(half, n - half, tok, gmid, vecs, back_order, (gp0, gp1, gp2), ws, after)
+    after = [gsend_b]
+    if quick:
+        gsend_b, lower_a = together(place, [rest, feed], gsend_b, lower_a)
+        after = wait_for([rest, feed])
+    lower_b = swap(gsend_b, "half", 1)
+    sums = table_call((db0, db1, db2), grad_up, grad_down, small, sums_in, peaks, after)
+    every = Everywhere(sums, (one_a, one_b), quick)
+    if quick:
+        rest.flying, feed.flying, lower_b = fence(rest.flying, feed.flying, lower_b)
+        together(place, [rest, every, feed])
+        together(place, [rest, every, feed])
+        together(place, [rest, every])
+        rest.flying, every.flying, feed.flying = fence(rest.flying, every.flying, feed.flying)
+        together(place, [rest, every, feed])
+        every.flying, feed.flying = fence(every.flying, feed.flying)
+        grad_expand, grad_reduce = feed_finish(spot, *feed.keep, *feed.flying)
+        together(place, [every])
+    else:
+        while not every.done:
+            together(place, [every])
+    sums = every.value[0]
+
     (grad_inbias, grad_outbias, grad_upbias, grad_downbias, grad_gain_1, grad_shift_1, grad_gain_2, grad_shift_2, grad_table,
      clipped, factors, maxima) = vector_finish(place, sums, threshold, inner_weight, shard_count)
 
     if quick:
-        grad_expand, grad_reduce = done
-        grad_inner, grad_outer = inner_finish(spot, ahead.keep + rest.keep, ahead.flying + rest.flying)
+        grad_inner, grad_outer = inner_finish(spot, *rest.keep, *rest.flying)
     else:
         def halves(keep, send, axis):
             lo = jnp.where(core == 0, keep, send)
@@ -1105,13 +1125,16 @@
         grad_reduce = settle(halves(rows_of(r_keep), rows_of(r_send), 1).reshape(FF, D))
         grad_expand = settle(whole(straight(e_keep), straight(e_send)))
         grad_outer = settle(whole(out_keep, out_send))
+        x_keep, x_send = straight(x_keep), straight(x_send)
         by_third = [
-            whole(straight(i0_keep), straight(i0_send)), whole(i1_keep, i1_send), whole(straight(i2_keep), straight(i2_send))
+            whole(x_keep[:, :1], x_send[:, :1]), whole(y_keep[:, :1], y_send[:, :1]), whole(x_keep[:, 1:], x_send[:, 1:])
         ]
         by_third = jnp.stack(by_third, axis=1).reshape(D, 3, 3, LP).transpose(0, 2, 1, 3).reshape(D, 3 * D)
         grad_inner = settle(by_third)
 
     block_out = jnp.concatenate([lower_out, stay], axis=1).reshape(images.shape)
+    lower_grad = jnp.concatenate([lower_a, lower_b])
+    gstay = jnp.concatenate([gstay_a, gstay_b])
     grad_images = jnp.concatenate([lower_grad, gstay], axis=1).reshape(images.shape)
     return (
         block_out,

time: 384 us -> 377 us (0.982)
  other arithmetic: 40.4 us -> 13.1 us
  Pallas kernels: 210 us -> 236 us
  waiting for transfers between devices: 67.2 us -> 58.3 us
  local copies, waits for them, and re-layouts: 9.88 us -> 14.7 us
    pallas_call x15 -> x23, Pallas kernels: 118 us -> 144 us  [run(): pl.pallas_call(body, in_specs=list(in_specs) + [any_space()] * len(after)...]
    convert_element_type x18 -> x2, other arithmetic: 26.6 us -> 6.78 us  [add(): return (a.astype(F32) + b.astype(F32)).astype(BF)]
    ppermute x59 -> x48, waiting for transfers between devices: 67.2 us -> 58.3 us  [swap(): lax.ppermute(block, axis, [(i, i ^ bit) for i in range(count) if i ^ bit...]
    select_n x13 -> x0, other arithmetic: 6.33 us -> none  [the longest x3 4.9 us: step(): self.sent = [jnp.where(low, b, a)]]
    unnamed x105 -> x113, local copies, waits for them, and re-layouts: 6.6 us -> 11.5 us
    ppermute x59 -> x48, starting transfers between devices: 48.4 us -> 45.8 us  [swap(): lax.ppermute(block, axis, [(i, i ^ bit) for i in range(count) if i ^ bit...]
  transfers between devices with their start and end apart: 59 -> 48, of which waited for: 21 -> 21; matrix products, arithmetic and copies ran while one was open for 10% -> 3% of each run, Pallas kernels for 36% -> 38%
where the time goes in v4:
time: 377 us; the launch traced here: 370 us
  Pallas kernels  236 us (63%)
  waiting for transfers between devices  58.3 us (15%)
  starting transfers between devices  45.8 us (12%)
  local copies, waits for them, and re-layouts  14.7 us (4%)
  other arithmetic  13.1 us (3%)
    pallas_call x23, Pallas kernels, run(): pl.pallas_call(body, in_specs=list(in_specs) + [any_space()] * len(after)...  144 us
    pallas_call x1, Pallas kernels, middle_call(): pl.pallas_call(body, grid_spec=grid_spec, out_shape=[SD((n, TOK, D), BF),...  69.2 us
    ppermute x48, waiting for transfers between devices, swap(): lax.ppermute(block, axis, [(i, i ^ bit) for i in range(count) if i ^ bit...  58.3 us
    ppermute x48, starting transfers between devices, swap(): lax.ppermute(block, axis, [(i, i ^ bit) for i in range(count) if i ^ bit...  45.8 us
    pallas_call x3, Pallas kernels, bias_call(): pl.pallas_call(bias_kernel, grid=(1,), in_specs=[smem(), pl.BlockSpec((HP...  14 us
    unnamed x113, local copies, waits for them, and re-layouts  11.5 us
  transfers between devices with their start and end apart: 48, of which 21 were waited for; matrix products, arithmetic and copies ran while one was open for 3% of the time, Pallas kernels for 38%

profile of v4, /device:TPU:0, one launch (start us, length us, event | category | flops | bytes accessed | tf_op | source)
XLA Modules:
  0.0 369.6 jit_solution(4586663201779011181)
XLA Ops:
  1.3 3.5 first.1
  10.0 4.7 %bias.3.refs_2_ = f32[2,8,144,144]{3,2,1,0:T(8,128)} custom-call(s32[2]{0:T(128)} %pad_add_fusion.spot_ref.refs_0_, f32[24,640]{1,0:T(8,128)} %pad_convert_fusion.table_ref, bf16[2,2,144,144]{3,2,1,0:T(8,128)(2,1)} %constant.56.clone.mask_ref, bf16[384,144]{1,0:T(8,128)(2,1)} %constant.57.clone.sq_ref, bf16[144,192]{1,0:T(8,128)(2,1)} %constant.58.clone.sk_ref), custom_call_target="tpu_custom_call" | custom-call | flops 2000000 | bytes 3145 | tf_op jit(solution)/shard_map/bias/pallas_call | solution.py:167
  24.8 6.2 %prep.1 = (bf16[4,288,768]{2,1,0:T(8,128)(2,1)}, bf16[4,288,768]{2,1,0:T(8,128)(2,1)}, f32[1,768]{1,0:T(1,128)}) custom-call(bf16[4,288,768]{2,1,0:T(8,128)(2,1)} %bitcast.32, bf16[4,288,768]{2,1,0:T(8,128)(2,1)} %bitcast.34, bf16[8,144,768]{2,1,0:T(8,128)(2,1)} %copy-done.6, f32[1,4]{1,0:T(1,128)} %convert_bitcast_fusion.refs_3_, ...), custom_call_target="tpu_custom_call" | custom-call | flops 3000000 | bytes 16777 | tf_op jit(solution)/shard_map/prep/pallas_call | solution.py:72
  34.5 5.5 %vectors.1 = (f32[3,1,768]{2,1,0:T(1,128)}, f32[4,1,768]{2,1,0:T(1,128)}, f32[8,768]{1,0:T(8,128)}, bf16[4,288,768]{2,1,0:T(8,128)(2,1)}, bf16[768,1152]{1,0:T(8,128)(2,1)}) custom-call(s32[2]{0:T(128)} %pad_add_fusion.spot_ref.refs_0_, bf16[208,768]{1,0:T(8,128)(2,1)} %get-tuple-element.244.pa_ref.refs_4_, bf16[208,768]{1,0:T(8,128)(2,1)} %copy-done.8, ...), custom_call_target="tpu_custom_call" | custom-call | flops 5000000 | bytes 8388 | tf_op jit(solution)/shard_map/vectors/pallas_call | solution.py:333
  44.3 12.3 %attend.3 = (bf16[4,288,768]{2,1,0:T(8,128)(2,1)}, bf16[4,2,8,144,144]{4,3,2,1,0:T(8,128)(2,1)}, bf16[4,288,256]{2,1,0:T(8,128)(2,1)}, f32[4,2,8,144]{3,2,1,0:T(8,128)}, bf16[768,768]{1,0:T(8,128)(2,1)}) custom-call(bf16[4,288,768]{2,1,0:T(8,128)(2,1)} %get-tuple-element.265.refs_0_, f32[3,1,768]{2,1,0:T(1,128)} %get-tuple-element.266.refs_1_, ...), custom_call_target="tpu_custom_call" | custom-call | flops 13000000 | bytes 12582 | tf_op jit(solution)/shard_map/attend/pallas_call | solution.py:72
  56.6 4.7 %bias.5.refs_11_.refs_2_ = f32[2,8,144,144]{3,2,1,0:T(8,128)} custom-call(s32[2]{0:T(128)} %pad_add_fusion.spot_ref.refs_0_, f32[24,640]{1,0:T(8,128)} %pad_convert_fusion.table_ref, bf16[2,2,144,144]{3,2,1,0:T(8,128)(2,1)} %constant.56.clone.mask_ref, bf16[384,144]{1,0:T(8,128)(2,1)} %constant.57.clone.sq_ref, bf16[144,192]{1,0:T(8,128)(2,1)} %constant.58.clone.sk_ref), custom_call_target="tpu_custom_call" | custom-call | flops 2000000 | bytes 3145 | tf_op jit(solution)/shard_map/bias/pallas_call | solution.py:167
  61.3 4.7 %bias.4.refs_2_ = f32[2,8,144,144]{3,2,1,0:T(8,128)} custom-call(s32[2]{0:T(128)} %pad_add_fusion.spot_ref.refs_0_, f32[24,640]{1,0:T(8,128)} %pad_convert_fusion.table_ref, bf16[2,2,144,144]{3,2,1,0:T(8,128)(2,1)} %constant.56.clone.mask_ref, bf16[384,144]{1,0:T(8,128)(2,1)} %constant.57.clone.sq_ref, bf16[144,192]{1,0:T(8,128)(2,1)} %constant.58.clone.sk_ref), custom_call_target="tpu_custom_call" | custom-call | flops 2000000 | bytes 3145 | tf_op jit(solution)/shard_map/bias/pallas_call | solution.py:167
  66.0 12.1 %attend.4 = (bf16[4,288,768]{2,1,0:T(8,128)(2,1)}, bf16[4,2,8,144,144]{4,3,2,1,0:T(8,128)(2,1)}, bf16[4,288,256]{2,1,0:T(8,128)(2,1)}, f32[4,2,8,144]{3,2,1,0:T(8,128)}, bf16[768,768]{1,0:T(8,128)(2,1)}) custom-call(bf16[4,288,768]{2,1,0:T(8,128)(2,1)} %get-tuple-element.265.refs_0_, f32[3,1,768]{2,1,0:T(1,128)} %get-tuple-element.266.refs_1_, ...), custom_call_target="tpu_custom_call" | custom-call | flops 13000000 | bytes 12582 | tf_op jit(solution)/shard_map/attend/pallas_call | solution.py:72
  82.5 12.2 %attend.5 = (bf16[4,288,768]{2,1,0:T(8,128)(2,1)}, bf16[4,2,8,144,144]{4,3,2,1,0:T(8,128)(2,1)}, bf16[4,288,256]{2,1,0:T(8,128)(2,1)}, f32[4,2,8,144]{3,2,1,0:T(8,128)}, bf16[768,768]{1,0:T(8,128)(2,1)}) custom-call(bf16[4,288,768]{2,1,0:T(8,128)(2,1)} %get-tuple-element.265.refs_0_, f32[3,1,768]{2,1,0:T(1,128)} %get-tuple-element.266.refs_1_, ...), custom_call_target="tpu_custom_call" | custom-call | flops 13000000 | bytes 12582 | tf_op jit(solution)/shard_map/attend/pallas_call | solution.py:72
  94.7 3.5 collective-permute-done.13.refs_16_
  102.7 69.2 %middle.1 = (bf16[4,144,768]{2,1,0:T(8,128)(2,1)}, bf16[4,144,768]{2,1,0:T(8,128)(2,1)}, f32[4,288,768]{2,1,0:T(8,128)}, bf16[4,288,768]{2,1,0:T(8,128)(2,1)}, b...) custom-call(s32[2]{0:T(128)} %pad_add_fusion.spot_ref.refs_0_, ...), custom_call_target="tpu_custom_call" | custom-call | flops 60000000 | bytes 41943 | tf_op jit(solution)/shard_map/middle/pallas_call | solution.py:566
  172.7 9.5 %attend_back.3 = (bf16[4,288,768]{2,1,0:T(8,128)(2,1)}, f32[8,144,144]{2,1,0:T(8,128)}) custom-call(bf16[4,288,768]{2,1,0:T(8,128)(2,1)} %get-tuple-element.338.refs_0_, bf16[4,2,8,144,144]{4,3,2,1,0:T(8,128)(2,1)} %get-tuple-element.339.refs_1_, bf16[4,288,768]{2,1,0:T(8,128)(2,1)} %get-tuple-element.340.refs_2_), custom_call_target="tpu_custom_call" | custom-call | flops 18000000 | bytes 10485 | tf_op jit(solution)/shard_map/attend_back/pallas_call | solution.py:72
  183.1 3.5 add_convert_fusion
  187.6 3.3 add_convert_fusion.1
  192.5 9.3 %attend_back.4 = (bf16[4,288,768]{2,1,0:T(8,128)(2,1)}, f32[8,144,144]{2,1,0:T(8,128)}) custom-call(bf16[4,288,768]{2,1,0:T(8,128)(2,1)} %get-tuple-element.349.refs_0_, bf16[4,2,8,144,144]{4,3,2,1,0:T(8,128)(2,1)} %get-tuple-element.350.refs_1_, bf16[4,288,768]{2,1,0:T(8,128)(2,1)} %get-tuple-element.340.refs_2_, bf16[2,4,192,384]{3,2,1,0:T(8,128)(2,1)} %copy-done.1, ...), custom_call_target="tpu_custom_call" | custom-call | flops 18000000 | bytes 10485 | tf_op jit(solution)/shard_map/attend_back/pallas_call | solution.py:72
  201.8 9.3 %attend_back.5 = (bf16[4,288,768]{2,1,0:T(8,128)(2,1)}, f32[8,144,144]{2,1,0:T(8,128)}) custom-call(bf16[4,288,768]{2,1,0:T(8,128)(2,1)} %get-tuple-element.356.refs_0_, bf16[4,2,8,144,144]{4,3,2,1,0:T(8,128)(2,1)} %get-tuple-element.357.refs_1_, bf16[4,288,768]{2,1,0:T(8,128)(2,1)} %get-tuple-element.340.refs_2_, ...), custom_call_target="tpu_custom_call" | custom-call | flops 18000000 | bytes 10485 | tf_op jit(solution)/shard_map/attend_back/pallas_call | solution.py:72
  211.1 12.3 %inner_grad.1 = (bf16[4,2,192,384]{3,2,1,0:T(8,128)(2,1)}, bf16[4,2,192,384]{3,2,1,0:T(8,128)(2,1)}, bf16[4,2,192,384]{3,2,1,0:T(8,128)(2,1)}, bf16[4,2,192,384]{3,2,1,0:T(8,128)(2,1)}, f32[3,1,768]{2,1,0:T(1,128)}) custom-call(s32[2]{0:T(128)} %pad_add_fusion.spot_ref.refs_0_, bf16[768,1152]{1,0:T(8,128)(2,1)} %get-tuple-element.347.refs_1_, ...), custom_call_target="tpu_custom_call" | custom-call | flops 12000000 | bytes 12582 | tf_op jit(solution)/shard_map/inner_grad/pallas_call | solution.py:72
  224.6 3.9 %hop.8 = (bf16[4,192,384]{2,1,0:T(8,128)(2,1)}, bf16[4,192,384]{2,1,0:T(8,128)(2,1)}, bf16[4,192,384]{2,1,0:T(8,128)(2,1)}, bf16[4,192,384]{2,1,0:T(8,128)(2,1)}) custom-call(s32[4]{0:T(128)} %pad_add_fusion.2.refs_0_, bf16[2,4,192,384]{3,2,1,0:T(8,128)(2,1)} %get-tuple-element.484.refs_1_, bf16[2,4,192,384]{3,2,1,0:T(8,128)(2,1)} %get-tuple-element.482.refs_2_, ...), custom_call_target="tpu_custom_call" | custom-call | flops 10000 | bytes 4194 | tf_op jit(solution)/shard_map/hop/pallas_call | solution.py:72
  230.3 8.6 %last.2 = (f32[8,768]{1,0:T(8,128)}, bf16[2,144,768]{2,1,0:T(8,128)(2,1)}, bf16[2,144,768]{2,1,0:T(8,128)(2,1)}) custom-call(bf16[4,288,768]{2,1,0:T(8,128)(2,1)} %get-tuple-element.259.tok_ref.refs_1_.refs_0_, f32[4,288,768]{2,1,0:T(8,128)} %get-tuple-element.371.refs_1_, f32[8,768]{1,0:T(8,128)} %get-tuple-element.330.refs_7_.refs_2_, ...), custom_call_target="tpu_custom_call" | custom-call | flops 20000000 | bytes 20971 | tf_op jit(solution)/shard_map/last/pallas_call | solution.py:72
  238.8 5.2 %collective-permute-done.25.refs_7_ = bf16[4,192,384]{2,1,0:T(8,128)(2,1)S(1)} collective-permute-done((bf16[4,192,384]{2,1,0:T(8,128)(2,1)}, bf16[4,192,384]{2,1,0:T(8,128)(2,1)S(1)}, u32[]{:S(2)}, u32[]{:S(2)}) %collective-permute-start.25) | collective-permute-done | bytes 589856 | tf_op jit(solution)/shard_map/ppermute | solution.py:785
  245.7 5.0 %hop.9 = (bf16[2,2,192,384]{3,2,1,0:T(8,128)(2,1)}, bf16[2,2,192,384]{3,2,1,0:T(8,128)(2,1)}, bf16[2,2,192,384]{3,2,1,0:T(8,128)(2,1)}, bf16[2,2,192,384]{3,2,1,...) custom-call(s32[4]{0:T(128)} %pad_add_fusion.2.refs_0_, ...), custom_call_target="tpu_custom_call" | custom-call | flops 10000 | bytes 4194 | tf_op jit(solution)/shard_map/hop/pallas_call | solution.py:72
  254.6 8.6 %last.3 = (f32[8,768]{1,0:T(8,128)}, bf16[2,144,768]{2,1,0:T(8,128)(2,1)}, bf16[2,144,768]{2,1,0:T(8,128)(2,1)}) custom-call(bf16[4,288,768]{2,1,0:T(8,128)(2,1)} %get-tuple-element.259.tok_ref.refs_1_.refs_0_, f32[4,288,768]{2,1,0:T(8,128)} %get-tuple-element.371.refs_1_, f32[8,768]{1,0:T(8,128)} %get-tuple-element.330.refs_7_.refs_2_, ...), custom_call_target="tpu_custom_call" | custom-call | flops 20000000 | bytes 20971 | tf_op jit(solution)/shard_map/last/pallas_call | solution.py:72
  267.6 3.3 hop.10
  276.0 7.8 %table.1.refs_5_ = f32[40,768]{1,0:T(8,128)} custom-call(f32[8,144,144]{2,1,0:T(8,128)} %get-tuple-element.410.refs_0_, f32[8,144,144]{2,1,0:T(8,128)} %get-tuple-element.411.refs_1_, f32[8,144,144]{2,1,0:T(8,128)} %get-tuple-element.412.refs_2_, f32[4,1,768]{2,1,0:T(1,128)} %get-tuple-element.413.refs_3_, f32[1,768]{1,0:T(1,128)} %get-tuple-element.414.refs_4_, ...), custom_call_target="tpu_custom_call" | custom-call | flops 6000000 | bytes 4194 | tf_op jit(solution)/shard_map/table/pallas_call | solution.py:72
  283.8 4.4 %collective-permute-done.33.refs_9_ = bf16[4,96,384]{2,1,0:T(8,128)(2,1)S(1)} collective-permute-done((bf16[4,96,384]{2,1,0:T(8,128)(2,1)}, bf16[4,96,384]{2,1,0:T(8,128)(2,1)S(1)}, u32[]{:S(2)}, u32[]{:S(2)}) %collective-permute-start.33) | collective-permute-done | bytes 294944 | tf_op jit(solution)/shard_map/ppermute | solution.py:785
  292.4 3.3 collective-permute-start.39
  299.1 3.6 collective-permute-done.38.refs_6_
  305.9 3.3 collective-permute-done.39.refs_8_
  315.4 18.5 %collective-permute-done.41.refs_4_ = f32[40,768]{1,0:T(8,128)S(1)} collective-permute-done((f32[40,768]{1,0:T(8,128)}, f32[40,768]{1,0:T(8,128)S(1)}, u32[]{:S(2)}, u32[]{:S(2)}) %collective-permute-start.41) | collective-permute-done | bytes 122912 | tf_op jit(solution)/shard_map/ppermute | solution.py:785
  338.9 3.6 collective-permute-start.43
  342.5 3.7 %collective-permute-done.43.refs_4_ = f32[40,768]{1,0:T(8,128)S(1)} collective-permute-done((f32[40,768]{1,0:T(8,128)}, f32[40,768]{1,0:T(8,128)S(1)}, u32[]{:S(2)}, u32[]{:S(2)}) %collective-permute-start.43) | collective-permute-done | bytes 122912 | tf_op jit(solution)/shard_map/ppermute | solution.py:785
  365.3 4.1 %feed_finish.1 = (f32[192,3072]{1,0:T(8,128)}, f32[768,768]{1,0:T(8,128)}) custom-call(s32[2]{0:T(128)} %pad_add_fusion.spot_ref.refs_0_, bf16[8,192,384]{2,1,0:T(8,128)(2,1)} %get-tuple-element.446.refs_1_, bf16[8,192,384]{2,1,0:T(8,128)(2,1)} %copy-done.15), custom_call_target="tpu_custom_call" | custom-call | flops 10000 | bytes 8388 | tf_op jit(solution)/shard_map/feed_finish/pallas_call | solution.py:72
  (221 shorter events, 95.9 us)
Async XLA Ops:
  4.8 12.9 %collective-permute-start.2 = (bf16[8,144,768]{2,1,0:T(8,128)(2,1)}, bf16[8,144,768]{2,1,0:T(8,128)(2,1)S(1)}, u32[]{:S(2)}, u32[]{:S(2)}) collective-permute-start(bf16[8,144,768]{2,1,0:T(8,128)(2,1)} %get-tuple-element.245), channel_id=1, source_target_pairs={{0,1},{1,0},{2,3},{3,2},{4,5},{5,4},{6,7},{7,6},{8,9},{9,8},{10,11... | collective-permute-start | bytes 5308424 | tf_op jit(solution)/shard_map/ppermute | solution.py:785
  5.3 10.9 %collective-permute-start.1 = (bf16[208,768]{1,0:T(8,128)(2,1)}, bf16[208,768]{1,0:T(8,128)(2,1)S(1)}, u32[]{:S(2)}, u32[]{:S(2)}) collective-permute-start(bf16[208,768]{1,0:T(8,128)(2,1)} %get-tuple-element.244.pa_ref.refs_4_), channel_id=1, source_target_pairs={{0,4},{2,6},{4,0},{6,2},{1,5},{3,7},{5,1},{7,3},{8,12},{10,14},{12... | collective-permute-start | bytes 958472 | tf_op jit(solution)/shard_map/ppermute | solution.py:785
  17.7 15.2 %collective-permute-start.3 = (bf16[208,768]{1,0:T(8,128)(2,1)S(1)}, bf16[208,768]{1,0:T(8,128)(2,1)S(1)}, u32[]{:S(2)}, u32[]{:S(2)}) collective-permute-start(bf16[208,768]{1,0:T(8,128)(2,1)S(1)} %collective-permute-done.pb_ref.refs_5_), channel_id=1, source_target_pairs={{0,4},{2,6},{4,0},{6,2},{1,5},{3,7},{5,1},{7,3},{8,12},{10,14},{12... | collective-permute-start | bytes 958472 | tf_op jit(solution)/shard_map/ppermute | solution.py:785
  18.1 14.8 %collective-permute-start.5 = (bf16[96,1536]{1,0:T(8,128)(2,1)S(1)}, bf16[96,1536]{1,0:T(8,128)(2,1)S(1)}, u32[]{:S(2)}, u32[]{:S(2)}) collective-permute-start(bf16[96,1536]{1,0:T(8,128)(2,1)S(1)} %copy-done.54), channel_id=1, source_target_pairs={{0,4},{2,6},{4,0},{6,2},{1,5},{3,7},{5,1},{7,3},{8,12},{10,14},{12... | collective-permute-start | bytes 884744 | tf_op jit(solution)/shard_map/ppermute | solution.py:785
  19.8 13.1 %collective-permute-start.4 = (bf16[96,1536]{1,0:T(8,128)(2,1)S(1)}, bf16[96,1536]{1,0:T(8,128)(2,1)S(1)}, u32[]{:S(2)}, u32[]{:S(2)}) collective-permute-start(bf16[96,1536]{1,0:T(8,128)(2,1)S(1)} %copy-done.54), channel_id=1, source_target_pairs={{0,2},{2,0},{4,6},{6,4},{1,3},{3,1},{5,7},{7,5},{8,10},{10,8},{12,... | collective-permute-start | bytes 884744 | tf_op jit(solution)/shard_map/ppermute | solution.py:785
  40.3 37.7 %collective-permute-start.11 = (bf16[864,768]{1,0:T(8,128)(2,1)}, bf16[864,768]{1,0:T(8,128)(2,1)S(1)}, u32[]{:S(2)}, u32[]{:S(2)}) collective-permute-start(bf16[864,768]{1,0:T(8,128)(2,1)} %cut.1), channel_id=1, source_target_pairs={{0,4},{2,6},{4,0},{6,2},{1,5},{3,7},{5,1},{7,3},{8,12},{10,14},{12... | collective-permute-start | bytes 3981320 | tf_op jit(solution)/shard_map/ppermute | solution.py:785
  41.3 36.8 %collective-permute-start.10 = (bf16[864,768]{1,0:T(8,128)(2,1)}, bf16[864,768]{1,0:T(8,128)(2,1)S(1)}, u32[]{:S(2)}, u32[]{:S(2)}) collective-permute-start(bf16[864,768]{1,0:T(8,128)(2,1)} %cut.1), channel_id=1, source_target_pairs={{0,2},{2,0},{4,6},{6,4},{1,3},{3,1},{5,7},{7,5},{8,10},{10,8},{12,... | collective-permute-start | bytes 3981320 | tf_op jit(solution)/shard_map/ppermute | solution.py:785
  42.6 14.0 %collective-permute-start.7 = (bf16[96,1536]{1,0:T(8,128)(2,1)S(1)}, bf16[96,1536]{1,0:T(8,128)(2,1)}, u32[]{:S(2)}, u32[]{:S(2)}) collective-permute-start(bf16[96,1536]{1,0:T(8,128)(2,1)S(1)} %collective-permute-done.4.refs_5_), channel_id=1, source_target_pairs={{0,1},{1,0},{2,3},{3,2},{4,5},{5,4},{6,7},{7,6},{8,9},{9,8},{10,11... | collective-permute-start | bytes 884744 | tf_op jit(solution)/shard_map/ppermute | solution.py:785
  42.6 14.0 %collective-permute-start.8 = (bf16[96,1536]{1,0:T(8,128)(2,1)S(1)}, bf16[96,1536]{1,0:T(8,128)(2,1)}, u32[]{:S(2)}, u32[]{:S(2)}) collective-permute-start(bf16[96,1536]{1,0:T(8,128)(2,1)S(1)} %collective-permute-done.5.refs_6_), channel_id=1, source_target_pairs={{0,1},{1,0},{2,3},{3,2},{4,5},{5,4},{6,7},{7,6},{8,9},{9,8},{10,11... | collective-permute-start | bytes 884744 | tf_op jit(solution)/shard_map/ppermute | solution.py:785
  43.1 13.5 %collective-permute-start.9 = (bf16[96,1536]{1,0:T(8,128)(2,1)S(1)}, bf16[96,1536]{1,0:T(8,128)(2,1)}, u32[]{:S(2)}, u32[]{:S(2)}) collective-permute-start(bf16[96,1536]{1,0:T(8,128)(2,1)S(1)} %collective-permute-done.6.refs_7_), channel_id=1, source_target_pairs={{0,1},{1,0},{2,3},{3,2},{4,5},{5,4},{6,7},{7,6},{8,9},{9,8},{10,11... | collective-permute-start | bytes 884744 | tf_op jit(solution)/shard_map/ppermute | solution.py:785
  78.1 20.7 %collective-permute-start.14 = (bf16[864,768]{1,0:T(8,128)(2,1)S(1)}, bf16[864,768]{1,0:T(8,128)(2,1)}, u32[]{:S(2)}, u32[]{:S(2)}) collective-permute-start(bf16[864,768]{1,0:T(8,128)(2,1)S(1)} %collective-permute-done.10.refs_13_), channel_id=1, source_target_pairs={{0,1},{1,0},{2,3},{3,2},{4,5},{5,4},{6,7},{7,6},{8,9},{9,8},{10,11... | collective-permute-start | bytes 3981320 | tf_op jit(solution)/shard_map/ppermute | solution.py:785
  78.7 20.1 %collective-permute-start.15 = (bf16[864,768]{1,0:T(8,128)(2,1)S(1)}, bf16[864,768]{1,0:T(8,128)(2,1)}, u32[]{:S(2)}, u32[]{:S(2)}) collective-permute-start(bf16[864,768]{1,0:T(8,128)(2,1)S(1)} %collective-permute-done.11.refs_14_), channel_id=1, source_target_pairs={{0,1},{1,0},{2,3},{3,2},{4,5},{5,4},{6,7},{7,6},{8,9},{9,8},{10,11... | collective-permute-start | bytes 3981320 | tf_op jit(solution)/shard_map/ppermute | solution.py:785
  80.7 17.5 %collective-permute-start.13 = (bf16[432,768]{1,0:T(8,128)(2,1)}, bf16[432,768]{1,0:T(8,128)(2,1)S(1)}, u32[]{:S(2)}, u32[]{:S(2)}) collective-permute-start(bf16[432,768]{1,0:T(8,128)(2,1)} %slice.31), channel_id=1, source_target_pairs={{0,2},{2,0},{4,6},{6,4},{1,3},{3,1},{5,7},{7,5},{8,10},{10,8},{12,... | collective-permute-start | bytes 1990664 | tf_op jit(solution)/shard_map/ppermute | solution.py:785
  81.4 17.4 %collective-permute-start.12 = (bf16[432,768]{1,0:T(8,128)(2,1)}, bf16[432,768]{1,0:T(8,128)(2,1)}, u32[]{:S(2)}, u32[]{:S(2)}) collective-permute-start(bf16[432,768]{1,0:T(8,128)(2,1)} %slice.30), channel_id=1, source_target_pairs={{0,4},{2,6},{4,0},{6,2},{1,5},{3,7},{5,1},{7,3},{8,12},{10,14},{12... | collective-permute-start | bytes 1990664 | tf_op jit(solution)/shard_map/ppermute | solution.py:785
  186.6 36.9 %collective-permute-start.22 = (bf16[2,4,192,384]{3,2,1,0:T(8,128)(2,1)S(1)}, bf16[2,4,192,384]{3,2,1,0:T(8,128)(2,1)S(1)}, u32[]{:S(2)}, u32[]{:S(2)}) collective-permute-start(bf16[2,4,192,384]{3,2,1,0:T(8,128)(2,1)S(1)} %get-tuple-element.483.refs_4_), channel_id=1, source_target_pairs={{0,4},{2,6},{4,0},{6,2},{1,5},{3,7},{5,1},{7,3},{8,12},{10,14},{12... | collective-permute-start | bytes 3538952 | tf_op jit(solution)/shard_map/ppermute | solution.py:785
  191.0 32.5 %collective-permute-start.21 = (bf16[2,4,192,384]{3,2,1,0:T(8,128)(2,1)S(1)}, bf16[2,4,192,384]{3,2,1,0:T(8,128)(2,1)}, u32[]{:S(2)}, u32[]{:S(2)}) collective-permute-start(bf16[2,4,192,384]{3,2,1,0:T(8,128)(2,1)S(1)} %get-tuple-element.485.refs_3_), channel_id=1, source_target_pairs={{0,2},{2,0},{4,6},{6,4},{1,3},{3,1},{5,7},{7,5},{8,10},{10,8},{12,... | collective-permute-start | bytes 3538952 | tf_op jit(solution)/shard_map/ppermute | solution.py:785
  223.4 21.1 %collective-permute-start.23 = (bf16[4,2,192,384]{3,2,1,0:T(8,128)(2,1)}, bf16[4,2,192,384]{3,2,1,0:T(8,128)(2,1)S(1)}, u32[]{:S(2)}, u32[]{:S(2)}) collective-permute-start(bf16[4,2,192,384]{3,2,1,0:T(8,128)(2,1)} %get-tuple-element.365), channel_id=1, source_target_pairs={{0,1},{1,0},{2,3},{3,2},{4,5},{5,4},{6,7},{7,6},{8,9},{9,8},{10,11... | collective-permute-start | bytes 3538952 | tf_op jit(solution)/shard_map/ppermute | solution.py:785
  223.5 21.0 %collective-permute-start.24 = (bf16[4,2,192,384]{3,2,1,0:T(8,128)(2,1)}, bf16[4,2,192,384]{3,2,1,0:T(8,128)(2,1)}, u32[]{:S(2)}, u32[]{:S(2)}) collective-permute-start(bf16[4,2,192,384]{3,2,1,0:T(8,128)(2,1)} %get-tuple-element.366), channel_id=1, source_target_pairs={{0,1},{1,0},{2,3},{3,2},{4,5},{5,4},{6,7},{7,6},{8,9},{9,8},{10,11... | collective-permute-start | bytes 3538952 | tf_op jit(solution)/shard_map/ppermute | solution.py:785
  228.5 15.5 %collective-permute-start.25 = (bf16[4,192,384]{2,1,0:T(8,128)(2,1)}, bf16[4,192,384]{2,1,0:T(8,128)(2,1)S(1)}, u32[]{:S(2)}, u32[]{:S(2)}) collective-permute-start(bf16[4,192,384]{2,1,0:T(8,128)(2,1)} %get-tuple-element.369.refs_10_), channel_id=1, source_target_pairs={{0,4},{2,6},{4,0},{6,2},{1,5},{3,7},{5,1},{7,3},{8,12},{10,14},{12... | collective-permute-start | bytes 1769480 | tf_op jit(solution)/shard_map/ppermute | solution.py:785
  229.3 15.2 %collective-permute-start.26 = (bf16[4,192,384]{2,1,0:T(8,128)(2,1)}, bf16[4,192,384]{2,1,0:T(8,128)(2,1)S(1)}, u32[]{:S(2)}, u32[]{:S(2)}) collective-permute-start(bf16[4,192,384]{2,1,0:T(8,128)(2,1)} %get-tuple-element.370.refs_11_), channel_id=1, source_target_pairs={{0,2},{2,0},{4,6},{6,4},{1,3},{3,1},{5,7},{7,5},{8,10},{10,8},{12,... | collective-permute-start | bytes 1769480 | tf_op jit(solution)/shard_map/ppermute | solution.py:785
  250.7 14.4 %collective-permute-start.27 = (bf16[2,2,192,384]{3,2,1,0:T(8,128)(2,1)}, bf16[2,2,192,384]{3,2,1,0:T(8,128)(2,1)S(1)}, u32[]{:S(2)}, u32[]{:S(2)}) collective-permute-start(bf16[2,2,192,384]{3,2,1,0:T(8,128)(2,1)} %get-tuple-element.384.refs_10_), channel_id=1, source_target_pairs={{0,2},{2,0},{4,6},{6,4},{1,3},{3,1},{5,7},{7,5},{8,10},{10,8},{12,... | collective-permute-start | bytes 1769480 | tf_op jit(solution)/shard_map/ppermute | solution.py:785
  251.7 14.1 %collective-permute-start.28 = (bf16[2,2,192,384]{3,2,1,0:T(8,128)(2,1)}, bf16[2,2,192,384]{3,2,1,0:T(8,128)(2,1)S(1)}, u32[]{:S(2)}, u32[]{:S(2)}) collective-permute-start(bf16[2,2,192,384]{3,2,1,0:T(8,128)(2,1)} %get-tuple-element.385.refs_11_), channel_id=1, source_target_pairs={{0,4},{2,6},{4,0},{6,2},{1,5},{3,7},{5,1},{7,3},{8,12},{10,14},{12... | collective-permute-start | bytes 1769480 | tf_op jit(solution)/shard_map/ppermute | solution.py:785
  253.0 13.8 %collective-permute-start.29 = (bf16[4,192,384]{2,1,0:T(8,128)(2,1)}, bf16[4,192,384]{2,1,0:T(8,128)(2,1)S(1)}, u32[]{:S(2)}, u32[]{:S(2)}) collective-permute-start(bf16[4,192,384]{2,1,0:T(8,128)(2,1)} %get-tuple-element.386.refs_12_), channel_id=1, source_target_pairs={{0,8},{8,0},{16,24},{24,16},{1,9},{9,1},{17,25},{25,17},{2,10},{10... | collective-permute-start | bytes 1769480 | tf_op jit(solution)/shard_map/ppermute | solution.py:785
  266.8 21.4 %collective-permute-start.34 = (bf16[2,144,768]{2,1,0:T(8,128)(2,1)}, bf16[2,144,768]{2,1,0:T(8,128)(2,1)S(1)}, u32[]{:S(2)}, u32[]{:S(2)}) collective-permute-start(bf16[2,144,768]{2,1,0:T(8,128)(2,1)} %get-tuple-element.399), channel_id=1, source_target_pairs={{0,1},{1,0},{2,3},{3,2},{4,5},{5,4},{6,7},{7,6},{8,9},{9,8},{10,11... | collective-permute-start | bytes 1327112 | tf_op jit(solution)/shard_map/ppermute | solution.py:785
  270.9 12.9 %collective-permute-start.31 = (bf16[2,192,384]{2,1,0:T(8,128)(2,1)}, bf16[2,192,384]{2,1,0:T(8,128)(2,1)S(1)}, u32[]{:S(2)}, u32[]{:S(2)}) collective-permute-start(bf16[2,192,384]{2,1,0:T(8,128)(2,1)} %get-tuple-element.396.refs_10_), channel_id=1, source_target_pairs={{0,4},{2,6},{4,0},{6,2},{1,5},{3,7},{5,1},{7,3},{8,12},{10,14},{12... | collective-permute-start | bytes 884744 | tf_op jit(solution)/shard_map/ppermute | solution.py:785
  271.7 12.1 %collective-permute-start.32 = (bf16[2,192,384]{2,1,0:T(8,128)(2,1)}, bf16[2,192,384]{2,1,0:T(8,128)(2,1)S(1)}, u32[]{:S(2)}, u32[]{:S(2)}) collective-permute-start(bf16[2,192,384]{2,1,0:T(8,128)(2,1)} %get-tuple-element.397.refs_11_), channel_id=1, source_target_pairs={{0,2},{2,0},{4,6},{6,4},{1,3},{3,1},{5,7},{7,5},{8,10},{10,8},{12,... | collective-permute-start | bytes 884744 | tf_op jit(solution)/shard_map/ppermute | solution.py:785
  272.7 15.5 %collective-permute-start.33 = (bf16[4,96,384]{2,1,0:T(8,128)(2,1)}, bf16[4,96,384]{2,1,0:T(8,128)(2,1)S(1)}, u32[]{:S(2)}, u32[]{:S(2)}) collective-permute-start(bf16[4,96,384]{2,1,0:T(8,128)(2,1)} %get-tuple-element.398.refs_12_), channel_id=1, source_target_pairs={{0,16},{8,24},{16,0},{24,8},{1,17},{9,25},{17,1},{25,9},{2,18},{10... | collective-permute-start | bytes 884744 | tf_op jit(solution)/shard_map/ppermute | solution.py:785
  291.6 14.3 %collective-permute-start.35 = (bf16[4,96,384]{2,1,0:T(8,128)(2,1)}, bf16[4,96,384]{2,1,0:T(8,128)(2,1)S(1)}, u32[]{:S(2)}, u32[]{:S(2)}) collective-permute-start(bf16[4,96,384]{2,1,0:T(8,128)(2,1)} %get-tuple-element.425), channel_id=1, source_target_pairs={{0,8},{8,0},{16,24},{24,16},{1,9},{9,1},{17,25},{25,17},{2,10},{10... | collective-permute-start | bytes 884744 | tf_op jit(solution)/shard_map/ppermute | solution.py:785
  292.4 16.8 %collective-permute-start.39 = (bf16[4,96,384]{2,1,0:T(8,128)(2,1)}, bf16[4,96,384]{2,1,0:T(8,128)(2,1)S(1)}, u32[]{:S(2)}, u32[]{:S(2)}) collective-permute-start(bf16[4,96,384]{2,1,0:T(8,128)(2,1)} %get-tuple-element.427.refs_7_), channel_id=1, source_target_pairs={{0,16},{8,24},{16,0},{24,8},{1,17},{9,25},{17,1},{25,9},{2,18},{10... | collective-permute-start | bytes 884744 | tf_op jit(solution)/shard_map/ppermute | solution.py:785
  312.3 21.5 %collective-permute-start.40 = (bf16[4,96,384]{2,1,0:T(8,128)(2,1)}, bf16[4,96,384]{2,1,0:T(8,128)(2,1)S(1)}, u32[]{:S(2)}, u32[]{:S(2)}) collective-permute-start(bf16[4,96,384]{2,1,0:T(8,128)(2,1)} %get-tuple-element.433.refs_1_), channel_id=1, source_target_pairs={{0,16},{8,24},{16,0},{24,8},{1,17},{9,25},{17,1},{25,9},{2,18},{10... | collective-permute-start | bytes 884744 | tf_op jit(solution)/shard_map/ppermute | solution.py:785
  312.4 34.9 %collective-permute-start.44 = (bf16[4,192,384]{2,1,0:T(8,128)(2,1)}, bf16[4,192,384]{2,1,0:T(8,128)(2,1)S(1)}, u32[]{:S(2)}, u32[]{:S(2)}) collective-permute-start(bf16[4,192,384]{2,1,0:T(8,128)(2,1)} %get-tuple-element.439.refs_5_), channel_id=1, source_target_pairs={{0,8},{8,0},{16,24},{24,16},{1,9},{9,1},{17,25},{25,17},{2,10},{10... | collective-permute-start | bytes 1769480 | tf_op jit(solution)/shard_map/ppermute | solution.py:785
  315.3 18.5 %collective-permute-start.41 = (f32[40,768]{1,0:T(8,128)}, f32[40,768]{1,0:T(8,128)S(1)}, u32[]{:S(2)}, u32[]{:S(2)}) collective-permute-start(f32[40,768]{1,0:T(8,128)} %get-tuple-element.434.refs_3_), channel_id=1, source_target_pairs={{0,8},{8,0},{16,24},{24,16},{1,9},{9,1},{17,25},{25,17},{2,10},{10... | collective-permute-start | bytes 368648 | tf_op jit(solution)/shard_map/ppermute | solution.py:785
  (72 other events, 539.6 us)

commit v5 on v4

--- a/solution.py
+++ b/solution.py
@@ -72,7 +72,7 @@
     return pl.pallas_call(body, in_specs=list(in_specs) + [any_space()] * len(after), **kw)(*args, *after)
 
 
-def params(limit=60):
+def params(limit=63):
     return pltpu.CompilerParams(vmem_limit_bytes=limit * MB)
 
 
@@ -695,16 +695,17 @@
     )
 
 
-def vector_finish_kernel(count, spot_ref, sums_ref, thr_ref, inner_ref, inb_ref, outb_ref, upb_ref, downb_ref, g1_ref, s1_ref,
-                         g2_ref, s2_ref, table_ref, clip_ref, factor_ref, max_ref):
+def vector_finish_kernel(count, spot_ref, mine_ref, other_ref, thr_ref, inner_ref, inb_ref, outb_ref, upb_ref, downb_ref, g1_ref, s1_ref,
+                         g2_ref, s2_ref, table_ref, clip_ref, factor_ref, max_ref, sums_ref):
     shard = spot_ref[2]
+    sums_ref[...] = join_vectors(mine_ref[...], other_ref[...])
 
     def part(ref, rows, step=1):
         size = ref.shape[0]
         start = shard * size
         row = sums_ref[pl.ds(rows + step * (start // D), 1), :]
         row = jnp.broadcast_to(row, (8, D))
-        ref[...] = pltpu.roll(row, D - start % D, 1)[0:1, :size].reshape(size)
+        ref[...] = pltpu.roll(row, (D - start % D) % D, 1)[0:1, :size].reshape(size)
 
     part(inb_ref, V_IN, 2)
     part(upb_ref, V_UP)
@@ -712,7 +713,7 @@
         part(ref, V_SMALL + i)
     part(g1_ref, V_ONE)
     part(s1_ref, V_ONE + 1)
-    table_ref[...] = sums_ref[V_TABLE : V_TABLE + HEADS, :WIDE].T[: SPAN * SPAN, :]
+    table_ref[...] = sums_ref[V_TABLE : V_TABLE + HEADS, : SPAN * SPAN]
     top = sums_ref[V_PEAK : V_PEAK + 1, :HEADS]
     factor = thr_ref[...].reshape(1, HEADS)
     factor = factor / jnp.maximum(top, factor)
@@ -728,12 +729,13 @@
     clip_ref[:, 2 * D :] = inner_ref[:, 2 * D :]
 
 
-def vector_finish(place, sums, threshold, inner, count):
+def vector_finish(place, mine, other, threshold, inner, count):
     line = SD((D // count,), F32)
     return single(
-        functools.partial(vector_finish_kernel, count), (place, sums, threshold, inner),
+        functools.partial(vector_finish_kernel, count), (place, mine, other, threshold, inner),
         [SD((2 * D // count,), F32), line, SD((FF // count,), F32), line, line, line, line, line,
-         SD((SPAN * SPAN, HEADS), F32), SD(inner.shape, BF), SD((HEADS,), F32), SD((HEADS,), F32)],
+         SD((HEADS, SPAN * SPAN), F32), SD(inner.shape, BF), SD((HEADS,), F32), SD((HEADS,), F32)],
+        scratch=[pltpu.VMEM((V_ROWS, D), F32)],
         cost_estimate=cost(1e7, 3 * MB), name="vector_finish",
     )
 
@@ -749,13 +751,6 @@
                     gr_ref[r : r + OWN, (b % 2) * CH : (b % 2 + 1) * CH] = ref[4 + b].astype(F32)
 
 
-def feed_finish(spot, mine, other):
-    return single(
-        feed_finish_kernel, (spot, mine, other), [SD((OWN, FF), F32), SD((2 * CH, D), F32)],
-        cost_estimate=cost(1e7, 8 * MB), name="feed_finish",
-    )
-
-
 def inner_columns(p, c):
     if c == 0:
         return [(0, LP, p * LP), (LP, LP // 2, D + p * LP)]
@@ -773,10 +768,21 @@
                 go_ref[:, c * CH : (c + 1) * CH] = ref[3].astype(F32)
 
 
-def inner_finish(spot, mine, other):
+def finish_kernel(count, place_ref, mine_ref, other_ref, thr_ref, inner_ref, fm_ref, fo_ref, im_ref, io_ref, *outs):
+    vectors, (ge_ref, gr_ref, gi_ref, go_ref, sums_ref) = outs[:12], outs[12:]
+    inner_finish_kernel(place_ref, im_ref, io_ref, gi_ref, go_ref)
+    feed_finish_kernel(place_ref, fm_ref, fo_ref, ge_ref, gr_ref)
+    vector_finish_kernel(count, place_ref, mine_ref, other_ref, thr_ref, inner_ref, *vectors, sums_ref)
+
+
+def finish(place, vectors, threshold, inner, feed, rest):
+    line = SD((D // 4,), F32)
     return single(
-        inner_finish_kernel, (spot, mine, other), [SD((OWN, 3 * D), F32), SD((OWN, D), F32)],
-        cost_estimate=cost(1e7, 4 * MB), name="inner_finish",
+        functools.partial(finish_kernel, 4), (place, *vectors, threshold, inner, *feed, *rest),
+        [SD((2 * D // 4,), F32), line, SD((FF // 4,), F32), line, line, line, line, line,
+         SD((HEADS, SPAN * SPAN), F32), SD(inner.shape, BF), SD((HEADS,), F32), SD((HEADS,), F32),
+         SD((OWN, FF), F32), SD((2 * CH, D), F32), SD((OWN, 3 * D), F32), SD((OWN, D), F32)],
+        scratch=[pltpu.VMEM((V_ROWS, D), F32)], cost_estimate=cost(1e7, 12 * MB), name="finish",
     )
 
 
@@ -794,7 +800,7 @@
     def __init__(self, sums, ones, direct):
         self.value = [sums, *ones]
         self.flying = []
-        self.hops = [("shard", (1, 2, 3)), ("replica", (1,)), ("replica", (2,)), ("half", (1,))]
+        self.hops = [("replica", (1,)), ("shard", (1, 2, 3)), ("replica", (2,)), ("half", (1,))]
         if not direct:
             self.hops = [
                 (axis, (1 << k,))
@@ -990,15 +996,15 @@
     if quick:
         others_back, results, spot = fence(others_back, results, spot)
     masks_1 = bias_call(1, spot, table_rows)
-    masks_2 = bias_call(2, spot, table_rows)
-    if quick:
-        masks_1, masks_2 = fence(masks_1, masks_2)
+    if quick:
+        masks_1, spot = fence(masks_1, spot)
         others_pieces = [others] + get_others + others_back
-    results.append(attend_call(1, n1, in_bias, masks_1, in_at, in_plans[1], others_pieces, [masks_2]))
-    if quick:
-        get_big, results, masks_2 = fence(get_big, results, masks_2)
+    results.append(attend_call(1, n1, in_bias, masks_1, in_at, in_plans[1], others_pieces, []))
+    if quick:
+        get_big, results, spot = fence(get_big, results, spot)
         far = [swap(get_big[0][: BIG // 2], "shard", 2), swap(get_big[1][BIG // 2 :], "shard", 1)]
         big_back = [swap(v, "half", 1) for v in get_big]
+    masks_2 = bias_call(2, spot, table_rows)
     results.append(attend_call(2, n1, in_bias, masks_2, in_at, in_plans[2], others_pieces, []))
     if quick:
         far, big_back, results = fence(far, big_back, results)
@@ -1055,7 +1061,7 @@
     lower_out = swap(send, "half", 1)
     gp0, db0 = back_call(0, projs[0], pts[0], datt, [])
     if quick:
-        gp0, lower_out, projs = together(place, [feed], gp0, lower_out, projs, plain=True)
+        gp0, lower_out, projs = together(place, [feed], gp0, lower_out, projs)
         after = wait_for([feed])
     gp1, db1 = back_call(1, projs[1], pts[1], datt, after)
     gp2, db2 = back_call(2, projs[2], pts[2], datt, [gp1])
@@ -1085,23 +1091,23 @@
     if quick:
         rest.flying, feed.flying, lower_b = fence(rest.flying, feed.flying, lower_b)
         together(place, [rest, every, feed])
-        together(place, [rest, every, feed])
-        together(place, [rest, every])
+        block_out = jnp.concatenate([lower_out, stay], axis=1)
+        (block_out,) = together(place, [rest, every, feed], block_out)
+        grad_images = jnp.concatenate([jnp.concatenate([lower_a, lower_b]), jnp.concatenate([gstay_a, gstay_b])], axis=1)
+        (grad_images,) = together(place, [rest, every], grad_images)
         rest.flying, every.flying, feed.flying = fence(rest.flying, every.flying, feed.flying)
         together(place, [rest, every, feed])
-        every.flying, feed.flying = fence(every.flying, feed.flying)
-        grad_expand, grad_reduce = feed_finish(spot, *feed.keep, *feed.flying)
-        together(place, [every])
     else:
-        while not every.done:
+        while every.hops:
             together(place, [every])
-    sums = every.value[0]
-
-    (grad_inbias, grad_outbias, grad_upbias, grad_downbias, grad_gain_1, grad_shift_1, grad_gain_2, grad_shift_2, grad_table,
-     clipped, factors, maxima) = vector_finish(place, sums, threshold, inner_weight, shard_count)
-
-    if quick:
-        grad_inner, grad_outer = inner_finish(spot, *rest.keep, *rest.flying)
+        block_out = jnp.concatenate([lower_out, stay], axis=1)
+        grad_images = jnp.concatenate([jnp.concatenate([lower_a, lower_b]), jnp.concatenate([gstay_a, gstay_b])], axis=1)
+
+    vectors = (every.value[0], every.flying[0])
+    if quick:
+        *vectors, grad_expand, grad_reduce, grad_inner, grad_outer = finish(
+            place, vectors, threshold, inner_weight, feed.keep + feed.flying, rest.keep + rest.flying
+        )
     else:
         def halves(keep, send, axis):
             lo = jnp.where(core == 0, keep, send)
@@ -1132,10 +1138,11 @@
         by_third = jnp.stack(by_third, axis=1).reshape(D, 3, 3, LP).transpose(0, 2, 1, 3).reshape(D, 3 * D)
         grad_inner = settle(by_third)
 
-    block_out = jnp.concatenate([lower_out, stay], axis=1).reshape(images.shape)
-    lower_grad = jnp.concatenate([lower_a, lower_b])
-    gstay = jnp.concatenate([gstay_a, gstay_b])
-    grad_images = jnp.concatenate([lower_grad, gstay], axis=1).reshape(images.shape)
+        vectors = vector_finish(place, *vectors, threshold, inner_weight, shard_count)
+    (grad_inbias, grad_outbias, grad_upbias, grad_downbias, grad_gain_1, grad_shift_1, grad_gain_2, grad_shift_2, grad_table,
+     clipped, factors, maxima) = vectors
+    block_out = block_out.reshape(images.shape)
+    grad_images = grad_images.reshape(images.shape)
     return (
         block_out,
         grad_images,
@@ -1151,7 +1158,7 @@
         grad_shift_1,
         grad_gain_2,
         grad_shift_2,
-        grad_table,
+        grad_table.T,
         clipped,
         factors,
         maxima,

time: 377 us -> 360 us (0.955)
  waiting for transfers between devices: 58.3 us -> 50.6 us
  local copies, waits for them, and re-layouts: 14.7 us -> 10 us
  other arithmetic: 13.1 us -> 8.9 us
    ppermute x48, waiting for transfers between devices: 58.3 us -> 50.6 us  [swap(): lax.ppermute(block, axis, [(i, i ^ bit) for i in range(count) if i ^ bit...]
    convert_element_type x2 -> x0, other arithmetic: 6.78 us -> none  [add(): return (a.astype(F32) + b.astype(F32)).astype(BF)]
    unnamed x113 -> x54, local copies, waits for them, and re-layouts: 11.5 us -> 4.82 us
    pallas_call x23 -> x21, Pallas kernels: 144 us -> 145 us  [run(): pl.pallas_call(body, in_specs=list(in_specs) + [any_space()] * len(after)...]
  transfers between devices with their start and end apart: 48 -> 48, of which waited for: 21 -> 21; matrix products, arithmetic and copies ran while one was open for 3% -> 4% of each run, Pallas kernels for 38% -> 39%
where the time goes in v5:
time: 360 us; the launch traced here: 355 us
  Pallas kernels  238 us (66%)
  waiting for transfers between devices  50.6 us (14%)
  starting transfers between devices  45.9 us (13%)
  local copies, waits for them, and re-layouts  10 us (3%)
  other arithmetic  8.9 us (2%)
    pallas_call x21, Pallas kernels, run(): pl.pallas_call(body, in_specs=list(in_specs) + [any_space()] * len(after)...  145 us
    pallas_call x1, Pallas kernels, middle_call(): pl.pallas_call(body, grid_spec=grid_spec, out_shape=[SD((n, TOK, D), BF),...  69.3 us
    ppermute x48, waiting for transfers between devices, swap(): lax.ppermute(block, axis, [(i, i ^ bit) for i in range(count) if i ^ bit...  50.6 us
    ppermute x48, starting transfers between devices, swap(): lax.ppermute(block, axis, [(i, i ^ bit) for i in range(count) if i ^ bit...  45.9 us
    pallas_call x3, Pallas kernels, bias_call(): pl.pallas_call(bias_kernel, grid=(1,), in_specs=[smem(), pl.BlockSpec((HP...  14.2 us
  transfers between devices with their start and end apart: 48, of which 21 were waited for; matrix products, arithmetic and copies ran while one was open for 4% of the time, Pallas kernels for 39%

profile of v5, /device:TPU:0, one launch (start us, length us, event | category | flops | bytes accessed | tf_op | source)
XLA Modules:
  0.0 354.6 jit_solution(5562056778294208205)
XLA Ops:
  1.2 3.5 first.1
  9.9 4.7 %bias.3.refs_2_ = f32[2,8,144,144]{3,2,1,0:T(8,128)} custom-call(s32[2]{0:T(128)} %pad_add_fusion.1.spot_ref.refs_0_, f32[24,640]{1,0:T(8,128)} %pad_convert_fusion.table_ref, bf16[2,2,144,144]{3,2,1,0:T(8,128)(2,1)} %constant.56.clone.mask_ref, bf16[384,144]{1,0:T(8,128)(2,1)} %constant.57.clone.sq_ref, bf16[144,192]{1,0:T(8,128)(2,1)} %constant.58.clone.sk_ref), custom_call_target="tpu_custom_call" | custom-call | flops 2000000 | bytes 3145 | tf_op jit(solution)/shard_map/bias/pallas_call | solution.py:167
  21.1 2.9 cut.1
  24.5 6.2 %prep.1 = (bf16[4,288,768]{2,1,0:T(8,128)(2,1)}, bf16[4,288,768]{2,1,0:T(8,128)(2,1)}, f32[1,768]{1,0:T(1,128)}) custom-call(bf16[4,288,768]{2,1,0:T(8,128)(2,1)} %bitcast.33, bf16[4,288,768]{2,1,0:T(8,128)(2,1)} %bitcast.35, bf16[8,144,768]{2,1,0:T(8,128)(2,1)} %collective-permute-done.2.refs_2_, f32[1,4]{1,0:T(1,128)} %convert_bitcast_fusion.refs_3_, ...), custom_call_target="tpu_custom_call" | custom-call | flops 3000000 | bytes 16777 | tf_op jit(solution)/shard_map/prep/pallas_call | solution.py:72
  34.3 5.5 %vectors.1 = (f32[3,1,768]{2,1,0:T(1,128)}, f32[4,1,768]{2,1,0:T(1,128)}, f32[8,768]{1,0:T(8,128)}, bf16[4,288,768]{2,1,0:T(8,128)(2,1)}, bf16[768,1152]{1,0:T(8,128)(2,1)}) custom-call(s32[2]{0:T(128)} %pad_add_fusion.1.spot_ref.refs_0_, bf16[208,768]{1,0:T(8,128)(2,1)} %get-tuple-element.248.pa_ref.refs_4_, bf16[208,768]{1,0:T(8,128)(2,1)} %copy-done.1, ...), custom_call_target="tpu_custom_call" | custom-call | flops 5000000 | bytes 8388 | tf_op jit(solution)/shard_map/vectors/pallas_call | solution.py:333
  44.4 12.3 %attend.3 = (bf16[4,288,768]{2,1,0:T(8,128)(2,1)}, bf16[4,2,8,144,144]{4,3,2,1,0:T(8,128)(2,1)}, bf16[4,288,256]{2,1,0:T(8,128)(2,1)}, f32[4,2,8,144]{3,2,1,0:T(8,128)}, bf16[768,768]{1,0:T(8,128)(2,1)}) custom-call(bf16[4,288,768]{2,1,0:T(8,128)(2,1)} %get-tuple-element.270.refs_0_, f32[3,1,768]{2,1,0:T(1,128)} %get-tuple-element.271.refs_1_, ...), custom_call_target="tpu_custom_call" | custom-call | flops 13000000 | bytes 12582 | tf_op jit(solution)/shard_map/attend/pallas_call | solution.py:72
  56.8 4.9 %bias.4.refs_2_ = f32[2,8,144,144]{3,2,1,0:T(8,128)} custom-call(s32[2]{0:T(128)} %pad_add_fusion.1.spot_ref.refs_0_, f32[24,640]{1,0:T(8,128)} %pad_convert_fusion.table_ref, bf16[2,2,144,144]{3,2,1,0:T(8,128)(2,1)} %constant.56.clone.mask_ref, bf16[384,144]{1,0:T(8,128)(2,1)} %constant.57.clone.sq_ref, bf16[144,192]{1,0:T(8,128)(2,1)} %constant.58.clone.sk_ref), custom_call_target="tpu_custom_call" | custom-call | flops 2000000 | bytes 3145 | tf_op jit(solution)/shard_map/bias/pallas_call | solution.py:167
  61.7 11.7 %attend.4 = (bf16[4,288,768]{2,1,0:T(8,128)(2,1)}, bf16[4,2,8,144,144]{4,3,2,1,0:T(8,128)(2,1)}, bf16[4,288,256]{2,1,0:T(8,128)(2,1)}, f32[4,2,8,144]{3,2,1,0:T(8,128)}, bf16[768,768]{1,0:T(8,128)(2,1)}) custom-call(bf16[4,288,768]{2,1,0:T(8,128)(2,1)} %get-tuple-element.270.refs_0_, f32[3,1,768]{2,1,0:T(1,128)} %get-tuple-element.271.refs_1_, ...), custom_call_target="tpu_custom_call" | custom-call | flops 13000000 | bytes 12582 | tf_op jit(solution)/shard_map/attend/pallas_call | solution.py:72
  79.8 4.7 %bias.5.refs_2_ = f32[2,8,144,144]{3,2,1,0:T(8,128)} custom-call(s32[2]{0:T(128)} %pad_add_fusion.1.spot_ref.refs_0_, f32[24,640]{1,0:T(8,128)} %pad_convert_fusion.table_ref, bf16[2,2,144,144]{3,2,1,0:T(8,128)(2,1)} %constant.56.clone.mask_ref, bf16[384,144]{1,0:T(8,128)(2,1)} %constant.57.clone.sq_ref, bf16[144,192]{1,0:T(8,128)(2,1)} %constant.58.clone.sk_ref), custom_call_target="tpu_custom_call" | custom-call | flops 2000000 | bytes 3145 | tf_op jit(solution)/shard_map/bias/pallas_call | solution.py:167
  84.5 12.3 %attend.5 = (bf16[4,288,768]{2,1,0:T(8,128)(2,1)}, bf16[4,2,8,144,144]{4,3,2,1,0:T(8,128)(2,1)}, bf16[4,288,256]{2,1,0:T(8,128)(2,1)}, f32[4,2,8,144]{3,2,1,0:T(8,128)}, bf16[768,768]{1,0:T(8,128)(2,1)}) custom-call(bf16[4,288,768]{2,1,0:T(8,128)(2,1)} %get-tuple-element.270.refs_0_, f32[3,1,768]{2,1,0:T(1,128)} %get-tuple-element.271.refs_1_, ...), custom_call_target="tpu_custom_call" | custom-call | flops 13000000 | bytes 12582 | tf_op jit(solution)/shard_map/attend/pallas_call | solution.py:72
  100.8 69.3 %middle.1 = (bf16[4,144,768]{2,1,0:T(8,128)(2,1)}, bf16[4,144,768]{2,1,0:T(8,128)(2,1)}, f32[4,288,768]{2,1,0:T(8,128)}, bf16[4,288,768]{2,1,0:T(8,128)(2,1)}, b...) custom-call(s32[2]{0:T(128)} %pad_add_fusion.1.spot_ref.refs_0_, ...), custom_call_target="tpu_custom_call" | custom-call | flops 60000000 | bytes 41943 | tf_op jit(solution)/shard_map/middle/pallas_call | solution.py:566
  171.4 9.3 %attend_back.3 = (bf16[4,288,768]{2,1,0:T(8,128)(2,1)}, f32[8,144,144]{2,1,0:T(8,128)}) custom-call(bf16[4,288,768]{2,1,0:T(8,128)(2,1)} %get-tuple-element.343.refs_0_, bf16[4,2,8,144,144]{4,3,2,1,0:T(8,128)(2,1)} %get-tuple-element.344.refs_1_, bf16[4,288,768]{2,1,0:T(8,128)(2,1)} %get-tuple-element.345.refs_2_), custom_call_target="tpu_custom_call" | custom-call | flops 18000000 | bytes 10485 | tf_op jit(solution)/shard_map/attend_back/pallas_call | solution.py:72
  180.8 6.6 %hop.8 = (bf16[2,4,192,384]{3,2,1,0:T(8,128)(2,1)}, bf16[2,4,192,384]{3,2,1,0:T(8,128)(2,1)}, bf16[2,4,192,384]{3,2,1,0:T(8,128)(2,1)}, bf16[2,4,192,384]{3,2,1,0:T(8,128)(2,1)}) custom-call(s32[4]{0:T(128)} %pad_add_fusion.refs_0_, bf16[4,4,192,384]{3,2,1,0:T(8,128)(2,1)} %get-tuple-element.353.refs_1_, ...), custom_call_target="tpu_custom_call" | custom-call | flops 10000 | bytes 4194 | tf_op jit(solution)/shard_map/hop/pallas_call | solution.py:72
  189.7 9.3 %attend_back.4 = (bf16[4,288,768]{2,1,0:T(8,128)(2,1)}, f32[8,144,144]{2,1,0:T(8,128)}) custom-call(bf16[4,288,768]{2,1,0:T(8,128)(2,1)} %get-tuple-element.351.refs_0_, bf16[4,2,8,144,144]{4,3,2,1,0:T(8,128)(2,1)} %get-tuple-element.352.refs_1_, bf16[4,288,768]{2,1,0:T(8,128)(2,1)} %get-tuple-element.345.refs_2_, ...), custom_call_target="tpu_custom_call" | custom-call | flops 18000000 | bytes 10485 | tf_op jit(solution)/shard_map/attend_back/pallas_call | solution.py:72
  199.1 9.3 %attend_back.5 = (bf16[4,288,768]{2,1,0:T(8,128)(2,1)}, f32[8,144,144]{2,1,0:T(8,128)}) custom-call(bf16[4,288,768]{2,1,0:T(8,128)(2,1)} %get-tuple-element.360.refs_0_, bf16[4,2,8,144,144]{4,3,2,1,0:T(8,128)(2,1)} %get-tuple-element.361.refs_1_, bf16[4,288,768]{2,1,0:T(8,128)(2,1)} %get-tuple-element.345.refs_2_, ...), custom_call_target="tpu_custom_call" | custom-call | flops 18000000 | bytes 10485 | tf_op jit(solution)/shard_map/attend_back/pallas_call | solution.py:72
  208.4 12.3 %inner_grad.1 = (bf16[4,2,192,384]{3,2,1,0:T(8,128)(2,1)}, bf16[4,2,192,384]{3,2,1,0:T(8,128)(2,1)}, bf16[4,2,192,384]{3,2,1,0:T(8,128)(2,1)}, bf16[4,2,192,384]{3,2,1,0:T(8,128)(2,1)}, f32[3,1,768]{2,1,0:T(1,128)}) custom-call(s32[2]{0:T(128)} %pad_add_fusion.1.spot_ref.refs_0_, bf16[768,1152]{1,0:T(8,128)(2,1)} %get-tuple-element.296.refs_1_, ...), custom_call_target="tpu_custom_call" | custom-call | flops 12000000 | bytes 12582 | tf_op jit(solution)/shard_map/inner_grad/pallas_call | solution.py:72
  221.3 3.9 %hop.9 = (bf16[4,192,384]{2,1,0:T(8,128)(2,1)}, bf16[4,192,384]{2,1,0:T(8,128)(2,1)}, bf16[4,192,384]{2,1,0:T(8,128)(2,1)}, bf16[4,192,384]{2,1,0:T(8,128)(2,1)}) custom-call(s32[4]{0:T(128)} %pad_add_fusion.refs_0_, bf16[2,4,192,384]{3,2,1,0:T(8,128)(2,1)} %get-tuple-element.371.refs_1_, bf16[2,4,192,384]{3,2,1,0:T(8,128)(2,1)} %get-tuple-element.372.refs_2_, ...), custom_call_target="tpu_custom_call" | custom-call | flops 10000 | bytes 4194 | tf_op jit(solution)/shard_map/hop/pallas_call | solution.py:72
  226.9 8.6 %last.2 = (f32[8,768]{1,0:T(8,128)}, bf16[2,144,768]{2,1,0:T(8,128)(2,1)}, bf16[2,144,768]{2,1,0:T(8,128)(2,1)}) custom-call(bf16[4,288,768]{2,1,0:T(8,128)(2,1)} %get-tuple-element.263.tok_ref.refs_1_.refs_0_, f32[4,288,768]{2,1,0:T(8,128)} %get-tuple-element.377.refs_1_, f32[8,768]{1,0:T(8,128)} %get-tuple-element.335.refs_7_.refs_2_, ...), custom_call_target="tpu_custom_call" | custom-call | flops 20000000 | bytes 20971 | tf_op jit(solution)/shard_map/last/pallas_call | solution.py:72
  235.4 5.3 %collective-permute-done.25.refs_7_ = bf16[4,192,384]{2,1,0:T(8,128)(2,1)S(1)} collective-permute-done((bf16[4,192,384]{2,1,0:T(8,128)(2,1)}, bf16[4,192,384]{2,1,0:T(8,128)(2,1)S(1)}, u32[]{:S(2)}, u32[]{:S(2)}) %collective-permute-start.25) | collective-permute-done | bytes 589856 | tf_op jit(solution)/shard_map/ppermute | solution.py:791
  241.7 5.0 %hop.10 = (bf16[2,2,192,384]{3,2,1,0:T(8,128)(2,1)}, bf16[2,2,192,384]{3,2,1,0:T(8,128)(2,1)}, bf16[2,2,192,384]{3,2,1,0:T(8,128)(2,1)}, bf16[2,2,192,384]{3,2,1...) custom-call(s32[4]{0:T(128)} %pad_add_fusion.refs_0_, ...), custom_call_target="tpu_custom_call" | custom-call | flops 10000 | bytes 4194 | tf_op jit(solution)/shard_map/hop/pallas_call | solution.py:72
  249.8 8.6 %last.3 = (f32[8,768]{1,0:T(8,128)}, bf16[2,144,768]{2,1,0:T(8,128)(2,1)}, bf16[2,144,768]{2,1,0:T(8,128)(2,1)}) custom-call(bf16[4,288,768]{2,1,0:T(8,128)(2,1)} %get-tuple-element.263.tok_ref.refs_1_.refs_0_, f32[4,288,768]{2,1,0:T(8,128)} %get-tuple-element.377.refs_1_, f32[8,768]{1,0:T(8,128)} %get-tuple-element.335.refs_7_.refs_2_, ...), custom_call_target="tpu_custom_call" | custom-call | flops 20000000 | bytes 20971 | tf_op jit(solution)/shard_map/last/pallas_call | solution.py:72
  258.4 2.9 collective-permute-done.27.refs_3_
  262.6 3.3 hop.11
  271.5 7.8 %table.1.refs_5_ = f32[40,768]{1,0:T(8,128)} custom-call(f32[8,144,144]{2,1,0:T(8,128)} %get-tuple-element.412.refs_0_, f32[8,144,144]{2,1,0:T(8,128)} %get-tuple-element.413.refs_1_, f32[8,144,144]{2,1,0:T(8,128)} %get-tuple-element.414.refs_2_, f32[4,1,768]{2,1,0:T(1,128)} %get-tuple-element.415.refs_3_, f32[1,768]{1,0:T(1,128)} %get-tuple-element.416.refs_4_, ...), custom_call_target="tpu_custom_call" | custom-call | flops 6000000 | bytes 4194 | tf_op jit(solution)/shard_map/table/pallas_call | solution.py:72
  279.3 5.3 %collective-permute-done.33.refs_9_ = bf16[4,96,384]{2,1,0:T(8,128)(2,1)} collective-permute-done((bf16[4,96,384]{2,1,0:T(8,128)(2,1)}, bf16[4,96,384]{2,1,0:T(8,128)(2,1)}, u32[]{:S(2)}, u32[]{:S(2)}) %collective-permute-start.33) | collective-permute-done | bytes 294944 | tf_op jit(solution)/shard_map/ppermute | solution.py:791
  287.8 3.4 collective-permute-start.37
  293.7 10.6 %collective-permute-done.36.refs_4_ = f32[40,768]{1,0:T(8,128)} collective-permute-done((f32[40,768]{1,0:T(8,128)}, f32[40,768]{1,0:T(8,128)}, u32[]{:S(2)}, u32[]{:S(2)}) %collective-permute-start.36) | collective-permute-done | bytes 122912 | tf_op jit(solution)/shard_map/ppermute | solution.py:791
  306.8 3.3 collective-permute-start.38
  326.8 3.3 collective-permute-start.43
  330.2 7.8 %collective-permute-done.43.refs_4_ = f32[40,768]{1,0:T(8,128)S(1)} collective-permute-done((f32[40,768]{1,0:T(8,128)}, f32[40,768]{1,0:T(8,128)S(1)}, u32[]{:S(2)}, u32[]{:S(2)}) %collective-permute-start.43) | collective-permute-done | bytes 122912 | tf_op jit(solution)/shard_map/ppermute | solution.py:791
  344.0 3.2 collective-permute-done.45.refs_2_
  348.0 6.3 %finish.1 = (f32[384]{0:T(512)}, f32[192]{0:T(256)}, f32[768]{0:T(1024)}, f32[192]{0:T(256)}, f32[192]{0:T(256)}, /*index=5*/f32[192]{0:T(256)}, f32[192]{0:T(25...) custom-call(s32[4]{0:T(128)} %pad_add_fusion.refs_0_, ...), custom_call_target="tpu_custom_call" | custom-call | flops 10000 | bytes 12582 | tf_op jit(solution)/shard_map/finish/pallas_call | solution.py:72
  (158 shorter events, 80.3 us)
Async XLA Ops:
  4.7 12.9 %collective-permute-start.2 = (bf16[8,144,768]{2,1,0:T(8,128)(2,1)}, bf16[8,144,768]{2,1,0:T(8,128)(2,1)}, u32[]{:S(2)}, u32[]{:S(2)}) collective-permute-start(bf16[8,144,768]{2,1,0:T(8,128)(2,1)} %get-tuple-element.249), channel_id=1, source_target_pairs={{0,1},{1,0},{2,3},{3,2},{4,5},{5,4},{6,7},{7,6},{8,9},{9,8},{10,11... | collective-permute-start | bytes 5308424 | tf_op jit(solution)/shard_map/ppermute | solution.py:791
  17.6 15.2 %collective-permute-start.3 = (bf16[208,768]{1,0:T(8,128)(2,1)S(1)}, bf16[208,768]{1,0:T(8,128)(2,1)S(1)}, u32[]{:S(2)}, u32[]{:S(2)}) collective-permute-start(bf16[208,768]{1,0:T(8,128)(2,1)S(1)} %collective-permute-done.pb_ref.refs_5_), channel_id=1, source_target_pairs={{0,4},{2,6},{4,0},{6,2},{1,5},{3,7},{5,1},{7,3},{8,12},{10,14},{12... | collective-permute-start | bytes 958472 | tf_op jit(solution)/shard_map/ppermute | solution.py:791
  17.9 14.8 %collective-permute-start.5 = (bf16[96,1536]{1,0:T(8,128)(2,1)}, bf16[96,1536]{1,0:T(8,128)(2,1)}, u32[]{:S(2)}, u32[]{:S(2)}) collective-permute-start(bf16[96,1536]{1,0:T(8,128)(2,1)} %get-tuple-element.254), channel_id=1, source_target_pairs={{0,4},{2,6},{4,0},{6,2},{1,5},{3,7},{5,1},{7,3},{8,12},{10,14},{12... | collective-permute-start | bytes 884744 | tf_op jit(solution)/shard_map/ppermute | solution.py:791
  19.6 13.2 %collective-permute-start.4 = (bf16[96,1536]{1,0:T(8,128)(2,1)}, bf16[96,1536]{1,0:T(8,128)(2,1)}, u32[]{:S(2)}, u32[]{:S(2)}) collective-permute-start(bf16[96,1536]{1,0:T(8,128)(2,1)} %get-tuple-element.254), channel_id=1, source_target_pairs={{0,2},{2,0},{4,6},{6,4},{1,3},{3,1},{5,7},{7,5},{8,10},{10,8},{12,... | collective-permute-start | bytes 884744 | tf_op jit(solution)/shard_map/ppermute | solution.py:791
  40.4 33.1 %collective-permute-start.8 = (bf16[864,768]{1,0:T(8,128)(2,1)}, bf16[864,768]{1,0:T(8,128)(2,1)}, u32[]{:S(2)}, u32[]{:S(2)}) collective-permute-start(bf16[864,768]{1,0:T(8,128)(2,1)} %cut.1), channel_id=1, source_target_pairs={{0,4},{2,6},{4,0},{6,2},{1,5},{3,7},{5,1},{7,3},{8,12},{10,14},{12... | collective-permute-start | bytes 3981320 | tf_op jit(solution)/shard_map/ppermute | solution.py:791
  41.4 32.1 %collective-permute-start.7 = (bf16[864,768]{1,0:T(8,128)(2,1)}, bf16[864,768]{1,0:T(8,128)(2,1)}, u32[]{:S(2)}, u32[]{:S(2)}) collective-permute-start(bf16[864,768]{1,0:T(8,128)(2,1)} %cut.1), channel_id=1, source_target_pairs={{0,2},{2,0},{4,6},{6,4},{1,3},{3,1},{5,7},{7,5},{8,10},{10,8},{12,... | collective-permute-start | bytes 3981320 | tf_op jit(solution)/shard_map/ppermute | solution.py:791
  42.7 14.1 %collective-permute-start.9 = (bf16[96,1536]{1,0:T(8,128)(2,1)}, bf16[96,1536]{1,0:T(8,128)(2,1)S(1)}, u32[]{:S(2)}, u32[]{:S(2)}) collective-permute-start(bf16[96,1536]{1,0:T(8,128)(2,1)} %collective-permute-done.4.refs_5_), channel_id=1, source_target_pairs={{0,1},{1,0},{2,3},{3,2},{4,5},{5,4},{6,7},{7,6},{8,9},{9,8},{10,11... | collective-permute-start | bytes 884744 | tf_op jit(solution)/shard_map/ppermute | solution.py:791
  42.7 14.1 %collective-permute-start.10 = (bf16[96,1536]{1,0:T(8,128)(2,1)}, bf16[96,1536]{1,0:T(8,128)(2,1)S(1)}, u32[]{:S(2)}, u32[]{:S(2)}) collective-permute-start(bf16[96,1536]{1,0:T(8,128)(2,1)} %collective-permute-done.5.refs_6_), channel_id=1, source_target_pairs={{0,1},{1,0},{2,3},{3,2},{4,5},{5,4},{6,7},{7,6},{8,9},{9,8},{10,11... | collective-permute-start | bytes 884744 | tf_op jit(solution)/shard_map/ppermute | solution.py:791
  43.2 13.6 %collective-permute-start.11 = (bf16[96,1536]{1,0:T(8,128)(2,1)S(1)}, bf16[96,1536]{1,0:T(8,128)(2,1)}, u32[]{:S(2)}, u32[]{:S(2)}) collective-permute-start(bf16[96,1536]{1,0:T(8,128)(2,1)S(1)} %collective-permute-done.6.refs_7_), channel_id=1, source_target_pairs={{0,1},{1,0},{2,3},{3,2},{4,5},{5,4},{6,7},{7,6},{8,9},{9,8},{10,11... | collective-permute-start | bytes 884744 | tf_op jit(solution)/shard_map/ppermute | solution.py:791
  73.5 23.3 %collective-permute-start.14 = (bf16[864,768]{1,0:T(8,128)(2,1)}, bf16[864,768]{1,0:T(8,128)(2,1)}, u32[]{:S(2)}, u32[]{:S(2)}) collective-permute-start(bf16[864,768]{1,0:T(8,128)(2,1)} %collective-permute-done.7.refs_13_), channel_id=1, source_target_pairs={{0,1},{1,0},{2,3},{3,2},{4,5},{5,4},{6,7},{7,6},{8,9},{9,8},{10,11... | collective-permute-start | bytes 3981320 | tf_op jit(solution)/shard_map/ppermute | solution.py:791
  74.0 22.8 %collective-permute-start.15 = (bf16[864,768]{1,0:T(8,128)(2,1)}, bf16[864,768]{1,0:T(8,128)(2,1)}, u32[]{:S(2)}, u32[]{:S(2)}) collective-permute-start(bf16[864,768]{1,0:T(8,128)(2,1)} %collective-permute-done.8.refs_14_), channel_id=1, source_target_pairs={{0,1},{1,0},{2,3},{3,2},{4,5},{5,4},{6,7},{7,6},{8,9},{9,8},{10,11... | collective-permute-start | bytes 3981320 | tf_op jit(solution)/shard_map/ppermute | solution.py:791
  78.1 18.7 %collective-permute-start.13 = (bf16[432,768]{1,0:T(8,128)(2,1)}, bf16[432,768]{1,0:T(8,128)(2,1)S(1)}, u32[]{:S(2)}, u32[]{:S(2)}) collective-permute-start(bf16[432,768]{1,0:T(8,128)(2,1)} %slice.7), channel_id=1, source_target_pairs={{0,2},{2,0},{4,6},{6,4},{1,3},{3,1},{5,7},{7,5},{8,10},{10,8},{12,... | collective-permute-start | bytes 1990664 | tf_op jit(solution)/shard_map/ppermute | solution.py:791
  78.8 18.0 %collective-permute-start.12 = (bf16[432,768]{1,0:T(8,128)(2,1)}, bf16[432,768]{1,0:T(8,128)(2,1)}, u32[]{:S(2)}, u32[]{:S(2)}) collective-permute-start(bf16[432,768]{1,0:T(8,128)(2,1)} %slice.6), channel_id=1, source_target_pairs={{0,4},{2,6},{4,0},{6,2},{1,5},{3,7},{5,1},{7,3},{8,12},{10,14},{12... | collective-permute-start | bytes 1990664 | tf_op jit(solution)/shard_map/ppermute | solution.py:791
  187.4 33.3 %collective-permute-start.21 = (bf16[2,4,192,384]{3,2,1,0:T(8,128)(2,1)}, bf16[2,4,192,384]{3,2,1,0:T(8,128)(2,1)}, u32[]{:S(2)}, u32[]{:S(2)}) collective-permute-start(bf16[2,4,192,384]{3,2,1,0:T(8,128)(2,1)} %get-tuple-element.357.refs_3_), channel_id=1, source_target_pairs={{0,2},{2,0},{4,6},{6,4},{1,3},{3,1},{5,7},{7,5},{8,10},{10,8},{12,... | collective-permute-start | bytes 3538952 | tf_op jit(solution)/shard_map/ppermute | solution.py:791
  188.9 31.8 %collective-permute-start.22 = (bf16[2,4,192,384]{3,2,1,0:T(8,128)(2,1)}, bf16[2,4,192,384]{3,2,1,0:T(8,128)(2,1)}, u32[]{:S(2)}, u32[]{:S(2)}) collective-permute-start(bf16[2,4,192,384]{3,2,1,0:T(8,128)(2,1)} %get-tuple-element.358.refs_4_), channel_id=1, source_target_pairs={{0,4},{2,6},{4,0},{6,2},{1,5},{3,7},{5,1},{7,3},{8,12},{10,14},{12... | collective-permute-start | bytes 3538952 | tf_op jit(solution)/shard_map/ppermute | solution.py:791
  220.7 21.0 %collective-permute-start.23 = (bf16[4,2,192,384]{3,2,1,0:T(8,128)(2,1)}, bf16[4,2,192,384]{3,2,1,0:T(8,128)(2,1)}, u32[]{:S(2)}, u32[]{:S(2)}) collective-permute-start(bf16[4,2,192,384]{3,2,1,0:T(8,128)(2,1)} %get-tuple-element.369), channel_id=1, source_target_pairs={{0,1},{1,0},{2,3},{3,2},{4,5},{5,4},{6,7},{7,6},{8,9},{9,8},{10,11... | collective-permute-start | bytes 3538952 | tf_op jit(solution)/shard_map/ppermute | solution.py:791
  220.8 20.9 %collective-permute-start.24 = (bf16[4,2,192,384]{3,2,1,0:T(8,128)(2,1)}, bf16[4,2,192,384]{3,2,1,0:T(8,128)(2,1)}, u32[]{:S(2)}, u32[]{:S(2)}) collective-permute-start(bf16[4,2,192,384]{3,2,1,0:T(8,128)(2,1)} %get-tuple-element.370), channel_id=1, source_target_pairs={{0,1},{1,0},{2,3},{3,2},{4,5},{5,4},{6,7},{7,6},{8,9},{9,8},{10,11... | collective-permute-start | bytes 3538952 | tf_op jit(solution)/shard_map/ppermute | solution.py:791
  225.2 15.5 %collective-permute-start.25 = (bf16[4,192,384]{2,1,0:T(8,128)(2,1)}, bf16[4,192,384]{2,1,0:T(8,128)(2,1)S(1)}, u32[]{:S(2)}, u32[]{:S(2)}) collective-permute-start(bf16[4,192,384]{2,1,0:T(8,128)(2,1)} %get-tuple-element.375.refs_10_), channel_id=1, source_target_pairs={{0,4},{2,6},{4,0},{6,2},{1,5},{3,7},{5,1},{7,3},{8,12},{10,14},{12... | collective-permute-start | bytes 1769480 | tf_op jit(solution)/shard_map/ppermute | solution.py:791
  226.3 15.3 %collective-permute-start.26 = (bf16[4,192,384]{2,1,0:T(8,128)(2,1)}, bf16[4,192,384]{2,1,0:T(8,128)(2,1)}, u32[]{:S(2)}, u32[]{:S(2)}) collective-permute-start(bf16[4,192,384]{2,1,0:T(8,128)(2,1)} %get-tuple-element.376.refs_11_), channel_id=1, source_target_pairs={{0,2},{2,0},{4,6},{6,4},{1,3},{3,1},{5,7},{7,5},{8,10},{10,8},{12,... | collective-permute-start | bytes 1769480 | tf_op jit(solution)/shard_map/ppermute | solution.py:791
  246.7 14.6 %collective-permute-start.27 = (bf16[2,2,192,384]{3,2,1,0:T(8,128)(2,1)}, bf16[2,2,192,384]{3,2,1,0:T(8,128)(2,1)S(1)}, u32[]{:S(2)}, u32[]{:S(2)}) collective-permute-start(bf16[2,2,192,384]{3,2,1,0:T(8,128)(2,1)} %get-tuple-element.392.refs_10_), channel_id=1, source_target_pairs={{0,2},{2,0},{4,6},{6,4},{1,3},{3,1},{5,7},{7,5},{8,10},{10,8},{12,... | collective-permute-start | bytes 1769480 | tf_op jit(solution)/shard_map/ppermute | solution.py:791
  247.2 14.6 %collective-permute-start.28 = (bf16[2,2,192,384]{3,2,1,0:T(8,128)(2,1)}, bf16[2,2,192,384]{3,2,1,0:T(8,128)(2,1)}, u32[]{:S(2)}, u32[]{:S(2)}) collective-permute-start(bf16[2,2,192,384]{3,2,1,0:T(8,128)(2,1)} %get-tuple-element.393.refs_11_), channel_id=1, source_target_pairs={{0,4},{2,6},{4,0},{6,2},{1,5},{3,7},{5,1},{7,3},{8,12},{10,14},{12... | collective-permute-start | bytes 1769480 | tf_op jit(solution)/shard_map/ppermute | solution.py:791
  248.3 14.3 %collective-permute-start.29 = (bf16[4,192,384]{2,1,0:T(8,128)(2,1)}, bf16[4,192,384]{2,1,0:T(8,128)(2,1)}, u32[]{:S(2)}, u32[]{:S(2)}) collective-permute-start(bf16[4,192,384]{2,1,0:T(8,128)(2,1)} %get-tuple-element.394.refs_12_), channel_id=1, source_target_pairs={{0,8},{8,0},{16,24},{24,16},{1,9},{9,1},{17,25},{25,17},{2,10},{10... | collective-permute-start | bytes 1769480 | tf_op jit(solution)/shard_map/ppermute | solution.py:791
  262.5 22.0 %collective-permute-start.34 = (bf16[2,144,768]{2,1,0:T(8,128)(2,1)}, bf16[2,144,768]{2,1,0:T(8,128)(2,1)}, u32[]{:S(2)}, u32[]{:S(2)}) collective-permute-start(bf16[2,144,768]{2,1,0:T(8,128)(2,1)} %get-tuple-element.406), channel_id=1, source_target_pairs={{0,1},{1,0},{2,3},{3,2},{4,5},{5,4},{6,7},{7,6},{8,9},{9,8},{10,11... | collective-permute-start | bytes 1327112 | tf_op jit(solution)/shard_map/ppermute | solution.py:791
  265.8 13.5 %collective-permute-start.31 = (bf16[2,192,384]{2,1,0:T(8,128)(2,1)}, bf16[2,192,384]{2,1,0:T(8,128)(2,1)}, u32[]{:S(2)}, u32[]{:S(2)}) collective-permute-start(bf16[2,192,384]{2,1,0:T(8,128)(2,1)} %get-tuple-element.403.refs_10_), channel_id=1, source_target_pairs={{0,4},{2,6},{4,0},{6,2},{1,5},{3,7},{5,1},{7,3},{8,12},{10,14},{12... | collective-permute-start | bytes 884744 | tf_op jit(solution)/shard_map/ppermute | solution.py:791
  266.9 12.4 %collective-permute-start.32 = (bf16[2,192,384]{2,1,0:T(8,128)(2,1)}, bf16[2,192,384]{2,1,0:T(8,128)(2,1)}, u32[]{:S(2)}, u32[]{:S(2)}) collective-permute-start(bf16[2,192,384]{2,1,0:T(8,128)(2,1)} %get-tuple-element.404.refs_11_), channel_id=1, source_target_pairs={{0,2},{2,0},{4,6},{6,4},{1,3},{3,1},{5,7},{7,5},{8,10},{10,8},{12,... | collective-permute-start | bytes 884744 | tf_op jit(solution)/shard_map/ppermute | solution.py:791
  268.2 16.4 %collective-permute-start.33 = (bf16[4,96,384]{2,1,0:T(8,128)(2,1)}, bf16[4,96,384]{2,1,0:T(8,128)(2,1)}, u32[]{:S(2)}, u32[]{:S(2)}) collective-permute-start(bf16[4,96,384]{2,1,0:T(8,128)(2,1)} %get-tuple-element.405.refs_12_), channel_id=1, source_target_pairs={{0,16},{8,24},{16,0},{24,8},{1,17},{9,25},{17,1},{25,9},{2,18},{10... | collective-permute-start | bytes 884744 | tf_op jit(solution)/shard_map/ppermute | solution.py:791
  287.2 17.2 %collective-permute-start.35 = (bf16[4,96,384]{2,1,0:T(8,128)(2,1)}, bf16[4,96,384]{2,1,0:T(8,128)(2,1)}, u32[]{:S(2)}, u32[]{:S(2)}) collective-permute-start(bf16[4,96,384]{2,1,0:T(8,128)(2,1)} %get-tuple-element.426), channel_id=1, source_target_pairs={{0,8},{8,0},{16,24},{24,16},{1,9},{9,1},{17,25},{25,17},{2,10},{10... | collective-permute-start | bytes 884744 | tf_op jit(solution)/shard_map/ppermute | solution.py:791
  287.8 16.6 %collective-permute-start.37 = (bf16[4,96,384]{2,1,0:T(8,128)(2,1)}, bf16[4,96,384]{2,1,0:T(8,128)(2,1)}, u32[]{:S(2)}, u32[]{:S(2)}) collective-permute-start(bf16[4,96,384]{2,1,0:T(8,128)(2,1)} %get-tuple-element.428.refs_5_), channel_id=1, source_target_pairs={{0,16},{8,24},{16,0},{24,8},{1,17},{9,25},{17,1},{25,9},{2,18},{10... | collective-permute-start | bytes 884744 | tf_op jit(solution)/shard_map/ppermute | solution.py:791
  291.2 13.1 %collective-permute-start.36 = (f32[40,768]{1,0:T(8,128)}, f32[40,768]{1,0:T(8,128)}, u32[]{:S(2)}, u32[]{:S(2)}) collective-permute-start(f32[40,768]{1,0:T(8,128)} %get-tuple-element.427.refs_3_), channel_id=1, source_target_pairs={{0,8},{8,0},{16,24},{24,16},{1,9},{9,1},{17,25},{25,17},{2,10},{10... | collective-permute-start | bytes 368648 | tf_op jit(solution)/shard_map/ppermute | solution.py:791
  306.8 16.6 %collective-permute-start.38 = (bf16[4,96,384]{2,1,0:T(8,128)(2,1)}, bf16[4,96,384]{2,1,0:T(8,128)(2,1)S(1)}, u32[]{:S(2)}, u32[]{:S(2)}) collective-permute-start(bf16[4,96,384]{2,1,0:T(8,128)(2,1)} %get-tuple-element.436.refs_1_), channel_id=1, source_target_pairs={{0,16},{8,24},{16,0},{24,8},{1,17},{9,25},{17,1},{25,9},{2,18},{10... | collective-permute-start | bytes 884744 | tf_op jit(solution)/shard_map/ppermute | solution.py:791
  310.1 29.0 %collective-permute-start.44 = (bf16[4,192,384]{2,1,0:T(8,128)(2,1)}, bf16[4,192,384]{2,1,0:T(8,128)(2,1)S(1)}, u32[]{:S(2)}, u32[]{:S(2)}) collective-permute-start(bf16[4,192,384]{2,1,0:T(8,128)(2,1)} %get-tuple-element.449.refs_5_), channel_id=1, source_target_pairs={{0,8},{8,0},{16,24},{24,16},{1,9},{9,1},{17,25},{25,17},{2,10},{10... | collective-permute-start | bytes 1769480 | tf_op jit(solution)/shard_map/ppermute | solution.py:791
  326.1 12.9 %collective-permute-start.42 = (bf16[4,96,384]{2,1,0:T(8,128)(2,1)}, bf16[4,96,384]{2,1,0:T(8,128)(2,1)S(1)}, u32[]{:S(2)}, u32[]{:S(2)}) collective-permute-start(bf16[4,96,384]{2,1,0:T(8,128)(2,1)} %get-tuple-element.447.refs_1_), channel_id=1, source_target_pairs={{0,8},{8,0},{16,24},{24,16},{1,9},{9,1},{17,25},{25,17},{2,10},{10... | collective-permute-start | bytes 884744 | tf_op jit(solution)/shard_map/ppermute | solution.py:791
  (43 other events, 233.1 us)

commit v6 on v5

--- a/solution.py
+++ b/solution.py
@@ -129,8 +129,9 @@
 
 
 def copies(plan, refs, at, targets, sems):
-    for i, (src, row, rows, col, cols, dst, put) in enumerate(plan):
-        place = pl.ds(pl.multiple_of(at[i], 16), rows)
+    base, entries = plan
+    for i, (src, row, rows, col, cols, dst, put) in enumerate(entries):
+        place = pl.ds(pl.multiple_of(at[base + i], 16), rows)
         yield pltpu.make_async_copy(
             refs[src].at[pl.ds(row, rows), pl.ds(col, cols)], targets[dst].at[place, pl.ds(put, cols)], sems.at[i]
         )
@@ -148,31 +149,28 @@
     return np.where(lab[:, :, :, None] != lab[:, :, None, :], MASKED, 0.0).astype(np.float32)
 
 
-def bias_kernel(spot_ref, table_ref, mask_ref, sq_ref, sk_ref, out_ref, tall):
-    masks = [mask_ref[spot_ref[1], w].astype(F32) for w in range(2)]
+def bias_kernel(table_ref, sq_ref, sk_ref, out_ref, tall):
     for h in range(HP):
         row = pltpu.roll(jnp.broadcast_to(table_ref[h : h + 1, :], (16, WIDE)), 0, 1, stride=1, stride_axis=0)
         for a in range(WIN):
             off = (SPAN * a - SPAN * (WIN - 1) - (WIN - 1)) % WIDE
             tall[16 * a : 16 * a + 16, :] = pltpu.roll(row, off, 1)[:, :NARROW].astype(BF)
         wide = nn(tall[...], sq_ref[...]).astype(BF)
-        bias = nn(sk_ref[...], wide)
-        for w in range(2):
-            out_ref[w, h] = (bias + masks[w]) * LOG2E
-
-
-def bias_call(group, spot, table):
-    args = (spot, table, jnp.asarray(region_masks(), BF), jnp.asarray(spread_q().T, BF), jnp.asarray(spread_k(False).T, BF))
-    out = SD((2, HP, TOK, TOK), F32)
+        out_ref[h] = nn(sk_ref[...], wide).astype(BF)
+
+
+def bias_call(group, table):
+    args = (table, jnp.asarray(spread_q().T, BF), jnp.asarray(spread_k(False).T, BF))
+    out = SD((HP, TOK, TOK), BF)
     return pl.pallas_call(
         bias_kernel,
         grid=(1,),
-        in_specs=[smem(), pl.BlockSpec((HP, WIDE), lambda i: (group, 0))] + [whole(v) for v in args[2:]],
+        in_specs=[pl.BlockSpec((HP, WIDE), lambda i: (group, 0))] + [whole(v) for v in args[1:]],
         out_specs=whole(out),
         out_shape=out,
         scratch_shapes=[pltpu.VMEM((TALL, NARROW), BF)],
         compiler_params=params(),
-        cost_estimate=cost(2e9, 3 * MB),
+        cost_estimate=cost(2e9, 2 * MB),
         name="bias",
     )(*args)
 
@@ -343,7 +341,7 @@
     )(spot, *parts, tok)
 
 
-def attend_kernel(plan, count, n1_ref, b_ref, bm_ref, at_ref, *rest):
+def attend_kernel(plan, count, spot_ref, n1_ref, b_ref, bias_ref, mask_ref, at_ref, *rest):
     pieces = rest[:count]
     proj_ref, pt_ref, att_ref, peak_ref, w_ref, sems = rest[count:]
 
@@ -359,6 +357,7 @@
     scale = HD**-0.5
     for w in range(2):
         r = slice(w * TOK, (w + 1) * TOK)
+        mask = mask_ref[spot_ref[1], w].astype(F32)
         for blk in range(LP // LB):
             l = blk * LB
             q = proj_ref[0, r, l : l + LB]
@@ -372,29 +371,31 @@
                 hh = blk * HB + h
                 st = sts[h * TOK : (h + 1) * TOK]
                 peak_ref[0, w, hh : hh + 1, :] = jnp.max(st, axis=0, keepdims=True) * scale
-                t = st * (scale * LOG2E) + bm_ref[w, hh]
-                e = jnp.exp2(t - jnp.max(t, axis=0, keepdims=True))
+                t = st * scale + (bias_ref[hh].astype(F32) + mask)
+                e = jnp.exp(t - jnp.max(t, axis=0, keepdims=True))
                 p = (e * (1.0 / colsum(e))).astype(BF)
                 pt_ref[0, w, hh] = p
                 outs.append(nn(vt[HD * h : HD * h + HD, :], p))
             att_ref[0, r, l : l + LB] = jnp.concatenate(outs, axis=0).astype(BF).T
 
 
-def attend_call(group, n1, b, bm, at, plan, pieces, after):
+def attend_call(group, spot, n1, b, bias, at, plan, pieces, after):
     n = n1.shape[0]
 
     def blk(*s):
         return pl.BlockSpec((1,) + s, lambda i: (i,) + (0,) * len(s))
 
     return run(
-        functools.partial(attend_kernel, plan, len(pieces)), 4 + len(pieces), (n1, b, bm, at, *pieces), after,
+        functools.partial(attend_kernel, plan, len(pieces)), 6 + len(pieces),
+        (spot, n1, b, bias, jnp.asarray(region_masks(), BF), at, *pieces), after,
         grid=(n,),
-        in_specs=[blk(ROWS, D), pl.BlockSpec((1, 1, 3 * LP), lambda i: (group, 0, 0)), full((2, HP, TOK, TOK), **ONE), smem()]
+        in_specs=[smem(), blk(ROWS, D), pl.BlockSpec((1, 1, 3 * LP), lambda i: (group, 0, 0)), full((HP, TOK, TOK), **ONE),
+                  full((2, 2, TOK, TOK), **ONE), smem()]
         + [any_space()] * len(pieces),
         out_specs=[blk(ROWS, 3 * LP), blk(2, HP, TOK, TOK), blk(ROWS, LP), blk(2, HP, TOK), full((D, 3 * LP), **ONE)],
         out_shape=[SD((n, ROWS, 3 * LP), BF), SD((n, 2, HP, TOK, TOK), BF), SD((n, ROWS, LP), BF), SD((n, 2, HP, TOK), F32),
                    SD((D, 3 * LP), BF)],
-        scratch_shapes=[pltpu.SemaphoreType.DMA((len(plan),))],
+        scratch_shapes=[pltpu.SemaphoreType.DMA((len(plan[1]),))],
         compiler_params=params(),
         cost_estimate=cost(1.3e10, 12 * MB, 1.4e6),
         name="attend",
@@ -422,7 +423,7 @@
     N = n * ROWS
     me = spot_ref[0]
     core = spot_ref[1]
-    early = [k for k, entry in enumerate(plan) if entry[5] == 0]
+    early = [k for k, entry in enumerate(plan[1]) if entry[5] == 0]
     out_b, red_b, gain, shift = vec_ref[0:1, :], vec_ref[1:2, :], vec_ref[3:4, :], vec_ref[4:5, :]
 
     def attended(i):
@@ -504,8 +505,8 @@
             gm = g[s, :].astype(F32) + r * (
                 d - jnp.mean(d, axis=-1, keepdims=True) - xh * jnp.mean(d * xh, axis=-1, keepdims=True)
             )
-            gmid_ref[i] = gm
             gb = gm.astype(BF)
+            gmid_ref[i] = gb
             ob = ob + colsum(gb.astype(F32))
             g[s, :] = gb
             datt_ref[i] = nt(gb, wo[...]).astype(BF)
@@ -561,12 +562,12 @@
         scratch_shapes=[pltpu.VMEM((D, D), BF), pltpu.VMEM((D, FF), BF), pltpu.VMEM((FF, D), BF),
                         pltpu.VMEM((N, D), F32), pltpu.VMEM((N, D), BF), pltpu.VMEM((N, D), BF), pltpu.VMEM((D, N), BF),
                         pltpu.VMEM((N, D), F32), pltpu.VMEM((N, D), F32), pltpu.VMEM((N, 2 * CH), BF), pltpu.VMEM((N, 2 * CH), BF),
-                        pltpu.SemaphoreType.DMA((len(plan),))],
+                        pltpu.SemaphoreType.DMA((len(plan[1]),))],
     )
     return pl.pallas_call(
         body,
         grid_spec=grid_spec,
-        out_shape=[SD((n, TOK, D), BF), SD((n, TOK, D), BF), SD((n, ROWS, D), F32), SD((n, ROWS, D), BF),
+        out_shape=[SD((n, TOK, D), BF), SD((n, TOK, D), BF), SD((n, ROWS, D), BF), SD((n, ROWS, D), BF),
                    SD((4, 1, OWN, CH), BF), SD((4, 1, OWN, CH), BF), blocks, blocks, blocks, blocks,
                    SD((4, 1, 2 * CH), F32), SD((8, D), F32)],
         compiler_params=params(62),
@@ -670,7 +671,7 @@
     small_ref[0:1, :] += colsum(d * xh)
     small_ref[1:2, :] += colsum(d)
     d = d * vec_ref[2:3, :]
-    gm = gmid_ref[0] + r * (d - jnp.mean(d, axis=-1, keepdims=True) - xh * jnp.mean(d * xh, axis=-1, keepdims=True))
+    gm = gmid_ref[0].astype(F32) + r * (d - jnp.mean(d, axis=-1, keepdims=True) - xh * jnp.mean(d * xh, axis=-1, keepdims=True))
     o = nn(pmt_ref[...], gm.astype(BF)).astype(BF)
     stay_ref[0] = o[:TOK]
     send_ref[0] = o[TOK:]
@@ -923,6 +924,87 @@
     return others
 
 
+def quick_layout(me, core):
+    def places(rows):
+        at = [me * rows]
+        for c in (core, 1 - core):
+            at += [(me ^ r) * rows + c * (rows // 2) for r in (1, 2, 3)]
+        return at
+
+    first = [(k, 0, OWN, 0, 3 * LP, 0, 0) for k in range(4)], [(me ^ r) * OWN for r in range(4)]
+    others = [
+        ([(k, 0, OWN if k == 0 else OWN // 2, c, 3 * LP, 0, 0) for k in range(7)], places(OWN)) for c in (0, 3 * LP)
+    ]
+    hlf = OWN // 2
+    short = places(OWN)
+    long = [None] + [c * 4 * CH + (me ^ r) * CH for c in (core, 1 - core) for r in (1, 2, 3)]
+    plan, at = [(0, 0, OWN, 0, D, 0, 0)], [short[0]]
+    for k in range(8):
+        plan.append((1, 0, OWN, hidden_block(k) * CH, CH, 1, k * CH))
+        at.append(short[0])
+    for c in range(2):
+        plan.append((2, c * CH, CH, 0, D, 2, 0))
+        at.append(c * 4 * CH + me * CH)
+    parts = [(b * hlf, hlf, 1, b * D) for b in range(4)] + [(4 * hlf, hlf, 0, 0), (5 * hlf, 4 * hlf, 2, 0)]
+
+    def add_piece(source, lo, hi, place):
+        for row, rows, target, column in parts:
+            a, b = max(row, lo), min(row + rows, hi)
+            if a < b and target == 1:
+                for c in range(2):
+                    plan.append((source, a - lo, b - a, c * CH, CH, 1, c * 4 * CH + column // 2))
+                    at.append(short[place] + (a - row))
+            elif a < b:
+                plan.append((source, a - lo, b - a, 0, D, target, column))
+                at.append((long if target == 2 else short)[place] + (a - row))
+
+    for side in range(2):
+        for k in range(2):
+            add_piece(3 + 4 * side + k, 0, BIG, 1 + 3 * side + k)
+        add_piece(5 + 4 * side, 0, BIG // 2, 3 + 3 * side)
+        add_piece(6 + 4 * side, BIG // 2, BIG, 3 + 3 * side)
+    return [first, *others, (plan, at)]
+
+
+def fallback_layout():
+    first = [([(0, 0, D, c, 3 * LP, 0, 0)], [0]) for c in (0, 0, 3 * LP)]
+    plan, at = [(0, 0, D, 0, D, 0, 0)], [0]
+    for k in range(8):
+        plan += [(1, 0, D, hidden_block(k) * CH, CH, 1, k * CH), (2, hidden_block(k) * CH, CH, 0, D, 2, 0)]
+        at += [0, k * CH]
+    return first + [(plan, at)]
+
+
+def plans_of(layout):
+    base, plans = 4, []
+    for entries, rows in layout:
+        plans.append((base, entries))
+        base += len(rows)
+    return plans
+
+
+def quick_plans():
+    return plans_of(quick_layout(0, 0))
+
+
+def fallback_plans():
+    return plans_of(fallback_layout())
+
+
+def fallback_places():
+    return [jnp.int32(v) for _, rows in fallback_layout() for v in rows]
+
+
+def index_table():
+    return np.array(
+        [
+            [me, core, me, replica] + [v for _, rows in quick_layout(me, core) for v in rows]
+            for replica in range(4) for me in range(4) for core in range(2)
+        ],
+        np.int32,
+    )
+
+
 def shards(images, cotangent, present, threshold, inner_weight, inner_bias, outer_weight, outer_bias, expand_weight,
            expand_bias, reduce_weight, reduce_bias, first_gain, first_shift, second_gain, second_shift, bias_table):
     n = images.shape[0]
@@ -932,8 +1014,11 @@
     shard_count = lax.axis_size("shard")
     quick = shard_count == 4 and lax.axis_size("replica") == 4
     me = shard if quick else jnp.int32(0)
-    spot = jnp.stack([me, core]).astype(jnp.int32)
-    place = jnp.stack([me, core, shard, replica]).astype(jnp.int32)
+    if quick:
+        spot = lax.dynamic_index_in_dim(jnp.asarray(index_table()), (replica * 4 + shard) * 2 + core, 0, False)
+    else:
+        spot = jnp.stack([me, core, shard, replica] + fallback_places()).astype(jnp.int32)
+    place = spot
     own_images = images.reshape(n, ROWS, D)
     own_grad = cotangent.reshape(n, ROWS, D)
     vectors = (inner_bias, outer_bias, expand_bias, reduce_bias, first_gain, first_shift, second_gain, second_shift)
@@ -946,12 +1031,12 @@
         first, up, spot, others_half = fence(first, up, spot, others_half)
         get_first = near(first)
         upper = swap(up, "half", 1)
-        masks_0 = bias_call(0, spot, table_rows)
-        get_first, upper, masks_0, others_half = fence(get_first, upper, masks_0, others_half)
+        masks_0 = bias_call(0, table_rows)
+        big = cut_call(spot, outer_weight, expand_weight, reduce_weight)
+        get_first, upper, masks_0, others_half, big = fence(get_first, upper, masks_0, others_half, big)
         get_first.append(swap(get_first[0], "shard", 2))
         get_others = near(others_half)
         tok, g, grad_down = prep_call(own_images, own_grad, upper, alive, order)
-        big = cut_call(spot, outer_weight, expand_weight, reduce_weight)
         get_first, get_others, tok, spot, big = fence(get_first, get_others, tok, spot, big)
         first_pieces = [first] + get_first
         get_others.append(swap(get_others[1], "shard", 1))
@@ -960,7 +1045,7 @@
         others_back = [swap(v, "half", 1) for v in get_others]
         get_big = near(big)
     else:
-        masks_0 = bias_call(0, spot, table_rows)
+        masks_0 = bias_call(0, table_rows)
         upper = jnp.concatenate([swap(own_images[:, :TOK], "half", 1), swap(own_grad[:, :TOK], "half", 1)])
         whole_vectors = [lax.all_gather(v, "shard", axis=0, tiled=True).reshape(4, -1) for v in vectors]
         parts = jnp.stack([jnp.pad(v, ((0, 0), (0, D - v.shape[1]))) for v in whole_vectors], axis=1)
@@ -973,81 +1058,38 @@
         in_bias, up_bias, vecs, n1, n1t = vector_call(spot, parts, tok)
 
     if quick:
-        def places(rows):
-            at = [me * rows]
-            for c in (core, 1 - core):
-                at += [(me ^ 1) * rows + c * (rows // 2), (me ^ 2) * rows + c * (rows // 2), (me ^ 3) * rows + c * (rows // 2)]
-            return at
-
-        first_at = jnp.stack([(me ^ r) * OWN for r in range(4)]).astype(jnp.int32)
-        in_at = jnp.stack(places(OWN)).astype(jnp.int32)
-
-        def in_plan(columns):
-            return [(k, 0, OWN if k == 0 else OWN // 2, columns, 3 * LP, 0, 0) for k in range(7)]
-
-        in_plans = [[(k, 0, OWN, 0, 3 * LP, 0, 0) for k in range(4)], in_plan(0), in_plan(3 * LP)]
+        first_at = in_at = spot
+        in_plans = quick_plans()[:3]
     else:
-        first_at = in_at = jnp.zeros((1,), jnp.int32)
+        first_at = in_at = spot
         first_pieces = [lax.all_gather(first, "shard", axis=0, tiled=True)]
         others_pieces = [lax.all_gather(others, "shard", axis=0, tiled=True)]
-        in_plans = [[(0, 0, D, k, 3 * LP, 0, 0)] for k in (0, 0, 3 * LP)]
-
-    results = [attend_call(0, n1, in_bias, masks_0, first_at, in_plans[0], first_pieces, [])]
-    if quick:
-        others_back, results, spot = fence(others_back, results, spot)
-    masks_1 = bias_call(1, spot, table_rows)
-    if quick:
-        masks_1, spot = fence(masks_1, spot)
+        in_plans = fallback_plans()[:3]
+
+    results = [attend_call(0, spot, n1, in_bias, masks_0, first_at, in_plans[0], first_pieces, [])]
+    if quick:
+        others_back, results, table_rows = fence(others_back, results, table_rows)
+    masks_1 = bias_call(1, table_rows)
+    if quick:
+        masks_1, spot, table_rows = fence(masks_1, spot, table_rows)
         others_pieces = [others] + get_others + others_back
-    results.append(attend_call(1, n1, in_bias, masks_1, in_at, in_plans[1], others_pieces, []))
-    if quick:
-        get_big, results, spot = fence(get_big, results, spot)
+    results.append(attend_call(1, spot, n1, in_bias, masks_1, in_at, in_plans[1], others_pieces, []))
+    if quick:
+        get_big, results, table_rows = fence(get_big, results, table_rows)
         far = [swap(get_big[0][: BIG // 2], "shard", 2), swap(get_big[1][BIG // 2 :], "shard", 1)]
         big_back = [swap(v, "half", 1) for v in get_big]
-    masks_2 = bias_call(2, spot, table_rows)
-    results.append(attend_call(2, n1, in_bias, masks_2, in_at, in_plans[2], others_pieces, []))
+    masks_2 = bias_call(2, table_rows)
+    results.append(attend_call(2, spot, n1, in_bias, masks_2, in_at, in_plans[2], others_pieces, []))
     if quick:
         far, big_back, results = fence(far, big_back, results)
         far_back = [swap(v, "half", 1) for v in far]
         far_back, results = fence(far_back, results)
         pieces = [outer_weight, expand_weight, reduce_weight] + get_big + far + big_back + far_back
-        hlf = OWN // 2
-        plan = [(0, 0, OWN, 0, D, 0, 0)]
-        short = places(OWN)
-        long = [None] + [c * 4 * CH + (me ^ r) * CH for c in (core, 1 - core) for r in (1, 2, 3)]
-        at = [short[0]]
-        for k in range(8):
-            plan.append((1, 0, OWN, hidden_block(k) * CH, CH, 1, k * CH))
-            at.append(short[0])
-        for c in range(2):
-            plan.append((2, c * CH, CH, 0, D, 2, 0))
-            at.append(c * 4 * CH + me * CH)
-        parts = [(b * hlf, hlf, 1, b * D) for b in range(4)] + [(4 * hlf, hlf, 0, 0), (5 * hlf, 4 * hlf, 2, 0)]
-
-        def add_piece(source, lo, hi, place):
-            for row, rows, target, column in parts:
-                a, b = max(row, lo), min(row + rows, hi)
-                if a < b and target == 1:
-                    for c in range(2):
-                        plan.append((source, a - lo, b - a, c * CH, CH, 1, c * 4 * CH + column // 2))
-                        at.append(short[place] + (a - row))
-                elif a < b:
-                    plan.append((source, a - lo, b - a, 0, D, target, column))
-                    at.append((long if target == 2 else short)[place] + (a - row))
-
-        for side in range(2):
-            for k in range(2):
-                add_piece(3 + 4 * side + k, 0, BIG, 1 + 3 * side + k)
-            add_piece(5 + 4 * side, 0, BIG // 2, 3 + 3 * side)
-            add_piece(6 + 4 * side, BIG // 2, BIG, 3 + 3 * side)
-        at = jnp.stack(at).astype(jnp.int32)
+        plan = quick_plans()[3]
     else:
         pieces = [lax.all_gather(v, "shard", axis=0, tiled=True) for v in (outer_weight, expand_weight, reduce_weight)]
-        plan, at = [(0, 0, D, 0, D, 0, 0)], [0]
-        for k in range(8):
-            plan += [(1, 0, D, hidden_block(k) * CH, CH, 1, k * CH), (2, hidden_block(k) * CH, CH, 0, D, 2, 0)]
-            at += [0, k * CH]
-        at = jnp.asarray(at, jnp.int32)
+        plan = fallback_plans()[3]
+    at = spot
     projs, pts, atts, peak, ws = zip(*results)
     (stay, send, gmid, datt, out_send, out_keep, e_send, e_keep, r_send, r_keep, grad_up, small) = middle_call(
         spot, tok, atts, g, back_order, vecs, up_bias, at, plan, pieces, []

time: 360 us -> 358 us (level)
  transfers between devices with their start and end apart: 48 -> 48, of which waited for: 21 -> 20; matrix products, arithmetic and copies ran while one was open for 4% -> 3% of each run, Pallas kernels for 39% -> 39%
where the time goes in v6:
time: 358 us; the launch traced here: 352 us
  Pallas kernels  235 us (66%)
  waiting for transfers between devices  52.6 us (15%)
  starting transfers between devices  45.9 us (13%)
  local copies, waits for them, and re-layouts  9.96 us (3%)
  other arithmetic  7.08 us (2%)
    pallas_call x21, Pallas kernels, run(): pl.pallas_call(body, in_specs=list(in_specs) + [any_space()] * len(after)...  146 us
    pallas_call x1, Pallas kernels, middle_call(): pl.pallas_call(body, grid_spec=grid_spec, out_shape=[SD((n, TOK, D), BF),...  68.6 us
    ppermute x48, waiting for transfers between devices, swap(): lax.ppermute(block, axis, [(i, i ^ bit) for i in range(count) if i ^ bit...  52.6 us
    ppermute x48, starting transfers between devices, swap(): lax.ppermute(block, axis, [(i, i ^ bit) for i in range(count) if i ^ bit...  45.9 us
    pallas_call x3, Pallas kernels, bias_call(): pl.pallas_call(bias_kernel, grid=(1,), in_specs=[pl.BlockSpec((HP, WIDE),...  12.1 us
  transfers between devices with their start and end apart: 48, of which 20 were waited for; matrix products, arithmetic and copies ran while one was open for 3% of the time, Pallas kernels for 39%

profile of v6, /device:TPU:0, one launch (start us, length us, event | category | flops | bytes accessed | tf_op | source)
XLA Modules:
  0.0 352.1 jit_solution(7488477960980926035)
XLA Ops:
  1.9 3.5 first.1
  13.5 4.0 %bias.3.refs_3_ = bf16[8,144,144]{2,1,0:T(8,128)(2,1)} custom-call(f32[24,640]{1,0:T(8,128)} %pad_convert_fusion.table_ref, bf16[384,144]{1,0:T(8,128)(2,1)} %constant.49.clone.sq_ref, bf16[144,192]{1,0:T(8,128)(2,1)} %constant.50.clone.sk_ref), custom_call_target="tpu_custom_call" | custom-call | flops 2000000 | bytes 2097 | tf_op jit(solution)/shard_map/bias/pallas_call | solution.py:165
  22.3 6.2 %prep.1 = (bf16[4,288,768]{2,1,0:T(8,128)(2,1)}, bf16[4,288,768]{2,1,0:T(8,128)(2,1)}, f32[1,768]{1,0:T(1,128)}) custom-call(bf16[4,288,768]{2,1,0:T(8,128)(2,1)} %bitcast.12, bf16[4,288,768]{2,1,0:T(8,128)(2,1)} %bitcast.14, bf16[8,144,768]{2,1,0:T(8,128)(2,1)} %collective-permute-done.2.refs_2_, f32[1,4]{1,0:T(1,128)} %convert_bitcast_fusion.refs_3_, ...), custom_call_target="tpu_custom_call" | custom-call | flops 3000000 | bytes 16777 | tf_op jit(solution)/shard_map/prep/pallas_call | solution.py:72
  28.5 5.0 %collective-permute-done.5.refs_8_ = bf16[96,1536]{1,0:T(8,128)(2,1)} collective-permute-done((bf16[96,1536]{1,0:T(8,128)(2,1)}, bf16[96,1536]{1,0:T(8,128)(2,1)}, u32[]{:S(2)}, u32[]{:S(2)}) %collective-permute-start.5) | collective-permute-done | bytes 294944 | tf_op jit(solution)/shard_map/ppermute | solution.py:792
  35.1 5.5 %vectors.1 = (f32[3,1,768]{2,1,0:T(1,128)}, f32[4,1,768]{2,1,0:T(1,128)}, f32[8,768]{1,0:T(8,128)}, bf16[4,288,768]{2,1,0:T(8,128)(2,1)}, bf16[768,1152]{1,0:T(8,128)(2,1)}) custom-call(s32[95]{0:T(128)} %dynamic-slice_bitcast_fusion.spot_ref.refs_0_.refs_5_.refs_9_, bf16[208,768]{1,0:T(8,128)(2,1)} %get-tuple-element.250.pa_ref.refs_6_, ...), custom_call_target="tpu_custom_call" | custom-call | flops 5000000 | bytes 8388 | tf_op jit(solution)/shard_map/vectors/pallas_call | solution.py:331
  44.0 12.5 %attend.3 = (bf16[4,288,768]{2,1,0:T(8,128)(2,1)}, bf16[4,2,8,144,144]{4,3,2,1,0:T(8,128)(2,1)}, bf16[4,288,256]{2,1,0:T(8,128)(2,1)}, f32[4,2,8,144]{3,2,1,0:T(8,128)}, bf16[768,768]{1,0:T(8,128)(2,1)}) custom-call(s32[95]{0:T(128)} %dynamic-slice_bitcast_fusion.spot_ref.refs_0_.refs_5_.refs_9_, bf16[4,288,768]{2,1,0:T(8,128)(2,1)} %get-tuple-element.272.refs_1_, ...), custom_call_target="tpu_custom_call" | custom-call | flops 13000000 | bytes 12582 | tf_op jit(solution)/shard_map/attend/pallas_call | solution.py:72
  56.6 4.2 %bias.4.refs_3_ = bf16[8,144,144]{2,1,0:T(8,128)(2,1)} custom-call(f32[24,640]{1,0:T(8,128)} %pad_convert_fusion.table_ref, bf16[384,144]{1,0:T(8,128)(2,1)} %constant.49.clone.sq_ref, bf16[144,192]{1,0:T(8,128)(2,1)} %constant.50.clone.sk_ref), custom_call_target="tpu_custom_call" | custom-call | flops 2000000 | bytes 2097 | tf_op jit(solution)/shard_map/bias/pallas_call | solution.py:165
  60.7 12.4 %attend.4 = (bf16[4,288,768]{2,1,0:T(8,128)(2,1)}, bf16[4,2,8,144,144]{4,3,2,1,0:T(8,128)(2,1)}, bf16[4,288,256]{2,1,0:T(8,128)(2,1)}, f32[4,2,8,144]{3,2,1,0:T(8,128)}, bf16[768,768]{1,0:T(8,128)(2,1)}) custom-call(s32[95]{0:T(128)} %dynamic-slice_bitcast_fusion.spot_ref.refs_0_.refs_5_.refs_9_, bf16[4,288,768]{2,1,0:T(8,128)(2,1)} %get-tuple-element.272.refs_1_, ...), custom_call_target="tpu_custom_call" | custom-call | flops 13000000 | bytes 12582 | tf_op jit(solution)/shard_map/attend/pallas_call | solution.py:72
  79.4 4.0 %bias.5.refs_3_ = bf16[8,144,144]{2,1,0:T(8,128)(2,1)} custom-call(f32[24,640]{1,0:T(8,128)} %pad_convert_fusion.table_ref, bf16[384,144]{1,0:T(8,128)(2,1)} %constant.49.clone.sq_ref, bf16[144,192]{1,0:T(8,128)(2,1)} %constant.50.clone.sk_ref), custom_call_target="tpu_custom_call" | custom-call | flops 2000000 | bytes 2097 | tf_op jit(solution)/shard_map/bias/pallas_call | solution.py:165
  83.4 12.4 %attend.5 = (bf16[4,288,768]{2,1,0:T(8,128)(2,1)}, bf16[4,2,8,144,144]{4,3,2,1,0:T(8,128)(2,1)}, bf16[4,288,256]{2,1,0:T(8,128)(2,1)}, f32[4,2,8,144]{3,2,1,0:T(8,128)}, bf16[768,768]{1,0:T(8,128)(2,1)}) custom-call(s32[95]{0:T(128)} %dynamic-slice_bitcast_fusion.spot_ref.refs_0_.refs_5_.refs_9_, bf16[4,288,768]{2,1,0:T(8,128)(2,1)} %get-tuple-element.272.refs_1_, ...), custom_call_target="tpu_custom_call" | custom-call | flops 13000000 | bytes 12582 | tf_op jit(solution)/shard_map/attend/pallas_call | solution.py:72
  99.8 68.6 %middle.1 = (bf16[4,144,768]{2,1,0:T(8,128)(2,1)}, bf16[4,144,768]{2,1,0:T(8,128)(2,1)}, bf16[4,288,768]{2,1,0:T(8,128)(2,1)}, bf16[4,288,768]{2,1,0:T(8,128)(2,...) custom-call(s32[95]{0:T(128)} %dynamic-slice_bitcast_fusion.spot_ref, ...), custom_call_target="tpu_custom_call" | custom-call | flops 60000000 | bytes 41943 | tf_op jit(solution)/shard_map/middle/pallas_call | solution.py:567
  169.1 9.3 %attend_back.3 = (bf16[4,288,768]{2,1,0:T(8,128)(2,1)}, f32[8,144,144]{2,1,0:T(8,128)}) custom-call(bf16[4,288,768]{2,1,0:T(8,128)(2,1)} %get-tuple-element.347.refs_0_, bf16[4,2,8,144,144]{4,3,2,1,0:T(8,128)(2,1)} %get-tuple-element.348.refs_1_, bf16[4,288,768]{2,1,0:T(8,128)(2,1)} %get-tuple-element.349.refs_2_), custom_call_target="tpu_custom_call" | custom-call | flops 18000000 | bytes 10485 | tf_op jit(solution)/shard_map/attend_back/pallas_call | solution.py:72
  178.5 6.5 %hop.8 = (bf16[2,4,192,384]{3,2,1,0:T(8,128)(2,1)}, bf16[2,4,192,384]{3,2,1,0:T(8,128)(2,1)}, bf16[2,4,192,384]{3,2,1,0:T(8,128)(2,1)}, bf16[2,4,192,384]{3,2,1,0:T(8,128)(2,1)}) custom-call(s32[95]{0:T(128)} %dynamic-slice_bitcast_fusion.spot_ref.refs_0_.refs_5_.refs_9_, bf16[4,4,192,384]{3,2,1,0:T(8,128)(2,1)} %get-tuple-element.357.refs_1_, ...), custom_call_target="tpu_custom_call" | custom-call | flops 10000 | bytes 4194 | tf_op jit(solution)/shard_map/hop/pallas_call | solution.py:72
  187.3 9.3 %attend_back.4 = (bf16[4,288,768]{2,1,0:T(8,128)(2,1)}, f32[8,144,144]{2,1,0:T(8,128)}) custom-call(bf16[4,288,768]{2,1,0:T(8,128)(2,1)} %get-tuple-element.355.refs_0_, bf16[4,2,8,144,144]{4,3,2,1,0:T(8,128)(2,1)} %get-tuple-element.356.refs_1_, bf16[4,288,768]{2,1,0:T(8,128)(2,1)} %get-tuple-element.349.refs_2_, ...), custom_call_target="tpu_custom_call" | custom-call | flops 18000000 | bytes 10485 | tf_op jit(solution)/shard_map/attend_back/pallas_call | solution.py:72
  196.7 9.3 %attend_back.5 = (bf16[4,288,768]{2,1,0:T(8,128)(2,1)}, f32[8,144,144]{2,1,0:T(8,128)}) custom-call(bf16[4,288,768]{2,1,0:T(8,128)(2,1)} %get-tuple-element.364.refs_0_, bf16[4,2,8,144,144]{4,3,2,1,0:T(8,128)(2,1)} %get-tuple-element.365.refs_1_, bf16[4,288,768]{2,1,0:T(8,128)(2,1)} %get-tuple-element.349.refs_2_, ...), custom_call_target="tpu_custom_call" | custom-call | flops 18000000 | bytes 10485 | tf_op jit(solution)/shard_map/attend_back/pallas_call | solution.py:72
  206.0 12.2 %inner_grad.1 = (bf16[4,2,192,384]{3,2,1,0:T(8,128)(2,1)}, bf16[4,2,192,384]{3,2,1,0:T(8,128)(2,1)}, bf16[4,2,192,384]{3,2,1,0:T(8,128)(2,1)}, bf16[4,2,192,384]{3,2,1,0:T(8,128)(2,1)}, f32[3,1,768]{2,1,0:T(1,128)}) custom-call(s32[95]{0:T(128)} %dynamic-slice_bitcast_fusion.spot_ref.refs_0_.refs_5_.refs_9_, bf16[768,1152]{1,0:T(8,128)(2,1)} %get-tuple-element.282.refs_1_, ...), custom_call_target="tpu_custom_call" | custom-call | flops 12000000 | bytes 12582 | tf_op jit(solution)/shard_map/inner_grad/pallas_call | solution.py:72
  218.8 3.9 %hop.9 = (bf16[4,192,384]{2,1,0:T(8,128)(2,1)}, bf16[4,192,384]{2,1,0:T(8,128)(2,1)}, bf16[4,192,384]{2,1,0:T(8,128)(2,1)}, bf16[4,192,384]{2,1,0:T(8,128)(2,1)}) custom-call(s32[95]{0:T(128)} %dynamic-slice_bitcast_fusion.spot_ref.refs_0_.refs_5_.refs_9_, bf16[2,4,192,384]{3,2,1,0:T(8,128)(2,1)} %get-tuple-element.375.refs_1_, ...), custom_call_target="tpu_custom_call" | custom-call | flops 10000 | bytes 4194 | tf_op jit(solution)/shard_map/hop/pallas_call | solution.py:72
  224.5 8.3 %last.2 = (f32[8,768]{1,0:T(8,128)}, bf16[2,144,768]{2,1,0:T(8,128)(2,1)}, bf16[2,144,768]{2,1,0:T(8,128)(2,1)}) custom-call(bf16[4,288,768]{2,1,0:T(8,128)(2,1)} %get-tuple-element.266.tok_ref.refs_1_.refs_0_, bf16[4,288,768]{2,1,0:T(8,128)(2,1)} %get-tuple-element.381.refs_1_, f32[8,768]{1,0:T(8,128)} %get-tuple-element.339.refs_7_.refs_2_, ...), custom_call_target="tpu_custom_call" | custom-call | flops 20000000 | bytes 20971 | tf_op jit(solution)/shard_map/last/pallas_call | solution.py:72
  232.7 5.5 %collective-permute-done.25.refs_7_ = bf16[4,192,384]{2,1,0:T(8,128)(2,1)S(1)} collective-permute-done((bf16[4,192,384]{2,1,0:T(8,128)(2,1)}, bf16[4,192,384]{2,1,0:T(8,128)(2,1)S(1)}, u32[]{:S(2)}, u32[]{:S(2)}) %collective-permute-start.25) | collective-permute-done | bytes 589856 | tf_op jit(solution)/shard_map/ppermute | solution.py:792
  239.3 5.0 %hop.10 = (bf16[2,2,192,384]{3,2,1,0:T(8,128)(2,1)}, bf16[2,2,192,384]{3,2,1,0:T(8,128)(2,1)}, bf16[2,2,192,384]{3,2,1,0:T(8,128)(2,1)}, bf16[2,2,192,384]{3,2,1...) custom-call(s32[95]{0:T(128)} %dynamic-slice_bitcast_fusion.spot_ref.refs_0_.refs_5_.refs_9_, ...), custom_call_target="tpu_custom_call" | custom-call | flops 10000 | bytes 4194 | tf_op jit(solution)/shard_map/hop/pallas_call | solution.py:72
  247.3 8.3 %last.3 = (f32[8,768]{1,0:T(8,128)}, bf16[2,144,768]{2,1,0:T(8,128)(2,1)}, bf16[2,144,768]{2,1,0:T(8,128)(2,1)}) custom-call(bf16[4,288,768]{2,1,0:T(8,128)(2,1)} %get-tuple-element.266.tok_ref.refs_1_.refs_0_, bf16[4,288,768]{2,1,0:T(8,128)(2,1)} %get-tuple-element.381.refs_1_, f32[8,768]{1,0:T(8,128)} %get-tuple-element.339.refs_7_.refs_2_, ...), custom_call_target="tpu_custom_call" | custom-call | flops 20000000 | bytes 20971 | tf_op jit(solution)/shard_map/last/pallas_call | solution.py:72
  255.6 3.2 collective-permute-done.27.refs_3_
  260.1 3.3 hop.11
  269.1 7.8 %table.1.refs_5_ = f32[40,768]{1,0:T(8,128)} custom-call(f32[8,144,144]{2,1,0:T(8,128)} %get-tuple-element.416.refs_0_, f32[8,144,144]{2,1,0:T(8,128)} %get-tuple-element.417.refs_1_, f32[8,144,144]{2,1,0:T(8,128)} %get-tuple-element.418.refs_2_, f32[4,1,768]{2,1,0:T(1,128)} %get-tuple-element.419.refs_3_, f32[1,768]{1,0:T(1,128)} %get-tuple-element.420.refs_4_, ...), custom_call_target="tpu_custom_call" | custom-call | flops 6000000 | bytes 4194 | tf_op jit(solution)/shard_map/table/pallas_call | solution.py:72
  276.9 5.2 %collective-permute-done.33.refs_9_ = bf16[4,96,384]{2,1,0:T(8,128)(2,1)} collective-permute-done((bf16[4,96,384]{2,1,0:T(8,128)(2,1)}, bf16[4,96,384]{2,1,0:T(8,128)(2,1)}, u32[]{:S(2)}, u32[]{:S(2)}) %collective-permute-start.33) | collective-permute-done | bytes 294944 | tf_op jit(solution)/shard_map/ppermute | solution.py:792
  285.4 3.4 collective-permute-start.37
  291.3 10.6 %collective-permute-done.36.refs_4_ = f32[40,768]{1,0:T(8,128)} collective-permute-done((f32[40,768]{1,0:T(8,128)}, f32[40,768]{1,0:T(8,128)}, u32[]{:S(2)}, u32[]{:S(2)}) %collective-permute-start.36) | collective-permute-done | bytes 122912 | tf_op jit(solution)/shard_map/ppermute | solution.py:792
  304.4 3.3 collective-permute-start.38
  324.4 3.3 collective-permute-start.43
  327.7 7.8 %collective-permute-done.43.refs_4_ = f32[40,768]{1,0:T(8,128)S(1)} collective-permute-done((f32[40,768]{1,0:T(8,128)}, f32[40,768]{1,0:T(8,128)S(1)}, u32[]{:S(2)}, u32[]{:S(2)}) %collective-permute-start.43) | collective-permute-done | bytes 122912 | tf_op jit(solution)/shard_map/ppermute | solution.py:792
  341.5 3.2 collective-permute-done.45.refs_2_
  345.6 6.3 %finish.1 = (f32[384]{0:T(512)}, f32[192]{0:T(256)}, f32[768]{0:T(1024)}, f32[192]{0:T(256)}, f32[192]{0:T(256)}, /*index=5*/f32[192]{0:T(256)}, f32[192]{0:T(25...) custom-call(s32[95]{0:T(128)} %dynamic-slice_bitcast_fusion.spot_ref, ...), custom_call_target="tpu_custom_call" | custom-call | flops 10000 | bytes 12582 | tf_op jit(solution)/shard_map/finish/pallas_call | solution.py:72
  (154 shorter events, 77.9 us)
Async XLA Ops:
  5.4 12.9 %collective-permute-start.2 = (bf16[8,144,768]{2,1,0:T(8,128)(2,1)}, bf16[8,144,768]{2,1,0:T(8,128)(2,1)}, u32[]{:S(2)}, u32[]{:S(2)}) collective-permute-start(bf16[8,144,768]{2,1,0:T(8,128)(2,1)} %get-tuple-element.251), channel_id=1, source_target_pairs={{0,1},{1,0},{2,3},{3,2},{4,5},{5,4},{6,7},{7,6},{8,9},{9,8},{10,11... | collective-permute-start | bytes 5308424 | tf_op jit(solution)/shard_map/ppermute | solution.py:792
  18.3 15.2 %collective-permute-start.3 = (bf16[208,768]{1,0:T(8,128)(2,1)S(1)}, bf16[208,768]{1,0:T(8,128)(2,1)S(1)}, u32[]{:S(2)}, u32[]{:S(2)}) collective-permute-start(bf16[208,768]{1,0:T(8,128)(2,1)S(1)} %collective-permute-done.pb_ref.refs_7_), channel_id=1, source_target_pairs={{0,4},{2,6},{4,0},{6,2},{1,5},{3,7},{5,1},{7,3},{8,12},{10,14},{12... | collective-permute-start | bytes 958472 | tf_op jit(solution)/shard_map/ppermute | solution.py:792
  18.6 14.8 %collective-permute-start.5 = (bf16[96,1536]{1,0:T(8,128)(2,1)}, bf16[96,1536]{1,0:T(8,128)(2,1)}, u32[]{:S(2)}, u32[]{:S(2)}) collective-permute-start(bf16[96,1536]{1,0:T(8,128)(2,1)} %get-tuple-element.256), channel_id=1, source_target_pairs={{0,4},{2,6},{4,0},{6,2},{1,5},{3,7},{5,1},{7,3},{8,12},{10,14},{12... | collective-permute-start | bytes 884744 | tf_op jit(solution)/shard_map/ppermute | solution.py:792
  20.3 13.2 %collective-permute-start.4 = (bf16[96,1536]{1,0:T(8,128)(2,1)}, bf16[96,1536]{1,0:T(8,128)(2,1)}, u32[]{:S(2)}, u32[]{:S(2)}) collective-permute-start(bf16[96,1536]{1,0:T(8,128)(2,1)} %get-tuple-element.256), channel_id=1, source_target_pairs={{0,2},{2,0},{4,6},{6,4},{1,3},{3,1},{5,7},{7,5},{8,10},{10,8},{12,... | collective-permute-start | bytes 884744 | tf_op jit(solution)/shard_map/ppermute | solution.py:792
  41.1 32.0 %collective-permute-start.11 = (bf16[864,768]{1,0:T(8,128)(2,1)}, bf16[864,768]{1,0:T(8,128)(2,1)}, u32[]{:S(2)}, u32[]{:S(2)}) collective-permute-start(bf16[864,768]{1,0:T(8,128)(2,1)} %cut.1), channel_id=1, source_target_pairs={{0,4},{2,6},{4,0},{6,2},{1,5},{3,7},{5,1},{7,3},{8,12},{10,14},{12... | collective-permute-start | bytes 3981320 | tf_op jit(solution)/shard_map/ppermute | solution.py:792
  42.1 31.0 %collective-permute-start.10 = (bf16[864,768]{1,0:T(8,128)(2,1)}, bf16[864,768]{1,0:T(8,128)(2,1)}, u32[]{:S(2)}, u32[]{:S(2)}) collective-permute-start(bf16[864,768]{1,0:T(8,128)(2,1)} %cut.1), channel_id=1, source_target_pairs={{0,2},{2,0},{4,6},{6,4},{1,3},{3,1},{5,7},{7,5},{8,10},{10,8},{12,... | collective-permute-start | bytes 3981320 | tf_op jit(solution)/shard_map/ppermute | solution.py:792
  43.5 13.0 %collective-permute-start.7 = (bf16[96,1536]{1,0:T(8,128)(2,1)}, bf16[96,1536]{1,0:T(8,128)(2,1)S(1)}, u32[]{:S(2)}, u32[]{:S(2)}) collective-permute-start(bf16[96,1536]{1,0:T(8,128)(2,1)} %collective-permute-done.4.refs_7_), channel_id=1, source_target_pairs={{0,1},{1,0},{2,3},{3,2},{4,5},{5,4},{6,7},{7,6},{8,9},{9,8},{10,11... | collective-permute-start | bytes 884744 | tf_op jit(solution)/shard_map/ppermute | solution.py:792
  43.5 13.1 %collective-permute-start.8 = (bf16[96,1536]{1,0:T(8,128)(2,1)}, bf16[96,1536]{1,0:T(8,128)(2,1)S(1)}, u32[]{:S(2)}, u32[]{:S(2)}) collective-permute-start(bf16[96,1536]{1,0:T(8,128)(2,1)} %collective-permute-done.5.refs_8_), channel_id=1, source_target_pairs={{0,1},{1,0},{2,3},{3,2},{4,5},{5,4},{6,7},{7,6},{8,9},{9,8},{10,11... | collective-permute-start | bytes 884744 | tf_op jit(solution)/shard_map/ppermute | solution.py:792
  44.0 12.6 %collective-permute-start.9 = (bf16[96,1536]{1,0:T(8,128)(2,1)S(1)}, bf16[96,1536]{1,0:T(8,128)(2,1)}, u32[]{:S(2)}, u32[]{:S(2)}) collective-permute-start(bf16[96,1536]{1,0:T(8,128)(2,1)S(1)} %collective-permute-done.6.refs_9_), channel_id=1, source_target_pairs={{0,1},{1,0},{2,3},{3,2},{4,5},{5,4},{6,7},{7,6},{8,9},{9,8},{10,11... | collective-permute-start | bytes 884744 | tf_op jit(solution)/shard_map/ppermute | solution.py:792
  73.1 22.7 %collective-permute-start.14 = (bf16[864,768]{1,0:T(8,128)(2,1)}, bf16[864,768]{1,0:T(8,128)(2,1)}, u32[]{:S(2)}, u32[]{:S(2)}) collective-permute-start(bf16[864,768]{1,0:T(8,128)(2,1)} %collective-permute-done.10.refs_13_), channel_id=1, source_target_pairs={{0,1},{1,0},{2,3},{3,2},{4,5},{5,4},{6,7},{7,6},{8,9},{9,8},{10,11... | collective-permute-start | bytes 3981320 | tf_op jit(solution)/shard_map/ppermute | solution.py:792
  73.7 22.1 %collective-permute-start.15 = (bf16[864,768]{1,0:T(8,128)(2,1)}, bf16[864,768]{1,0:T(8,128)(2,1)}, u32[]{:S(2)}, u32[]{:S(2)}) collective-permute-start(bf16[864,768]{1,0:T(8,128)(2,1)} %collective-permute-done.11.refs_14_), channel_id=1, source_target_pairs={{0,1},{1,0},{2,3},{3,2},{4,5},{5,4},{6,7},{7,6},{8,9},{9,8},{10,11... | collective-permute-start | bytes 3981320 | tf_op jit(solution)/shard_map/ppermute | solution.py:792
  77.7 18.1 %collective-permute-start.13 = (bf16[432,768]{1,0:T(8,128)(2,1)}, bf16[432,768]{1,0:T(8,128)(2,1)S(1)}, u32[]{:S(2)}, u32[]{:S(2)}) collective-permute-start(bf16[432,768]{1,0:T(8,128)(2,1)} %slice.7), channel_id=1, source_target_pairs={{0,2},{2,0},{4,6},{6,4},{1,3},{3,1},{5,7},{7,5},{8,10},{10,8},{12,... | collective-permute-start | bytes 1990664 | tf_op jit(solution)/shard_map/ppermute | solution.py:792
  78.4 17.4 %collective-permute-start.12 = (bf16[432,768]{1,0:T(8,128)(2,1)}, bf16[432,768]{1,0:T(8,128)(2,1)}, u32[]{:S(2)}, u32[]{:S(2)}) collective-permute-start(bf16[432,768]{1,0:T(8,128)(2,1)} %slice.6), channel_id=1, source_target_pairs={{0,4},{2,6},{4,0},{6,2},{1,5},{3,7},{5,1},{7,3},{8,12},{10,14},{12... | collective-permute-start | bytes 1990664 | tf_op jit(solution)/shard_map/ppermute | solution.py:792
  185.0 33.2 %collective-permute-start.21 = (bf16[2,4,192,384]{3,2,1,0:T(8,128)(2,1)}, bf16[2,4,192,384]{3,2,1,0:T(8,128)(2,1)}, u32[]{:S(2)}, u32[]{:S(2)}) collective-permute-start(bf16[2,4,192,384]{3,2,1,0:T(8,128)(2,1)} %get-tuple-element.361.refs_3_), channel_id=1, source_target_pairs={{0,2},{2,0},{4,6},{6,4},{1,3},{3,1},{5,7},{7,5},{8,10},{10,8},{12,... | collective-permute-start | bytes 3538952 | tf_op jit(solution)/shard_map/ppermute | solution.py:792
  186.5 31.7 %collective-permute-start.22 = (bf16[2,4,192,384]{3,2,1,0:T(8,128)(2,1)}, bf16[2,4,192,384]{3,2,1,0:T(8,128)(2,1)}, u32[]{:S(2)}, u32[]{:S(2)}) collective-permute-start(bf16[2,4,192,384]{3,2,1,0:T(8,128)(2,1)} %get-tuple-element.362.refs_4_), channel_id=1, source_target_pairs={{0,4},{2,6},{4,0},{6,2},{1,5},{3,7},{5,1},{7,3},{8,12},{10,14},{12... | collective-permute-start | bytes 3538952 | tf_op jit(solution)/shard_map/ppermute | solution.py:792
  218.2 21.0 %collective-permute-start.23 = (bf16[4,2,192,384]{3,2,1,0:T(8,128)(2,1)}, bf16[4,2,192,384]{3,2,1,0:T(8,128)(2,1)}, u32[]{:S(2)}, u32[]{:S(2)}) collective-permute-start(bf16[4,2,192,384]{3,2,1,0:T(8,128)(2,1)} %get-tuple-element.373), channel_id=1, source_target_pairs={{0,1},{1,0},{2,3},{3,2},{4,5},{5,4},{6,7},{7,6},{8,9},{9,8},{10,11... | collective-permute-start | bytes 3538952 | tf_op jit(solution)/shard_map/ppermute | solution.py:792
  218.3 21.0 %collective-permute-start.24 = (bf16[4,2,192,384]{3,2,1,0:T(8,128)(2,1)}, bf16[4,2,192,384]{3,2,1,0:T(8,128)(2,1)}, u32[]{:S(2)}, u32[]{:S(2)}) collective-permute-start(bf16[4,2,192,384]{3,2,1,0:T(8,128)(2,1)} %get-tuple-element.374), channel_id=1, source_target_pairs={{0,1},{1,0},{2,3},{3,2},{4,5},{5,4},{6,7},{7,6},{8,9},{9,8},{10,11... | collective-permute-start | bytes 3538952 | tf_op jit(solution)/shard_map/ppermute | solution.py:792
  222.7 15.5 %collective-permute-start.25 = (bf16[4,192,384]{2,1,0:T(8,128)(2,1)}, bf16[4,192,384]{2,1,0:T(8,128)(2,1)S(1)}, u32[]{:S(2)}, u32[]{:S(2)}) collective-permute-start(bf16[4,192,384]{2,1,0:T(8,128)(2,1)} %get-tuple-element.379.refs_10_), channel_id=1, source_target_pairs={{0,4},{2,6},{4,0},{6,2},{1,5},{3,7},{5,1},{7,3},{8,12},{10,14},{12... | collective-permute-start | bytes 1769480 | tf_op jit(solution)/shard_map/ppermute | solution.py:792
  223.9 15.3 %collective-permute-start.26 = (bf16[4,192,384]{2,1,0:T(8,128)(2,1)}, bf16[4,192,384]{2,1,0:T(8,128)(2,1)}, u32[]{:S(2)}, u32[]{:S(2)}) collective-permute-start(bf16[4,192,384]{2,1,0:T(8,128)(2,1)} %get-tuple-element.380.refs_11_), channel_id=1, source_target_pairs={{0,2},{2,0},{4,6},{6,4},{1,3},{3,1},{5,7},{7,5},{8,10},{10,8},{12,... | collective-permute-start | bytes 1769480 | tf_op jit(solution)/shard_map/ppermute | solution.py:792
  244.2 14.6 %collective-permute-start.27 = (bf16[2,2,192,384]{3,2,1,0:T(8,128)(2,1)}, bf16[2,2,192,384]{3,2,1,0:T(8,128)(2,1)S(1)}, u32[]{:S(2)}, u32[]{:S(2)}) collective-permute-start(bf16[2,2,192,384]{3,2,1,0:T(8,128)(2,1)} %get-tuple-element.396.refs_10_), channel_id=1, source_target_pairs={{0,2},{2,0},{4,6},{6,4},{1,3},{3,1},{5,7},{7,5},{8,10},{10,8},{12,... | collective-permute-start | bytes 1769480 | tf_op jit(solution)/shard_map/ppermute | solution.py:792
  244.8 14.6 %collective-permute-start.28 = (bf16[2,2,192,384]{3,2,1,0:T(8,128)(2,1)}, bf16[2,2,192,384]{3,2,1,0:T(8,128)(2,1)}, u32[]{:S(2)}, u32[]{:S(2)}) collective-permute-start(bf16[2,2,192,384]{3,2,1,0:T(8,128)(2,1)} %get-tuple-element.397.refs_11_), channel_id=1, source_target_pairs={{0,4},{2,6},{4,0},{6,2},{1,5},{3,7},{5,1},{7,3},{8,12},{10,14},{12... | collective-permute-start | bytes 1769480 | tf_op jit(solution)/shard_map/ppermute | solution.py:792
  245.8 14.3 %collective-permute-start.29 = (bf16[4,192,384]{2,1,0:T(8,128)(2,1)}, bf16[4,192,384]{2,1,0:T(8,128)(2,1)}, u32[]{:S(2)}, u32[]{:S(2)}) collective-permute-start(bf16[4,192,384]{2,1,0:T(8,128)(2,1)} %get-tuple-element.398.refs_12_), channel_id=1, source_target_pairs={{0,8},{8,0},{16,24},{24,16},{1,9},{9,1},{17,25},{25,17},{2,10},{10... | collective-permute-start | bytes 1769480 | tf_op jit(solution)/shard_map/ppermute | solution.py:792
  260.1 22.0 %collective-permute-start.34 = (bf16[2,144,768]{2,1,0:T(8,128)(2,1)}, bf16[2,144,768]{2,1,0:T(8,128)(2,1)}, u32[]{:S(2)}, u32[]{:S(2)}) collective-permute-start(bf16[2,144,768]{2,1,0:T(8,128)(2,1)} %get-tuple-element.410), channel_id=1, source_target_pairs={{0,1},{1,0},{2,3},{3,2},{4,5},{5,4},{6,7},{7,6},{8,9},{9,8},{10,11... | collective-permute-start | bytes 1327112 | tf_op jit(solution)/shard_map/ppermute | solution.py:792
  263.4 13.4 %collective-permute-start.31 = (bf16[2,192,384]{2,1,0:T(8,128)(2,1)}, bf16[2,192,384]{2,1,0:T(8,128)(2,1)}, u32[]{:S(2)}, u32[]{:S(2)}) collective-permute-start(bf16[2,192,384]{2,1,0:T(8,128)(2,1)} %get-tuple-element.407.refs_10_), channel_id=1, source_target_pairs={{0,4},{2,6},{4,0},{6,2},{1,5},{3,7},{5,1},{7,3},{8,12},{10,14},{12... | collective-permute-start | bytes 884744 | tf_op jit(solution)/shard_map/ppermute | solution.py:792
  264.4 12.4 %collective-permute-start.32 = (bf16[2,192,384]{2,1,0:T(8,128)(2,1)}, bf16[2,192,384]{2,1,0:T(8,128)(2,1)}, u32[]{:S(2)}, u32[]{:S(2)}) collective-permute-start(bf16[2,192,384]{2,1,0:T(8,128)(2,1)} %get-tuple-element.408.refs_11_), channel_id=1, source_target_pairs={{0,2},{2,0},{4,6},{6,4},{1,3},{3,1},{5,7},{7,5},{8,10},{10,8},{12,... | collective-permute-start | bytes 884744 | tf_op jit(solution)/shard_map/ppermute | solution.py:792
  265.7 16.4 %collective-permute-start.33 = (bf16[4,96,384]{2,1,0:T(8,128)(2,1)}, bf16[4,96,384]{2,1,0:T(8,128)(2,1)}, u32[]{:S(2)}, u32[]{:S(2)}) collective-permute-start(bf16[4,96,384]{2,1,0:T(8,128)(2,1)} %get-tuple-element.409.refs_12_), channel_id=1, source_target_pairs={{0,16},{8,24},{16,0},{24,8},{1,17},{9,25},{17,1},{25,9},{2,18},{10... | collective-permute-start | bytes 884744 | tf_op jit(solution)/shard_map/ppermute | solution.py:792
  284.7 17.2 %collective-permute-start.35 = (bf16[4,96,384]{2,1,0:T(8,128)(2,1)}, bf16[4,96,384]{2,1,0:T(8,128)(2,1)}, u32[]{:S(2)}, u32[]{:S(2)}) collective-permute-start(bf16[4,96,384]{2,1,0:T(8,128)(2,1)} %get-tuple-element.430), channel_id=1, source_target_pairs={{0,8},{8,0},{16,24},{24,16},{1,9},{9,1},{17,25},{25,17},{2,10},{10... | collective-permute-start | bytes 884744 | tf_op jit(solution)/shard_map/ppermute | solution.py:792
  285.4 16.6 %collective-permute-start.37 = (bf16[4,96,384]{2,1,0:T(8,128)(2,1)}, bf16[4,96,384]{2,1,0:T(8,128)(2,1)}, u32[]{:S(2)}, u32[]{:S(2)}) collective-permute-start(bf16[4,96,384]{2,1,0:T(8,128)(2,1)} %get-tuple-element.432.refs_5_), channel_id=1, source_target_pairs={{0,16},{8,24},{16,0},{24,8},{1,17},{9,25},{17,1},{25,9},{2,18},{10... | collective-permute-start | bytes 884744 | tf_op jit(solution)/shard_map/ppermute | solution.py:792
  288.8 13.1 %collective-permute-start.36 = (f32[40,768]{1,0:T(8,128)}, f32[40,768]{1,0:T(8,128)}, u32[]{:S(2)}, u32[]{:S(2)}) collective-permute-start(f32[40,768]{1,0:T(8,128)} %get-tuple-element.431.refs_3_), channel_id=1, source_target_pairs={{0,8},{8,0},{16,24},{24,16},{1,9},{9,1},{17,25},{25,17},{2,10},{10... | collective-permute-start | bytes 368648 | tf_op jit(solution)/shard_map/ppermute | solution.py:792
  304.4 16.6 %collective-permute-start.38 = (bf16[4,96,384]{2,1,0:T(8,128)(2,1)}, bf16[4,96,384]{2,1,0:T(8,128)(2,1)S(1)}, u32[]{:S(2)}, u32[]{:S(2)}) collective-permute-start(bf16[4,96,384]{2,1,0:T(8,128)(2,1)} %get-tuple-element.440.refs_1_), channel_id=1, source_target_pairs={{0,16},{8,24},{16,0},{24,8},{1,17},{9,25},{17,1},{25,9},{2,18},{10... | collective-permute-start | bytes 884744 | tf_op jit(solution)/shard_map/ppermute | solution.py:792
  307.6 29.0 %collective-permute-start.44 = (bf16[4,192,384]{2,1,0:T(8,128)(2,1)}, bf16[4,192,384]{2,1,0:T(8,128)(2,1)S(1)}, u32[]{:S(2)}, u32[]{:S(2)}) collective-permute-start(bf16[4,192,384]{2,1,0:T(8,128)(2,1)} %get-tuple-element.453.refs_5_), channel_id=1, source_target_pairs={{0,8},{8,0},{16,24},{24,16},{1,9},{9,1},{17,25},{25,17},{2,10},{10... | collective-permute-start | bytes 1769480 | tf_op jit(solution)/shard_map/ppermute | solution.py:792
  323.7 12.9 %collective-permute-start.42 = (bf16[4,96,384]{2,1,0:T(8,128)(2,1)}, bf16[4,96,384]{2,1,0:T(8,128)(2,1)S(1)}, u32[]{:S(2)}, u32[]{:S(2)}) collective-permute-start(bf16[4,96,384]{2,1,0:T(8,128)(2,1)} %get-tuple-element.451.refs_1_), channel_id=1, source_target_pairs={{0,8},{8,0},{16,24},{24,16},{1,9},{9,1},{17,25},{25,17},{2,10},{10... | collective-permute-start | bytes 884744 | tf_op jit(solution)/shard_map/ppermute | solution.py:792
  (43 other events, 242.8 us)

commit v7 on v6

--- a/solution.py
+++ b/solution.py
@@ -276,6 +276,26 @@
     return single(
         cut_kernel, (spot, outer, expand, reduce), [SD((BIG, D), BF)], cost_estimate=cost(1e6, 3 * MB), name="cut"
     )[0]
+
+
+def halves_kernel(a_ref, b_ref, lower_ref, upper_ref):
+    lower_ref[...] = a_ref[...]
+    upper_ref[...] = b_ref[...]
+
+
+def halves_call(a, b):
+    rows, columns = a.shape
+    half = SD((rows // 2, columns), BF)
+    return pl.pallas_call(
+        halves_kernel,
+        grid=(1,),
+        in_specs=[full((rows // 2, columns)), pl.BlockSpec((rows // 2, columns), lambda i: (1, 0))],
+        out_specs=[full(half.shape), full(half.shape)],
+        out_shape=[half, half],
+        compiler_params=params(),
+        cost_estimate=cost(1e6, 3 * MB),
+        name="far_halves",
+    )(a, b)
 
 
 def prep_kernel(own_ref, gown_ref, recv_ref, alive_ref, pm_ref, tok_ref, g_ref, sum_ref):
@@ -1076,7 +1096,8 @@
     results.append(attend_call(1, spot, n1, in_bias, masks_1, in_at, in_plans[1], others_pieces, []))
     if quick:
         get_big, results, table_rows = fence(get_big, results, table_rows)
-        far = [swap(get_big[0][: BIG // 2], "shard", 2), swap(get_big[1][BIG // 2 :], "shard", 1)]
+        lower, upper_rows = halves_call(*get_big)
+        far = [swap(lower, "shard", 2), swap(upper_rows, "shard", 1)]
         big_back = [swap(v, "half", 1) for v in get_big]
     masks_2 = bias_call(2, table_rows)
     results.append(attend_call(2, spot, n1, in_bias, masks_2, in_at, in_plans[2], others_pieces, []))

time: 358 us -> 356 us (level)
  local copies, waits for them, and re-layouts: 9.96 us -> 5.18 us
    slice x2 -> x0, local copies, waits for them, and re-layouts: 3.94 us -> none  [the longest x1 1.97 us: shards(): get_big[0][:BIG // 2]]
  transfers between devices with their start and end apart: 48 -> 48, of which waited for: 20 -> 21; matrix products, arithmetic and copies ran while one was open for 3% -> 2% of each run, Pallas kernels for 39% -> 40%
where the time goes in v7:
time: 356 us; the launch traced here: 350 us
  Pallas kernels  238 us (67%)
  waiting for transfers between devices  53 us (15%)
  starting transfers between devices  45.8 us (13%)
  other arithmetic  7.08 us (2%)
  local copies, waits for them, and re-layouts  5.18 us (1%)
    pallas_call x21, Pallas kernels, run(): pl.pallas_call(body, in_specs=list(in_specs) + [any_space()] * len(after)...  146 us
    pallas_call x1, Pallas kernels, middle_call(): pl.pallas_call(body, grid_spec=grid_spec, out_shape=[SD((n, TOK, D), BF),...  68.6 us
    ppermute x48, waiting for transfers between devices, swap(): lax.ppermute(block, axis, [(i, i ^ bit) for i in range(count) if i ^ bit...  53 us
    ppermute x48, starting transfers between devices, swap(): lax.ppermute(block, axis, [(i, i ^ bit) for i in range(count) if i ^ bit...  45.8 us
    pallas_call x3, Pallas kernels, bias_call(): pl.pallas_call(bias_kernel, grid=(1,), in_specs=[pl.BlockSpec((HP, WIDE),...  12.1 us
  transfers between devices with their start and end apart: 48, of which 21 were waited for; matrix products, arithmetic and copies ran while one was open for 2% of the time, Pallas kernels for 40%

profile of v7, /device:TPU:0, one launch (start us, length us, event | category | flops | bytes accessed | tf_op | source)
XLA Modules:
  0.0 350.1 jit_solution(2439195738449597651)
XLA Ops:
  1.9 3.5 first.1
  13.5 4.0 %bias.3.refs_3_ = bf16[8,144,144]{2,1,0:T(8,128)(2,1)} custom-call(f32[24,640]{1,0:T(8,128)} %pad_convert_fusion.table_ref, bf16[384,144]{1,0:T(8,128)(2,1)} %constant.49.clone.sq_ref, bf16[144,192]{1,0:T(8,128)(2,1)} %constant.50.clone.sk_ref), custom_call_target="tpu_custom_call" | custom-call | flops 2000000 | bytes 2097 | tf_op jit(solution)/shard_map/bias/pallas_call | solution.py:165
  22.3 6.2 %prep.1 = (bf16[4,288,768]{2,1,0:T(8,128)(2,1)}, bf16[4,288,768]{2,1,0:T(8,128)(2,1)}, f32[1,768]{1,0:T(1,128)}) custom-call(bf16[4,288,768]{2,1,0:T(8,128)(2,1)} %bitcast.12, bf16[4,288,768]{2,1,0:T(8,128)(2,1)} %bitcast.14, bf16[8,144,768]{2,1,0:T(8,128)(2,1)} %collective-permute-done.2.refs_2_, f32[1,4]{1,0:T(1,128)} %convert_bitcast_fusion.refs_3_, ...), custom_call_target="tpu_custom_call" | custom-call | flops 3000000 | bytes 16777 | tf_op jit(solution)/shard_map/prep/pallas_call | solution.py:72
  28.5 5.0 %collective-permute-done.5.refs_8_ = bf16[96,1536]{1,0:T(8,128)(2,1)} collective-permute-done((bf16[96,1536]{1,0:T(8,128)(2,1)}, bf16[96,1536]{1,0:T(8,128)(2,1)}, u32[]{:S(2)}, u32[]{:S(2)}) %collective-permute-start.5) | collective-permute-done | bytes 294944 | tf_op jit(solution)/shard_map/ppermute | solution.py:812
  35.1 5.5 %vectors.1 = (f32[3,1,768]{2,1,0:T(1,128)}, f32[4,1,768]{2,1,0:T(1,128)}, f32[8,768]{1,0:T(8,128)}, bf16[4,288,768]{2,1,0:T(8,128)(2,1)}, bf16[768,1152]{1,0:T(8,128)(2,1)}) custom-call(s32[95]{0:T(128)} %dynamic-slice_bitcast_fusion.spot_ref.refs_0_.refs_5_.refs_9_, bf16[208,768]{1,0:T(8,128)(2,1)} %get-tuple-element.252.pa_ref.refs_6_, ...), custom_call_target="tpu_custom_call" | custom-call | flops 5000000 | bytes 8388 | tf_op jit(solution)/shard_map/vectors/pallas_call | solution.py:351
  44.0 12.5 %attend.3 = (bf16[4,288,768]{2,1,0:T(8,128)(2,1)}, bf16[4,2,8,144,144]{4,3,2,1,0:T(8,128)(2,1)}, bf16[4,288,256]{2,1,0:T(8,128)(2,1)}, f32[4,2,8,144]{3,2,1,0:T(8,128)}, bf16[768,768]{1,0:T(8,128)(2,1)}) custom-call(s32[95]{0:T(128)} %dynamic-slice_bitcast_fusion.spot_ref.refs_0_.refs_5_.refs_9_, bf16[4,288,768]{2,1,0:T(8,128)(2,1)} %get-tuple-element.274.refs_1_, ...), custom_call_target="tpu_custom_call" | custom-call | flops 13000000 | bytes 12582 | tf_op jit(solution)/shard_map/attend/pallas_call | solution.py:72
  56.6 4.2 %bias.4.refs_3_ = bf16[8,144,144]{2,1,0:T(8,128)(2,1)} custom-call(f32[24,640]{1,0:T(8,128)} %pad_convert_fusion.table_ref, bf16[384,144]{1,0:T(8,128)(2,1)} %constant.49.clone.sq_ref, bf16[144,192]{1,0:T(8,128)(2,1)} %constant.50.clone.sk_ref), custom_call_target="tpu_custom_call" | custom-call | flops 2000000 | bytes 2097 | tf_op jit(solution)/shard_map/bias/pallas_call | solution.py:165
  60.7 12.4 %attend.4 = (bf16[4,288,768]{2,1,0:T(8,128)(2,1)}, bf16[4,2,8,144,144]{4,3,2,1,0:T(8,128)(2,1)}, bf16[4,288,256]{2,1,0:T(8,128)(2,1)}, f32[4,2,8,144]{3,2,1,0:T(8,128)}, bf16[768,768]{1,0:T(8,128)(2,1)}) custom-call(s32[95]{0:T(128)} %dynamic-slice_bitcast_fusion.spot_ref.refs_0_.refs_5_.refs_9_, bf16[4,288,768]{2,1,0:T(8,128)(2,1)} %get-tuple-element.274.refs_1_, ...), custom_call_target="tpu_custom_call" | custom-call | flops 13000000 | bytes 12582 | tf_op jit(solution)/shard_map/attend/pallas_call | solution.py:72
  77.9 4.0 %bias.5.refs_3_ = bf16[8,144,144]{2,1,0:T(8,128)(2,1)} custom-call(f32[24,640]{1,0:T(8,128)} %pad_convert_fusion.table_ref, bf16[384,144]{1,0:T(8,128)(2,1)} %constant.49.clone.sq_ref, bf16[144,192]{1,0:T(8,128)(2,1)} %constant.50.clone.sk_ref), custom_call_target="tpu_custom_call" | custom-call | flops 2000000 | bytes 2097 | tf_op jit(solution)/shard_map/bias/pallas_call | solution.py:165
  81.9 12.4 %attend.5 = (bf16[4,288,768]{2,1,0:T(8,128)(2,1)}, bf16[4,2,8,144,144]{4,3,2,1,0:T(8,128)(2,1)}, bf16[4,288,256]{2,1,0:T(8,128)(2,1)}, f32[4,2,8,144]{3,2,1,0:T(8,128)}, bf16[768,768]{1,0:T(8,128)(2,1)}) custom-call(s32[95]{0:T(128)} %dynamic-slice_bitcast_fusion.spot_ref.refs_0_.refs_5_.refs_9_, bf16[4,288,768]{2,1,0:T(8,128)(2,1)} %get-tuple-element.274.refs_1_, ...), custom_call_target="tpu_custom_call" | custom-call | flops 13000000 | bytes 12582 | tf_op jit(solution)/shard_map/attend/pallas_call | solution.py:72
  98.1 68.6 %middle.1 = (bf16[4,144,768]{2,1,0:T(8,128)(2,1)}, bf16[4,144,768]{2,1,0:T(8,128)(2,1)}, bf16[4,288,768]{2,1,0:T(8,128)(2,1)}, bf16[4,288,768]{2,1,0:T(8,128)(2,...) custom-call(s32[95]{0:T(128)} %dynamic-slice_bitcast_fusion.spot_ref, ...), custom_call_target="tpu_custom_call" | custom-call | flops 60000000 | bytes 41943 | tf_op jit(solution)/shard_map/middle/pallas_call | solution.py:587
  167.4 9.3 %attend_back.3 = (bf16[4,288,768]{2,1,0:T(8,128)(2,1)}, f32[8,144,144]{2,1,0:T(8,128)}) custom-call(bf16[4,288,768]{2,1,0:T(8,128)(2,1)} %get-tuple-element.351.refs_0_, bf16[4,2,8,144,144]{4,3,2,1,0:T(8,128)(2,1)} %get-tuple-element.352.refs_1_, bf16[4,288,768]{2,1,0:T(8,128)(2,1)} %get-tuple-element.353.refs_2_), custom_call_target="tpu_custom_call" | custom-call | flops 18000000 | bytes 10485 | tf_op jit(solution)/shard_map/attend_back/pallas_call | solution.py:72
  176.7 6.5 %hop.8 = (bf16[2,4,192,384]{3,2,1,0:T(8,128)(2,1)}, bf16[2,4,192,384]{3,2,1,0:T(8,128)(2,1)}, bf16[2,4,192,384]{3,2,1,0:T(8,128)(2,1)}, bf16[2,4,192,384]{3,2,1,0:T(8,128)(2,1)}) custom-call(s32[95]{0:T(128)} %dynamic-slice_bitcast_fusion.spot_ref.refs_0_.refs_5_.refs_9_, bf16[4,4,192,384]{3,2,1,0:T(8,128)(2,1)} %get-tuple-element.361.refs_1_, ...), custom_call_target="tpu_custom_call" | custom-call | flops 10000 | bytes 4194 | tf_op jit(solution)/shard_map/hop/pallas_call | solution.py:72
  185.3 9.3 %attend_back.4 = (bf16[4,288,768]{2,1,0:T(8,128)(2,1)}, f32[8,144,144]{2,1,0:T(8,128)}) custom-call(bf16[4,288,768]{2,1,0:T(8,128)(2,1)} %get-tuple-element.359.refs_0_, bf16[4,2,8,144,144]{4,3,2,1,0:T(8,128)(2,1)} %get-tuple-element.360.refs_1_, bf16[4,288,768]{2,1,0:T(8,128)(2,1)} %get-tuple-element.353.refs_2_, ...), custom_call_target="tpu_custom_call" | custom-call | flops 18000000 | bytes 10485 | tf_op jit(solution)/shard_map/attend_back/pallas_call | solution.py:72
  194.6 9.3 %attend_back.5 = (bf16[4,288,768]{2,1,0:T(8,128)(2,1)}, f32[8,144,144]{2,1,0:T(8,128)}) custom-call(bf16[4,288,768]{2,1,0:T(8,128)(2,1)} %get-tuple-element.368.refs_0_, bf16[4,2,8,144,144]{4,3,2,1,0:T(8,128)(2,1)} %get-tuple-element.369.refs_1_, bf16[4,288,768]{2,1,0:T(8,128)(2,1)} %get-tuple-element.353.refs_2_, ...), custom_call_target="tpu_custom_call" | custom-call | flops 18000000 | bytes 10485 | tf_op jit(solution)/shard_map/attend_back/pallas_call | solution.py:72
  204.0 12.2 %inner_grad.1 = (bf16[4,2,192,384]{3,2,1,0:T(8,128)(2,1)}, bf16[4,2,192,384]{3,2,1,0:T(8,128)(2,1)}, bf16[4,2,192,384]{3,2,1,0:T(8,128)(2,1)}, bf16[4,2,192,384]{3,2,1,0:T(8,128)(2,1)}, f32[3,1,768]{2,1,0:T(1,128)}) custom-call(s32[95]{0:T(128)} %dynamic-slice_bitcast_fusion.spot_ref.refs_0_.refs_5_.refs_9_, bf16[768,1152]{1,0:T(8,128)(2,1)} %get-tuple-element.284.refs_1_, ...), custom_call_target="tpu_custom_call" | custom-call | flops 12000000 | bytes 12582 | tf_op jit(solution)/shard_map/inner_grad/pallas_call | solution.py:72
  216.8 3.9 %hop.9 = (bf16[4,192,384]{2,1,0:T(8,128)(2,1)}, bf16[4,192,384]{2,1,0:T(8,128)(2,1)}, bf16[4,192,384]{2,1,0:T(8,128)(2,1)}, bf16[4,192,384]{2,1,0:T(8,128)(2,1)}) custom-call(s32[95]{0:T(128)} %dynamic-slice_bitcast_fusion.spot_ref.refs_0_.refs_5_.refs_9_, bf16[2,4,192,384]{3,2,1,0:T(8,128)(2,1)} %get-tuple-element.379.refs_1_, ...), custom_call_target="tpu_custom_call" | custom-call | flops 10000 | bytes 4194 | tf_op jit(solution)/shard_map/hop/pallas_call | solution.py:72
  222.7 8.3 %last.2 = (f32[8,768]{1,0:T(8,128)}, bf16[2,144,768]{2,1,0:T(8,128)(2,1)}, bf16[2,144,768]{2,1,0:T(8,128)(2,1)}) custom-call(bf16[4,288,768]{2,1,0:T(8,128)(2,1)} %get-tuple-element.268.tok_ref.refs_1_.refs_0_, bf16[4,288,768]{2,1,0:T(8,128)(2,1)} %get-tuple-element.385.refs_1_, f32[8,768]{1,0:T(8,128)} %get-tuple-element.343.refs_7_.refs_2_, ...), custom_call_target="tpu_custom_call" | custom-call | flops 20000000 | bytes 20971 | tf_op jit(solution)/shard_map/last/pallas_call | solution.py:72
  231.0 5.2 %collective-permute-done.25.refs_7_ = bf16[4,192,384]{2,1,0:T(8,128)(2,1)S(1)} collective-permute-done((bf16[4,192,384]{2,1,0:T(8,128)(2,1)}, bf16[4,192,384]{2,1,0:T(8,128)(2,1)S(1)}, u32[]{:S(2)}, u32[]{:S(2)}) %collective-permute-start.25) | collective-permute-done | bytes 589856 | tf_op jit(solution)/shard_map/ppermute | solution.py:812
  237.2 5.0 %hop.10 = (bf16[2,2,192,384]{3,2,1,0:T(8,128)(2,1)}, bf16[2,2,192,384]{3,2,1,0:T(8,128)(2,1)}, bf16[2,2,192,384]{3,2,1,0:T(8,128)(2,1)}, bf16[2,2,192,384]{3,2,1...) custom-call(s32[95]{0:T(128)} %dynamic-slice_bitcast_fusion.spot_ref.refs_0_.refs_5_.refs_9_, ...), custom_call_target="tpu_custom_call" | custom-call | flops 10000 | bytes 4194 | tf_op jit(solution)/shard_map/hop/pallas_call | solution.py:72
  245.5 8.3 %last.3 = (f32[8,768]{1,0:T(8,128)}, bf16[2,144,768]{2,1,0:T(8,128)(2,1)}, bf16[2,144,768]{2,1,0:T(8,128)(2,1)}) custom-call(bf16[4,288,768]{2,1,0:T(8,128)(2,1)} %get-tuple-element.268.tok_ref.refs_1_.refs_0_, bf16[4,288,768]{2,1,0:T(8,128)(2,1)} %get-tuple-element.385.refs_1_, f32[8,768]{1,0:T(8,128)} %get-tuple-element.343.refs_7_.refs_2_, ...), custom_call_target="tpu_custom_call" | custom-call | flops 20000000 | bytes 20971 | tf_op jit(solution)/shard_map/last/pallas_call | solution.py:72
  253.9 2.9 collective-permute-done.27.refs_3_
  258.3 3.3 hop.11
  267.0 7.8 %table.1.refs_5_ = f32[40,768]{1,0:T(8,128)} custom-call(f32[8,144,144]{2,1,0:T(8,128)} %get-tuple-element.420.refs_0_, f32[8,144,144]{2,1,0:T(8,128)} %get-tuple-element.421.refs_1_, f32[8,144,144]{2,1,0:T(8,128)} %get-tuple-element.422.refs_2_, f32[4,1,768]{2,1,0:T(1,128)} %get-tuple-element.423.refs_3_, f32[1,768]{1,0:T(1,128)} %get-tuple-element.424.refs_4_, ...), custom_call_target="tpu_custom_call" | custom-call | flops 6000000 | bytes 4194 | tf_op jit(solution)/shard_map/table/pallas_call | solution.py:72
  274.8 5.3 %collective-permute-done.33.refs_9_ = bf16[4,96,384]{2,1,0:T(8,128)(2,1)} collective-permute-done((bf16[4,96,384]{2,1,0:T(8,128)(2,1)}, bf16[4,96,384]{2,1,0:T(8,128)(2,1)}, u32[]{:S(2)}, u32[]{:S(2)}) %collective-permute-start.33) | collective-permute-done | bytes 294944 | tf_op jit(solution)/shard_map/ppermute | solution.py:812
  283.3 3.4 collective-permute-start.37
  289.2 10.6 %collective-permute-done.36.refs_4_ = f32[40,768]{1,0:T(8,128)} collective-permute-done((f32[40,768]{1,0:T(8,128)}, f32[40,768]{1,0:T(8,128)}, u32[]{:S(2)}, u32[]{:S(2)}) %collective-permute-start.36) | collective-permute-done | bytes 122912 | tf_op jit(solution)/shard_map/ppermute | solution.py:812
  302.3 3.3 collective-permute-start.38
  322.3 3.3 collective-permute-start.43
  325.6 7.8 %collective-permute-done.43.refs_4_ = f32[40,768]{1,0:T(8,128)S(1)} collective-permute-done((f32[40,768]{1,0:T(8,128)}, f32[40,768]{1,0:T(8,128)S(1)}, u32[]{:S(2)}, u32[]{:S(2)}) %collective-permute-start.43) | collective-permute-done | bytes 122912 | tf_op jit(solution)/shard_map/ppermute | solution.py:812
  339.5 3.2 collective-permute-done.45.refs_2_
  343.5 6.3 %finish.1 = (f32[384]{0:T(512)}, f32[192]{0:T(256)}, f32[768]{0:T(1024)}, f32[192]{0:T(256)}, f32[192]{0:T(256)}, /*index=5*/f32[192]{0:T(256)}, f32[192]{0:T(25...) custom-call(s32[95]{0:T(128)} %dynamic-slice_bitcast_fusion.spot_ref, ...), custom_call_target="tpu_custom_call" | custom-call | flops 10000 | bytes 12582 | tf_op jit(solution)/shard_map/finish/pallas_call | solution.py:72
  (151 shorter events, 76.3 us)
Async XLA Ops:
  5.4 12.9 %collective-permute-start.2 = (bf16[8,144,768]{2,1,0:T(8,128)(2,1)}, bf16[8,144,768]{2,1,0:T(8,128)(2,1)}, u32[]{:S(2)}, u32[]{:S(2)}) collective-permute-start(bf16[8,144,768]{2,1,0:T(8,128)(2,1)} %get-tuple-element.253), channel_id=1, source_target_pairs={{0,1},{1,0},{2,3},{3,2},{4,5},{5,4},{6,7},{7,6},{8,9},{9,8},{10,11... | collective-permute-start | bytes 5308424 | tf_op jit(solution)/shard_map/ppermute | solution.py:812
  18.3 15.2 %collective-permute-start.3 = (bf16[208,768]{1,0:T(8,128)(2,1)S(1)}, bf16[208,768]{1,0:T(8,128)(2,1)S(1)}, u32[]{:S(2)}, u32[]{:S(2)}) collective-permute-start(bf16[208,768]{1,0:T(8,128)(2,1)S(1)} %collective-permute-done.pb_ref.refs_7_), channel_id=1, source_target_pairs={{0,4},{2,6},{4,0},{6,2},{1,5},{3,7},{5,1},{7,3},{8,12},{10,14},{12... | collective-permute-start | bytes 958472 | tf_op jit(solution)/shard_map/ppermute | solution.py:812
  18.6 14.8 %collective-permute-start.5 = (bf16[96,1536]{1,0:T(8,128)(2,1)}, bf16[96,1536]{1,0:T(8,128)(2,1)}, u32[]{:S(2)}, u32[]{:S(2)}) collective-permute-start(bf16[96,1536]{1,0:T(8,128)(2,1)} %get-tuple-element.258), channel_id=1, source_target_pairs={{0,4},{2,6},{4,0},{6,2},{1,5},{3,7},{5,1},{7,3},{8,12},{10,14},{12... | collective-permute-start | bytes 884744 | tf_op jit(solution)/shard_map/ppermute | solution.py:812
  20.3 13.2 %collective-permute-start.4 = (bf16[96,1536]{1,0:T(8,128)(2,1)}, bf16[96,1536]{1,0:T(8,128)(2,1)}, u32[]{:S(2)}, u32[]{:S(2)}) collective-permute-start(bf16[96,1536]{1,0:T(8,128)(2,1)} %get-tuple-element.258), channel_id=1, source_target_pairs={{0,2},{2,0},{4,6},{6,4},{1,3},{3,1},{5,7},{7,5},{8,10},{10,8},{12,... | collective-permute-start | bytes 884744 | tf_op jit(solution)/shard_map/ppermute | solution.py:812
  41.1 32.0 %collective-permute-start.11 = (bf16[864,768]{1,0:T(8,128)(2,1)}, bf16[864,768]{1,0:T(8,128)(2,1)}, u32[]{:S(2)}, u32[]{:S(2)}) collective-permute-start(bf16[864,768]{1,0:T(8,128)(2,1)} %cut.1), channel_id=1, source_target_pairs={{0,4},{2,6},{4,0},{6,2},{1,5},{3,7},{5,1},{7,3},{8,12},{10,14},{12... | collective-permute-start | bytes 3981320 | tf_op jit(solution)/shard_map/ppermute | solution.py:812
  42.1 31.0 %collective-permute-start.10 = (bf16[864,768]{1,0:T(8,128)(2,1)}, bf16[864,768]{1,0:T(8,128)(2,1)}, u32[]{:S(2)}, u32[]{:S(2)}) collective-permute-start(bf16[864,768]{1,0:T(8,128)(2,1)} %cut.1), channel_id=1, source_target_pairs={{0,2},{2,0},{4,6},{6,4},{1,3},{3,1},{5,7},{7,5},{8,10},{10,8},{12,... | collective-permute-start | bytes 3981320 | tf_op jit(solution)/shard_map/ppermute | solution.py:812
  43.5 13.0 %collective-permute-start.7 = (bf16[96,1536]{1,0:T(8,128)(2,1)}, bf16[96,1536]{1,0:T(8,128)(2,1)S(1)}, u32[]{:S(2)}, u32[]{:S(2)}) collective-permute-start(bf16[96,1536]{1,0:T(8,128)(2,1)} %collective-permute-done.4.refs_7_), channel_id=1, source_target_pairs={{0,1},{1,0},{2,3},{3,2},{4,5},{5,4},{6,7},{7,6},{8,9},{9,8},{10,11... | collective-permute-start | bytes 884744 | tf_op jit(solution)/shard_map/ppermute | solution.py:812
  43.5 13.1 %collective-permute-start.8 = (bf16[96,1536]{1,0:T(8,128)(2,1)}, bf16[96,1536]{1,0:T(8,128)(2,1)S(1)}, u32[]{:S(2)}, u32[]{:S(2)}) collective-permute-start(bf16[96,1536]{1,0:T(8,128)(2,1)} %collective-permute-done.5.refs_8_), channel_id=1, source_target_pairs={{0,1},{1,0},{2,3},{3,2},{4,5},{5,4},{6,7},{7,6},{8,9},{9,8},{10,11... | collective-permute-start | bytes 884744 | tf_op jit(solution)/shard_map/ppermute | solution.py:812
  44.0 12.6 %collective-permute-start.9 = (bf16[96,1536]{1,0:T(8,128)(2,1)S(1)}, bf16[96,1536]{1,0:T(8,128)(2,1)}, u32[]{:S(2)}, u32[]{:S(2)}) collective-permute-start(bf16[96,1536]{1,0:T(8,128)(2,1)S(1)} %collective-permute-done.6.refs_9_), channel_id=1, source_target_pairs={{0,1},{1,0},{2,3},{3,2},{4,5},{5,4},{6,7},{7,6},{8,9},{9,8},{10,11... | collective-permute-start | bytes 884744 | tf_op jit(solution)/shard_map/ppermute | solution.py:812
  73.1 21.5 %collective-permute-start.14 = (bf16[864,768]{1,0:T(8,128)(2,1)}, bf16[864,768]{1,0:T(8,128)(2,1)}, u32[]{:S(2)}, u32[]{:S(2)}) collective-permute-start(bf16[864,768]{1,0:T(8,128)(2,1)} %collective-permute-done.10.a_ref.refs_13_), channel_id=1, source_target_pairs={{0,1},{1,0},{2,3},{3,2},{4,5},{5,4},{6,7},{7,6},{8,9},{9,8},{10,11... | collective-permute-start | bytes 3981320 | tf_op jit(solution)/shard_map/ppermute | solution.py:812
  73.7 20.9 %collective-permute-start.15 = (bf16[864,768]{1,0:T(8,128)(2,1)}, bf16[864,768]{1,0:T(8,128)(2,1)}, u32[]{:S(2)}, u32[]{:S(2)}) collective-permute-start(bf16[864,768]{1,0:T(8,128)(2,1)} %collective-permute-done.11.b_ref.refs_14_), channel_id=1, source_target_pairs={{0,1},{1,0},{2,3},{3,2},{4,5},{5,4},{6,7},{7,6},{8,9},{9,8},{10,11... | collective-permute-start | bytes 3981320 | tf_op jit(solution)/shard_map/ppermute | solution.py:812
  76.2 18.1 %collective-permute-start.12 = (bf16[432,768]{1,0:T(8,128)(2,1)}, bf16[432,768]{1,0:T(8,128)(2,1)S(1)}, u32[]{:S(2)}, u32[]{:S(2)}) collective-permute-start(bf16[432,768]{1,0:T(8,128)(2,1)} %get-tuple-element.304), channel_id=1, source_target_pairs={{0,4},{2,6},{4,0},{6,2},{1,5},{3,7},{5,1},{7,3},{8,12},{10,14},{12... | collective-permute-start | bytes 1990664 | tf_op jit(solution)/shard_map/ppermute | solution.py:812
  77.3 17.3 %collective-permute-start.13 = (bf16[432,768]{1,0:T(8,128)(2,1)}, bf16[432,768]{1,0:T(8,128)(2,1)}, u32[]{:S(2)}, u32[]{:S(2)}) collective-permute-start(bf16[432,768]{1,0:T(8,128)(2,1)} %get-tuple-element.305), channel_id=1, source_target_pairs={{0,2},{2,0},{4,6},{6,4},{1,3},{3,1},{5,7},{7,5},{8,10},{10,8},{12,... | collective-permute-start | bytes 1990664 | tf_op jit(solution)/shard_map/ppermute | solution.py:812
  183.2 33.0 %collective-permute-start.21 = (bf16[2,4,192,384]{3,2,1,0:T(8,128)(2,1)}, bf16[2,4,192,384]{3,2,1,0:T(8,128)(2,1)}, u32[]{:S(2)}, u32[]{:S(2)}) collective-permute-start(bf16[2,4,192,384]{3,2,1,0:T(8,128)(2,1)} %get-tuple-element.365.refs_3_), channel_id=1, source_target_pairs={{0,2},{2,0},{4,6},{6,4},{1,3},{3,1},{5,7},{7,5},{8,10},{10,8},{12,... | collective-permute-start | bytes 3538952 | tf_op jit(solution)/shard_map/ppermute | solution.py:812
  184.5 31.7 %collective-permute-start.22 = (bf16[2,4,192,384]{3,2,1,0:T(8,128)(2,1)}, bf16[2,4,192,384]{3,2,1,0:T(8,128)(2,1)}, u32[]{:S(2)}, u32[]{:S(2)}) collective-permute-start(bf16[2,4,192,384]{3,2,1,0:T(8,128)(2,1)} %get-tuple-element.366.refs_4_), channel_id=1, source_target_pairs={{0,4},{2,6},{4,0},{6,2},{1,5},{3,7},{5,1},{7,3},{8,12},{10,14},{12... | collective-permute-start | bytes 3538952 | tf_op jit(solution)/shard_map/ppermute | solution.py:812
  216.2 21.0 %collective-permute-start.23 = (bf16[4,2,192,384]{3,2,1,0:T(8,128)(2,1)}, bf16[4,2,192,384]{3,2,1,0:T(8,128)(2,1)}, u32[]{:S(2)}, u32[]{:S(2)}) collective-permute-start(bf16[4,2,192,384]{3,2,1,0:T(8,128)(2,1)} %get-tuple-element.377), channel_id=1, source_target_pairs={{0,1},{1,0},{2,3},{3,2},{4,5},{5,4},{6,7},{7,6},{8,9},{9,8},{10,11... | collective-permute-start | bytes 3538952 | tf_op jit(solution)/shard_map/ppermute | solution.py:812
  216.3 20.9 %collective-permute-start.24 = (bf16[4,2,192,384]{3,2,1,0:T(8,128)(2,1)}, bf16[4,2,192,384]{3,2,1,0:T(8,128)(2,1)}, u32[]{:S(2)}, u32[]{:S(2)}) collective-permute-start(bf16[4,2,192,384]{3,2,1,0:T(8,128)(2,1)} %get-tuple-element.378), channel_id=1, source_target_pairs={{0,1},{1,0},{2,3},{3,2},{4,5},{5,4},{6,7},{7,6},{8,9},{9,8},{10,11... | collective-permute-start | bytes 3538952 | tf_op jit(solution)/shard_map/ppermute | solution.py:812
  220.7 15.5 %collective-permute-start.25 = (bf16[4,192,384]{2,1,0:T(8,128)(2,1)}, bf16[4,192,384]{2,1,0:T(8,128)(2,1)S(1)}, u32[]{:S(2)}, u32[]{:S(2)}) collective-permute-start(bf16[4,192,384]{2,1,0:T(8,128)(2,1)} %get-tuple-element.383.refs_10_), channel_id=1, source_target_pairs={{0,4},{2,6},{4,0},{6,2},{1,5},{3,7},{5,1},{7,3},{8,12},{10,14},{12... | collective-permute-start | bytes 1769480 | tf_op jit(solution)/shard_map/ppermute | solution.py:812
  221.9 15.3 %collective-permute-start.26 = (bf16[4,192,384]{2,1,0:T(8,128)(2,1)}, bf16[4,192,384]{2,1,0:T(8,128)(2,1)}, u32[]{:S(2)}, u32[]{:S(2)}) collective-permute-start(bf16[4,192,384]{2,1,0:T(8,128)(2,1)} %get-tuple-element.384.refs_11_), channel_id=1, source_target_pairs={{0,2},{2,0},{4,6},{6,4},{1,3},{3,1},{5,7},{7,5},{8,10},{10,8},{12,... | collective-permute-start | bytes 1769480 | tf_op jit(solution)/shard_map/ppermute | solution.py:812
  242.2 14.6 %collective-permute-start.27 = (bf16[2,2,192,384]{3,2,1,0:T(8,128)(2,1)}, bf16[2,2,192,384]{3,2,1,0:T(8,128)(2,1)S(1)}, u32[]{:S(2)}, u32[]{:S(2)}) collective-permute-start(bf16[2,2,192,384]{3,2,1,0:T(8,128)(2,1)} %get-tuple-element.400.refs_10_), channel_id=1, source_target_pairs={{0,2},{2,0},{4,6},{6,4},{1,3},{3,1},{5,7},{7,5},{8,10},{10,8},{12,... | collective-permute-start | bytes 1769480 | tf_op jit(solution)/shard_map/ppermute | solution.py:812
  243.0 14.4 %collective-permute-start.28 = (bf16[2,2,192,384]{3,2,1,0:T(8,128)(2,1)}, bf16[2,2,192,384]{3,2,1,0:T(8,128)(2,1)}, u32[]{:S(2)}, u32[]{:S(2)}) collective-permute-start(bf16[2,2,192,384]{3,2,1,0:T(8,128)(2,1)} %get-tuple-element.401.refs_11_), channel_id=1, source_target_pairs={{0,4},{2,6},{4,0},{6,2},{1,5},{3,7},{5,1},{7,3},{8,12},{10,14},{12... | collective-permute-start | bytes 1769480 | tf_op jit(solution)/shard_map/ppermute | solution.py:812
  244.0 14.3 %collective-permute-start.29 = (bf16[4,192,384]{2,1,0:T(8,128)(2,1)}, bf16[4,192,384]{2,1,0:T(8,128)(2,1)}, u32[]{:S(2)}, u32[]{:S(2)}) collective-permute-start(bf16[4,192,384]{2,1,0:T(8,128)(2,1)} %get-tuple-element.402.refs_12_), channel_id=1, source_target_pairs={{0,8},{8,0},{16,24},{24,16},{1,9},{9,1},{17,25},{25,17},{2,10},{10... | collective-permute-start | bytes 1769480 | tf_op jit(solution)/shard_map/ppermute | solution.py:812
  258.3 21.8 %collective-permute-start.34 = (bf16[2,144,768]{2,1,0:T(8,128)(2,1)}, bf16[2,144,768]{2,1,0:T(8,128)(2,1)}, u32[]{:S(2)}, u32[]{:S(2)}) collective-permute-start(bf16[2,144,768]{2,1,0:T(8,128)(2,1)} %get-tuple-element.414), channel_id=1, source_target_pairs={{0,1},{1,0},{2,3},{3,2},{4,5},{5,4},{6,7},{7,6},{8,9},{9,8},{10,11... | collective-permute-start | bytes 1327112 | tf_op jit(solution)/shard_map/ppermute | solution.py:812
  261.6 13.2 %collective-permute-start.31 = (bf16[2,192,384]{2,1,0:T(8,128)(2,1)}, bf16[2,192,384]{2,1,0:T(8,128)(2,1)}, u32[]{:S(2)}, u32[]{:S(2)}) collective-permute-start(bf16[2,192,384]{2,1,0:T(8,128)(2,1)} %get-tuple-element.411.refs_10_), channel_id=1, source_target_pairs={{0,4},{2,6},{4,0},{6,2},{1,5},{3,7},{5,1},{7,3},{8,12},{10,14},{12... | collective-permute-start | bytes 884744 | tf_op jit(solution)/shard_map/ppermute | solution.py:812
  262.5 12.3 %collective-permute-start.32 = (bf16[2,192,384]{2,1,0:T(8,128)(2,1)}, bf16[2,192,384]{2,1,0:T(8,128)(2,1)}, u32[]{:S(2)}, u32[]{:S(2)}) collective-permute-start(bf16[2,192,384]{2,1,0:T(8,128)(2,1)} %get-tuple-element.412.refs_11_), channel_id=1, source_target_pairs={{0,2},{2,0},{4,6},{6,4},{1,3},{3,1},{5,7},{7,5},{8,10},{10,8},{12,... | collective-permute-start | bytes 884744 | tf_op jit(solution)/shard_map/ppermute | solution.py:812
  263.7 16.4 %collective-permute-start.33 = (bf16[4,96,384]{2,1,0:T(8,128)(2,1)}, bf16[4,96,384]{2,1,0:T(8,128)(2,1)}, u32[]{:S(2)}, u32[]{:S(2)}) collective-permute-start(bf16[4,96,384]{2,1,0:T(8,128)(2,1)} %get-tuple-element.413.refs_12_), channel_id=1, source_target_pairs={{0,16},{8,24},{16,0},{24,8},{1,17},{9,25},{17,1},{25,9},{2,18},{10... | collective-permute-start | bytes 884744 | tf_op jit(solution)/shard_map/ppermute | solution.py:812
  282.7 17.2 %collective-permute-start.35 = (bf16[4,96,384]{2,1,0:T(8,128)(2,1)}, bf16[4,96,384]{2,1,0:T(8,128)(2,1)}, u32[]{:S(2)}, u32[]{:S(2)}) collective-permute-start(bf16[4,96,384]{2,1,0:T(8,128)(2,1)} %get-tuple-element.434), channel_id=1, source_target_pairs={{0,8},{8,0},{16,24},{24,16},{1,9},{9,1},{17,25},{25,17},{2,10},{10... | collective-permute-start | bytes 884744 | tf_op jit(solution)/shard_map/ppermute | solution.py:812
  283.3 16.6 %collective-permute-start.37 = (bf16[4,96,384]{2,1,0:T(8,128)(2,1)}, bf16[4,96,384]{2,1,0:T(8,128)(2,1)}, u32[]{:S(2)}, u32[]{:S(2)}) collective-permute-start(bf16[4,96,384]{2,1,0:T(8,128)(2,1)} %get-tuple-element.436.refs_5_), channel_id=1, source_target_pairs={{0,16},{8,24},{16,0},{24,8},{1,17},{9,25},{17,1},{25,9},{2,18},{10... | collective-permute-start | bytes 884744 | tf_op jit(solution)/shard_map/ppermute | solution.py:812
  286.7 13.1 %collective-permute-start.36 = (f32[40,768]{1,0:T(8,128)}, f32[40,768]{1,0:T(8,128)}, u32[]{:S(2)}, u32[]{:S(2)}) collective-permute-start(f32[40,768]{1,0:T(8,128)} %get-tuple-element.435.refs_3_), channel_id=1, source_target_pairs={{0,8},{8,0},{16,24},{24,16},{1,9},{9,1},{17,25},{25,17},{2,10},{10... | collective-permute-start | bytes 368648 | tf_op jit(solution)/shard_map/ppermute | solution.py:812
  302.3 16.6 %collective-permute-start.38 = (bf16[4,96,384]{2,1,0:T(8,128)(2,1)}, bf16[4,96,384]{2,1,0:T(8,128)(2,1)S(1)}, u32[]{:S(2)}, u32[]{:S(2)}) collective-permute-start(bf16[4,96,384]{2,1,0:T(8,128)(2,1)} %get-tuple-element.444.refs_1_), channel_id=1, source_target_pairs={{0,16},{8,24},{16,0},{24,8},{1,17},{9,25},{17,1},{25,9},{2,18},{10... | collective-permute-start | bytes 884744 | tf_op jit(solution)/shard_map/ppermute | solution.py:812
  305.5 29.0 %collective-permute-start.44 = (bf16[4,192,384]{2,1,0:T(8,128)(2,1)}, bf16[4,192,384]{2,1,0:T(8,128)(2,1)S(1)}, u32[]{:S(2)}, u32[]{:S(2)}) collective-permute-start(bf16[4,192,384]{2,1,0:T(8,128)(2,1)} %get-tuple-element.457.refs_5_), channel_id=1, source_target_pairs={{0,8},{8,0},{16,24},{24,16},{1,9},{9,1},{17,25},{25,17},{2,10},{10... | collective-permute-start | bytes 1769480 | tf_op jit(solution)/shard_map/ppermute | solution.py:812
  321.6 12.9 %collective-permute-start.42 = (bf16[4,96,384]{2,1,0:T(8,128)(2,1)}, bf16[4,96,384]{2,1,0:T(8,128)(2,1)S(1)}, u32[]{:S(2)}, u32[]{:S(2)}) collective-permute-start(bf16[4,96,384]{2,1,0:T(8,128)(2,1)} %get-tuple-element.455.refs_1_), channel_id=1, source_target_pairs={{0,8},{8,0},{16,24},{24,16},{1,9},{9,1},{17,25},{25,17},{2,10},{10... | collective-permute-start | bytes 884744 | tf_op jit(solution)/shard_map/ppermute | solution.py:812
  (42 other events, 240.4 us)
